TPU v7x, 32 devices: a whole 2x2x4 slice. The times are simulated.
32 devices in a mesh: dp: 16 (over z, y, core), tensor: 2 (over x).
Axes of the slice: x: 2, y: 2, z: 4, core: 2. Of those that a mesh axis runs over, the one named last changes fastest.
Arguments:
- tokens: bfloat16 [6, 1024, 2048], P(None, 'dp'), may hold values from -6 to 6
- cotangent: bfloat16 [6, 1024, 2048], P(None, 'dp'), may hold values from -6 to 6
- active: int32 [3, 2], replicated, may hold values from 0 to 1, as said below
- assignment: int32 [6], replicated, may hold values from 0 to 5, each once
- attention_gain: bfloat16 [2048], P('dp'), may hold values from 0.099609375 to 1.8984375
- query_weight: bfloat16 [2048, 2048], P('dp', 'tensor'), may hold values from -0.1875 to 0.1875
- key_weight: bfloat16 [2048, 512], P('dp', 'tensor'), may hold values from -0.125 to 0.125
- value_weight: bfloat16 [2048, 512], P('dp', 'tensor'), may hold values from -0.125 to 0.125
- out_weight: bfloat16 [2048, 2048], P('tensor', 'dp'), may hold values from -2 to 2
- feedforward_gain: bfloat16 [2048], P('dp'), may hold values from 0.099609375 to 1.8984375
- gate_weight: bfloat16 [2048, 5632], P('dp', 'tensor'), may hold values from -0.125 to 0.125
- up_weight: bfloat16 [2048, 5632], P('dp', 'tensor'), may hold values from -0.125 to 0.125
- down_weight: bfloat16 [5632, 2048], P('tensor', 'dp'), may hold values from -0.109375 to 0.109375
Outputs:
- result: bfloat16 [6, 1024, 2048], P(None, 'dp')
- input_grad: float32 [6, 1024, 2048], P(None, 'dp')
- attention_gain_grad: float32 [2048], P('dp')
- query_weight_grad: float32 [2048, 2048], P('dp', 'tensor')
- key_weight_grad: float32 [2048, 512], P('dp', 'tensor')
- value_weight_grad: float32 [2048, 512], P('dp', 'tensor')
- out_weight_grad: float32 [2048, 2048], P('tensor', 'dp')
- feedforward_gain_grad: float32 [2048], P('dp')
- gate_weight_grad: float32 [2048, 5632], P('dp', 'tensor')
- up_weight_grad: float32 [2048, 5632], P('dp', 'tensor')
- down_weight_grad: float32 [5632, 2048], P('tensor', 'dp')
Inputs may be any that keep to these rules, and one draw needn't show every extreme that they name: `active`: exactly one of the 6 slots is 0, the others are 1. Slot j of micro-batch m holds sequence assignment[m * 2 + j]; every sequence is in one slot.
All inputs are finite; a program needn't handle non-finite values.
Results may differ from a plain program's by a relative error of at most 0.018.
Values may be sent and summed in bfloat16 or wider, within the bound.
No kernel may reach another device: no remote copies, remote signals or barrier semaphores. Data moves between devices by JAX's collectives and lax.ppermute only.
A program may use at most 320 MiB of HBM per device.

v0:
```python
import jax
import jax.numpy as jnp
from jax import lax
from jax.sharding import PartitionSpec as P

HD = 128
KEY_BLOCK = 512
NMB = 3
SEQ_MB = 2


EPSILON = 1e-05
NEGATIVE = -1e30


def rms_scale(values):
    return lax.rsqrt(jnp.mean(values * values, axis=-1, keepdims=True) + EPSILON)


def rotary_tables(positions, head_size):
    half_width = head_size // 2
    frequency = jnp.exp(
        -jnp.log(10000.0) * (2.0 * jnp.arange(half_width, dtype=jnp.float32) / head_size)
    )
    angles = positions.astype(jnp.float32)[:, None] * frequency[None, :]
    return (jnp.cos(angles), jnp.sin(angles))


def rotate(values, cosine_table, sine_table):
    half_width = values.shape[-1] // 2
    first_half = values[..., :half_width]
    second_half = values[..., half_width:]
    cosine_part = cosine_table[None, :, None, :]
    sine_part = sine_table[None, :, None, :]
    return jnp.concatenate(
        [
            first_half * cosine_part - second_half * sine_part,
            second_half * cosine_part + first_half * sine_part,
        ],
        axis=-1,
    )


def fetch_weights(bundle):
    return (
        lax.all_gather(bundle[0], "dp", axis=0, tiled=True),
        lax.all_gather(bundle[1], "dp", axis=0, tiled=True),
        lax.all_gather(bundle[2], "dp", axis=0, tiled=True),
        lax.all_gather(bundle[3], "dp", axis=0, tiled=True),
        lax.all_gather(bundle[4], "dp", axis=1, tiled=True),
        lax.all_gather(bundle[5], "dp", axis=0, tiled=True),
        lax.all_gather(bundle[6], "dp", axis=0, tiled=True),
        lax.all_gather(bundle[7], "dp", axis=0, tiled=True),
        lax.all_gather(bundle[8], "dp", axis=1, tiled=True),
    )


def reduce_grads(bundle):
    return (
        lax.psum_scatter(bundle[0], "dp", scatter_dimension=0, tiled=True),
        lax.psum_scatter(bundle[1], "dp", scatter_dimension=0, tiled=True),
        lax.psum_scatter(bundle[2], "dp", scatter_dimension=0, tiled=True),
        lax.psum_scatter(bundle[3], "dp", scatter_dimension=0, tiled=True),
        lax.psum_scatter(bundle[4], "dp", scatter_dimension=1, tiled=True),
        lax.psum_scatter(bundle[5], "dp", scatter_dimension=0, tiled=True),
        lax.psum_scatter(bundle[6], "dp", scatter_dimension=0, tiled=True),
        lax.psum_scatter(bundle[7], "dp", scatter_dimension=0, tiled=True),
        lax.psum_scatter(bundle[8], "dp", scatter_dimension=1, tiled=True),
    )


def tensor_total(partial_rows):
    return lax.psum(partial_rows.astype(jnp.bfloat16), "tensor").astype(jnp.float32)


def add_bundles(first_bundle, second_bundle):
    if first_bundle is None:
        return second_bundle
    return jax.tree.map(jnp.add, first_bundle, second_bundle)


def local(
    tokens,
    cotangent,
    active,
    assignment,
    attention_gain,
    query_weight,
    key_weight,
    value_weight,
    out_weight,
    feedforward_gain,
    gate_weight,
    up_weight,
    down_weight,
):
    bf16 = jnp.bfloat16
    f32 = jnp.float32
    local_rows = tokens.shape[1]
    local_heads = query_weight.shape[1] // HD
    local_kv = key_weight.shape[1] // HD
    group_size = local_heads // local_kv
    rows_count = group_size * local_rows
    score_scale = HD ** (-0.5)
    device_index = lax.axis_index("dp")
    positions = device_index * local_rows + jnp.arange(local_rows, dtype=jnp.int32)
    cosine_table, sine_table = rotary_tables(positions, HD)
    row_positions = jnp.tile(positions, group_size)
    block_count = (device_index * local_rows + local_rows + KEY_BLOCK - 1) // KEY_BLOCK
    flat_active = active.reshape(-1).astype(f32)
    stored = (
        attention_gain,
        query_weight,
        key_weight,
        value_weight,
        out_weight,
        feedforward_gain,
        gate_weight,
        up_weight,
        down_weight,
    )
    result_all = jnp.zeros(tokens.shape, bf16)
    grad_all = jnp.zeros(tokens.shape, f32)
    shard_totals = None
    full_totals = None
    for batch_index in range(NMB):
        gathered = fetch_weights(stored)
        (
            full_gain_attn,
            full_query,
            full_key,
            full_value,
            full_out,
            full_gain_mlp,
            full_gate,
            full_up,
            full_down,
        ) = gathered
        gain_attn = full_gain_attn.astype(f32)
        gain_mlp = full_gain_mlp.astype(f32)
        picked = assignment[batch_index * SEQ_MB : (batch_index + 1) * SEQ_MB]
        live_scale = flat_active[batch_index * SEQ_MB : (batch_index + 1) * SEQ_MB][:, None, None]
        token_rows = jnp.take(tokens, picked, axis=0).astype(f32)
        upstream = jnp.take(cotangent, picked, axis=0).astype(f32)
        attn_scale = rms_scale(token_rows)
        normed_attn = token_rows * attn_scale
        hidden = (normed_attn * gain_attn).astype(bf16)
        query_raw = jnp.dot(hidden, full_query, preferred_element_type=f32)
        key_raw = jnp.dot(hidden, full_key, preferred_element_type=f32)
        value_raw = jnp.dot(hidden, full_value, preferred_element_type=f32)
        queries = rotate(
            query_raw.reshape(SEQ_MB, local_rows, local_heads, HD), cosine_table, sine_table
        ).astype(bf16)
        keys_local = rotate(
            key_raw.reshape(SEQ_MB, local_rows, local_kv, HD), cosine_table, sine_table
        ).astype(bf16)
        values_local = value_raw.reshape(SEQ_MB, local_rows, local_kv, HD).astype(bf16)
        query_rows = queries.reshape(SEQ_MB, local_rows, local_kv, group_size, HD).transpose(
            0, 2, 3, 1, 4
        )
        query_rows = query_rows.reshape(SEQ_MB, local_kv, rows_count, HD)
        keys_full, values_full = (
            lax.all_gather(keys_local.transpose(0, 2, 1, 3), "dp", axis=2, tiled=True),
            lax.all_gather(values_local.transpose(0, 2, 1, 3), "dp", axis=2, tiled=True),
        )

        def block_scores(block_index):
            block_start = block_index * KEY_BLOCK
            key_block = lax.dynamic_slice_in_dim(keys_full, block_start, KEY_BLOCK, 2)
            value_block = lax.dynamic_slice_in_dim(values_full, block_start, KEY_BLOCK, 2)
            scores = (
                jnp.einsum("bkrd,bktd->bkrt", query_rows, key_block, preferred_element_type=f32)
                * score_scale
            )
            allowed = (
                row_positions[:, None]
                >= (block_start + jnp.arange(KEY_BLOCK, dtype=jnp.int32))[None, :]
            )
            return (jnp.where(allowed, scores, NEGATIVE), key_block, value_block, block_start)

        def running_total(block_index, running):
            row_max, row_sum = running
            scores, key_block, value_block, block_start = block_scores(block_index)
            new_max = jnp.maximum(row_max, jnp.max(scores, axis=-1, keepdims=True))
            row_sum = row_sum * jnp.exp(row_max - new_max) + jnp.sum(
                jnp.exp(scores - new_max), axis=-1, keepdims=True
            )
            return (new_max, row_sum)

        start_max = jnp.full((SEQ_MB, local_kv, rows_count, 1), NEGATIVE, f32)
        start_sum = jnp.zeros((SEQ_MB, local_kv, rows_count, 1), f32)
        row_max, row_sum = lax.fori_loop(0, block_count, running_total, (start_max, start_sum))
        log_total = row_max + jnp.log(row_sum)

        def weighted_sum(block_index, running):
            scores, key_block, value_block, block_start = block_scores(block_index)
            soft_low = jnp.exp(scores - log_total).astype(bf16)
            return running + jnp.einsum(
                "bkrt,bktd->bkrd", soft_low, value_block, preferred_element_type=f32
            )

        attended = lax.fori_loop(
            0, block_count, weighted_sum, jnp.zeros((SEQ_MB, local_kv, rows_count, HD), f32)
        )
        mixed_out = attended.reshape(SEQ_MB, local_kv, group_size, local_rows, HD).transpose(
            0, 3, 1, 2, 4
        )
        mixed_out = mixed_out.reshape(SEQ_MB, local_rows, local_heads * HD).astype(bf16)
        branch = tensor_total(jnp.dot(mixed_out, full_out, preferred_element_type=f32))
        middle = token_rows + live_scale * branch
        mlp_scale = rms_scale(middle)
        normed_mlp = middle * mlp_scale
        hidden_mlp = (normed_mlp * gain_mlp).astype(bf16)
        gate_values = jnp.dot(hidden_mlp, full_gate, preferred_element_type=f32)
        up_values = jnp.dot(hidden_mlp, full_up, preferred_element_type=f32)
        sigmoid_gate = jax.nn.sigmoid(gate_values)
        silu_gate = gate_values * sigmoid_gate
        product = (silu_gate * up_values).astype(bf16)
        down_values = tensor_total(jnp.dot(product, full_down, preferred_element_type=f32))
        result = middle + live_scale * down_values
        result_all = result_all.at[picked].set(result.astype(bf16))
        down_grad = (live_scale * upstream).astype(bf16)
        grad_down = jnp.einsum("bsf,bsd->fd", product, down_grad, preferred_element_type=f32)
        product_grad = jnp.einsum("bsd,fd->bsf", down_grad, full_down, preferred_element_type=f32)
        gate_grad = (
            product_grad * up_values * (sigmoid_gate * (1.0 + gate_values * (1.0 - sigmoid_gate)))
        ).astype(bf16)
        up_grad = (product_grad * silu_gate).astype(bf16)
        grad_gate = jnp.einsum("bsd,bsf->df", hidden_mlp, gate_grad, preferred_element_type=f32)
        grad_up = jnp.einsum("bsd,bsf->df", hidden_mlp, up_grad, preferred_element_type=f32)
        hidden_mlp_grad = tensor_total(
            jnp.einsum("bsf,df->bsd", gate_grad, full_gate, preferred_element_type=f32)
            + jnp.einsum("bsf,df->bsd", up_grad, full_up, preferred_element_type=f32)
        )
        grad_gain_mlp = jnp.sum(hidden_mlp_grad * normed_mlp, axis=(0, 1))
        normed_grad = hidden_mlp_grad * gain_mlp
        middle_grad = upstream + mlp_scale * (
            normed_grad - normed_mlp * jnp.mean(normed_grad * normed_mlp, axis=-1, keepdims=True)
        )
        branch_grad = (live_scale * middle_grad).astype(bf16)
        grad_out = jnp.einsum("bsh,bsd->hd", mixed_out, branch_grad, preferred_element_type=f32)
        mixed_grad = jnp.einsum(
            "bsd,hd->bsh", branch_grad, full_out, preferred_element_type=f32
        ).astype(bf16)
        grad_rows = mixed_grad.reshape(SEQ_MB, local_rows, local_kv, group_size, HD).transpose(
            0, 2, 3, 1, 4
        )
        grad_rows = grad_rows.reshape(SEQ_MB, local_kv, rows_count, HD)
        row_delta = jnp.sum(grad_rows.astype(f32) * attended, axis=-1, keepdims=True)
        full_length = keys_full.shape[2]

        def backward_block(block_index, running):
            query_grad, key_grads, value_grads = running
            scores, key_block, value_block, block_start = block_scores(block_index)
            soft_block = jnp.exp(scores - log_total)
            soft_low = soft_block.astype(bf16)
            prob_grad = jnp.einsum(
                "bkrd,bktd->bkrt", grad_rows, value_block, preferred_element_type=f32
            )
            score_grad = (soft_block * (prob_grad - row_delta)).astype(bf16)
            query_grad = query_grad + jnp.einsum(
                "bkrt,bktd->bkrd", score_grad, key_block, preferred_element_type=f32
            )
            key_piece = jnp.einsum(
                "bkrt,bkrd->bktd", score_grad, query_rows, preferred_element_type=f32
            )
            value_piece = jnp.einsum(
                "bkrt,bkrd->bktd", soft_low, grad_rows, preferred_element_type=f32
            )
            key_grads = lax.dynamic_update_slice_in_dim(
                key_grads,
                lax.dynamic_slice_in_dim(key_grads, block_start, KEY_BLOCK, 2) + key_piece,
                block_start,
                2,
            )
            value_grads = lax.dynamic_update_slice_in_dim(
                value_grads,
                lax.dynamic_slice_in_dim(value_grads, block_start, KEY_BLOCK, 2) + value_piece,
                block_start,
                2,
            )
            return (query_grad, key_grads, value_grads)

        start_query = jnp.zeros((SEQ_MB, local_kv, rows_count, HD), f32)
        start_keys = jnp.zeros((SEQ_MB, local_kv, full_length, HD), f32)
        query_grad, key_grads, value_grads = lax.fori_loop(
            0, block_count, backward_block, (start_query, start_keys, start_keys)
        )
        key_own, value_own = (
            lax.psum_scatter(key_grads * score_scale, "dp", scatter_dimension=2, tiled=True),
            lax.psum_scatter(value_grads, "dp", scatter_dimension=2, tiled=True),
        )
        query_turned = (query_grad * score_scale).reshape(
            SEQ_MB, local_kv, group_size, local_rows, HD
        )
        query_turned = query_turned.transpose(0, 3, 1, 2, 4).reshape(
            SEQ_MB, local_rows, local_heads, HD
        )
        query_raw_grad = (
            rotate(query_turned, cosine_table, -sine_table)
            .reshape(SEQ_MB, local_rows, local_heads * HD)
            .astype(bf16)
        )
        key_raw_grad = rotate(key_own.transpose(0, 2, 1, 3), cosine_table, -sine_table)
        key_raw_grad = key_raw_grad.reshape(SEQ_MB, local_rows, local_kv * HD).astype(bf16)
        value_raw_grad = (
            value_own.transpose(0, 2, 1, 3).reshape(SEQ_MB, local_rows, local_kv * HD).astype(bf16)
        )
        grad_query = jnp.einsum("bsd,bsh->dh", hidden, query_raw_grad, preferred_element_type=f32)
        grad_key = jnp.einsum("bsd,bsh->dh", hidden, key_raw_grad, preferred_element_type=f32)
        grad_value = jnp.einsum("bsd,bsh->dh", hidden, value_raw_grad, preferred_element_type=f32)
        hidden_grad = tensor_total(
            jnp.einsum("bsh,dh->bsd", query_raw_grad, full_query, preferred_element_type=f32)
            + jnp.einsum("bsh,dh->bsd", key_raw_grad, full_key, preferred_element_type=f32)
            + jnp.einsum("bsh,dh->bsd", value_raw_grad, full_value, preferred_element_type=f32)
        )
        grad_gain_attn = jnp.sum(hidden_grad * normed_attn, axis=(0, 1))
        normed_attn_grad = hidden_grad * gain_attn
        input_rows_grad = middle_grad + attn_scale * (
            normed_attn_grad
            - normed_attn * jnp.mean(normed_attn_grad * normed_attn, axis=-1, keepdims=True)
        )
        grad_all = grad_all.at[picked].set(input_rows_grad)
        grads_now = (
            grad_gain_attn,
            grad_query,
            grad_key,
            grad_value,
            grad_out,
            grad_gain_mlp,
            grad_gate,
            grad_up,
            grad_down,
        )
        full_totals = add_bundles(full_totals, grads_now)
    shard_totals = reduce_grads(full_totals)
    return (
        result_all,
        grad_all,
        shard_totals[0],
        shard_totals[1],
        shard_totals[2],
        shard_totals[3],
        shard_totals[4],
        shard_totals[5],
        shard_totals[6],
        shard_totals[7],
        shard_totals[8],
    )


def solution(mesh):
    placed = (
        P(None, "dp", None),
        P(None, "dp", None),
        P(),
        P(),
        P("dp"),
        P("dp", "tensor"),
        P("dp", "tensor"),
        P("dp", "tensor"),
        P("tensor", "dp"),
        P("dp"),
        P("dp", "tensor"),
        P("dp", "tensor"),
        P("tensor", "dp"),
    )
    return jax.shard_map(
        local,
        mesh=mesh,
        in_specs=placed,
        out_specs=(
            P(None, "dp", None),
            P(None, "dp", None),
            P("dp"),
            P("dp", "tensor"),
            P("dp", "tensor"),
            P("dp", "tensor"),
            P("tensor", "dp"),
            P("dp"),
            P("dp", "tensor"),
            P("dp", "tensor"),
            P("tensor", "dp"),
        ),
        check_vma=False,
    )
```

profile of v0, /device:TPU:0, one launch (start us, length us, event | category | flops | bytes accessed | tf_op | source)
XLA Modules:
  0.0 2460.5 jit_solution(12199999513428916456)
XLA Ops:
  9.5 23.2 all-gather
  37.2 13.7 all-gather.16.cloned.1.call-done
  55.1 34.8 %all-gather.22.cloned.1.call-done = bf16[2048,256]{1,0:T(8,128)(2,1)} async-done(((bf16[128,256]{1,0:T(8,128)(2,1)}), bf16[2048,256]{1,0:T(8,128)(2,1)}) %all-gather.22.cloned.1.call-update) | async-done | bytes 1048592 | tf_op jit(solution)/shard_map/all_gather | solution.py:49
  96.7 44.9 %all-gather.20.cloned.1.call-done = bf16[2048,1024]{1,0:T(8,128)(2,1)} async-done(((bf16[128,1024]{1,0:T(8,128)(2,1)}), bf16[2048,1024]{1,0:T(8,128)(2,1)}) %all-gather.20.cloned.1.call-update) | async-done | bytes 4194320 | tf_op jit(solution)/shard_map/all_gather | solution.py:47
  148.6 32.1 %all-gather.18.cloned.1.call-done = bf16[2,2,1024,128]{3,2,1,0:T(8,128)(2,1)} async-done(((bf16[2,2,64,128]{3,2,1,0:T(8,128)(2,1)}), bf16[2,2,1024,128]{3,2,1,0:T(8,128)(2,1)}) %all-gather.18.cloned.1.call-update) | async-done | bytes 1048592 | tf_op jit(solution)/shard_map/all_gather | solution.py:163
  183.0 37.2 %all-gather.24.cloned.1.call-done = bf16[2,2,1024,128]{3,2,1,0:T(8,128)(2,1)} async-done(((bf16[2,2,64,128]{3,2,1,0:T(8,128)(2,1)}), bf16[2,2,1024,128]{3,2,1,0:T(8,128)(2,1)}) %all-gather.24.cloned.1.call-update) | async-done | bytes 1048592 | tf_op jit(solution)/shard_map/all_gather | solution.py:164
  225.3 34.5 %all-gather.34.cloned.1.call-done = bf16[2,2,1024,128]{3,2,1,0:T(8,128)(2,1)} async-done(((bf16[2,2,64,128]{3,2,1,0:T(8,128)(2,1)}), bf16[2,2,1024,128]{3,2,1,0:T(8,128)(2,1)}) %all-gather.34.cloned.1.call-update) | async-done | bytes 1048592 | tf_op jit(solution)/shard_map/all_gather | solution.py:163
  262.1 37.3 %all-gather.36.cloned.1.call-done = bf16[2,2,1024,128]{3,2,1,0:T(8,128)(2,1)} async-done(((bf16[2,2,64,128]{3,2,1,0:T(8,128)(2,1)}), bf16[2,2,1024,128]{3,2,1,0:T(8,128)(2,1)}) %all-gather.36.cloned.1.call-update) | async-done | bytes 1048592 | tf_op jit(solution)/shard_map/all_gather | solution.py:164
  305.7 33.4 %all-gather.38.cloned.1.call-done = bf16[2,2,1024,128]{3,2,1,0:T(8,128)(2,1)} async-done(((bf16[2,2,64,128]{3,2,1,0:T(8,128)(2,1)}), bf16[2,2,1024,128]{3,2,1,0:T(8,128)(2,1)}) %all-gather.38.cloned.1.call-update) | async-done | bytes 1048592 | tf_op jit(solution)/shard_map/all_gather | solution.py:163
  341.4 36.8 %all-gather.40.cloned.1.call-done = bf16[2,2,1024,128]{3,2,1,0:T(8,128)(2,1)} async-done(((bf16[2,2,64,128]{3,2,1,0:T(8,128)(2,1)}), bf16[2,2,1024,128]{3,2,1,0:T(8,128)(2,1)}) %all-gather.40.cloned.1.call-update) | async-done | bytes 1048592 | tf_op jit(solution)/shard_map/all_gather | solution.py:164
  382.9 49.4 %all-gather.26.cloned.1.call-done = bf16[1024,2048]{1,0:T(8,128)(2,1)} async-done(((bf16[1024,128]{1,0:T(8,128)(2,1)}), bf16[1024,2048]{1,0:T(8,128)(2,1)}) %all-gather.26.cloned.1.call-update) | async-done | bytes 4194320 | tf_op jit(solution)/shard_map/all_gather | solution.py:50
  432.4 3.9 fusion.223
  449.4 19.0 all-gather.1
  468.7 20.8 all-reduce.14.cloned.1.call-done
  495.0 94.2 %all-gather.32.cloned.1.call-done = bf16[2816,2048]{1,0:T(8,128)(2,1)} async-done(((bf16[2816,128]{1,0:T(8,128)(2,1)}), bf16[2816,2048]{1,0:T(8,128)(2,1)}) %all-gather.32.cloned.1.call-update) | async-done | bytes 11534352 | tf_op jit(solution)/shard_map/all_gather | solution.py:54
  589.1 9.6 fusion.118
  598.8 5.0 fusion.116
  603.8 5.0 fusion.114
  608.9 75.3 %all-gather.30.cloned.1.call-done = bf16[2048,2816]{1,0:T(8,128)(2,1)} async-done(((bf16[128,2816]{1,0:T(8,128)(2,1)}), bf16[2048,2816]{1,0:T(8,128)(2,1)}) %all-gather.30.cloned.1.call-update) | async-done | bytes 11534352 | tf_op jit(solution)/shard_map/all_gather | solution.py:53
  684.2 7.2 fusion.136
  698.2 80.9 %all-gather.28.cloned.1.call-done = bf16[2048,2816]{1,0:T(8,128)(2,1)} async-done(((bf16[128,2816]{1,0:T(8,128)(2,1)}), bf16[2048,2816]{1,0:T(8,128)(2,1)}) %all-gather.28.cloned.1.call-update) | async-done | bytes 11534352 | tf_op jit(solution)/shard_map/all_gather | solution.py:52
  779.1 8.5 multiply_convert_fusion.5
  788.5 8.2 fusion.130
  796.7 8.2 multiply_convert_fusion.3
  804.9 3.8 fusion.128
  808.7 8.8 multiply_convert_fusion.1
  817.6 3.8 fusion.126
  821.4 9.2 fusion.211
  830.6 9.0 fusion.208
  839.6 5.7 fusion.205
  845.4 50.1 %all-reduce.12.cloned.1.call-done = (bf16[2,64,2048]{2,1,0:T(8,128)(2,1)}, bf16[2,64,2048]{2,1,0:T(8,128)(2,1)}, bf16[2,64,2048]{2,1,0:T(8,128)(2,1)}) async-done(((bf16[2,64,2048]{2,1,0:T(8,128)(2,1)}, bf16[2,64,2048]{2,1,0:T(8,128)(2,1)}, bf16[2,64,2048]{2,1,0:T(8,128)(2,1)}), (bf16[2,64,2048]{2,1,0:T(8,128)(2,1)}, bf16[2,64,2048]{2,1,0:T(8,128)(2,1)}, ...) | async-done | bytes 1572880 | tf_op jit(solution)/shard_map/psum | solution.py:73
  895.5 4.0 fusion.294
  906.7 8.3 while.125
  919.2 4.0 fusion.268
  928.5 8.3 while.124
  936.9 4.5 fusion.265
  948.8 8.1 while.123
  961.5 6.9 fusion.232
  968.4 6.8 fusion.235
  976.3 6.8 fusion.238
  994.2 58.4 %reduce-scatter.18.cloned.1.call-done = f32[2,2,64,128]{3,2,1,0:T(8,128)} async-done(((f32[2,2,1024,128]{3,2,1,0:T(8,128)}), f32[2,2,64,128]{3,2,1,0:T(8,128)}) %reduce-scatter.18.cloned.1.call-update) | async-done | bytes 131088 | tf_op jit(solution)/shard_map/reduce_scatter | solution.py:290
  1052.6 64.7 %reduce-scatter.14.cloned.1.call-done = f32[2,2,64,128]{3,2,1,0:T(8,128)} async-done(((f32[2,2,1024,128]{3,2,1,0:T(8,128)}), f32[2,2,64,128]{3,2,1,0:T(8,128)}) %reduce-scatter.14.cloned.1.call-update) | async-done | bytes 131088 | tf_op jit(solution)/shard_map/reduce_scatter | solution.py:290
  1119.5 62.7 %reduce-scatter.16.cloned.1.call-done = f32[2,2,64,128]{3,2,1,0:T(8,128)} async-done(((f32[2,2,1024,128]{3,2,1,0:T(8,128)}), f32[2,2,64,128]{3,2,1,0:T(8,128)}) %reduce-scatter.16.cloned.1.call-update) | async-done | bytes 131088 | tf_op jit(solution)/shard_map/reduce_scatter | solution.py:291
  1184.5 61.8 %reduce-scatter.20.cloned.1.call-done = f32[2,2,64,128]{3,2,1,0:T(8,128)} async-done(((f32[2,2,1024,128]{3,2,1,0:T(8,128)}), f32[2,2,64,128]{3,2,1,0:T(8,128)}) %reduce-scatter.20.cloned.1.call-update) | async-done | bytes 131088 | tf_op jit(solution)/shard_map/reduce_scatter | solution.py:291
  1249.1 62.0 %reduce-scatter.24.cloned.1.call-done = f32[2,2,64,128]{3,2,1,0:T(8,128)} async-done(((f32[2,2,1024,128]{3,2,1,0:T(8,128)}), f32[2,2,64,128]{3,2,1,0:T(8,128)}) %reduce-scatter.24.cloned.1.call-update) | async-done | bytes 131088 | tf_op jit(solution)/shard_map/reduce_scatter | solution.py:291
  1334.4 4.8 bitcast_add_fusion.11
  1345.0 5.1 bitcast_add_fusion.9
  1351.1 10.7 fusion.388
  1361.8 9.6 fusion.387
  1371.4 25.5 %bitcast_add_fusion.7 = f32[2048,2816]{1,0:T(8,128)} fusion(f32[2048,2816,1]{1,0,2:T(8,128)} %fusion.388, f32[2048,2816,1]{1,0,2:T(8,128)} %fusion.387, bf16[2,64,2048]{2,1,0:T(8,128)(2,1)S(1)} %copy-done.41, bf16[2,64,2816]{2,1,0:T(8,128)(2,1)S(1)} %copy-done.88), kind=kOutput, calls=%fused_computation.163 | convolution fusion | flops 1487929344 | bytes 70451200 | tf_op jit(solution)/shard_map/bsd,bsf->df/dot_general | solution.py:229
  1397.0 10.6 fusion.390
  1407.6 9.3 fusion.389
  1416.9 25.0 %bitcast_add_fusion.5 = f32[2048,2816]{1,0:T(8,128)} fusion(f32[2048,2816,1]{1,0,2:T(8,128)} %fusion.390, f32[2048,2816,1]{1,0,2:T(8,128)} %fusion.389, bf16[2,64,2048]{2,1,0:T(8,128)(2,1)S(1)} %copy-done.41, bf16[2,64,2816]{2,1,0:T(8,128)(2,1)S(1)} %copy-done.87), kind=kOutput, calls=%fused_computation.161 | convolution fusion | flops 1487929344 | bytes 70451200 | tf_op jit(solution)/shard_map/bsd,bsf->df/dot_general | solution.py:230
  1442.2 10.9 fusion.358
  1453.1 9.5 fusion.361
  1462.7 24.3 bitcast_add_fusion.3
  1491.2 3.7 fusion.278
  1495.0 57.9 %all-reduce.2 = (f32[2048]{0:T(1024)S(1)}, f32[2048]{0:T(1024)S(1)}) all-reduce(f32[2048]{0:T(1024)S(1)} %add_add_fusion.1, f32[2048]{0:T(1024)S(1)} %add_add_fusion), channel_id=8, replica_groups=mesh['dp'=16,'tensor'=2] {'dp'}, use_global_device_ids=true, to_apply=%region_66.68.clone | all-reduce | flops 4096 | bytes 32768
  1554.1 3.7 fusion.286
  1578.3 71.3 %reduce-scatter.26.cloned.1.call-done = f32[128,1024]{1,0:T(8,128)} async-done(((f32[2048,1024]{1,0:T(8,128)}), f32[128,1024]{1,0:T(8,128)}) %reduce-scatter.26.cloned.1.call-update) | async-done | bytes 524304 | tf_op jit(solution)/shard_map/reduce_scatter | solution.py:61
  1649.6 109.6 %reduce-scatter.32.cloned.1.call-done = f32[1024,128]{1,0:T(8,128)} async-done(((f32[1024,2048]{1,0:T(8,128)}), f32[1024,128]{1,0:T(8,128)}) %reduce-scatter.32.cloned.1.call-update) | async-done | bytes 524304 | tf_op jit(solution)/shard_map/reduce_scatter | solution.py:64
  1759.3 231.7 %reduce-scatter.34.cloned.1.call-done = f32[128,2816]{1,0:T(8,128)} async-done(((f32[2048,2816]{1,0:T(8,128)}), f32[128,2816]{1,0:T(8,128)}) %reduce-scatter.34.cloned.1.call-update) | async-done | bytes 1441808 | tf_op jit(solution)/shard_map/reduce_scatter | solution.py:66
  1991.0 231.3 %reduce-scatter.36.cloned.1.call-done = f32[128,2816]{1,0:T(8,128)} async-done(((f32[2048,2816]{1,0:T(8,128)}), f32[128,2816]{1,0:T(8,128)}) %reduce-scatter.36.cloned.1.call-update) | async-done | bytes 1441808 | tf_op jit(solution)/shard_map/reduce_scatter | solution.py:67
  2222.2 231.3 %reduce-scatter.38.cloned.1.call-done = f32[2816,128]{1,0:T(8,128)} async-done(((f32[2816,2048]{1,0:T(8,128)}), f32[2816,128]{1,0:T(8,128)}) %reduce-scatter.38.cloned.1.call-update) | async-done | bytes 1441808 | tf_op jit(solution)/shard_map/reduce_scatter | solution.py:68
  (679 shorter events, 214.8 us)
Async XLA Ops:
  7.2 43.7 %all-gather.16.cloned.1.call-start = ((), (), s32[]{:S(2)}) async-start(), calls=%async_computation.13 | async-start | bytes 1114112 | tf_op jit(solution)/shard_map/all_gather | solution.py:48
  7.9 82.0 %all-gather.22.cloned.1.call-start = ((), (), s32[]{:S(2)}) async-start(), calls=%async_computation.16 | async-start | bytes 1114112 | tf_op jit(solution)/shard_map/all_gather | solution.py:49
  8.7 132.9 %all-gather.20.cloned.1.call-start = ((), (), s32[]{:S(2)}) async-start(), calls=%async_computation.15 | async-start | bytes 4456448 | tf_op jit(solution)/shard_map/all_gather | solution.py:47
  9.4 171.3 %all-gather.18.cloned.1.call-start = ((), (), s32[]{:S(2)}) async-start(), calls=%async_computation.14 | async-start | bytes 1114112 | tf_op jit(solution)/shard_map/all_gather | solution.py:163
  32.6 113.3 %copy-start.102 = (f32[16,1,128]{2,1,0:T(1,128)}, f32[16,1,128]{2,1,0:T(1,128)S(1)}, u32[]{:S(2)}) copy-start(f32[16,1,128]{2,1,0:T(1,128)S(1)} %convert_element_type.439) | copy-start | bytes 24580
  33.5 866.0 %copy-start.129 = (pred[2]{0:T(512)(128)(4,1)}, pred[2]{0:T(512)(128)(4,1)S(1)}, u32[]{:S(2)}) copy-start(pred[2]{0:T(512)(128)(4,1)S(1)} %get-tuple-element.860) | copy-start | bytes 10
  34.2 1310.8 %copy-start.8 = (bf16[2,64,2048]{2,1,0:T(8,128)(2,1)}, bf16[2,64,2048]{2,1,0:T(8,128)(2,1)S(1)}, u32[]{:S(2)}) copy-start(bf16[2,64,2048]{2,1,0:T(8,128)(2,1)S(1)} %gather_fusion.2) | copy-start | bytes 1572868
  34.8 1304.6 %copy-start.6 = (bf16[2,64,2048]{2,1,0:T(8,128)(2,1)}, bf16[2,64,2048]{2,1,0:T(8,128)(2,1)S(1)}, u32[]{:S(2)}) copy-start(bf16[2,64,2048]{2,1,0:T(8,128)(2,1)S(1)} %gather_fusion.1) | copy-start | bytes 1572868
  35.4 1307.8 %copy-start.4 = (bf16[2,64,2048]{2,1,0:T(8,128)(2,1)}, bf16[2,64,2048]{2,1,0:T(8,128)(2,1)S(1)}, u32[]{:S(2)}) copy-start(bf16[2,64,2048]{2,1,0:T(8,128)(2,1)S(1)} %gather_fusion) | copy-start | bytes 1572868
  36.3 105.3 %copy-start.143 = (f32[2,64]{1,0:T(2,128)}, f32[2,64]{1,0:T(2,128)S(1)}, u32[]{:S(2)}) copy-start(f32[2,64]{1,0:T(2,128)S(1)} %add_rsqrt_fusion.1) | copy-start | bytes 1540
  36.3 108.5 %copy-start.131 = (f32[2,64]{1,0:T(2,128)}, f32[2,64]{1,0:T(2,128)S(1)}, u32[]{:S(2)}) copy-start(f32[2,64]{1,0:T(2,128)S(1)} %add_rsqrt_fusion.3) | copy-start | bytes 1540
  36.4 109.6 %copy-start.134 = (f32[2,64]{1,0:T(2,128)}, f32[2,64]{1,0:T(2,128)S(1)}, u32[]{:S(2)}) copy-start(f32[2,64]{1,0:T(2,128)S(1)} %add_rsqrt_fusion.5) | copy-start | bytes 1540
  37.2 109.7 %copy-start.111 = (f32[64,64]{1,0:T(8,128)}, f32[64,64]{1,0:T(8,128)S(1)}, u32[]{:S(2)}) copy-start(f32[64,64]{1,0:T(8,128)S(1)} %get-tuple-element.946) | copy-start | bytes 49156
  55.0 165.2 %all-gather.24.cloned.1.call-start = ((), (), s32[]{:S(2)}) async-start(), calls=%async_computation.17 | async-start | bytes 1114112 | tf_op jit(solution)/shard_map/all_gather | solution.py:164
  92.3 167.5 %all-gather.34.cloned.1.call-start = ((), (), s32[]{:S(2)}) async-start(), calls=%async_computation.22 | async-start | bytes 1114112 | tf_op jit(solution)/shard_map/all_gather | solution.py:163
  93.1 206.4 %all-gather.36.cloned.1.call-start = ((), (), s32[]{:S(2)}) async-start(), calls=%async_computation.23 | async-start | bytes 1114112 | tf_op jit(solution)/shard_map/all_gather | solution.py:164
  94.2 244.9 %all-gather.38.cloned.1.call-start = ((), (), s32[]{:S(2)}) async-start(), calls=%async_computation.24 | async-start | bytes 1114112 | tf_op jit(solution)/shard_map/all_gather | solution.py:163
  95.0 283.2 %all-gather.40.cloned.1.call-start = ((), (), s32[]{:S(2)}) async-start(), calls=%async_computation.25 | async-start | bytes 1114112 | tf_op jit(solution)/shard_map/all_gather | solution.py:164
  96.1 336.3 %all-gather.26.cloned.1.call-start = ((), (), s32[]{:S(2)}) async-start(), calls=%async_computation.18 | async-start | bytes 4456448 | tf_op jit(solution)/shard_map/all_gather | solution.py:50
  96.6 392.8 %all-reduce.14.cloned.1.call-start = ((), (), s32[]{:S(2)}) async-start(), calls=%async_computation.41 | async-start | bytes 3145728 | tf_op jit(solution)/shard_map/psum | solution.py:73
  222.9 36.9 %copy-start.75 = (f32[2,2,256,128]{3,2,1,0:T(8,128)}, f32[2,2,256,128]{3,2,1,0:T(8,128)S(1)}, u32[]{:S(2)}) copy-start(f32[2,2,256,128]{3,2,1,0:T(8,128)S(1)} %get-tuple-element.455) | copy-start | bytes 1572868
  222.9 36.9 %copy-start.26 = (bf16[2,2,256,128]{3,2,1,0:T(8,128)(2,1)}, bf16[2,2,256,128]{3,2,1,0:T(8,128)(2,1)S(1)}, u32[]{:S(2)}) copy-start(bf16[2,2,256,128]{3,2,1,0:T(8,128)(2,1)S(1)} %get-tuple-element.1892) | copy-start | bytes 786436
  222.9 36.9 %copy-start.176 = (f32[2,2,256,1]{2,1,0,3:T(2,128)}, f32[2,2,256,1]{2,1,0,3:T(2,128)S(1)}, u32[]{:S(2)}) copy-start(f32[2,2,256,1]{2,1,0,3:T(2,128)S(1)} %get-tuple-element.1994) | copy-start | bytes 12292
  225.0 207.4 %copy-start.94 = (bf16[2,64,1024]{2,1,0:T(8,128)(2,1)}, bf16[2,64,1024]{2,1,0:T(8,128)(2,1)S(1)}, u32[]{:S(2)}) copy-start(bf16[2,64,1024]{2,1,0:T(8,128)(2,1)S(1)} %convert_element_type.352) | copy-start | bytes 786436
  302.3 36.8 %copy-start.77 = (f32[2,2,256,128]{3,2,1,0:T(8,128)}, f32[2,2,256,128]{3,2,1,0:T(8,128)S(1)}, u32[]{:S(2)}) copy-start(f32[2,2,256,128]{3,2,1,0:T(8,128)S(1)} %get-tuple-element.458) | copy-start | bytes 1572868
  304.4 131.9 %copy-start.96 = (bf16[2,64,1024]{2,1,0:T(8,128)(2,1)}, bf16[2,64,1024]{2,1,0:T(8,128)(2,1)S(1)}, u32[]{:S(2)}) copy-start(bf16[2,64,1024]{2,1,0:T(8,128)(2,1)S(1)} %convert_element_type.368) | copy-start | bytes 786436
  380.8 55.4 %copy-start.78 = (f32[2,2,256,128]{3,2,1,0:T(8,128)}, f32[2,2,256,128]{3,2,1,0:T(8,128)S(1)}, u32[]{:S(2)}) copy-start(f32[2,2,256,128]{3,2,1,0:T(8,128)S(1)} %get-tuple-element.461) | copy-start | bytes 1572868
  382.9 54.8 %copy-start.100 = (bf16[2,64,1024]{2,1,0:T(8,128)(2,1)}, bf16[2,64,1024]{2,1,0:T(8,128)(2,1)S(1)}, u32[]{:S(2)}) copy-start(bf16[2,64,1024]{2,1,0:T(8,128)(2,1)S(1)} %convert_element_type.383) | copy-start | bytes 786436
  439.3 149.8 %all-gather.32.cloned.1.call-start = ((), (), s32[]{:S(2)}) async-start(), calls=%async_computation.21 | async-start | bytes 12255232 | tf_op jit(solution)/shard_map/all_gather | solution.py:54
  439.9 244.3 %all-gather.30.cloned.1.call-start = ((), (), s32[]{:S(2)}) async-start(), calls=%async_computation.20 | async-start | bytes 12255232 | tf_op jit(solution)/shard_map/all_gather | solution.py:53
  440.7 338.4 %all-gather.28.cloned.1.call-start = ((), (), s32[]{:S(2)}) async-start(), calls=%async_computation.19 | async-start | bytes 12255232 | tf_op jit(solution)/shard_map/all_gather | solution.py:52
  441.3 454.3 %all-reduce.12.cloned.1.call-start = ((), (), s32[]{:S(2)}) async-start(), calls=%async_computation.40 | async-start | bytes 3145728 | tf_op jit(solution)/shard_map/psum | solution.py:73
  446.3 152.5 %copy-start.42 = (bf16[2,64,2048]{2,1,0:T(8,128)(2,1)}, bf16[2,64,2048]{2,1,0:T(8,128)(2,1)S(1)}, u32[]{:S(2)}) copy-start(bf16[2,64,2048]{2,1,0:T(8,128)(2,1)S(1)} %gather_fusion.4) | copy-start | bytes 1572868
  468.4 876.5 %copy-start.113 = (f32[16,1,128]{2,1,0:T(1,128)}, f32[16,1,128]{2,1,0:T(1,128)S(1)}, u32[]{:S(2)}) copy-start(f32[16,1,128]{2,1,0:T(1,128)S(1)} %convert_element_type.440) | copy-start | bytes 24580
  468.6 430.9 %copy-start.141 = (f32[2]{0:T(128)}, f32[2]{0:T(128)S(1)}, u32[]{:S(2)}) copy-start(f32[2]{0:T(128)S(1)} %get-tuple-element.681) | copy-start | bytes 28
  468.6 449.5 %copy-start.139 = (f32[2]{0:T(128)}, f32[2]{0:T(128)S(1)}, u32[]{:S(2)}) copy-start(f32[2]{0:T(128)S(1)} %get-tuple-element.682) | copy-start | bytes 28
  468.6 468.2 %copy-start.137 = (f32[2]{0:T(128)}, f32[2]{0:T(128)S(1)}, u32[]{:S(2)}) copy-start(f32[2]{0:T(128)S(1)} %get-tuple-element.683) | copy-start | bytes 28
  492.9 406.7 %copy-start.155 = (f32[2,64]{1,0:T(2,128)}, f32[2,64]{1,0:T(2,128)S(1)}, u32[]{:S(2)}) copy-start(f32[2,64]{1,0:T(2,128)S(1)} %add_rsqrt_fusion) | copy-start | bytes 1540
  492.9 425.3 %copy-start.149 = (f32[2,64]{1,0:T(2,128)}, f32[2,64]{1,0:T(2,128)S(1)}, u32[]{:S(2)}) copy-start(f32[2,64]{1,0:T(2,128)S(1)} %add_rsqrt_fusion.2) | copy-start | bytes 1540
  492.9 443.9 %copy-start.152 = (f32[2,64]{1,0:T(2,128)}, f32[2,64]{1,0:T(2,128)S(1)}, u32[]{:S(2)}) copy-start(f32[2,64]{1,0:T(2,128)S(1)} %add_rsqrt_fusion.4) | copy-start | bytes 1540
  495.0 313.7 %copy-start.40 = (bf16[2,64,2048]{2,1,0:T(8,128)(2,1)}, bf16[2,64,2048]{2,1,0:T(8,128)(2,1)S(1)}, u32[]{:S(2)}) copy-start(bf16[2,64,2048]{2,1,0:T(8,128)(2,1)S(1)} %get-tuple-element.941) | copy-start | bytes 1572868
  603.8 80.4 %copy-start.64 = (bf16[2,64,2048]{2,1,0:T(8,128)(2,1)S(1)}, bf16[2,64,2048]{2,1,0:T(8,128)(2,1)}, u32[]{:S(2)}) copy-start(bf16[2,64,2048]{2,1,0:T(8,128)(2,1)} %get-tuple-element.943) | copy-start | bytes 1572868
  839.6 56.0 %copy-start.52 = (bf16[2,64,2048]{2,1,0:T(8,128)(2,1)S(1)}, bf16[2,64,2048]{2,1,0:T(8,128)(2,1)}, u32[]{:S(2)}) copy-start(bf16[2,64,2048]{2,1,0:T(8,128)(2,1)} %get-tuple-element.857) | copy-start | bytes 1572868
  845.4 148.9 %reduce-scatter.22.cloned.1.call-start = ((), (), s32[]{:S(2)}) async-start(), calls=%async_computation.30 | async-start | bytes 2228224 | tf_op jit(solution)/shard_map/reduce_scatter | solution.py:290
  918.1 134.6 %reduce-scatter.18.cloned.1.call-start = ((), (), s32[]{:S(2)}) async-start(), calls=%async_computation.28 | async-start | bytes 2228224 | tf_op jit(solution)/shard_map/reduce_scatter | solution.py:290
  945.0 172.4 %reduce-scatter.14.cloned.1.call-start = ((), (), s32[]{:S(2)}) async-start(), calls=%async_computation.26 | async-start | bytes 2228224 | tf_op jit(solution)/shard_map/reduce_scatter | solution.py:290
  960.0 222.1 %reduce-scatter.16.cloned.1.call-start = ((), (), s32[]{:S(2)}) async-start(), calls=%async_computation.27 | async-start | bytes 2228224 | tf_op jit(solution)/shard_map/reduce_scatter | solution.py:291
  960.8 285.5 %reduce-scatter.20.cloned.1.call-start = ((), (), s32[]{:S(2)}) async-start(), calls=%async_computation.29 | async-start | bytes 2228224 | tf_op jit(solution)/shard_map/reduce_scatter | solution.py:291
  961.4 349.7 %reduce-scatter.24.cloned.1.call-start = ((), (), s32[]{:S(2)}) async-start(), calls=%async_computation.31 | async-start | bytes 2228224 | tf_op jit(solution)/shard_map/reduce_scatter | solution.py:291
  975.2 513.7 %all-reduce.10.cloned.1.call-start = ((), (), s32[]{:S(2)}) async-start(), calls=%async_computation.39 | async-start | bytes 6291456 | tf_op jit(solution)/shard_map/psum | solution.py:73
  987.3 194.9 %copy-start.63 = (bf16[2048,256]{1,0:T(8,128)(2,1)S(1)}, bf16[2048,256]{1,0:T(8,128)(2,1)}, u32[]{:S(2)}) copy-start(bf16[2048,256]{1,0:T(8,128)(2,1)} %all-gather.22.cloned.1.call-done) | copy-start | bytes 3145732
  1184.5 128.4 %copy-start.61 = (bf16[2048,256]{1,0:T(8,128)(2,1)S(1)}, bf16[2048,256]{1,0:T(8,128)(2,1)}, u32[]{:S(2)}) copy-start(bf16[2048,256]{1,0:T(8,128)(2,1)} %all-gather.16.cloned.1.call-done) | copy-start | bytes 3145732
  1323.7 254.7 %reduce-scatter.28.cloned.1.call-start = ((), (), s32[]{:S(2)}) async-start(), calls=%async_computation.33 | async-start | bytes 2228224 | tf_op jit(solution)/shard_map/reduce_scatter | solution.py:62
  1327.5 250.8 %reduce-scatter.30.cloned.1.call-start = ((), (), s32[]{:S(2)}) async-start(), calls=%async_computation.34 | async-start | bytes 2228224 | tf_op jit(solution)/shard_map/reduce_scatter | solution.py:63
  1331.6 318.0 %reduce-scatter.26.cloned.1.call-start = ((), (), s32[]{:S(2)}) async-start(), calls=%async_computation.32 | async-start | bytes 8912896 | tf_op jit(solution)/shard_map/reduce_scatter | solution.py:61
  1339.3 420.0 %reduce-scatter.32.cloned.1.call-start = ((), (), s32[]{:S(2)}) async-start(), calls=%async_computation.35 | async-start | bytes 8912896 | tf_op jit(solution)/shard_map/reduce_scatter | solution.py:64
  1350.1 640.9 %reduce-scatter.34.cloned.1.call-start = ((), (), s32[]{:S(2)}) async-start(), calls=%async_computation.36 | async-start | bytes 24510464 | tf_op jit(solution)/shard_map/reduce_scatter | solution.py:66
  1397.0 825.3 %reduce-scatter.36.cloned.1.call-start = ((), (), s32[]{:S(2)}) async-start(), calls=%async_computation.37 | async-start | bytes 24510464 | tf_op jit(solution)/shard_map/reduce_scatter | solution.py:67
  1441.9 1011.6 %reduce-scatter.38.cloned.1.call-start = ((), (), s32[]{:S(2)}) async-start(), calls=%async_computation.38 | async-start | bytes 24510464 | tf_op jit(solution)/shard_map/reduce_scatter | solution.py:68
  1491.2 62.9 %copy-start.47 = (bf16[2,64,2048]{2,1,0:T(8,128)(2,1)S(1)}, bf16[2,64,2048]{2,1,0:T(8,128)(2,1)}, u32[]{:S(2)}) copy-start(bf16[2,64,2048]{2,1,0:T(8,128)(2,1)} %gather_fusion.3) | copy-start | bytes 1572868
  1491.2 62.9 %copy-start.54 = (bf16[2,64,2048]{2,1,0:T(8,128)(2,1)S(1)}, bf16[2,64,2048]{2,1,0:T(8,128)(2,1)}, u32[]{:S(2)}) copy-start(bf16[2,64,2048]{2,1,0:T(8,128)(2,1)} %get-tuple-element.857) | copy-start | bytes 1572868
  1491.2 62.9 %copy-start.154 = (f32[2,64]{1,0:T(2,128)S(1)}, f32[2,64]{1,0:T(2,128)}, u32[]{:S(2)}) copy-start(f32[2,64]{1,0:T(2,128)} %copy-done.152) | copy-start | bytes 1540
  1491.2 62.9 %copy-start.163 = (f32[2,64]{1,0:T(2,128)S(1)}, f32[2,64]{1,0:T(2,128)}, u32[]{:S(2)}) copy-start(f32[2,64]{1,0:T(2,128)} %copy-done.161) | copy-start | bytes 1540
  1571.9 881.6 %copy-start.1 = (bf16[6,64,2048]{2,1,0:T(8,128)(2,1)S(1)}, bf16[6,64,2048]{2,1,0:T(8,128)(2,1)}, u32[]{:S(2)}) copy-start(bf16[6,64,2048]{2,1,0:T(8,128)(2,1)} %param.33) | copy-start | bytes 4718596
  (152 other events, 608.5 us)
Sparse Core Ops, SparseCore 0:
  10.2 40.6 all-gather.15
  53.0 36.8 all-gather.21
  92.1 49.4 all-gather.19
  144.2 36.4 all-gather.17
  183.3 36.8 all-gather.23
  222.8 36.8 all-gather.33
  262.5 36.8 all-gather.35
  302.2 36.8 all-gather.37
  341.3 36.8 all-gather.39
  380.2 52.1 all-gather.25
  439.4 49.9 all-reduce.13
  491.7 97.3 all-gather.31
  591.7 92.4 all-gather.29
  686.6 92.4 all-gather.27
  845.5 50.0 all-reduce.11
  918.2 69.7 reduce-scatter.21
  992.0 60.6 reduce-scatter.17
  1056.8 60.5 reduce-scatter.13
  1121.6 60.5 reduce-scatter.15
  1185.8 60.5 reduce-scatter.19
  1250.5 60.5 reduce-scatter.23
  1323.7 85.6 all-reduce.9
  1414.2 61.5 reduce-scatter.27
  1480.0 60.7 reduce-scatter.29
  1546.0 103.5 reduce-scatter.25
  1654.7 104.5 reduce-scatter.31
  1764.4 226.5 reduce-scatter.33
  1996.2 225.9 reduce-scatter.35
  2227.5 225.9 reduce-scatter.37
where the time goes:
time: 2470 us; the launch traced here: 2460 us
  waiting for transfers between devices  1870 us (76%)
  matrix products  344 us (14%)
  blocking collectives  100 us (4%)
  local copies, waits for them, and re-layouts  77.9 us (3%)
  other arithmetic  51.5 us (2%)
    reduce_scatter x1, waiting for transfers between devices, reduce_grads(): lax.psum_scatter(bundle[6], 'dp', scatter_dimension=0, tiled=True)  232 us
    reduce_scatter x1, waiting for transfers between devices, reduce_grads(): lax.psum_scatter(bundle[8], 'dp', scatter_dimension=1, tiled=True)  231 us
    reduce_scatter x1, waiting for transfers between devices, reduce_grads(): lax.psum_scatter(bundle[7], 'dp', scatter_dimension=0, tiled=True)  231 us
    reduce_scatter x3, waiting for transfers between devices, local(): lax.psum_scatter(value_grads, 'dp', scatter_dimension=2, tiled=True)  187 us
    reduce_scatter x3, waiting for transfers between devices, local(): lax.psum_scatter(key_grads * score_scale, 'dp', scatter_dimension=2, tile...  123 us
    all_gather x3, waiting for transfers between devices, local(): lax.all_gather(values_local.transpose(0, 2, 1, 3), 'dp', axis=2, tiled=True)  111 us
    reduce_scatter x1, waiting for transfers between devices, reduce_grads(): lax.psum_scatter(bundle[4], 'dp', scatter_dimension=1, tiled=True)  110 us
    all_gather x3, waiting for transfers between devices, local(): lax.all_gather(keys_local.transpose(0, 2, 1, 3), 'dp', axis=2, tiled=True)  99.9 us
  transfers between devices with their start and end apart: 29, of which 25 were waited for; matrix products, arithmetic and copies ran while one was open for 14% of the time, Pallas kernels for 0%

commit v1 on v0

v1 whole, which is shorter than its diff:
```python
import functools

import jax
import jax.numpy as jnp
from jax import lax
from jax.experimental import pallas as pl
from jax.experimental.pallas import tpu as pltpu
from jax.sharding import PartitionSpec as P

HD = 128
EPSILON = 1e-05
NEGATIVE = -1e30
VMEM_LIMIT = 48 * 1024 * 1024

bf16 = jnp.bfloat16
f32 = jnp.float32


def rms_scale(values):
    return lax.rsqrt(jnp.mean(values * values, axis=-1, keepdims=True) + EPSILON)


def dot(a, b, ca, cb):
    return lax.dot_general(a, b, (((ca,), (cb,)), ((), ())), preferred_element_type=f32)


def params(**kwargs):
    return pltpu.CompilerParams(vmem_limit_bytes=VMEM_LIMIT, **kwargs)


def turn(v, cosine, sine):
    return v * cosine + pltpu.roll(v, HD // 2, 1) * sine


def rope_kernel(q_cols, k_cols, raw_ref, cos_ref, sin_ref, q_ref, kv_ref):
    cosine, sine = cos_ref[...], sin_ref[...]
    for c in range(0, q_cols, HD):
        q_ref[:, c : c + HD] = turn(raw_ref[:, c : c + HD], cosine, sine).astype(bf16)
    for c in range(0, k_cols, HD):
        v = raw_ref[:, q_cols + c : q_cols + c + HD]
        kv_ref[:, c : c + HD] = turn(v, cosine, sine).astype(bf16)
    kv_ref[:, k_cols:] = raw_ref[:, q_cols + k_cols :].astype(bf16)


def rope(raw, cosine, sine, rows, q_cols, k_cols):
    total = raw.shape[0]
    width = raw.shape[1]
    table = pl.BlockSpec((rows, HD), lambda i: (0, 0))
    return pl.pallas_call(
        functools.partial(rope_kernel, q_cols, k_cols),
        grid=(total // rows,),
        in_specs=[pl.BlockSpec((rows, width), lambda i: (i, 0)), table, table],
        out_specs=[
            pl.BlockSpec((rows, q_cols), lambda i: (i, 0)),
            pl.BlockSpec((rows, 2 * k_cols), lambda i: (i, 0)),
        ],
        out_shape=[
            jax.ShapeDtypeStruct((total, q_cols), bf16),
            jax.ShapeDtypeStruct((total, 2 * k_cols), bf16),
        ],
        compiler_params=params(),
        name="rope",
    )(raw, cosine, sine)


def heads_to_rows(block, kv, group):
    return jnp.concatenate(
        [block[:, (kv * group + g) * HD : (kv * group + g + 1) * HD] for g in range(group)], axis=0
    )


def keys_of(near_ref, far_ref, c):
    parts = [r[:, 0, :, c : c + HD].reshape(-1, HD) for r in (near_ref, far_ref)]
    return jnp.concatenate(parts, axis=0)


def attend_kernel(local_kv, group, q_ref, near_ref, far_ref, qpos_ref, kpos_ref, out_ref, log_ref):
    rows = q_ref.shape[0]
    allowed = kpos_ref[...] <= qpos_ref[...]
    for kv in range(local_kv):
        q = heads_to_rows(q_ref, kv, group)
        keys = keys_of(near_ref, far_ref, kv * HD)
        values = keys_of(near_ref, far_ref, (local_kv + kv) * HD)
        s = jnp.where(allowed, dot(q, keys, 1, 1) * (HD**-0.5), NEGATIVE)
        top = jnp.max(s, axis=-1, keepdims=True)
        e = jnp.exp(s - top)
        total = jnp.sum(e, axis=-1, keepdims=True)
        probs = (e * (1.0 / total)).astype(bf16)
        out = dot(probs, values, 1, 0)
        for g in range(group):
            c = (kv * group + g) * HD
            out_ref[:, c : c + HD] = out[g * rows : (g + 1) * rows].astype(bf16)
        log_ref[kv] = top + jnp.log(total)


def attend(q, near, far, qpos, kpos, rows, local_kv, group):
    total, width = q.shape
    seqs = total // rows
    blocks, _, _, kv_width = near.shape
    kv_spec = pl.BlockSpec((blocks, 1, rows, kv_width), lambda i: (0, i, 0, 0))
    return pl.pallas_call(
        functools.partial(attend_kernel, local_kv, group),
        grid=(seqs,),
        in_specs=[
            pl.BlockSpec((rows, width), lambda i: (i, 0)),
            kv_spec,
            kv_spec,
            pl.BlockSpec(qpos.shape, lambda i: (0, 0)),
            pl.BlockSpec(kpos.shape, lambda i: (0, 0)),
        ],
        out_specs=[
            pl.BlockSpec((rows, width), lambda i: (i, 0)),
            pl.BlockSpec((local_kv, group * rows, 1), lambda i: (i, 0, 0)),
        ],
        out_shape=[
            jax.ShapeDtypeStruct((total, width), bf16),
            jax.ShapeDtypeStruct((seqs * local_kv, group * rows, 1), f32),
        ],
        compiler_params=params(),
        name="attend",
    )(q, near, far, qpos, kpos)


def attend_back_kernel(
    local_kv, group, q_ref, near_ref, far_ref, qpos_ref, kpos_ref, log_ref, grad_ref, cos_ref, sin_ref,
    dq_ref, dnear_ref, dfar_ref,
):
    rows = q_ref.shape[0]
    half = near_ref.shape[0] * rows
    scale = HD**-0.5
    allowed = kpos_ref[...] <= qpos_ref[...]
    cosine, sine = cos_ref[...], sin_ref[...]
    for kv in range(local_kv):
        ck, cv = kv * HD, (local_kv + kv) * HD
        q = heads_to_rows(q_ref, kv, group)
        grad = heads_to_rows(grad_ref, kv, group)
        keys = keys_of(near_ref, far_ref, ck)
        values = keys_of(near_ref, far_ref, cv)
        s = jnp.where(allowed, dot(q, keys, 1, 1) * scale, NEGATIVE)
        probs = jnp.exp(s - log_ref[kv])
        prob_grad = dot(grad, values, 1, 1)
        both = probs * prob_grad
        delta = jnp.sum(both, axis=-1, keepdims=True)
        ds = (both - probs * delta).astype(bf16)
        dq = dot(ds, keys, 1, 0) * scale
        for g in range(group):
            c = (kv * group + g) * HD
            dq_ref[:, c : c + HD] = turn(dq[g * rows : (g + 1) * rows], cosine, -sine).astype(bf16)
        dk = (dot(ds, q, 0, 0) * scale).astype(bf16)
        dv = dot(probs.astype(bf16), grad, 0, 0).astype(bf16)
        for d, c in ((dk, ck), (dv, cv)):
            dnear_ref[:, 0, :, c : c + HD] = d[:half].reshape(-1, rows, HD)
            dfar_ref[:, 0, :, c : c + HD] = d[half:].reshape(-1, rows, HD)


def attend_back(q, near, far, qpos, kpos, log, grad, cosine, sine, rows, local_kv, group):
    total, width = q.shape
    seqs = total // rows
    blocks, _, _, kv_width = near.shape
    kv_spec = pl.BlockSpec((blocks, 1, rows, kv_width), lambda i: (0, i, 0, 0))
    row_spec = pl.BlockSpec((rows, width), lambda i: (i, 0))
    table = pl.BlockSpec((rows, HD), lambda i: (0, 0))
    return pl.pallas_call(
        functools.partial(attend_back_kernel, local_kv, group),
        grid=(seqs,),
        in_specs=[
            row_spec,
            kv_spec,
            kv_spec,
            pl.BlockSpec(qpos.shape, lambda i: (0, 0)),
            pl.BlockSpec(kpos.shape, lambda i: (0, 0)),
            pl.BlockSpec((local_kv, group * rows, 1), lambda i: (i, 0, 0)),
            row_spec,
            table,
            table,
        ],
        out_specs=[row_spec, kv_spec, kv_spec],
        out_shape=[
            jax.ShapeDtypeStruct((total, width), bf16),
            jax.ShapeDtypeStruct(near.shape, bf16),
            jax.ShapeDtypeStruct(far.shape, bf16),
        ],
        compiler_params=params(),
        name="attend_back",
    )(q, near, far, qpos, kpos, log, grad, cosine, sine)


def arrange_kernel(block, order_ref, a_ref, keep_ref, send_ref):
    half = order_ref.shape[0] // 2
    for j in range(half):
        for out_ref, at in ((keep_ref, j), (send_ref, half + j)):
            start = pl.multiple_of(order_ref[at] * block, block)
            out_ref[:, j * block : (j + 1) * block] = a_ref[:, pl.ds(start, block)]


def arrange(a, order):
    rows, width = a.shape
    count = order.shape[0]
    block = width // count
    if block % 128:
        moved = jnp.take(a.reshape(rows, count, block), order, axis=1).reshape(rows, width)
        return moved[:, : width // 2], moved[:, width // 2 :]
    out = jax.ShapeDtypeStruct((rows, width // 2), a.dtype)
    return pl.pallas_call(
        functools.partial(arrange_kernel, block),
        in_specs=[
            pl.BlockSpec(memory_space=pltpu.SMEM),
            pl.BlockSpec(memory_space=pltpu.VMEM),
        ],
        out_specs=[pl.BlockSpec(memory_space=pltpu.VMEM)] * 2,
        out_shape=[out, out],
        compiler_params=params(),
        name="arrange",
    )(order, a)


def local(
    n_dp,
    tokens,
    cotangent,
    active,
    assignment,
    attention_gain,
    query_weight,
    key_weight,
    value_weight,
    out_weight,
    feedforward_gain,
    gate_weight,
    up_weight,
    down_weight,
):
    rows, width = tokens.shape[1:]
    live_seqs = tokens.shape[0] - 1
    total = live_seqs * rows
    block = width // n_dp
    groups = n_dp // 4
    q_cols, k_cols = query_weight.shape[1], key_weight.shape[1]
    hidden_units = gate_weight.shape[1]
    local_kv = k_cols // HD
    group = q_cols // k_cols
    me = lax.axis_index("dp").astype(jnp.int32)

    def flip(v, bits):
        return lax.ppermute(v, "dp", [(i, i ^ bits) for i in range(n_dp)])

    def tensor_flip(v):
        return lax.ppermute(v, "tensor", [(0, 1), (1, 0)])

    def tensor_total(partial_rows):
        mine = lax.optimization_barrier(partial_rows.astype(bf16))
        return mine.astype(f32) + tensor_flip(mine).astype(f32)

    near_places = [far * 4 + pair * 2 for pair in range(2) for far in range(groups)]
    places = near_places + [place + 1 for place in near_places]
    owners = jnp.bitwise_xor(me, jnp.asarray(places, jnp.int32))

    positions = me * rows + jnp.arange(rows, dtype=jnp.int32)
    frequency = jnp.exp(
        -jnp.log(10000.0) * (2.0 * jnp.arange(HD // 2, dtype=f32) / HD)
    )
    angles = positions.astype(f32)[:, None] * frequency[None, :]
    cosine = jnp.concatenate([jnp.cos(angles)] * 2, axis=1)
    sine = jnp.concatenate([-jnp.sin(angles), jnp.sin(angles)], axis=1)
    qpos = jnp.tile(positions, group)[:, None]
    kpos = (owners[:, None] * rows + jnp.arange(rows, dtype=jnp.int32)[None, :]).reshape(1, -1)

    gains = jnp.stack([attention_gain, feedforward_gain], axis=1)
    gains = jnp.pad(gains, ((0, 0), (0, 126)))
    first = lax.all_gather(
        jnp.concatenate([query_weight, key_weight, value_weight, out_weight.T, gains], axis=1),
        "dp", axis=0, tiled=True,
    )
    second = lax.all_gather(
        jnp.concatenate([gate_weight, up_weight], axis=1), "dp", axis=0, tiled=True
    )
    down_turned = lax.all_gather(down_weight.T, "dp", axis=0, tiled=True)
    qkv_cols = q_cols + 2 * k_cols
    qkv_full = first[:, :qkv_cols]
    out_turned = first[:, qkv_cols : qkv_cols + q_cols]
    gain_attn = first[:, qkv_cols + q_cols].astype(f32)[None, :]
    gain_mlp = first[:, qkv_cols + q_cols + 1].astype(f32)[None, :]

    dead_slot = jnp.argmin(active.reshape(-1))
    dead = assignment[dead_slot]
    is_dead = (jnp.arange(live_seqs, dtype=jnp.int32) == dead)[:, None, None]

    def pick(v):
        return jnp.where(is_dead, v[live_seqs:], v[:live_seqs]).reshape(total, width)

    def unpick(live_values, skipped):
        live_values = live_values.reshape(live_seqs, rows, width)
        last = lax.dynamic_slice_in_dim(live_values, jnp.minimum(dead, live_seqs - 1), 1, 0)
        return jnp.concatenate(
            [
                jnp.where(is_dead, skipped[:live_seqs], live_values),
                jnp.where(dead == live_seqs, skipped[live_seqs:], last),
            ],
            axis=0,
        )

    token_rows = pick(tokens).astype(f32)
    down_grad = lax.optimization_barrier(pick(cotangent))
    upstream = down_grad.astype(f32)

    attn_scale = rms_scale(token_rows)
    hidden = (token_rows * attn_scale * gain_attn).astype(bf16)
    qkv_raw = dot(hidden, qkv_full, 1, 0)
    queries, kv_own = rope(qkv_raw, cosine, sine, rows, q_cols, k_cols)
    kv_own = kv_own.reshape(1, live_seqs, rows, 2 * k_cols)
    kv_far = jnp.concatenate([kv_own] + [flip(kv_own, 4 * k) for k in range(1, groups)], axis=0)
    kv_near = jnp.concatenate([kv_far, flip(kv_far, 2)], axis=0)
    kv_other = flip(kv_near, 1)
    mixed_out, log_total = attend(
        queries, kv_near, kv_other, qpos, kpos, rows, local_kv, group
    )
    branch = tensor_total(dot(mixed_out, out_turned, 1, 1))
    middle = token_rows + branch

    mlp_scale = rms_scale(middle)
    normed_mlp = middle * mlp_scale
    hidden_mlp = (normed_mlp * gain_mlp).astype(bf16)
    gate_up = dot(hidden_mlp, second, 1, 0)
    gate_values, up_values = gate_up[:, :hidden_units], gate_up[:, hidden_units:]
    sigmoid_gate = jax.nn.sigmoid(gate_values)
    silu_gate = gate_values * sigmoid_gate
    product = (silu_gate * up_values).astype(bf16)

    def side(a):
        keep, send = arrange(a, owners)
        return jnp.concatenate([keep, flip(send, 1)], axis=0)

    def both_cores(b):
        return jnp.concatenate([b, flip(b, 1)], axis=0)

    def summed(a_side, b):
        half = groups * block
        sent = dot(a_side[:, half:], b, 0, 0).astype(bf16)
        kept = dot(a_side[:, :half], b, 0, 0)
        pair = (kept + flip(sent, 2).astype(f32)).reshape(groups, block, b.shape[1])
        out = pair[0]
        for k in range(1, groups):
            out = out + flip(pair[k].astype(bf16), 4 * k).astype(f32)
        return out

    grad_down = summed(side(down_grad), both_cores(product)).T
    down_values = tensor_total(dot(product, down_turned, 1, 1))
    result = unpick((middle + down_values).astype(bf16), tokens)

    product_grad = dot(down_grad, down_turned, 1, 0)
    gate_grad = (
        product_grad * up_values * (sigmoid_gate * (1.0 + gate_values * (1.0 - sigmoid_gate)))
    ).astype(bf16)
    up_grad = (product_grad * silu_gate).astype(bf16)
    gate_up_grad = jnp.concatenate([gate_grad, up_grad], axis=1)
    mlp_side = side(hidden_mlp)
    grad_gate = summed(mlp_side, both_cores(gate_grad))
    grad_up = summed(mlp_side, both_cores(up_grad))
    hidden_mlp_grad = tensor_total(dot(gate_up_grad, second, 1, 1))
    gain_mlp_rows = jnp.sum(hidden_mlp_grad * normed_mlp, axis=0)
    normed_grad = hidden_mlp_grad * gain_mlp
    middle_grad = upstream + mlp_scale * (
        normed_grad - normed_mlp * jnp.mean(normed_grad * normed_mlp, axis=-1, keepdims=True)
    )

    branch_grad = middle_grad.astype(bf16)
    grad_out = summed(side(branch_grad), both_cores(mixed_out)).T
    mixed_grad = dot(branch_grad, out_turned, 1, 0).astype(bf16)
    query_grad, dkv_near, dkv_other = attend_back(
        queries, kv_near, kv_other, qpos, kpos, log_total, mixed_grad, cosine, sine,
        rows, local_kv, group,
    )
    dkv_near = dkv_near.astype(f32) + flip(dkv_other, 1).astype(f32)
    dkv_far = dkv_near[:groups] + flip(dkv_near[groups:].astype(bf16), 2).astype(f32)
    dkv = dkv_far[0]
    for k in range(1, groups):
        dkv = dkv + flip(dkv_far[k].astype(bf16), 4 * k).astype(f32)
    dkv = dkv.reshape(total, 2 * k_cols)
    key_grad, _ = rope(
        jnp.concatenate([dkv[:, :k_cols], dkv], axis=1), cosine, -sine, rows, k_cols, k_cols
    )
    qkv_grad = jnp.concatenate([query_grad, key_grad, dkv[:, k_cols:].astype(bf16)], axis=1)
    grad_qkv = summed(side(hidden), both_cores(qkv_grad))
    hidden_grad = tensor_total(dot(qkv_grad, qkv_full, 1, 1))
    normed_attn = token_rows * attn_scale
    gain_attn_rows = jnp.sum(hidden_grad * normed_attn, axis=0)
    normed_attn_grad = hidden_grad * gain_attn
    input_grad = middle_grad + attn_scale * (
        normed_attn_grad
        - normed_attn * jnp.mean(normed_attn_grad * normed_attn, axis=-1, keepdims=True)
    )
    input_grad = unpick(input_grad, cotangent.astype(f32))

    gain_rows = jnp.stack([gain_attn_rows, gain_mlp_rows]).reshape(2, n_dp, block)
    gain_rows = jnp.take(gain_rows, owners, axis=1)
    gain_rows = gain_rows[:, : 2 * groups] + flip(gain_rows[:, 2 * groups :], 1)
    gain_rows = gain_rows[:, :groups] + flip(gain_rows[:, groups:], 2)
    gain_own = gain_rows[:, 0]
    for k in range(1, groups):
        gain_own = gain_own + flip(gain_rows[:, k], 4 * k)

    return (
        result,
        input_grad,
        gain_own[0],
        grad_qkv[:, :q_cols],
        grad_qkv[:, q_cols : q_cols + k_cols],
        grad_qkv[:, q_cols + k_cols :],
        grad_out,
        gain_own[1],
        grad_gate,
        grad_up,
        grad_down,
    )


def solution(mesh):
    rows = P(None, "dp", None)
    split = P("dp", "tensor")
    turned = P("tensor", "dp")
    gain = P("dp")
    weights = (gain, split, split, split, turned, gain, split, split, turned)
    return jax.shard_map(
        functools.partial(local, mesh.shape["dp"]),
        mesh=mesh,
        in_specs=(rows, rows, P(), P(), *weights),
        out_specs=(rows, rows, *weights),
        check_vma=False,
    )
```

time: 2470 us -> 939 us (0.38)
  waiting for transfers between devices: 1870 us -> 622 us
  matrix products: 344 us -> 120 us
  blocking collectives: 100 us -> 0 us
  starting transfers between devices: 2.21 us -> 67.7 us
  local copies, waits for them, and re-layouts: 77.9 us -> 21.5 us
  Pallas kernels: 0 us -> 29.4 us
    reduce_scatter x13 -> x0, waiting for transfers between devices: 1180 us -> none  [the longest x1 232 us: reduce_grads(): lax.psum_scatter(bundle[6], 'dp', scatter_dimension=0, tiled=True)]
    ppermute x0 -> x48, waiting for transfers between devices: none -> 457 us  [the longest x44 382 us: flip(): return lax.ppermute(v, 'dp', [(i, i ^ bits) for i in range(n_dp)])]
    all_gather x13 -> x3, waiting for transfers between devices: 604 us -> 164 us  [the longest x1 88.7 us: local(): lax.all_gather(jnp.concatenate([query_weight, key_weight, value_weight, o...]
    dot_general x84 -> x18, matrix products: 344 us -> 120 us  [dot(): lax.dot_general(a, b, (((ca,), (cb,)), ((), ())), preferred_element_type=...]
    psum x3 -> x0, waiting for transfers between devices: 71 us -> none  [tensor_total(): lax.psum(partial_rows.astype(jnp.bfloat16), 'tensor').astype(jnp.float32)]
    ppermute x0 -> x48, starting transfers between devices: none -> 67.6 us  [the longest x44 62.5 us: flip(): return lax.ppermute(v, 'dp', [(i, i ^ bits) for i in range(n_dp)])]
    unnamed x1 -> x0, blocking collectives: 57.9 us -> none
    all_gather x2 -> x0, blocking collectives: 42.1 us -> none  [the longest x1 23.2 us: fetch_weights(): lax.all_gather(bundle[0], 'dp', axis=0, tiled=True)]
  transfers between devices with their start and end apart: 29 -> 51, of which waited for: 25 -> 25; matrix products, arithmetic and copies ran while one was open for 14% -> 16% of each run, Pallas kernels for 0% -> 3%
where the time goes in v1:
time: 939 us; the launch traced here: 929 us
  waiting for transfers between devices  622 us (66%)
  matrix products  120 us (13%)
  starting transfers between devices  67.7 us (7%)
  other arithmetic  50.3 us (5%)
  Pallas kernels  29.4 us (3%)
  local copies, waits for them, and re-layouts  21.5 us (2%)
  between operations  18.5 us (2%)
    ppermute x44, waiting for transfers between devices, flip(): return lax.ppermute(v, 'dp', [(i, i ^ bits) for i in range(n_dp)])  382 us
    dot_general x18, matrix products, dot(): lax.dot_general(a, b, (((ca,), (cb,)), ((), ())), preferred_element_type=...  120 us
    all_gather x1, waiting for transfers between devices, local(): lax.all_gather(jnp.concatenate([query_weight, key_weight, value_weight, o...  88.7 us
    ppermute x4, waiting for transfers between devices, tensor_flip(): return lax.ppermute(v, 'tensor', [(0, 1), (1, 0)])  75.4 us
    all_gather x1, waiting for transfers between devices, local(): down_turned = lax.all_gather(down_weight.T, 'dp', axis=0, tiled=True)  75 us
    ppermute x44, starting transfers between devices, flip(): return lax.ppermute(v, 'dp', [(i, i ^ bits) for i in range(n_dp)])  62.5 us
  transfers between devices with their start and end apart: 51, of which 25 were waited for; matrix products, arithmetic and copies ran while one was open for 16% of the time, Pallas kernels for 3%

profile of v1, /device:TPU:0, one launch (start us, length us, event | category | flops | bytes accessed | tf_op | source)
XLA Modules:
  0.0 929.0 jit_solution(8986695118327315518)
XLA Ops:
  13.0 2.4 pad_maximum_fusion.12
  21.3 88.7 %all-gather.4.cloned.1.call-done = bf16[2048,2688]{0,1:T(8,128)(2,1)} async-done(((bf16[128,2688]{0,1:T(8,128)(2,1)}), bf16[2048,2688]{0,1:T(8,128)(2,1)}) %all-gather.4.cloned.1.call-update) | async-done | bytes 11010064 | tf_op jit(solution)/shard_map/all_gather | solution.py:270
  110.9 2.0 bitcast_multiply_fusion
  112.9 5.5 fusion.2.raw_ref
  119.3 2.0 collective-permute-start.1
  121.3 2.4 collective-permute-start.2
  123.7 20.0 %collective-permute-done = bf16[1,5,64,512]{3,2,1,0:T(8,128)(2,1)S(1)} collective-permute-done((bf16[1,5,64,512]{3,2,1,0:T(8,128)(2,1)S(1)}, bf16[1,5,64,512]{3,2,1,0:T(8,128)(2,1)S(1)}, u32[]{:S(2)}, u32[]{:S(2)}) %collective-permute-start) | collective-permute-done | bytes 327712 | tf_op jit(solution)/shard_map/ppermute | solution.py:245
  143.6 4.8 collective-permute-done.1
  148.4 17.2 %collective-permute-done.2 = bf16[1,5,64,512]{3,2,1,0:T(8,128)(2,1)S(1)} collective-permute-done((bf16[1,5,64,512]{3,2,1,0:T(8,128)(2,1)S(1)}, bf16[1,5,64,512]{3,2,1,0:T(8,128)(2,1)S(1)}, u32[]{:S(2)}, u32[]{:S(2)}) %collective-permute-start.2) | collective-permute-done | bytes 327712 | tf_op jit(solution)/shard_map/ppermute | solution.py:245
  166.5 57.5 %collective-permute-done.3 = bf16[4,5,64,512]{3,2,1,0:T(8,128)(2,1)S(1)} collective-permute-done((bf16[4,5,64,512]{3,2,1,0:T(8,128)(2,1)S(1)}, bf16[4,5,64,512]{3,2,1,0:T(8,128)(2,1)S(1)}, u32[]{:S(2)}, u32[]{:S(2)}) %collective-permute-start.3) | collective-permute-done | bytes 1310752 | tf_op jit(solution)/shard_map/ppermute | solution.py:245
  224.6 4.7 collective-permute-done.4.far_ref
  229.3 8.6 attend.1
  237.9 4.6 fusion.16
  244.3 29.2 %collective-permute-done.5 = bf16[320,2048]{1,0:T(8,128)(2,1)S(1)} collective-permute-done((bf16[320,2048]{1,0:T(8,128)(2,1)S(1)}, bf16[320,2048]{1,0:T(8,128)(2,1)S(1)}, u32[]{:S(2)}, u32[]{:S(2)}) %collective-permute-start.5) | collective-permute-done | bytes 1310752 | tf_op jit(solution)/shard_map/ppermute | solution.py:248
  276.1 15.6 %fusion.84 = f32[320,5632]{1,0:T(8,128)} fusion(bf16[320,2048]{1,0:T(8,128)(2,1)S(1)} %multiply_convert_fusion.3.a_ref, bf16[2048,5632]{1,0:T(8,128)(2,1)} %all-gather.6.cloned.1.call-done), kind=kOutput, calls=%fused_computation.189 | convolution fusion | flops 7381975040 | bytes 31588352 | tf_op jit(solution)/shard_map/dot_general | solution.py:24
  291.7 75.0 %all-gather.8.cloned.1.call-done = bf16[2048,2816]{0,1:T(8,128)(2,1)} async-done(((bf16[128,2816]{0,1:T(8,128)(2,1)}), bf16[2048,2816]{0,1:T(8,128)(2,1)}) %all-gather.8.cloned.1.call-update) | async-done | bytes 11534352 | tf_op jit(solution)/shard_map/all_gather | solution.py:277
  366.7 15.7 %multiply_convert_fusion.1 = (bf16[320,2816]{1,0:T(8,128)(2,1)}, bf16[320,2816]{1,0:T(8,128)(2,1)}, bf16[320,2816]{1,0:T(8,128)(2,1)}) fusion(f32[320,5632]{1,0:T(8,128)} %fusion.84, bf16[320,2048]{1,0:T(8,128)(2,1)S(1)} %bitcast.78, bf16[2048,2816]{0,1:T(8,128)(2,1)} %all-gather.8.cloned.1.call-done), kind=kOutput, calls=%fused_computation.24 | convolution fusion | flops 3704504320 | bytes 25460736 | tf_op jit(solution)/shard_map/dot_general | solution.py:24
  382.4 14.0 %fusion.19 = bf16[320,2048]{1,0:T(8,128)(2,1)} fusion(bf16[2048,5632]{1,0:T(8,128)(2,1)} %all-gather.6.cloned.1.call-done, bf16[320,2816]{1,0:T(8,128)(2,1)} %get-tuple-element.80, bf16[320,2816]{1,0:T(8,128)(2,1)} %get-tuple-element.79), kind=kOutput, calls=%fused_computation.34 | convolution fusion | flops 7389839360 | bytes 27983872 | tf_op jit(solution)/shard_map/dot_general | solution.py:24
  401.7 3.5 convert_element_type.244
  412.0 15.7 %collective-permute-done.7 = bf16[320,2048]{1,0:T(8,128)(2,1)} collective-permute-done((bf16[320,2048]{1,0:T(8,128)(2,1)}, bf16[320,2048]{1,0:T(8,128)(2,1)}, u32[]{:S(2)}, u32[]{:S(2)}) %collective-permute-start.7) | collective-permute-done | bytes 1310752 | tf_op jit(solution)/shard_map/ppermute | solution.py:248
  427.6 2.4 multiply_reduce_fusion
  430.0 2.4 fusion.70.a_ref
  438.1 3.9 fusion.32.grad_ref
  441.9 13.1 %attend_back.1 = (bf16[320,1024]{1,0:T(8,128)(2,1)S(1)}, bf16[8,5,64,512]{3,2,1,0:T(8,128)(2,1)S(1)}, bf16[8,5,64,512]{3,2,1,0:T(8,128)(2,1)}) custom-call(bf16[320,1024]{1,0:T(8,128)(2,1)S(1)} %get-tuple-element.29.q_ref, bf16[8,5,64,512]{3,2,1,0:T(8,128)(2,1)} %copy-done, bf16[8,5,64,512]{3,2,1,0:T(8,128)(2,1)} %collective-permute-done.4.far_ref, ...), custom_call_target="tpu_custom_call" | custom-call | tf_op jit(solution)/shard_map/attend_back/pallas_call | solution.py:163
  455.2 7.2 convolution_convert_fusion.2
  463.0 6.4 convolution_convert_fusion.1
  472.7 6.6 convolution_convert_fusion.4
  481.0 10.5 %collective-permute-start.28 = (bf16[128,1024]{1,0:T(8,128)(2,1)S(1)}, bf16[128,1024]{1,0:T(8,128)(2,1)S(1)}, u32[]{:S(2)}, u32[]{:S(2)}) collective-permute-start(bf16[128,1024]{1,0:T(8,128)(2,1)S(1)} %get-tuple-element.101), channel_id=1, source_target_pairs={{0,8},{2,10},{4,12},{6,14},{8,0},{10,2},{12,4},{14,6},{16,24},{18,... | collective-permute-start | bytes 786440 | tf_op jit(solution)/shard_map/ppermute | solution.py:245
  491.6 6.1 convolution_convert_fusion
  500.8 2.0 copy.37
  502.9 3.9 convert_add_fusion.3
  508.4 19.6 %collective-permute-done.33 = bf16[512,2816]{1,0:T(8,128)(2,1)} collective-permute-done((bf16[512,2816]{1,0:T(8,128)(2,1)}, bf16[512,2816]{1,0:T(8,128)(2,1)}, u32[]{:S(2)}, u32[]{:S(2)}) %collective-permute-start.33) | collective-permute-done | bytes 2883616 | tf_op jit(solution)/shard_map/ppermute | solution.py:245
  528.1 4.9 fusion.81
  534.2 55.7 %collective-permute-done.38 = bf16[512,2816]{1,0:T(8,128)(2,1)} collective-permute-done((bf16[512,2816]{1,0:T(8,128)(2,1)}, bf16[512,2816]{1,0:T(8,128)(2,1)}, u32[]{:S(2)}, u32[]{:S(2)}) %collective-permute-start.38) | collective-permute-done | bytes 2883616 | tf_op jit(solution)/shard_map/ppermute | solution.py:245
  589.9 7.8 fusion.82
  599.1 52.6 %collective-permute-done.44 = bf16[512,2816]{1,0:T(8,128)(2,1)} collective-permute-done((bf16[512,2816]{1,0:T(8,128)(2,1)}, bf16[512,2816]{1,0:T(8,128)(2,1)}, u32[]{:S(2)}, u32[]{:S(2)}) %collective-permute-start.44) | collective-permute-done | bytes 2883616 | tf_op jit(solution)/shard_map/ppermute | solution.py:245
  652.7 7.9 fusion.83
  660.7 17.8 %collective-permute-done.9 = bf16[4,5,64,512]{3,2,1,0:T(8,128)(2,1)S(1)} collective-permute-done((bf16[4,5,64,512]{3,2,1,0:T(8,128)(2,1)S(1)}, bf16[4,5,64,512]{3,2,1,0:T(8,128)(2,1)S(1)}, u32[]{:S(2)}, u32[]{:S(2)}) %collective-permute-start.9) | collective-permute-done | bytes 1310752 | tf_op jit(solution)/shard_map/ppermute | solution.py:245
  680.2 1.9 collective-permute-start.11
  682.2 2.0 collective-permute-start.10
  685.6 18.4 %collective-permute-done.12 = bf16[5,64,512]{2,1,0:T(8,128)(2,1)S(1)} collective-permute-done((bf16[5,64,512]{2,1,0:T(8,128)(2,1)S(1)}, bf16[5,64,512]{2,1,0:T(8,128)(2,1)S(1)}, u32[]{:S(2)}, u32[]{:S(2)}) %collective-permute-start.12) | collective-permute-done | bytes 327712 | tf_op jit(solution)/shard_map/ppermute | solution.py:245
  703.9 3.4 collective-permute-start.47
  707.3 59.3 %collective-permute-done.11 = bf16[5,64,512]{2,1,0:T(8,128)(2,1)S(1)} collective-permute-done((bf16[5,64,512]{2,1,0:T(8,128)(2,1)S(1)}, bf16[5,64,512]{2,1,0:T(8,128)(2,1)S(1)}, u32[]{:S(2)}, u32[]{:S(2)}) %collective-permute-start.11) | collective-permute-done | bytes 327712 | tf_op jit(solution)/shard_map/ppermute | solution.py:245
  766.6 2.2 collective-permute-start.45
  769.1 2.4 rope.3
  771.6 5.0 fusion.13
  777.7 12.7 %collective-permute-start.39 = (bf16[128,2816]{1,0:T(8,128)(2,1)}, bf16[128,2816]{1,0:T(8,128)(2,1)}, u32[]{:S(2)}, u32[]{:S(2)}) collective-permute-start(bf16[128,2816]{1,0:T(8,128)(2,1)} %get-tuple-element.85), channel_id=1, source_target_pairs={{0,8},{2,10},{4,12},{6,14},{8,0},{10,2},{12,4},{14,6},{16,24},{18,... | collective-permute-start | bytes 2162696 | tf_op jit(solution)/shard_map/ppermute | solution.py:245
  790.3 12.6 %collective-permute-done.46 = bf16[128,2816]{1,0:T(8,128)(2,1)S(1)} collective-permute-done((bf16[128,2816]{1,0:T(8,128)(2,1)S(1)}, bf16[128,2816]{1,0:T(8,128)(2,1)S(1)}, u32[]{:S(2)}, u32[]{:S(2)}) %collective-permute-start.46) | collective-permute-done | bytes 720928 | tf_op jit(solution)/shard_map/ppermute | solution.py:245
  804.4 2.7 fusion.27
  807.2 2.9 copy.38
  810.7 6.3 collective-permute-done.39
  817.0 3.4 fusion.29
  820.4 3.9 convolution_convert_fusion.3
  825.9 8.8 collective-permute-done.13
  834.8 2.9 multiply_reduce_fusion.1
  837.7 21.7 %collective-permute-done.6 = bf16[320,2048]{1,0:T(8,128)(2,1)S(1)} collective-permute-done((bf16[320,2048]{1,0:T(8,128)(2,1)}, bf16[320,2048]{1,0:T(8,128)(2,1)S(1)}, u32[]{:S(2)}, u32[]{:S(2)}) %collective-permute-start.6) | collective-permute-done | bytes 1310752 | tf_op jit(solution)/shard_map/ppermute | solution.py:248
  859.4 4.9 multiply_add_fusion
  865.4 3.1 slice_select_fusion
  870.8 2.0 pad_maximum_fusion.3
  876.5 3.8 collective-permute-start.18
  880.9 3.2 fusion.79
  884.2 3.8 collective-permute-start.24
  889.2 9.0 collective-permute-done.24
  898.2 22.1 %collective-permute-done.23 = bf16[128,1536]{1,0:T(8,128)(2,1)S(1)} collective-permute-done((bf16[128,1536]{1,0:T(8,128)(2,1)S(1)}, bf16[128,1536]{1,0:T(8,128)(2,1)S(1)}, u32[]{:S(2)}, u32[]{:S(2)}) %collective-permute-start.23) | collective-permute-done | bytes 393248 | tf_op jit(solution)/shard_map/ppermute | solution.py:245
  (260 shorter events, 66.5 us)
Async XLA Ops:
  7.2 102.8 %all-gather.4.cloned.1.call-start = ((), (), s32[]{:S(2)}) async-start(), calls=%async_computation | async-start | bytes 11698176 | tf_op jit(solution)/shard_map/all_gather | solution.py:270
  13.0 263.1 %all-gather.6.cloned.1.call-start = ((), (), s32[]{:S(2)}) async-start(), calls=%async_computation.1 | async-start | bytes 24510464 | tf_op jit(solution)/shard_map/all_gather | solution.py:274
  15.5 351.2 %all-gather.8.cloned.1.call-start = ((), (), s32[]{:S(2)}) async-start(), calls=%async_computation.2 | async-start | bytes 12255232 | tf_op jit(solution)/shard_map/all_gather | solution.py:277
  20.3 92.6 %copy-start.20 = (bf16[64,2048]{1,0:T(8,128)(2,1)}, bf16[64,2048]{1,0:T(8,128)(2,1)S(1)}, u32[]{:S(2)}) copy-start(bf16[64,2048]{1,0:T(8,128)(2,1)S(1)} %slice_bitcast_fusion.5) | copy-start | bytes 786436
  119.2 24.4 %collective-permute-start = (bf16[1,5,64,512]{3,2,1,0:T(8,128)(2,1)S(1)}, bf16[1,5,64,512]{3,2,1,0:T(8,128)(2,1)S(1)}, u32[]{:S(2)}, u32[]{:S(2)}) collective-permute-start(bf16[1,5,64,512]{3,2,1,0:T(8,128)(2,1)S(1)} %bitcast.82), channel_id=1, source_target_pairs={{0,8},{2,10},{4,12},{6,14},{8,0},{10,2},{12,4},{14,6},{16,24},{18,... | collective-permute-start | bytes 983048 | tf_op jit(solution)/shard_map/ppermute | solution.py:245
  119.3 29.1 %collective-permute-start.1 = (bf16[1,5,64,512]{3,2,1,0:T(8,128)(2,1)S(1)}, bf16[1,5,64,512]{3,2,1,0:T(8,128)(2,1)S(1)}, u32[]{:S(2)}, u32[]{:S(2)}) collective-permute-start(bf16[1,5,64,512]{3,2,1,0:T(8,128)(2,1)S(1)} %bitcast.83), channel_id=1, source_target_pairs={{0,16},{2,18},{4,20},{6,22},{8,24},{10,26},{12,28},{14,30},{16,0},... | collective-permute-start | bytes 983048 | tf_op jit(solution)/shard_map/ppermute | solution.py:245
  121.3 44.4 %collective-permute-start.2 = (bf16[1,5,64,512]{3,2,1,0:T(8,128)(2,1)S(1)}, bf16[1,5,64,512]{3,2,1,0:T(8,128)(2,1)S(1)}, u32[]{:S(2)}, u32[]{:S(2)}) collective-permute-start(bf16[1,5,64,512]{3,2,1,0:T(8,128)(2,1)S(1)} %bitcast.84), channel_id=1, source_target_pairs={{0,24},{2,26},{4,28},{6,30},{8,16},{10,18},{12,20},{14,22},{16,8},... | collective-permute-start | bytes 983048 | tf_op jit(solution)/shard_map/ppermute | solution.py:245
  165.8 58.6 %copy-start.39 = (s32[16]{0:T(128)S(1)}, s32[16]{0:T(128)}, u32[]{:S(2)}) copy-start(s32[16]{0:T(128)} %constant.60.clone) | copy-start | bytes 196
  165.8 58.2 %collective-permute-start.3 = (bf16[4,5,64,512]{3,2,1,0:T(8,128)(2,1)S(1)}, bf16[4,5,64,512]{3,2,1,0:T(8,128)(2,1)S(1)}, u32[]{:S(2)}, u32[]{:S(2)}) collective-permute-start(bf16[4,5,64,512]{3,2,1,0:T(8,128)(2,1)S(1)} %pad_maximum_fusion.13), channel_id=1, source_target_pairs={{0,4},{2,6},{4,0},{6,2},{8,12},{10,14},{12,8},{14,10},{16,20},{18,... | collective-permute-start | bytes 3932168 | tf_op jit(solution)/shard_map/ppermute | solution.py:245
  224.2 5.1 collective-permute-start.4
  242.5 30.9 %copy-start.15 = (bf16[6,64,2048]{2,1,0:T(8,128)(2,1)S(1)}, bf16[6,64,2048]{2,1,0:T(8,128)(2,1)}, u32[]{:S(2)}) copy-start(bf16[6,64,2048]{2,1,0:T(8,128)(2,1)} %param.14) | copy-start | bytes 4718596
  242.6 30.9 %copy-start.21 = (bf16[64,2048]{1,0:T(8,128)(2,1)S(1)}, bf16[64,2048]{1,0:T(8,128)(2,1)}, u32[]{:S(2)}) copy-start(bf16[64,2048]{1,0:T(8,128)(2,1)} %copy-done.20) | copy-start | bytes 786436
  242.6 30.9 %collective-permute-start.5 = (bf16[320,2048]{1,0:T(8,128)(2,1)S(1)}, bf16[320,2048]{1,0:T(8,128)(2,1)S(1)}, u32[]{:S(2)}, u32[]{:S(2)}) collective-permute-start(bf16[320,2048]{1,0:T(8,128)(2,1)S(1)} %fusion.16), channel_id=1, source_target_pairs={{0,1},{1,0},{2,3},{3,2},{4,5},{5,4},{6,7},{7,6},{8,9},{9,8},{10,11... | collective-permute-start | bytes 3932168 | tf_op jit(solution)/shard_map/ppermute | solution.py:248
  396.4 31.3 %collective-permute-start.7 = (bf16[320,2048]{1,0:T(8,128)(2,1)}, bf16[320,2048]{1,0:T(8,128)(2,1)}, u32[]{:S(2)}, u32[]{:S(2)}) collective-permute-start(bf16[320,2048]{1,0:T(8,128)(2,1)} %fusion.19), channel_id=1, source_target_pairs={{0,1},{1,0},{2,3},{3,2},{4,5},{5,4},{6,7},{7,6},{8,9},{9,8},{10,11... | collective-permute-start | bytes 3932168 | tf_op jit(solution)/shard_map/ppermute | solution.py:248
  400.4 7.1 collective-permute-start.42
  408.8 82.8 %copy-start.34 = (bf16[640,1024]{1,0:T(8,128)(2,1)}, bf16[640,1024]{1,0:T(8,128)(2,1)S(1)}, u32[]{:S(2)}) copy-start(bf16[640,1024]{1,0:T(8,128)(2,1)S(1)} %constant_dynamic-update-slice_fusion.17) | copy-start | bytes 3932164
  409.7 23.7 %collective-permute-start.19 = (bf16[320,1024]{1,0:T(8,128)(2,1)S(1)}, bf16[320,1024]{1,0:T(8,128)(2,1)S(1)}, u32[]{:S(2)}, u32[]{:S(2)}) collective-permute-start(bf16[320,1024]{1,0:T(8,128)(2,1)S(1)} %get-tuple-element.38), channel_id=1, source_target_pairs={{0,2},{2,0},{4,6},{6,4},{8,10},{10,8},{12,14},{14,12},{16,18},{18,... | collective-permute-start | bytes 1966088 | tf_op jit(solution)/shard_map/ppermute | solution.py:245
  410.3 23.7 %collective-permute-start.26 = (bf16[320,1024]{1,0:T(8,128)(2,1)S(1)}, bf16[320,1024]{1,0:T(8,128)(2,1)S(1)}, u32[]{:S(2)}, u32[]{:S(2)}) collective-permute-start(bf16[320,1024]{1,0:T(8,128)(2,1)S(1)} %copy-done.7), channel_id=1, source_target_pairs={{0,2},{2,0},{4,6},{6,4},{8,10},{10,8},{12,14},{14,12},{16,18},{18,... | collective-permute-start | bytes 1966088 | tf_op jit(solution)/shard_map/ppermute | solution.py:245
  411.3 22.8 %collective-permute-start.31 = (bf16[320,1024]{1,0:T(8,128)(2,1)S(1)}, bf16[320,1024]{1,0:T(8,128)(2,1)S(1)}, u32[]{:S(2)}, u32[]{:S(2)}) collective-permute-start(bf16[320,1024]{1,0:T(8,128)(2,1)S(1)} %get-tuple-element.42), channel_id=1, source_target_pairs={{0,2},{2,0},{4,6},{6,4},{8,10},{10,8},{12,14},{14,12},{16,18},{18,... | collective-permute-start | bytes 1966088 | tf_op jit(solution)/shard_map/ppermute | solution.py:245
  411.9 43.3 %collective-permute-start.32 = (bf16[320,2816]{1,0:T(8,128)(2,1)}, bf16[320,2816]{1,0:T(8,128)(2,1)}, u32[]{:S(2)}, u32[]{:S(2)}) collective-permute-start(bf16[320,2816]{1,0:T(8,128)(2,1)} %get-tuple-element.79), channel_id=1, source_target_pairs={{0,2},{2,0},{4,6},{6,4},{8,10},{10,8},{12,14},{14,12},{16,18},{18,... | collective-permute-start | bytes 5406728 | tf_op jit(solution)/shard_map/ppermute | solution.py:245
  433.3 2.2 collective-permute-start.25
  433.5 29.5 %collective-permute-start.37 = (bf16[320,2816]{1,0:T(8,128)(2,1)}, bf16[320,2816]{1,0:T(8,128)(2,1)}, u32[]{:S(2)}, u32[]{:S(2)}) collective-permute-start(bf16[320,2816]{1,0:T(8,128)(2,1)} %get-tuple-element.80), channel_id=1, source_target_pairs={{0,2},{2,0},{4,6},{6,4},{8,10},{10,8},{12,14},{14,12},{16,18},{18,... | collective-permute-start | bytes 5406728 | tf_op jit(solution)/shard_map/ppermute | solution.py:245
  434.5 28.5 %copy-start.36 = (bf16[640,1024]{1,0:T(8,128)(2,1)}, bf16[640,1024]{1,0:T(8,128)(2,1)S(1)}, u32[]{:S(2)}) copy-start(bf16[640,1024]{1,0:T(8,128)(2,1)S(1)} %constant_dynamic-update-slice_fusion.15) | copy-start | bytes 3932164
  434.5 44.8 %collective-permute-start.43 = (bf16[320,2816]{1,0:T(8,128)(2,1)}, bf16[320,2816]{1,0:T(8,128)(2,1)}, u32[]{:S(2)}, u32[]{:S(2)}) collective-permute-start(bf16[320,2816]{1,0:T(8,128)(2,1)} %get-tuple-element.81), channel_id=1, source_target_pairs={{0,2},{2,0},{4,6},{6,4},{8,10},{10,8},{12,14},{14,12},{16,18},{18,... | collective-permute-start | bytes 5406728 | tf_op jit(solution)/shard_map/ppermute | solution.py:245
  436.6 34.0 %collective-permute-start.27 = (bf16[512,1024]{1,0:T(8,128)(2,1)S(1)}, bf16[512,1024]{1,0:T(8,128)(2,1)S(1)}, u32[]{:S(2)}, u32[]{:S(2)}) collective-permute-start(bf16[512,1024]{1,0:T(8,128)(2,1)S(1)} %convolution_convert_fusion.5), channel_id=1, source_target_pairs={{0,4},{2,6},{4,0},{6,2},{8,12},{10,14},{12,8},{14,10},{16,20},{18,... | collective-permute-start | bytes 3145736 | tf_op jit(solution)/shard_map/ppermute | solution.py:245
  455.1 47.8 %collective-permute-start.8 = (bf16[8,5,64,512]{3,2,1,0:T(8,128)(2,1)}, bf16[8,5,64,512]{3,2,1,0:T(8,128)(2,1)}, u32[]{:S(2)}, u32[]{:S(2)}) collective-permute-start(bf16[8,5,64,512]{3,2,1,0:T(8,128)(2,1)} %get-tuple-element.35), channel_id=1, source_target_pairs={{0,2},{2,0},{4,6},{6,4},{8,10},{10,8},{12,14},{14,12},{16,18},{18,... | collective-permute-start | bytes 7864328 | tf_op jit(solution)/shard_map/ppermute | solution.py:245
  462.4 65.7 %collective-permute-start.33 = (bf16[512,2816]{1,0:T(8,128)(2,1)}, bf16[512,2816]{1,0:T(8,128)(2,1)}, u32[]{:S(2)}, u32[]{:S(2)}) collective-permute-start(bf16[512,2816]{1,0:T(8,128)(2,1)} %convolution_convert_fusion.2), channel_id=1, source_target_pairs={{0,4},{2,6},{4,0},{6,2},{8,12},{10,14},{12,8},{14,10},{16,20},{18,... | collective-permute-start | bytes 8650760 | tf_op jit(solution)/shard_map/ppermute | solution.py:245
  469.4 120.5 %collective-permute-start.38 = (bf16[512,2816]{1,0:T(8,128)(2,1)}, bf16[512,2816]{1,0:T(8,128)(2,1)}, u32[]{:S(2)}, u32[]{:S(2)}) collective-permute-start(bf16[512,2816]{1,0:T(8,128)(2,1)} %convolution_convert_fusion.1), channel_id=1, source_target_pairs={{0,4},{2,6},{4,0},{6,2},{8,12},{10,14},{12,8},{14,10},{16,20},{18,... | collective-permute-start | bytes 8650760 | tf_op jit(solution)/shard_map/ppermute | solution.py:245
  471.6 9.4 %collective-permute-start.30 = (bf16[128,1024]{1,0:T(8,128)(2,1)S(1)}, bf16[128,1024]{1,0:T(8,128)(2,1)S(1)}, u32[]{:S(2)}, u32[]{:S(2)}) collective-permute-start(bf16[128,1024]{1,0:T(8,128)(2,1)S(1)} %get-tuple-element.102), channel_id=1, source_target_pairs={{0,24},{2,26},{4,28},{6,30},{8,16},{10,18},{12,20},{14,22},{16,8},... | collective-permute-start | bytes 786440 | tf_op jit(solution)/shard_map/ppermute | solution.py:245
  479.3 18.4 %collective-permute-start.29 = (bf16[128,1024]{1,0:T(8,128)(2,1)S(1)}, bf16[128,1024]{1,0:T(8,128)(2,1)S(1)}, u32[]{:S(2)}, u32[]{:S(2)}) collective-permute-start(bf16[128,1024]{1,0:T(8,128)(2,1)S(1)} %get-tuple-element.103), channel_id=1, source_target_pairs={{0,16},{2,18},{4,20},{6,22},{8,24},{10,26},{12,28},{14,30},{16,0},... | collective-permute-start | bytes 786440 | tf_op jit(solution)/shard_map/ppermute | solution.py:245
  481.0 18.9 %collective-permute-start.28 = (bf16[128,1024]{1,0:T(8,128)(2,1)S(1)}, bf16[128,1024]{1,0:T(8,128)(2,1)S(1)}, u32[]{:S(2)}, u32[]{:S(2)}) collective-permute-start(bf16[128,1024]{1,0:T(8,128)(2,1)S(1)} %get-tuple-element.101), channel_id=1, source_target_pairs={{0,8},{2,10},{4,12},{6,14},{8,0},{10,2},{12,4},{14,6},{16,24},{18,... | collective-permute-start | bytes 786440 | tf_op jit(solution)/shard_map/ppermute | solution.py:245
  497.7 153.9 %collective-permute-start.44 = (bf16[512,2816]{1,0:T(8,128)(2,1)}, bf16[512,2816]{1,0:T(8,128)(2,1)}, u32[]{:S(2)}, u32[]{:S(2)}) collective-permute-start(bf16[512,2816]{1,0:T(8,128)(2,1)} %convolution_convert_fusion), channel_id=1, source_target_pairs={{0,4},{2,6},{4,0},{6,2},{8,12},{10,14},{12,8},{14,10},{16,20},{18,... | collective-permute-start | bytes 8650760 | tf_op jit(solution)/shard_map/ppermute | solution.py:245
  502.9 25.2 %copy-start.41 = (bf16[320,2816]{1,0:T(8,128)(2,1)S(1)}, bf16[320,2816]{1,0:T(8,128)(2,1)}, u32[]{:S(2)}) copy-start(bf16[320,2816]{1,0:T(8,128)(2,1)} %get-tuple-element.79) | copy-start | bytes 5406724
  506.8 21.3 %copy-start.37 = (bf16[640,1024]{1,0:T(8,128)(2,1)S(1)}, bf16[640,1024]{1,0:T(8,128)(2,1)}, u32[]{:S(2)}) copy-start(bf16[640,1024]{1,0:T(8,128)(2,1)} %copy-done.36) | copy-start | bytes 3932164
  507.0 171.4 %collective-permute-start.9 = (bf16[4,5,64,512]{3,2,1,0:T(8,128)(2,1)S(1)}, bf16[4,5,64,512]{3,2,1,0:T(8,128)(2,1)S(1)}, u32[]{:S(2)}, u32[]{:S(2)}) collective-permute-start(bf16[4,5,64,512]{3,2,1,0:T(8,128)(2,1)S(1)} %slice.465), channel_id=1, source_target_pairs={{0,4},{2,6},{4,0},{6,2},{8,12},{10,14},{12,8},{14,10},{16,20},{18,... | collective-permute-start | bytes 3932168 | tf_op jit(solution)/shard_map/ppermute | solution.py:245
  533.1 146.6 %collective-permute-start.36 = (bf16[128,2816]{1,0:T(8,128)(2,1)S(1)}, bf16[128,2816]{1,0:T(8,128)(2,1)S(1)}, u32[]{:S(2)}, u32[]{:S(2)}) collective-permute-start(bf16[128,2816]{1,0:T(8,128)(2,1)S(1)} %get-tuple-element.89), channel_id=1, source_target_pairs={{0,24},{2,26},{4,28},{6,30},{8,16},{10,18},{12,20},{14,22},{16,8},... | collective-permute-start | bytes 2162696 | tf_op jit(solution)/shard_map/ppermute | solution.py:245
  534.2 146.0 %collective-permute-start.35 = (bf16[128,2816]{1,0:T(8,128)(2,1)S(1)}, bf16[128,2816]{1,0:T(8,128)(2,1)S(1)}, u32[]{:S(2)}, u32[]{:S(2)}) collective-permute-start(bf16[128,2816]{1,0:T(8,128)(2,1)S(1)} %get-tuple-element.90), channel_id=1, source_target_pairs={{0,16},{2,18},{4,20},{6,22},{8,24},{10,26},{12,28},{14,30},{16,0},... | collective-permute-start | bytes 2162696 | tf_op jit(solution)/shard_map/ppermute | solution.py:245
  589.9 92.3 %collective-permute-start.34 = (bf16[128,2816]{1,0:T(8,128)(2,1)S(1)}, bf16[128,2816]{1,0:T(8,128)(2,1)S(1)}, u32[]{:S(2)}, u32[]{:S(2)}) collective-permute-start(bf16[128,2816]{1,0:T(8,128)(2,1)S(1)} %get-tuple-element.88), channel_id=1, source_target_pairs={{0,8},{2,10},{4,12},{6,14},{8,0},{10,2},{12,4},{14,6},{16,24},{18,... | collective-permute-start | bytes 2162696 | tf_op jit(solution)/shard_map/ppermute | solution.py:245
  597.7 55.0 %copy-start.35 = (bf16[640,1024]{1,0:T(8,128)(2,1)S(1)}, bf16[640,1024]{1,0:T(8,128)(2,1)}, u32[]{:S(2)}) copy-start(bf16[640,1024]{1,0:T(8,128)(2,1)} %copy-done.34) | copy-start | bytes 3932164
  651.7 158.4 %collective-permute-start.41 = (bf16[128,2816]{1,0:T(8,128)(2,1)}, bf16[128,2816]{1,0:T(8,128)(2,1)}, u32[]{:S(2)}, u32[]{:S(2)}) collective-permute-start(bf16[128,2816]{1,0:T(8,128)(2,1)} %get-tuple-element.86), channel_id=1, source_target_pairs={{0,24},{2,26},{4,28},{6,30},{8,16},{10,18},{12,20},{14,22},{16,8},... | collective-permute-start | bytes 2162696 | tf_op jit(solution)/shard_map/ppermute | solution.py:245
  678.5 132.2 %collective-permute-start.40 = (bf16[128,2816]{1,0:T(8,128)(2,1)}, bf16[128,2816]{1,0:T(8,128)(2,1)}, u32[]{:S(2)}, u32[]{:S(2)}) collective-permute-start(bf16[128,2816]{1,0:T(8,128)(2,1)} %get-tuple-element.87), channel_id=1, source_target_pairs={{0,16},{2,18},{4,20},{6,22},{8,24},{10,26},{12,28},{14,30},{16,0},... | collective-permute-start | bytes 2162696 | tf_op jit(solution)/shard_map/ppermute | solution.py:245
  679.7 24.2 %collective-permute-start.12 = (bf16[5,64,512]{2,1,0:T(8,128)(2,1)S(1)}, bf16[5,64,512]{2,1,0:T(8,128)(2,1)S(1)}, u32[]{:S(2)}, u32[]{:S(2)}) collective-permute-start(bf16[5,64,512]{2,1,0:T(8,128)(2,1)S(1)} %get-tuple-element.99), channel_id=1, source_target_pairs={{0,24},{2,26},{4,28},{6,30},{8,16},{10,18},{12,20},{14,22},{16,8},... | collective-permute-start | bytes 983048 | tf_op jit(solution)/shard_map/ppermute | solution.py:245
  680.2 86.3 %collective-permute-start.11 = (bf16[5,64,512]{2,1,0:T(8,128)(2,1)S(1)}, bf16[5,64,512]{2,1,0:T(8,128)(2,1)S(1)}, u32[]{:S(2)}, u32[]{:S(2)}) collective-permute-start(bf16[5,64,512]{2,1,0:T(8,128)(2,1)S(1)} %get-tuple-element.100), channel_id=1, source_target_pairs={{0,16},{2,18},{4,20},{6,22},{8,24},{10,26},{12,28},{14,30},{16,0},... | collective-permute-start | bytes 983048 | tf_op jit(solution)/shard_map/ppermute | solution.py:245
  682.2 84.4 %collective-permute-start.10 = (bf16[5,64,512]{2,1,0:T(8,128)(2,1)S(1)}, bf16[5,64,512]{2,1,0:T(8,128)(2,1)S(1)}, u32[]{:S(2)}, u32[]{:S(2)}) collective-permute-start(bf16[5,64,512]{2,1,0:T(8,128)(2,1)S(1)} %get-tuple-element.98), channel_id=1, source_target_pairs={{0,8},{2,10},{4,12},{6,14},{8,0},{10,2},{12,4},{14,6},{16,24},{18,... | collective-permute-start | bytes 983048 | tf_op jit(solution)/shard_map/ppermute | solution.py:245
  703.9 73.7 %collective-permute-start.47 = (bf16[128,2816]{1,0:T(8,128)(2,1)S(1)}, bf16[128,2816]{1,0:T(8,128)(2,1)S(1)}, u32[]{:S(2)}, u32[]{:S(2)}) collective-permute-start(bf16[128,2816]{1,0:T(8,128)(2,1)S(1)} %get-tuple-element.83), channel_id=1, source_target_pairs={{0,24},{2,26},{4,28},{6,30},{8,16},{10,18},{12,20},{14,22},{16,8},... | collective-permute-start | bytes 2162696 | tf_op jit(solution)/shard_map/ppermute | solution.py:245
  766.6 36.4 %collective-permute-start.46 = (bf16[128,2816]{1,0:T(8,128)(2,1)S(1)}, bf16[128,2816]{1,0:T(8,128)(2,1)S(1)}, u32[]{:S(2)}, u32[]{:S(2)}) collective-permute-start(bf16[128,2816]{1,0:T(8,128)(2,1)S(1)} %get-tuple-element.84), channel_id=1, source_target_pairs={{0,16},{2,18},{4,20},{6,22},{8,24},{10,26},{12,28},{14,30},{16,0},... | collective-permute-start | bytes 2162696 | tf_op jit(solution)/shard_map/ppermute | solution.py:245
  766.6 37.8 %collective-permute-start.45 = (bf16[128,2816]{1,0:T(8,128)(2,1)S(1)}, bf16[128,2816]{1,0:T(8,128)(2,1)S(1)}, u32[]{:S(2)}, u32[]{:S(2)}) collective-permute-start(bf16[128,2816]{1,0:T(8,128)(2,1)S(1)} %get-tuple-element.82), channel_id=1, source_target_pairs={{0,8},{2,10},{4,12},{6,14},{8,0},{10,2},{12,4},{14,6},{16,24},{18,... | collective-permute-start | bytes 2162696 | tf_op jit(solution)/shard_map/ppermute | solution.py:245
  776.6 58.2 %copy-start.24 = (bf16[320,2048]{1,0:T(8,128)(2,1)}, bf16[320,2048]{1,0:T(8,128)(2,1)S(1)}, u32[]{:S(2)}) copy-start(bf16[320,2048]{1,0:T(8,128)(2,1)S(1)} %fusion.13) | copy-start | bytes 3932164
  777.7 39.4 %collective-permute-start.39 = (bf16[128,2816]{1,0:T(8,128)(2,1)}, bf16[128,2816]{1,0:T(8,128)(2,1)}, u32[]{:S(2)}, u32[]{:S(2)}) collective-permute-start(bf16[128,2816]{1,0:T(8,128)(2,1)} %get-tuple-element.85), channel_id=1, source_target_pairs={{0,8},{2,10},{4,12},{6,14},{8,0},{10,2},{12,4},{14,6},{16,24},{18,... | collective-permute-start | bytes 2162696 | tf_op jit(solution)/shard_map/ppermute | solution.py:245
  803.0 31.8 %collective-permute-start.13 = (bf16[320,2048]{1,0:T(8,128)(2,1)S(1)}, bf16[320,2048]{1,0:T(8,128)(2,1)}, u32[]{:S(2)}, u32[]{:S(2)}) collective-permute-start(bf16[320,2048]{1,0:T(8,128)(2,1)S(1)} %fusion.13), channel_id=1, source_target_pairs={{0,1},{1,0},{2,3},{3,2},{4,5},{5,4},{6,7},{7,6},{8,9},{9,8},{10,11... | collective-permute-start | bytes 3932168 | tf_op jit(solution)/shard_map/ppermute | solution.py:248
  804.4 16.0 %collective-permute-start.20 = (bf16[320,1536]{1,0:T(8,128)(2,1)}, bf16[320,1536]{1,0:T(8,128)(2,1)}, u32[]{:S(2)}, u32[]{:S(2)}) collective-permute-start(bf16[320,1536]{1,0:T(8,128)(2,1)} %pad_maximum_fusion.15), channel_id=1, source_target_pairs={{0,2},{2,0},{4,6},{6,4},{8,10},{10,8},{12,14},{14,12},{16,18},{18,... | collective-permute-start | bytes 2949128 | tf_op jit(solution)/shard_map/ppermute | solution.py:245
  810.1 49.3 %collective-permute-start.6 = (bf16[320,2048]{1,0:T(8,128)(2,1)}, bf16[320,2048]{1,0:T(8,128)(2,1)S(1)}, u32[]{:S(2)}, u32[]{:S(2)}) collective-permute-start(bf16[320,2048]{1,0:T(8,128)(2,1)} %convolution_convert_fusion.4), channel_id=1, source_target_pairs={{0,1},{1,0},{2,3},{3,2},{4,5},{5,4},{6,7},{7,6},{8,9},{9,8},{10,11... | collective-permute-start | bytes 3932168 | tf_op jit(solution)/shard_map/ppermute | solution.py:248
  824.4 56.5 %collective-permute-start.21 = (bf16[512,1536]{1,0:T(8,128)(2,1)}, bf16[512,1536]{1,0:T(8,128)(2,1)}, u32[]{:S(2)}, u32[]{:S(2)}) collective-permute-start(bf16[512,1536]{1,0:T(8,128)(2,1)} %convolution_convert_fusion.3), channel_id=1, source_target_pairs={{0,4},{2,6},{4,0},{6,2},{8,12},{10,14},{12,8},{14,10},{16,20},{18,... | collective-permute-start | bytes 4718600 | tf_op jit(solution)/shard_map/ppermute | solution.py:245
  834.8 24.6 %copy-start.13 = (f32[320,2048]{1,0:T(8,128)S(1)}, f32[320,2048]{1,0:T(8,128)}, u32[]{:S(2)}) copy-start(f32[320,2048]{1,0:T(8,128)} %copy-done.11) | copy-start | bytes 7864324
  834.8 24.6 %copy-start.18 = (bf16[320,2048]{1,0:T(8,128)(2,1)S(1)}, bf16[320,2048]{1,0:T(8,128)(2,1)}, u32[]{:S(2)}) copy-start(bf16[320,2048]{1,0:T(8,128)(2,1)} %fusion.19) | copy-start | bytes 3932164
  834.8 24.6 %copy-start.26 = (bf16[320,2048]{1,0:T(8,128)(2,1)S(1)}, bf16[320,2048]{1,0:T(8,128)(2,1)}, u32[]{:S(2)}) copy-start(bf16[320,2048]{1,0:T(8,128)(2,1)} %convolution_convert_fusion.4) | copy-start | bytes 3932164
  865.3 7.4 collective-permute-start.14
  872.8 3.7 collective-permute-start.15
  876.5 11.5 %collective-permute-start.18 = (f32[2,128]{1,0:T(2,128)S(1)}, f32[2,128]{1,0:T(2,128)S(1)}, u32[]{:S(2)}, u32[]{:S(2)}) collective-permute-start(f32[2,128]{1,0:T(2,128)S(1)} %get-tuple-element.107), channel_id=1, source_target_pairs={{0,24},{2,26},{4,28},{6,30},{8,16},{10,18},{12,20},{14,22},{16,8},... | collective-permute-start | bytes 3080 | tf_op jit(solution)/shard_map/ppermute | solution.py:245
  880.2 8.4 collective-permute-start.17
  880.2 8.4 collective-permute-start.16
  884.2 14.0 %collective-permute-start.24 = (bf16[128,1536]{1,0:T(8,128)(2,1)S(1)}, bf16[128,1536]{1,0:T(8,128)(2,1)S(1)}, u32[]{:S(2)}, u32[]{:S(2)}) collective-permute-start(bf16[128,1536]{1,0:T(8,128)(2,1)S(1)} %get-tuple-element.96), channel_id=1, source_target_pairs={{0,24},{2,26},{4,28},{6,30},{8,16},{10,18},{12,20},{14,22},{16,8},... | collective-permute-start | bytes 1179656 | tf_op jit(solution)/shard_map/ppermute | solution.py:245
  888.0 32.3 %collective-permute-start.23 = (bf16[128,1536]{1,0:T(8,128)(2,1)S(1)}, bf16[128,1536]{1,0:T(8,128)(2,1)S(1)}, u32[]{:S(2)}, u32[]{:S(2)}) collective-permute-start(bf16[128,1536]{1,0:T(8,128)(2,1)S(1)} %get-tuple-element.97), channel_id=1, source_target_pairs={{0,16},{2,18},{4,20},{6,22},{8,24},{10,26},{12,28},{14,30},{16,0},... | collective-permute-start | bytes 1179656 | tf_op jit(solution)/shard_map/ppermute | solution.py:245
  888.0 32.3 %collective-permute-start.22 = (bf16[128,1536]{1,0:T(8,128)(2,1)S(1)}, bf16[128,1536]{1,0:T(8,128)(2,1)S(1)}, u32[]{:S(2)}, u32[]{:S(2)}) collective-permute-start(bf16[128,1536]{1,0:T(8,128)(2,1)S(1)} %get-tuple-element.95), channel_id=1, source_target_pairs={{0,8},{2,10},{4,12},{6,14},{8,0},{10,2},{12,4},{14,6},{16,24},{18,... | collective-permute-start | bytes 1179656 | tf_op jit(solution)/shard_map/ppermute | solution.py:245
  (33 other events, 273.2 us)
Sparse Core Ops, SparseCore 0:
  13.1 96.9 all-gather.3
  112.2 155.3 all-gather.5
  269.7 96.9 all-gather.7

commit v2 on v1

--- a/solution.py
+++ b/solution.py
@@ -1,4 +1,5 @@
 import functools
+import math
 
 import jax
 import jax.numpy as jnp
@@ -12,6 +13,8 @@
 NEGATIVE = -1e30
 VMEM_LIMIT = 48 * 1024 * 1024
 
+HINT = pl.CostEstimate(flops=1, bytes_accessed=1, transcendentals=0)
+
 bf16 = jnp.bfloat16
 f32 = jnp.float32
 
@@ -32,7 +35,16 @@
     return v * cosine + pltpu.roll(v, HD // 2, 1) * sine
 
 
-def rope_kernel(q_cols, k_cols, raw_ref, cos_ref, sin_ref, q_ref, kv_ref):
+def first_tiles(arrays):
+    return [v[(0,) * (v.ndim - 2)][:16, :128] for v in arrays]
+
+
+def unread(others):
+    return [pl.BlockSpec(memory_space=pl.ANY)] * len(others)
+
+
+def rope_kernel(q_cols, k_cols, raw_ref, cos_ref, sin_ref, *refs):
+    q_ref, kv_ref = refs[-2:]
     cosine, sine = cos_ref[...], sin_ref[...]
     for c in range(0, q_cols, HD):
         q_ref[:, c : c + HD] = turn(raw_ref[:, c : c + HD], cosine, sine).astype(bf16)
@@ -42,14 +54,14 @@
     kv_ref[:, k_cols:] = raw_ref[:, q_cols + k_cols :].astype(bf16)
 
 
-def rope(raw, cosine, sine, rows, q_cols, k_cols):
+def rope(raw, cosine, sine, rows, q_cols, k_cols, others=()):
     total = raw.shape[0]
     width = raw.shape[1]
     table = pl.BlockSpec((rows, HD), lambda i: (0, 0))
     return pl.pallas_call(
         functools.partial(rope_kernel, q_cols, k_cols),
         grid=(total // rows,),
-        in_specs=[pl.BlockSpec((rows, width), lambda i: (i, 0)), table, table],
+        in_specs=[pl.BlockSpec((rows, width), lambda i: (i, 0)), table, table, *unread(others)],
         out_specs=[
             pl.BlockSpec((rows, q_cols), lambda i: (i, 0)),
             pl.BlockSpec((rows, 2 * k_cols), lambda i: (i, 0)),
@@ -59,8 +71,9 @@
             jax.ShapeDtypeStruct((total, 2 * k_cols), bf16),
         ],
         compiler_params=params(),
+        cost_estimate=HINT,
         name="rope",
-    )(raw, cosine, sine)
+    )(raw, cosine, sine, *first_tiles(others))
 
 
 def heads_to_rows(block, kv, group):
@@ -117,14 +130,16 @@
             jax.ShapeDtypeStruct((seqs * local_kv, group * rows, 1), f32),
         ],
         compiler_params=params(),
+        cost_estimate=HINT,
         name="attend",
     )(q, near, far, qpos, kpos)
 
 
 def attend_back_kernel(
     local_kv, group, q_ref, near_ref, far_ref, qpos_ref, kpos_ref, log_ref, grad_ref, cos_ref, sin_ref,
-    dq_ref, dnear_ref, dfar_ref,
+    *refs,
 ):
+    dq_ref, dnear_ref, dfar_ref = refs[-3:]
     rows = q_ref.shape[0]
     half = near_ref.shape[0] * rows
     scale = HD**-0.5
@@ -153,7 +168,9 @@
             dfar_ref[:, 0, :, c : c + HD] = d[half:].reshape(-1, rows, HD)
 
 
-def attend_back(q, near, far, qpos, kpos, log, grad, cosine, sine, rows, local_kv, group):
+def attend_back(
+    q, near, far, qpos, kpos, log, grad, cosine, sine, rows, local_kv, group, others
+):
     total, width = q.shape
     seqs = total // rows
     blocks, _, _, kv_width = near.shape
@@ -173,6 +190,7 @@
             row_spec,
             table,
             table,
+            *unread(others),
         ],
         out_specs=[row_spec, kv_spec, kv_spec],
         out_shape=[
@@ -181,8 +199,9 @@
             jax.ShapeDtypeStruct(far.shape, bf16),
         ],
         compiler_params=params(),
+        cost_estimate=HINT,
         name="attend_back",
-    )(q, near, far, qpos, kpos, log, grad, cosine, sine)
+    )(q, near, far, qpos, kpos, log, grad, cosine, sine, *first_tiles(others))
 
 
 def arrange_kernel(block, order_ref, a_ref, keep_ref, send_ref):
@@ -210,8 +229,197 @@
         out_specs=[pl.BlockSpec(memory_space=pltpu.VMEM)] * 2,
         out_shape=[out, out],
         compiler_params=params(),
+        cost_estimate=HINT,
         name="arrange",
     )(order, a)
+
+
+def forward_kernel(hidden_ref, gate_w_ref, up_w_ref, gate_ref, up_ref, product_ref):
+    hidden = hidden_ref[...]
+    gate = dot(hidden, gate_w_ref[...], 1, 0)
+    up = dot(hidden, up_w_ref[...], 1, 0)
+    gate_ref[...] = gate
+    up_ref[...] = up
+    product_ref[...] = (gate * jax.nn.sigmoid(gate) * up).astype(bf16)
+
+
+def feed_forward(hidden, weights, units):
+    rows, width = hidden.shape
+    tile = math.gcd(units, 256)
+    tiles = units // tile
+    whole = pl.BlockSpec((rows, width), lambda i: (0, 0))
+    column = pl.BlockSpec((rows, tile), lambda i: (0, i))
+    return pl.pallas_call(
+        forward_kernel,
+        grid=(tiles,),
+        in_specs=[
+            whole,
+            pl.BlockSpec((width, tile), lambda i: (0, i)),
+            pl.BlockSpec((width, tile), lambda i: (0, tiles + i)),
+        ],
+        out_specs=[column] * 3,
+        out_shape=[jax.ShapeDtypeStruct((rows, units), t) for t in (f32, f32, bf16)],
+        compiler_params=params(),
+        cost_estimate=HINT,
+        name="feed_forward",
+    )(hidden, weights, weights)
+
+
+def backward_kernel(down_grad_ref, gate_ref, up_ref, gate_w_ref, up_w_ref, down_w_ref, *refs):
+    gate_grad_ref, up_grad_ref, partial_ref, sum_ref = refs[-4:]
+    product_grad = dot(down_grad_ref[...], down_w_ref[...], 1, 0)
+    gate, up = gate_ref[...], up_ref[...]
+    sigmoid = jax.nn.sigmoid(gate)
+    gate_grad = (product_grad * up * (sigmoid * (1.0 + gate * (1.0 - sigmoid)))).astype(bf16)
+    up_grad = (product_grad * gate * sigmoid).astype(bf16)
+    gate_grad_ref[...] = gate_grad
+    up_grad_ref[...] = up_grad
+    term = dot(gate_grad, gate_w_ref[...], 1, 1) + dot(up_grad, up_w_ref[...], 1, 1)
+
+    @pl.when(pl.program_id(0) == 0)
+    def _():
+        sum_ref[...] = term
+
+    @pl.when(pl.program_id(0) != 0)
+    def _():
+        sum_ref[...] += term
+
+    @pl.when(pl.program_id(0) == pl.num_programs(0) - 1)
+    def _():
+        partial_ref[...] = sum_ref[...].astype(bf16)
+
+
+def feed_forward_back(down_grad, gate, up, weights, units, others):
+    rows, width = down_grad.shape
+    tile = math.gcd(units, 256)
+    tiles = units // tile
+    whole = pl.BlockSpec((rows, width), lambda i: (0, 0))
+    column = pl.BlockSpec((rows, tile), lambda i: (0, i))
+    return pl.pallas_call(
+        backward_kernel,
+        grid=(tiles,),
+        in_specs=[
+            whole,
+            column,
+            column,
+            pl.BlockSpec((width, tile), lambda i: (0, i)),
+            pl.BlockSpec((width, tile), lambda i: (0, tiles + i)),
+            pl.BlockSpec((width, tile), lambda i: (0, 2 * tiles + i)),
+        ]
+        + unread(others),
+        out_specs=[column, column, whole],
+        out_shape=[
+            jax.ShapeDtypeStruct((rows, units), bf16),
+            jax.ShapeDtypeStruct((rows, units), bf16),
+            jax.ShapeDtypeStruct((rows, width), bf16),
+        ],
+        scratch_shapes=[pltpu.VMEM((rows, width), f32)],
+        compiler_params=params(),
+        cost_estimate=HINT,
+        name="feed_forward_back",
+    )(down_grad, gate, up, weights, weights, weights, *first_tiles(others))
+
+
+def product_kernel(extra, *refs):
+    a_ref, a2_ref, b_ref, b2_ref = refs[:4]
+    out_ref, turned_ref = refs[-2:]
+
+    @pl.when(pl.program_id(0) == 0)
+    def _():
+        turned_ref[...] = jnp.concatenate([a_ref[...], a2_ref[...]], axis=0).T
+
+    b = jnp.concatenate([b_ref[...], b2_ref[...]], axis=0)
+    out = dot(turned_ref[...], b, 1, 0)
+    if extra:
+        out = out + refs[4][...].astype(f32)
+    out_ref[...] = out.astype(bf16)
+
+
+def side_product(side, half, b, b2, columns, added=None, others=()):
+    a, a2 = side
+    rows = a.shape[0]
+    height = a.shape[1] // 2
+    start, count = columns
+    tile = math.gcd(math.gcd(start, count), 256)
+    first = start // tile
+    a_spec = pl.BlockSpec((rows, height), lambda i: (0, half))
+    b_spec = pl.BlockSpec((rows, tile), lambda i: (0, first + i))
+    out_spec = pl.BlockSpec((height, tile), lambda i: (0, i))
+    extra = [] if added is None else [added]
+    return pl.pallas_call(
+        functools.partial(product_kernel, len(extra)),
+        grid=(count // tile,),
+        in_specs=[a_spec, a_spec, b_spec, b_spec]
+        + [out_spec] * len(extra)
+        + unread(others),
+        out_specs=out_spec,
+        out_shape=jax.ShapeDtypeStruct((height, count), bf16),
+        scratch_shapes=[pltpu.VMEM((height, 2 * rows), bf16)],
+        compiler_params=params(),
+        cost_estimate=HINT,
+        name="side_product",
+    )(a, a2, b, b2, *extra, *first_tiles(others))
+
+
+def norm_back_kernel(mine_ref, theirs_ref, v_ref, gain_ref, base_ref, *refs):
+    grad_ref, low_ref, gain_grad_ref = refs[-3:]
+    hidden_grad = mine_ref[...].astype(f32) + theirs_ref[...].astype(f32)
+    v = v_ref[...].astype(f32)
+    scale = rms_scale(v)
+    normed = v * scale
+    gain_grad = jnp.sum(hidden_grad * normed, axis=0, keepdims=True)
+
+    @pl.when(pl.program_id(0) == 0)
+    def _():
+        gain_grad_ref[...] = gain_grad
+
+    @pl.when(pl.program_id(0) != 0)
+    def _():
+        gain_grad_ref[...] += gain_grad
+
+    g = hidden_grad * gain_ref[...]
+    out = base_ref[...].astype(f32) + scale * (
+        g - normed * jnp.mean(g * normed, axis=-1, keepdims=True)
+    )
+    grad_ref[...] = out
+    low_ref[...] = out.astype(bf16)
+
+
+def norm_back(mine, theirs, v, gain, base, rows, others=()):
+    total, width = mine.shape
+    spec = pl.BlockSpec((rows, width), lambda i: (i, 0))
+    row = pl.BlockSpec((1, width), lambda i: (0, 0))
+    return pl.pallas_call(
+        norm_back_kernel,
+        grid=(total // rows,),
+        in_specs=[spec, spec, spec, row, spec, *unread(others)],
+        out_specs=[spec, spec, row],
+        out_shape=[
+            jax.ShapeDtypeStruct((total, width), f32),
+            jax.ShapeDtypeStruct((total, width), bf16),
+            jax.ShapeDtypeStruct((1, width), f32),
+        ],
+        compiler_params=params(),
+        cost_estimate=HINT,
+        name="norm_back",
+    )(mine, theirs, v, gain, base, *first_tiles(others))
+
+
+def pass_kernel(*refs):
+    pass
+
+
+def after(v, *others):
+    spec = pl.BlockSpec(memory_space=pl.ANY)
+    return pl.pallas_call(
+        pass_kernel,
+        in_specs=[spec] * (1 + len(others)),
+        out_specs=spec,
+        out_shape=jax.ShapeDtypeStruct(v.shape, v.dtype),
+        input_output_aliases={0: 0},
+        cost_estimate=HINT,
+        name="after",
+    )(v, *first_tiles(others))
 
 
 def local(
@@ -251,7 +459,11 @@
         mine = lax.optimization_barrier(partial_rows.astype(bf16))
         return mine.astype(f32) + tensor_flip(mine).astype(f32)
 
-    near_places = [far * 4 + pair * 2 for pair in range(2) for far in range(groups)]
+    far_bits = [1 << b for b in range(groups.bit_length() - 1)]
+    fars = [0]
+    for bit in reversed(far_bits):
+        fars = fars + [far + bit for far in fars]
+    near_places = [far * 4 + pair * 2 for pair in range(2) for far in fars]
     places = near_places + [place + 1 for place in near_places]
     owners = jnp.bitwise_xor(me, jnp.asarray(places, jnp.int32))
 
@@ -272,9 +484,9 @@
         "dp", axis=0, tiled=True,
     )
     second = lax.all_gather(
-        jnp.concatenate([gate_weight, up_weight], axis=1), "dp", axis=0, tiled=True
-    )
-    down_turned = lax.all_gather(down_weight.T, "dp", axis=0, tiled=True)
+        jnp.concatenate([gate_weight, up_weight, down_weight.T], axis=1), "dp", axis=0, tiled=True
+    )
+    down_turned = second[:, 2 * hidden_units :]
     qkv_cols = q_cols + 2 * k_cols
     qkv_full = first[:, :qkv_cols]
     out_turned = first[:, qkv_cols : qkv_cols + q_cols]
@@ -299,17 +511,17 @@
             axis=0,
         )
 
-    token_rows = pick(tokens).astype(f32)
+    token_low = lax.optimization_barrier(pick(tokens))
+    token_rows = token_low.astype(f32)
     down_grad = lax.optimization_barrier(pick(cotangent))
-    upstream = down_grad.astype(f32)
-
-    attn_scale = rms_scale(token_rows)
-    hidden = (token_rows * attn_scale * gain_attn).astype(bf16)
+
+    hidden = (token_rows * rms_scale(token_rows) * gain_attn).astype(bf16)
     qkv_raw = dot(hidden, qkv_full, 1, 0)
     queries, kv_own = rope(qkv_raw, cosine, sine, rows, q_cols, k_cols)
     kv_own = kv_own.reshape(1, live_seqs, rows, 2 * k_cols)
-    kv_far = jnp.concatenate([kv_own] + [flip(kv_own, 4 * k) for k in range(1, groups)], axis=0)
-    kv_near = jnp.concatenate([kv_far, flip(kv_far, 2)], axis=0)
+    kv_near = kv_own
+    for bits in [4 * bit for bit in reversed(far_bits)] + [2]:
+        kv_near = jnp.concatenate([kv_near, flip(kv_near, bits)], axis=0)
     kv_other = flip(kv_near, 1)
     mixed_out, log_total = attend(
         queries, kv_near, kv_other, qpos, kpos, rows, local_kv, group
@@ -317,87 +529,110 @@
     branch = tensor_total(dot(mixed_out, out_turned, 1, 1))
     middle = token_rows + branch
 
-    mlp_scale = rms_scale(middle)
-    normed_mlp = middle * mlp_scale
-    hidden_mlp = (normed_mlp * gain_mlp).astype(bf16)
-    gate_up = dot(hidden_mlp, second, 1, 0)
-    gate_values, up_values = gate_up[:, :hidden_units], gate_up[:, hidden_units:]
-    sigmoid_gate = jax.nn.sigmoid(gate_values)
-    silu_gate = gate_values * sigmoid_gate
-    product = (silu_gate * up_values).astype(bf16)
+    hidden_mlp = (middle * rms_scale(middle) * gain_mlp).astype(bf16)
+    gate_values, up_values, product = feed_forward(hidden_mlp, second, hidden_units)
 
     def side(a):
         keep, send = arrange(a, owners)
-        return jnp.concatenate([keep, flip(send, 1)], axis=0)
-
-    def both_cores(b):
-        return jnp.concatenate([b, flip(b, 1)], axis=0)
-
-    def summed(a_side, b):
-        half = groups * block
-        sent = dot(a_side[:, half:], b, 0, 0).astype(bf16)
-        kept = dot(a_side[:, :half], b, 0, 0)
-        pair = (kept + flip(sent, 2).astype(f32)).reshape(groups, block, b.shape[1])
-        out = pair[0]
-        for k in range(1, groups):
-            out = out + flip(pair[k].astype(bf16), 4 * k).astype(f32)
-        return out
-
-    grad_down = summed(side(down_grad), both_cores(product)).T
-    down_values = tensor_total(dot(product, down_turned, 1, 1))
-    result = unpick((middle + down_values).astype(bf16), tokens)
-
-    product_grad = dot(down_grad, down_turned, 1, 0)
-    gate_grad = (
-        product_grad * up_values * (sigmoid_gate * (1.0 + gate_values * (1.0 - sigmoid_gate)))
-    ).astype(bf16)
-    up_grad = (product_grad * silu_gate).astype(bf16)
-    gate_up_grad = jnp.concatenate([gate_grad, up_grad], axis=1)
+        return keep, flip(send, 1)
+
+    def fold(kept, sent, bits):
+        return kept.astype(f32) + flip(sent, bits).astype(f32)
+
+    def fold_far(v, beside=None):
+        for bit in far_bits:
+            half = v.shape[0] // 2
+            received = flip(v[half:], 4 * bit)
+            if beside is not None:
+                beside = beside[:half] + after(flip(beside[half:], 4 * bit), received)
+            v = v[:half].astype(f32) + received.astype(f32)
+            v = v if bit == far_bits[-1] else v.astype(bf16)
+        return v, beside
+
+    def send_pair(sent, *others):
+        return flip(after(sent, *others) if others else sent, 2)
+
+    def finish(a_side, b, b2, columns, received, beside=None):
+        kept = side_product(a_side, 0, b, b2, columns, received)
+        out, beside = fold_far(kept.reshape(groups, block, columns[1]), beside)
+        out = out.reshape(block, columns[1])
+        return out if beside is None else (out, beside)
+
+    split_at = -(-hidden_units // 512) * 256
+    hidden_cols = ((0, split_at), (split_at, hidden_units - split_at))
+    down_side = side(down_grad)
     mlp_side = side(hidden_mlp)
-    grad_gate = summed(mlp_side, both_cores(gate_grad))
-    grad_up = summed(mlp_side, both_cores(up_grad))
-    hidden_mlp_grad = tensor_total(dot(gate_up_grad, second, 1, 1))
-    gain_mlp_rows = jnp.sum(hidden_mlp_grad * normed_mlp, axis=0)
-    normed_grad = hidden_mlp_grad * gain_mlp
-    middle_grad = upstream + mlp_scale * (
-        normed_grad - normed_mlp * jnp.mean(normed_grad * normed_mlp, axis=-1, keepdims=True)
-    )
-
-    branch_grad = middle_grad.astype(bf16)
-    grad_out = summed(side(branch_grad), both_cores(mixed_out)).T
+    product2 = flip(product, 1)
+    sent_down = [side_product(down_side, 1, product, product2, c) for c in hidden_cols]
+    got_down = [send_pair(sent_down[0])]
+
+    gate_grad, up_grad, hidden_partial = feed_forward_back(
+        down_grad, gate_values, up_values, second, hidden_units, sent_down
+    )
+    gate_grad2, up_grad2 = flip(gate_grad, 1), flip(up_grad, 1)
+    got_down.append(send_pair(sent_down[1], got_down[0]))
+    hidden_partial = after(hidden_partial, got_down[0])
+    hidden_theirs = tensor_flip(hidden_partial)
+    sent_gate = [side_product(mlp_side, 1, gate_grad, gate_grad2, c) for c in hidden_cols]
+    sent_up = [side_product(mlp_side, 1, up_grad, up_grad2, c) for c in hidden_cols]
+    middle_grad, branch_grad, gain_mlp_rows = norm_back(
+        hidden_partial, hidden_theirs, middle, gain_mlp, down_grad, rows,
+        [*sent_gate, *sent_up, got_down[1]],
+    )
+    got_gate = [send_pair(sent_gate[0], got_down[1])]
+    grad_down = [
+        finish(down_side, product, product2, c, r)
+        for c, r in zip(hidden_cols, got_down, strict=True)
+    ]
+
     mixed_grad = dot(branch_grad, out_turned, 1, 0).astype(bf16)
     query_grad, dkv_near, dkv_other = attend_back(
-        queries, kv_near, kv_other, qpos, kpos, log_total, mixed_grad, cosine, sine,
-        rows, local_kv, group,
-    )
-    dkv_near = dkv_near.astype(f32) + flip(dkv_other, 1).astype(f32)
-    dkv_far = dkv_near[:groups] + flip(dkv_near[groups:].astype(bf16), 2).astype(f32)
-    dkv = dkv_far[0]
-    for k in range(1, groups):
-        dkv = dkv + flip(dkv_far[k].astype(bf16), 4 * k).astype(f32)
+        queries, kv_near, kv_other, qpos, kpos, log_total, mixed_grad,
+        cosine, sine, rows, local_kv, group, [],
+    )
+    dkv = fold(dkv_near, dkv_other, 1).astype(bf16)
+    got_dkv = flip(after(dkv[groups:], got_gate[0]), 2)
+    dkv, _ = fold_far((dkv[:groups].astype(f32) + got_dkv.astype(f32)).astype(bf16))
+    got_gate.append(send_pair(sent_gate[1], got_gate[0], got_dkv))
+    grad_gate = [
+        finish(mlp_side, gate_grad, gate_grad2, c, r)
+        for c, r in zip(hidden_cols, got_gate, strict=True)
+    ]
+    got_up = [send_pair(sent_up[0], got_gate[1])]
     dkv = dkv.reshape(total, 2 * k_cols)
     key_grad, _ = rope(
-        jnp.concatenate([dkv[:, :k_cols], dkv], axis=1), cosine, -sine, rows, k_cols, k_cols
+        jnp.concatenate([dkv[:, :k_cols], dkv], axis=1), cosine, -sine, rows, k_cols, k_cols,
+        [got_gate[1]],
     )
     qkv_grad = jnp.concatenate([query_grad, key_grad, dkv[:, k_cols:].astype(bf16)], axis=1)
-    grad_qkv = summed(side(hidden), both_cores(qkv_grad))
-    hidden_grad = tensor_total(dot(qkv_grad, qkv_full, 1, 1))
-    normed_attn = token_rows * attn_scale
-    gain_attn_rows = jnp.sum(hidden_grad * normed_attn, axis=0)
-    normed_attn_grad = hidden_grad * gain_attn
-    input_grad = middle_grad + attn_scale * (
-        normed_attn_grad
-        - normed_attn * jnp.mean(normed_attn_grad * normed_attn, axis=-1, keepdims=True)
+    attn_side, qkv_grad2, all_cols = side(hidden), flip(qkv_grad, 1), (0, qkv_cols)
+    sent_qkv = side_product(attn_side, 1, qkv_grad, qkv_grad2, all_cols, others=[got_up[0]])
+    got_qkv = send_pair(sent_qkv)
+    got_up.append(send_pair(sent_up[1], got_qkv))
+    grad_up = [
+        finish(mlp_side, up_grad, up_grad2, c, r)
+        for c, r in zip(hidden_cols, got_up, strict=True)
+    ]
+    grad_qkv = finish(attn_side, qkv_grad, qkv_grad2, all_cols, got_qkv)
+    attn_partial = dot(qkv_grad, qkv_full, 1, 1).astype(bf16)
+    input_grad, _, gain_attn_rows = norm_back(
+        attn_partial, tensor_flip(attn_partial), token_low, gain_attn, middle_grad, rows
     )
     input_grad = unpick(input_grad, cotangent.astype(f32))
 
-    gain_rows = jnp.stack([gain_attn_rows, gain_mlp_rows]).reshape(2, n_dp, block)
-    gain_rows = jnp.take(gain_rows, owners, axis=1)
-    gain_rows = gain_rows[:, : 2 * groups] + flip(gain_rows[:, 2 * groups :], 1)
-    gain_rows = gain_rows[:, :groups] + flip(gain_rows[:, groups:], 2)
-    gain_own = gain_rows[:, 0]
-    for k in range(1, groups):
-        gain_own = gain_own + flip(gain_rows[:, k], 4 * k)
+    down_values = tensor_total(dot(after(product, query_grad), down_turned, 1, 1))
+    result = unpick((middle + down_values).astype(bf16), tokens)
+
+    gain_rows = jnp.concatenate([gain_attn_rows, gain_mlp_rows]).reshape(2, n_dp, block)
+    gain_rows = jnp.take(gain_rows, owners, axis=1).transpose(1, 0, 2)
+    gain_rows = gain_rows[: 2 * groups] + flip(gain_rows[2 * groups :], 1)
+    out_side, mixed2, out_cols = side(branch_grad), flip(mixed_out, 1), (0, q_cols)
+    sent_out = side_product(out_side, 1, mixed_out, mixed2, out_cols)
+    got_gains = flip(after(gain_rows[groups:], got_qkv), 2)
+    got_out = send_pair(sent_out, got_up[1])
+    gain_rows = gain_rows[:groups] + after(got_gains, got_out)
+    grad_out, gain_rows = finish(out_side, mixed_out, mixed2, out_cols, got_out, gain_rows)
+    gain_own = gain_rows[0]
 
     return (
         result,
@@ -406,11 +641,11 @@
         grad_qkv[:, :q_cols],
         grad_qkv[:, q_cols : q_cols + k_cols],
         grad_qkv[:, q_cols + k_cols :],
-        grad_out,
+        grad_out.T,
         gain_own[1],
-        grad_gate,
-        grad_up,
-        grad_down,
+        jnp.concatenate(grad_gate, axis=1),
+        jnp.concatenate(grad_up, axis=1),
+        jnp.concatenate(grad_down, axis=1).T,
     )
 
 

time: 939 us -> 811 us (0.86)
  waiting for transfers between devices: 622 us -> 440 us
  Pallas kernels: 29.4 us -> 158 us
  matrix products: 120 us -> 29 us
  local copies, waits for them, and re-layouts: 21.5 us -> 60 us
  starting transfers between devices: 67.7 us -> 39.2 us
    pallas_call x0 -> x33, Pallas kernels: none -> 128 us  [the longest x16 71.5 us: side_product(): pl.pallas_call(functools.partial(product_kernel, len(extra)), grid=(count...]
    ppermute x44 -> x45, waiting for transfers between devices: 382 us -> 286 us  [flip(): return lax.ppermute(v, 'dp', [(i, i ^ bits) for i in range(n_dp)])]
    dot_general x18 -> x5, matrix products: 120 us -> 29 us  [dot(): lax.dot_general(a, b, (((ca,), (cb,)), ((), ())), preferred_element_type=...]
    all_gather x2 -> x1, waiting for transfers between devices: 75 us -> 29 us  [local(): lax.all_gather(jnp.concatenate([gate_weight, up_weight, down_weight.T], a...]
    ppermute x4, waiting for transfers between devices: 75.4 us -> 39.7 us  [tensor_flip(): return lax.ppermute(v, 'tensor', [(0, 1), (1, 0)])]
    ppermute x44 -> x45, starting transfers between devices: 62.5 us -> 35.6 us  [flip(): return lax.ppermute(v, 'dp', [(i, i ^ bits) for i in range(n_dp)])]
    slice x8 -> x43, local copies, waits for them, and re-layouts: 1.99 us -> 22.2 us  [the longest x19 10.3 us: fold_far(): received = flip(v[half:], 4 * bit)]
    convert_element_type x3 -> x15, other arithmetic: 3.52 us -> 19.2 us  [the longest x9 10.2 us: fold_far(): v = v if bit == far_bits[-1] else v.astype(bf16)]
  transfers between devices with their start and end apart: 51 -> 51, of which waited for: 25 -> 24; matrix products, arithmetic and copies ran while one was open for 16% -> 14% of each run, Pallas kernels for 3% -> 17%
where the time goes in v2:
time: 811 us; the launch traced here: 800 us
  waiting for transfers between devices  440 us (54%)
  Pallas kernels  158 us (19%)
  local copies, waits for them, and re-layouts  60 us (7%)
  other arithmetic  54.5 us (7%)
  starting transfers between devices  39.2 us (5%)
  matrix products  29 us (4%)
  between operations  19.3 us (2%)
    ppermute x45, waiting for transfers between devices, flip(): return lax.ppermute(v, 'dp', [(i, i ^ bits) for i in range(n_dp)])  286 us
    all_gather x1, waiting for transfers between devices, local(): lax.all_gather(jnp.concatenate([query_weight, key_weight, value_weight, o...  85 us
    pallas_call x16, Pallas kernels, side_product(): pl.pallas_call(functools.partial(product_kernel, len(extra)), grid=(count...  71.5 us
    ppermute x4, waiting for transfers between devices, tensor_flip(): return lax.ppermute(v, 'tensor', [(0, 1), (1, 0)])  39.7 us
    ppermute x45, starting transfers between devices, flip(): return lax.ppermute(v, 'dp', [(i, i ^ bits) for i in range(n_dp)])  35.6 us
    dot_general x5, matrix products, dot(): lax.dot_general(a, b, (((ca,), (cb,)), ((), ())), preferred_element_type=...  29 us
    all_gather x1, waiting for transfers between devices, local(): lax.all_gather(jnp.concatenate([gate_weight, up_weight, down_weight.T], a...  29 us
    pallas_call x1, Pallas kernels, feed_forward_back(): pl.pallas_call(backward_kernel, grid=(tiles,), in_specs=[whole, column, c...  28 us
  transfers between devices with their start and end apart: 51, of which 24 were waited for; matrix products, arithmetic and copies ran while one was open for 14% of the time, Pallas kernels for 17%

profile of v2, /device:TPU:0, one launch (start us, length us, event | category | flops | bytes accessed | tf_op | source)
XLA Modules:
  0.0 799.7 jit_solution(15371334745085788458)
XLA Ops:
  11.8 2.6 pad_maximum_fusion.2
  20.2 2.4 slice_select_fusion.1
  23.4 85.0 %all-gather.3.cloned.1.call-done = bf16[2048,2688]{0,1:T(8,128)(2,1)} async-done(((bf16[128,2688]{0,1:T(8,128)(2,1)}), bf16[2048,2688]{0,1:T(8,128)(2,1)}) %all-gather.3.cloned.1.call-update) | async-done | bytes 11010064 | tf_op jit(solution)/shard_map/all_gather | solution.py:482
  109.7 5.5 fusion.4.raw_ref
  117.6 22.9 %collective-permute-done = bf16[1,5,64,512]{3,2,1,0:T(8,128)(2,1)S(1)} collective-permute-done((bf16[1,5,64,512]{3,2,1,0:T(8,128)(2,1)S(1)}, bf16[1,5,64,512]{3,2,1,0:T(8,128)(2,1)S(1)}, u32[]{:S(2)}, u32[]{:S(2)}) %collective-permute-start) | collective-permute-done | bytes 327712 | tf_op jit(solution)/shard_map/ppermute | solution.py:453
  140.6 31.2 %collective-permute-done.1 = bf16[2,5,64,512]{3,2,1,0:T(8,128)(2,1)S(1)} collective-permute-done((bf16[2,5,64,512]{3,2,1,0:T(8,128)(2,1)S(1)}, bf16[2,5,64,512]{3,2,1,0:T(8,128)(2,1)S(1)}, u32[]{:S(2)}, u32[]{:S(2)}) %collective-permute-start.1) | collective-permute-done | bytes 655392 | tf_op jit(solution)/shard_map/ppermute | solution.py:453
  172.7 56.6 %collective-permute-done.2 = bf16[4,5,64,512]{3,2,1,0:T(8,128)(2,1)S(1)} collective-permute-done((bf16[4,5,64,512]{3,2,1,0:T(8,128)(2,1)S(1)}, bf16[4,5,64,512]{3,2,1,0:T(8,128)(2,1)S(1)}, u32[]{:S(2)}, u32[]{:S(2)}) %collective-permute-start.2) | collective-permute-done | bytes 1310752 | tf_op jit(solution)/shard_map/ppermute | solution.py:453
  231.3 5.3 collective-permute-done.3.far_ref
  236.6 8.6 %attend.1 = (bf16[320,1024]{1,0:T(8,128)(2,1)S(1)}, f32[10,256,1]{2,1,0:T(8,128)S(1)}) custom-call(bf16[320,1024]{1,0:T(8,128)(2,1)S(1)} %get-tuple-element.40.q_ref, bf16[8,5,64,512]{3,2,1,0:T(8,128)(2,1)} %pad_maximum_fusion.1.near_ref, bf16[8,5,64,512]{3,2,1,0:T(8,128)(2,1)} %collective-permute-done.3.far_ref, ...), custom_call_target="tpu_custom_call" | custom-call | flops 1 | bytes 1 | tf_op jit(solution)/shard_map/attend/pallas_call | solution.py:114
  245.3 4.4 fusion.13
  251.2 29.6 %collective-permute-done.4 = bf16[320,2048]{1,0:T(8,128)(2,1)S(1)} collective-permute-done((bf16[320,2048]{1,0:T(8,128)(2,1)S(1)}, bf16[320,2048]{1,0:T(8,128)(2,1)S(1)}, u32[]{:S(2)}, u32[]{:S(2)}) %collective-permute-start.4) | collective-permute-done | bytes 1310752 | tf_op jit(solution)/shard_map/ppermute | solution.py:456
  284.5 29.0 %all-gather.5.cloned.1.call-done.gate_w_ref.up_w_ref.down_w_ref = bf16[2048,8448]{1,0:T(8,128)(2,1)} async-done(((bf16[128,8448]{1,0:T(8,128)(2,1)}), bf16[2048,8448]{1,0:T(8,128)(2,1)}) %all-gather.5.cloned.1.call-update) | async-done | bytes 34603024 | tf_op jit(solution)/shard_map/all_gather | solution.py:486
  314.9 16.9 %feed_forward.1 = (f32[320,2816]{1,0:T(8,128)}, f32[320,2816]{1,0:T(8,128)}, bf16[320,2816]{1,0:T(8,128)(2,1)S(1)}) custom-call(bf16[320,2048]{1,0:T(8,128)(2,1)S(1)} %copy-done.10, bf16[2048,8448]{1,0:T(8,128)(2,1)} %all-gather.5.cloned.1.call-done.gate_w_ref.up_w_ref.down_w_ref, bf16[2048,8448]{1,0:T(8,128)(2,1)} %all-gather.5.cloned.1.call-done.gate_w_ref.up_w_ref.down_w_ref), custom_call_target="tpu_custom_call" | custom-call | flops 1 | bytes 1 | tf_op jit(solution)/shard_map/feed_forward/pallas_call | solution.py:252
  333.2 3.2 collective-permute-done.5.refs_1_
  337.6 4.7 side_product.16
  344.9 2.4 side_product.17.refs_0_
  347.4 28.0 %feed_forward_back.1 = (bf16[320,2816]{1,0:T(8,128)(2,1)}, bf16[320,2816]{1,0:T(8,128)(2,1)}, bf16[320,2048]{1,0:T(8,128)(2,1)S(1)}) custom-call(bf16[320,2048]{1,0:T(8,128)(2,1)S(1)} %bitcast.86, f32[320,2816]{1,0:T(8,128)} %get-tuple-element.45.gate_ref, f32[320,2816]{1,0:T(8,128)} %get-tuple-element.46.up_ref, ...), custom_call_target="tpu_custom_call" | custom-call | flops 1 | bytes 1 | tf_op jit(solution)/shard_map/feed_forward_back/pallas_call | solution.py:298
  378.9 5.3 side_product.30
  390.4 3.4 convert_element_type.282
  400.5 2.6 copy.57
  403.1 4.2 side_product.21.refs_0_
  407.4 4.9 side_product.20.refs_0_
  412.3 5.3 side_product.18.refs_0_
  417.6 5.0 side_product.19.refs_0_
  425.3 2.3 collective-permute-start.46
  427.7 4.6 side_product.31
  438.7 6.0 norm_back.2
  444.7 4.3 fusion.25.grad_ref
  449.0 13.2 %attend_back.1 = (bf16[320,1024]{1,0:T(8,128)(2,1)S(1)}, bf16[8,5,64,512]{3,2,1,0:T(8,128)(2,1)S(1)}, bf16[8,5,64,512]{3,2,1,0:T(8,128)(2,1)}) custom-call(bf16[320,1024]{1,0:T(8,128)(2,1)S(1)} %copy-done.27, bf16[8,5,64,512]{3,2,1,0:T(8,128)(2,1)} %pad_maximum_fusion.1.near_ref, bf16[8,5,64,512]{3,2,1,0:T(8,128)(2,1)} %collective-permute-done.3.far_ref, ...), custom_call_target="tpu_custom_call" | custom-call | flops 1 | bytes 1 | tf_op jit(solution)/shard_map/attend_back/pallas_call | solution.py:180
  464.4 9.9 %fusion.16 = bf16[320,2048]{1,0:T(8,128)(2,1)} fusion(bf16[320,2816]{1,0:T(8,128)(2,1)} %after.15, bf16[2048,8448]{1,0:T(8,128)(2,1)} %all-gather.5.cloned.1.call-done.gate_w_ref.up_w_ref.down_w_ref), kind=kOutput, calls=%fused_computation.18 | convolution fusion | flops 3691642880 | bytes 14647296 | tf_op jit(solution)/shard_map/dot_general | solution.py:27
  476.0 2.6 copy.59
  481.2 2.2 collective-permute-start.48
  484.6 3.6 side_product.23.refs_0_
  488.2 10.3 %collective-permute-done.48 = bf16[1,128,1280]{1,2,0:T(8,128)(2,1)S(1)} collective-permute-done((bf16[1,128,1280]{1,2,0:T(8,128)(2,1)S(1)}, bf16[1,128,1280]{1,2,0:T(8,128)(2,1)S(1)}, u32[]{:S(2)}, u32[]{:S(2)}) %collective-permute-start.48) | collective-permute-done | bytes 327712 | tf_op jit(solution)/shard_map/ppermute | solution.py:453
  499.9 2.8 add_convert_fusion
  507.3 4.7 collective-permute-done.13
  511.9 3.1 add_convert_fusion.2
  516.3 5.2 side_product.26
  524.5 11.3 %collective-permute-done.16 = bf16[4,5,64,512]{3,2,1,0:T(8,128)(2,1)S(1)} collective-permute-done((bf16[4,5,64,512]{3,2,1,0:T(8,128)(2,1)}, bf16[4,5,64,512]{3,2,1,0:T(8,128)(2,1)S(1)}, u32[]{:S(2)}, u32[]{:S(2)}) %collective-permute-start.16) | collective-permute-done | bytes 1310752 | tf_op jit(solution)/shard_map/ppermute | solution.py:453
  540.7 2.6 pad_maximum_fusion.3
  543.3 12.3 %collective-permute-done.17 = bf16[2,5,64,512]{3,2,1,0:T(8,128)(2,1)} collective-permute-done((bf16[2,5,64,512]{3,2,1,0:T(8,128)(2,1)}, bf16[2,5,64,512]{3,2,1,0:T(8,128)(2,1)}, u32[]{:S(2)}, u32[]{:S(2)}) %collective-permute-start.17) | collective-permute-done | bytes 655392 | tf_op jit(solution)/shard_map/ppermute | solution.py:453
  562.1 20.5 %collective-permute-done.18 = bf16[1,5,64,512]{3,2,1,0:T(8,128)(2,1)S(1)} collective-permute-done((bf16[1,5,64,512]{3,2,1,0:T(8,128)(2,1)S(1)}, bf16[1,5,64,512]{3,2,1,0:T(8,128)(2,1)S(1)}, u32[]{:S(2)}, u32[]{:S(2)}) %collective-permute-start.18) | collective-permute-done | bytes 327712 | tf_op jit(solution)/shard_map/ppermute | solution.py:453
  586.8 4.5 side_product.27
  592.0 2.4 rope.3
  594.3 5.0 fusion.10.mine_ref
  599.6 6.9 collective-permute-done.39
  608.6 13.3 %collective-permute-done.40 = bf16[1,128,1280]{2,1,0:T(8,128)(2,1)S(1)} collective-permute-done((bf16[1,128,1280]{2,1,0:T(8,128)(2,1)S(1)}, bf16[1,128,1280]{2,1,0:T(8,128)(2,1)S(1)}, u32[]{:S(2)}, u32[]{:S(2)}) %collective-permute-start.40) | collective-permute-done | bytes 327712 | tf_op jit(solution)/shard_map/ppermute | solution.py:453
  623.2 5.3 collective-permute-done.20.theirs_ref
  628.5 6.0 norm_back.3
  637.1 3.9 side_product.22
  641.4 3.8 slice_select_fusion
  645.2 5.2 side_product.28
  654.8 20.2 %collective-permute-done.25.refs_4_ = bf16[512,1536]{1,0:T(8,128)(2,1)S(1)} collective-permute-done((bf16[512,1536]{1,0:T(8,128)(2,1)S(1)}, bf16[512,1536]{1,0:T(8,128)(2,1)S(1)}, u32[]{:S(2)}, u32[]{:S(2)}) %collective-permute-start.25) | collective-permute-done | bytes 1572896 | tf_op jit(solution)/shard_map/ppermute | solution.py:453
  677.0 3.9 pad_maximum_fusion
  684.6 4.9 side_product.25
  690.8 17.4 %collective-permute-done.29.refs_4_ = bf16[512,1280]{1,0:T(8,128)(2,1)S(1)} collective-permute-done((bf16[512,1280]{1,0:T(8,128)(2,1)}, bf16[512,1280]{1,0:T(8,128)(2,1)S(1)}, u32[]{:S(2)}, u32[]{:S(2)}) %collective-permute-start.29) | collective-permute-done | bytes 1310752 | tf_op jit(solution)/shard_map/ppermute | solution.py:453
  708.2 4.4 side_product.29
  714.9 3.2 collective-permute-done.35
  722.6 17.1 %collective-permute-done.43 = bf16[2,128,1280]{2,1,0:T(8,128)(2,1)} collective-permute-done((bf16[2,128,1280]{2,1,0:T(8,128)(2,1)}, bf16[2,128,1280]{2,1,0:T(8,128)(2,1)}, u32[]{:S(2)}, u32[]{:S(2)}) %collective-permute-start.43) | collective-permute-done | bytes 655392 | tf_op jit(solution)/shard_map/ppermute | solution.py:453
  742.7 14.4 %collective-permute-done.44 = bf16[1,128,1280]{2,1,0:T(8,128)(2,1)S(1)} collective-permute-done((bf16[1,128,1280]{2,1,0:T(8,128)(2,1)S(1)}, bf16[1,128,1280]{2,1,0:T(8,128)(2,1)S(1)}, u32[]{:S(2)}, u32[]{:S(2)}) %collective-permute-start.44) | collective-permute-done | bytes 327712 | tf_op jit(solution)/shard_map/ppermute | solution.py:453
  757.3 3.4 side_product.24
  766.0 8.8 %collective-permute-done.32 = bf16[2,128,1024]{2,1,0:T(8,128)(2,1)S(1)} collective-permute-done((bf16[2,128,1024]{2,1,0:T(8,128)(2,1)S(1)}, bf16[2,128,1024]{2,1,0:T(8,128)(2,1)S(1)}, u32[]{:S(2)}, u32[]{:S(2)}) %collective-permute-start.32) | collective-permute-done | bytes 524320 | tf_op jit(solution)/shard_map/ppermute | solution.py:453
  777.5 2.3 collective-permute-start.33
  779.8 9.1 %collective-permute-done.34 = bf16[1,128,1024]{2,1,0:T(8,128)(2,1)S(1)} collective-permute-done((bf16[1,128,1024]{2,1,0:T(8,128)(2,1)S(1)}, bf16[1,128,1024]{2,1,0:T(8,128)(2,1)S(1)}, u32[]{:S(2)}, u32[]{:S(2)}) %collective-permute-start.34) | collective-permute-done | bytes 262176 | tf_op jit(solution)/shard_map/ppermute | solution.py:453
  (374 shorter events, 124.3 us)
Async XLA Ops:
  7.2 101.2 %all-gather.3.cloned.1.call-start = ((), (), s32[]{:S(2)}) async-start(), calls=%async_computation | async-start | bytes 11698176 | tf_op jit(solution)/shard_map/all_gather | solution.py:482
  11.5 302.1 %all-gather.5.cloned.1.call-start = ((), (), s32[]{:S(2)}) async-start(), calls=%async_computation.1 | async-start | bytes 36765696 | tf_op jit(solution)/shard_map/all_gather | solution.py:486
  22.7 258.2 %copy-start.2 = (bf16[5,64,2048]{2,1,0:T(8,128)(2,1)}, bf16[5,64,2048]{2,1,0:T(8,128)(2,1)S(1)}, u32[]{:S(2)}) copy-start(bf16[5,64,2048]{2,1,0:T(8,128)(2,1)S(1)} %get-tuple-element.125) | copy-start | bytes 3932164
  22.7 324.7 %copy-start.8 = (bf16[5,64,2048]{2,1,0:T(8,128)(2,1)}, bf16[5,64,2048]{2,1,0:T(8,128)(2,1)S(1)}, u32[]{:S(2)}) copy-start(bf16[5,64,2048]{2,1,0:T(8,128)(2,1)S(1)} %get-tuple-element.124) | copy-start | bytes 3932164
  116.0 120.6 %copy-start.26 = (bf16[320,1024]{1,0:T(8,128)(2,1)}, bf16[320,1024]{1,0:T(8,128)(2,1)S(1)}, u32[]{:S(2)}) copy-start(bf16[320,1024]{1,0:T(8,128)(2,1)S(1)} %get-tuple-element.40.q_ref) | copy-start | bytes 1966084
  116.0 24.4 %collective-permute-start = (bf16[1,5,64,512]{3,2,1,0:T(8,128)(2,1)S(1)}, bf16[1,5,64,512]{3,2,1,0:T(8,128)(2,1)S(1)}, u32[]{:S(2)}, u32[]{:S(2)}) collective-permute-start(bf16[1,5,64,512]{3,2,1,0:T(8,128)(2,1)S(1)} %bitcast.88), channel_id=1, source_target_pairs={{0,16},{2,18},{4,20},{6,22},{8,24},{10,26},{12,28},{14,30},{16,0},... | collective-permute-start | bytes 983048 | tf_op jit(solution)/shard_map/ppermute | solution.py:453
  140.5 31.2 %collective-permute-start.1 = (bf16[2,5,64,512]{3,2,1,0:T(8,128)(2,1)S(1)}, bf16[2,5,64,512]{3,2,1,0:T(8,128)(2,1)S(1)}, u32[]{:S(2)}, u32[]{:S(2)}) collective-permute-start(bf16[2,5,64,512]{3,2,1,0:T(8,128)(2,1)S(1)} %pad_maximum_fusion.9), channel_id=1, source_target_pairs={{0,8},{2,10},{4,12},{6,14},{8,0},{10,2},{12,4},{14,6},{16,24},{18,... | collective-permute-start | bytes 1966088 | tf_op jit(solution)/shard_map/ppermute | solution.py:453
  171.9 59.2 %copy-start.73 = (s32[16]{0:T(128)S(1)}, s32[16]{0:T(128)}, u32[]{:S(2)}) copy-start(s32[16]{0:T(128)} %constant.56.clone) | copy-start | bytes 196
  171.9 57.4 %collective-permute-start.2 = (bf16[4,5,64,512]{3,2,1,0:T(8,128)(2,1)S(1)}, bf16[4,5,64,512]{3,2,1,0:T(8,128)(2,1)S(1)}, u32[]{:S(2)}, u32[]{:S(2)}) collective-permute-start(bf16[4,5,64,512]{3,2,1,0:T(8,128)(2,1)S(1)} %pad_maximum_fusion.6), channel_id=1, source_target_pairs={{0,4},{2,6},{4,0},{6,2},{8,12},{10,14},{12,8},{14,10},{16,20},{18,... | collective-permute-start | bytes 3932168 | tf_op jit(solution)/shard_map/ppermute | solution.py:453
  231.0 5.7 collective-permute-start.3
  249.7 31.2 %collective-permute-start.4 = (bf16[320,2048]{1,0:T(8,128)(2,1)S(1)}, bf16[320,2048]{1,0:T(8,128)(2,1)S(1)}, u32[]{:S(2)}, u32[]{:S(2)}) collective-permute-start(bf16[320,2048]{1,0:T(8,128)(2,1)S(1)} %fusion.13), channel_id=1, source_target_pairs={{0,1},{1,0},{2,3},{3,2},{4,5},{5,4},{6,7},{7,6},{8,9},{9,8},{10,11... | collective-permute-start | bytes 3932168 | tf_op jit(solution)/shard_map/ppermute | solution.py:456
  331.7 4.7 collective-permute-start.6
  332.9 3.5 collective-permute-start.5
  342.3 36.6 %collective-permute-start.7 = (bf16[512,1536]{1,0:T(8,128)(2,1)S(1)}, bf16[512,1536]{1,0:T(8,128)(2,1)S(1)}, u32[]{:S(2)}, u32[]{:S(2)}) collective-permute-start(bf16[512,1536]{1,0:T(8,128)(2,1)S(1)} %side_product.16), channel_id=1, source_target_pairs={{0,4},{2,6},{4,0},{6,2},{8,12},{10,14},{12,8},{14,10},{16,20},{18,... | collective-permute-start | bytes 4718600 | tf_op jit(solution)/shard_map/ppermute | solution.py:453
  347.4 28.1 %copy-start.20 = (bf16[512,1280]{1,0:T(8,128)(2,1)}, bf16[512,1280]{1,0:T(8,128)(2,1)S(1)}, u32[]{:S(2)}) copy-start(bf16[512,1280]{1,0:T(8,128)(2,1)S(1)} %side_product.17.refs_0_) | copy-start | bytes 3932164
  347.4 28.6 %copy-start.11 = (bf16[320,2048]{1,0:T(8,128)(2,1)S(1)}, bf16[320,2048]{1,0:T(8,128)(2,1)}, u32[]{:S(2)}) copy-start(bf16[320,2048]{1,0:T(8,128)(2,1)} %multiply_convert_fusion.hidden_ref.a_ref) | copy-start | bytes 3932164
  375.4 27.7 %collective-permute-start.11 = (bf16[320,2816]{1,0:T(8,128)(2,1)}, bf16[320,2816]{1,0:T(8,128)(2,1)}, u32[]{:S(2)}, u32[]{:S(2)}) collective-permute-start(bf16[320,2816]{1,0:T(8,128)(2,1)} %get-tuple-element.53.refs_2_), channel_id=1, source_target_pairs={{0,2},{2,0},{4,6},{6,4},{8,10},{10,8},{12,14},{14,12},{16,18},{18,... | collective-permute-start | bytes 5406728 | tf_op jit(solution)/shard_map/ppermute | solution.py:453
  375.5 36.8 %collective-permute-start.10 = (bf16[320,2816]{1,0:T(8,128)(2,1)}, bf16[320,2816]{1,0:T(8,128)(2,1)}, u32[]{:S(2)}, u32[]{:S(2)}) collective-permute-start(bf16[320,2816]{1,0:T(8,128)(2,1)} %get-tuple-element.52.refs_2_), channel_id=1, source_target_pairs={{0,2},{2,0},{4,6},{6,4},{8,10},{10,8},{12,14},{14,12},{16,18},{18,... | collective-permute-start | bytes 5406728 | tf_op jit(solution)/shard_map/ppermute | solution.py:453
  376.9 18.3 %collective-permute-start.9 = (bf16[320,1024]{1,0:T(8,128)(2,1)S(1)}, bf16[320,1024]{1,0:T(8,128)(2,1)S(1)}, u32[]{:S(2)}, u32[]{:S(2)}) collective-permute-start(bf16[320,1024]{1,0:T(8,128)(2,1)S(1)} %get-tuple-element.51), channel_id=1, source_target_pairs={{0,2},{2,0},{4,6},{6,4},{8,10},{10,8},{12,14},{14,12},{16,18},{18,... | collective-permute-start | bytes 1966088 | tf_op jit(solution)/shard_map/ppermute | solution.py:453
  388.1 34.7 %collective-permute-start.45 = (bf16[2,128,1536]{1,2,0:T(8,128)(2,1)}, bf16[2,128,1536]{1,2,0:T(8,128)(2,1)}, u32[]{:S(2)}, u32[]{:S(2)}) collective-permute-start(bf16[2,128,1536]{1,2,0:T(8,128)(2,1)} %copy.56), channel_id=1, source_target_pairs={{0,8},{2,10},{4,12},{6,14},{8,0},{10,2},{12,4},{14,6},{16,24},{18,... | collective-permute-start | bytes 2359304 | tf_op jit(solution)/shard_map/ppermute | solution.py:453
  389.3 38.3 %collective-permute-start.12 = (bf16[512,1280]{1,0:T(8,128)(2,1)}, bf16[512,1280]{1,0:T(8,128)(2,1)}, u32[]{:S(2)}, u32[]{:S(2)}) collective-permute-start(bf16[512,1280]{1,0:T(8,128)(2,1)} %after.14), channel_id=1, source_target_pairs={{0,4},{2,6},{4,0},{6,2},{8,12},{10,14},{12,8},{14,10},{16,20},{18,... | collective-permute-start | bytes 3932168 | tf_op jit(solution)/shard_map/ppermute | solution.py:453
  395.2 42.2 %collective-permute-start.8 = (bf16[320,2048]{1,0:T(8,128)(2,1)}, bf16[320,2048]{1,0:T(8,128)(2,1)}, u32[]{:S(2)}, u32[]{:S(2)}) collective-permute-start(bf16[320,2048]{1,0:T(8,128)(2,1)} %after.13.mine_ref), channel_id=1, source_target_pairs={{0,1},{1,0},{2,3},{3,2},{4,5},{5,4},{6,7},{7,6},{8,9},{9,8},{10,11... | collective-permute-start | bytes 3932168 | tf_op jit(solution)/shard_map/ppermute | solution.py:456
  403.1 77.7 %collective-permute-start.28 = (bf16[320,1024]{1,0:T(8,128)(2,1)}, bf16[320,1024]{1,0:T(8,128)(2,1)}, u32[]{:S(2)}, u32[]{:S(2)}) collective-permute-start(bf16[320,1024]{1,0:T(8,128)(2,1)} %copy-done.28), channel_id=1, source_target_pairs={{0,2},{2,0},{4,6},{6,4},{8,10},{10,8},{12,14},{14,12},{16,18},{18,... | collective-permute-start | bytes 1966088 | tf_op jit(solution)/shard_map/ppermute | solution.py:453
  425.3 55.9 %collective-permute-start.46 = (bf16[1,128,1536]{1,2,0:T(8,128)(2,1)}, bf16[1,128,1536]{1,2,0:T(8,128)(2,1)}, u32[]{:S(2)}, u32[]{:S(2)}) collective-permute-start(bf16[1,128,1536]{1,2,0:T(8,128)(2,1)} %slice.460), channel_id=1, source_target_pairs={{0,16},{2,18},{4,20},{6,22},{8,24},{10,26},{12,28},{14,30},{16,0},... | collective-permute-start | bytes 1179656 | tf_op jit(solution)/shard_map/ppermute | solution.py:453
  435.6 43.0 %collective-permute-start.47 = (bf16[2,128,1280]{1,2,0:T(8,128)(2,1)}, bf16[2,128,1280]{1,2,0:T(8,128)(2,1)}, u32[]{:S(2)}, u32[]{:S(2)}) collective-permute-start(bf16[2,128,1280]{1,2,0:T(8,128)(2,1)} %copy.58), channel_id=1, source_target_pairs={{0,8},{2,10},{4,12},{6,14},{8,0},{10,2},{12,4},{14,6},{16,24},{18,... | collective-permute-start | bytes 1966088 | tf_op jit(solution)/shard_map/ppermute | solution.py:453
  435.6 63.0 %collective-permute-start.15 = (bf16[512,1536]{1,0:T(8,128)(2,1)}, bf16[512,1536]{1,0:T(8,128)(2,1)}, u32[]{:S(2)}, u32[]{:S(2)}) collective-permute-start(bf16[512,1536]{1,0:T(8,128)(2,1)} %after.16), channel_id=1, source_target_pairs={{0,4},{2,6},{4,0},{6,2},{8,12},{10,14},{12,8},{14,10},{16,20},{18,... | collective-permute-start | bytes 4718600 | tf_op jit(solution)/shard_map/ppermute | solution.py:453
  464.3 35.6 %collective-permute-start.14 = (bf16[8,5,64,512]{3,2,1,0:T(8,128)(2,1)}, bf16[8,5,64,512]{3,2,1,0:T(8,128)(2,1)}, u32[]{:S(2)}, u32[]{:S(2)}) collective-permute-start(bf16[8,5,64,512]{3,2,1,0:T(8,128)(2,1)} %get-tuple-element.57), channel_id=1, source_target_pairs={{0,2},{2,0},{4,6},{6,4},{8,10},{10,8},{12,14},{14,12},{16,18},{18,... | collective-permute-start | bytes 7864328 | tf_op jit(solution)/shard_map/ppermute | solution.py:453
  478.6 5.9 collective-permute-start.27
  480.8 31.1 %collective-permute-start.13 = (bf16[320,2048]{1,0:T(8,128)(2,1)}, bf16[320,2048]{1,0:T(8,128)(2,1)}, u32[]{:S(2)}, u32[]{:S(2)}) collective-permute-start(bf16[320,2048]{1,0:T(8,128)(2,1)} %fusion.16), channel_id=1, source_target_pairs={{0,1},{1,0},{2,3},{3,2},{4,5},{5,4},{6,7},{7,6},{8,9},{9,8},{10,11... | collective-permute-start | bytes 3932168 | tf_op jit(solution)/shard_map/ppermute | solution.py:456
  481.2 17.3 %collective-permute-start.48 = (bf16[1,128,1280]{1,2,0:T(8,128)(2,1)S(1)}, bf16[1,128,1280]{1,2,0:T(8,128)(2,1)S(1)}, u32[]{:S(2)}, u32[]{:S(2)}) collective-permute-start(bf16[1,128,1280]{1,2,0:T(8,128)(2,1)S(1)} %slice.464), channel_id=1, source_target_pairs={{0,16},{2,18},{4,20},{6,22},{8,24},{10,26},{12,28},{14,30},{16,0},... | collective-permute-start | bytes 983048 | tf_op jit(solution)/shard_map/ppermute | solution.py:453
  484.5 151.4 %collective-permute-start.22 = (bf16[320,1024]{1,0:T(8,128)(2,1)}, bf16[320,1024]{1,0:T(8,128)(2,1)}, u32[]{:S(2)}, u32[]{:S(2)}) collective-permute-start(bf16[320,1024]{1,0:T(8,128)(2,1)} %get-tuple-element.64), channel_id=1, source_target_pairs={{0,2},{2,0},{4,6},{6,4},{8,10},{10,8},{12,14},{14,12},{16,18},{18,... | collective-permute-start | bytes 1966088 | tf_op jit(solution)/shard_map/ppermute | solution.py:453
  505.9 29.9 %collective-permute-start.16 = (bf16[4,5,64,512]{3,2,1,0:T(8,128)(2,1)}, bf16[4,5,64,512]{3,2,1,0:T(8,128)(2,1)S(1)}, u32[]{:S(2)}, u32[]{:S(2)}) collective-permute-start(bf16[4,5,64,512]{3,2,1,0:T(8,128)(2,1)} %after.17), channel_id=1, source_target_pairs={{0,4},{2,6},{4,0},{6,2},{8,12},{10,14},{12,8},{14,10},{16,20},{18,... | collective-permute-start | bytes 3932168 | tf_op jit(solution)/shard_map/ppermute | solution.py:453
  522.6 36.2 %collective-permute-start.37 = (bf16[2,128,1536]{2,1,0:T(8,128)(2,1)S(1)}, bf16[2,128,1536]{2,1,0:T(8,128)(2,1)}, u32[]{:S(2)}, u32[]{:S(2)}) collective-permute-start(bf16[2,128,1536]{2,1,0:T(8,128)(2,1)S(1)} %bitcast.110), channel_id=1, source_target_pairs={{0,8},{2,10},{4,12},{6,14},{8,0},{10,2},{12,4},{14,6},{16,24},{18,... | collective-permute-start | bytes 2359304 | tf_op jit(solution)/shard_map/ppermute | solution.py:453
  538.8 16.8 %collective-permute-start.17 = (bf16[2,5,64,512]{3,2,1,0:T(8,128)(2,1)}, bf16[2,5,64,512]{3,2,1,0:T(8,128)(2,1)}, u32[]{:S(2)}, u32[]{:S(2)}) collective-permute-start(bf16[2,5,64,512]{3,2,1,0:T(8,128)(2,1)} %slice.406), channel_id=1, source_target_pairs={{0,8},{2,10},{4,12},{6,14},{8,0},{10,2},{12,4},{14,6},{16,24},{18,... | collective-permute-start | bytes 1966088 | tf_op jit(solution)/shard_map/ppermute | solution.py:453
  538.9 16.7 %copy-start.58 = (bf16[4,5,64,512]{3,2,1,0:T(8,128)(2,1)S(1)}, bf16[4,5,64,512]{3,2,1,0:T(8,128)(2,1)}, u32[]{:S(2)}) copy-start(bf16[4,5,64,512]{3,2,1,0:T(8,128)(2,1)} %copy-done.57) | copy-start | bytes 3932164
  538.9 43.9 %collective-permute-start.19 = (bf16[512,1280]{1,0:T(8,128)(2,1)}, bf16[512,1280]{1,0:T(8,128)(2,1)S(1)}, u32[]{:S(2)}, u32[]{:S(2)}) collective-permute-start(bf16[512,1280]{1,0:T(8,128)(2,1)} %after.18), channel_id=1, source_target_pairs={{0,4},{2,6},{4,0},{6,2},{8,12},{10,14},{12,8},{14,10},{16,20},{18,... | collective-permute-start | bytes 3932168 | tf_op jit(solution)/shard_map/ppermute | solution.py:453
  543.3 15.5 %copy-start.63 = (bf16[256,1536]{1,0:T(8,128)(2,1)S(1)}, bf16[256,1536]{1,0:T(8,128)(2,1)}, u32[]{:S(2)}) copy-start(bf16[256,1536]{1,0:T(8,128)(2,1)} %get-tuple-element.104) | copy-start | bytes 2359300
  556.9 25.7 %collective-permute-start.18 = (bf16[1,5,64,512]{3,2,1,0:T(8,128)(2,1)S(1)}, bf16[1,5,64,512]{3,2,1,0:T(8,128)(2,1)S(1)}, u32[]{:S(2)}, u32[]{:S(2)}) collective-permute-start(bf16[1,5,64,512]{3,2,1,0:T(8,128)(2,1)S(1)} %slice.408), channel_id=1, source_target_pairs={{0,16},{2,18},{4,20},{6,22},{8,24},{10,26},{12,28},{14,30},{16,0},... | collective-permute-start | bytes 983048 | tf_op jit(solution)/shard_map/ppermute | solution.py:453
  560.1 22.6 %copy-start.61 = (bf16[2,128,1536]{2,1,0:T(8,128)(2,1)}, bf16[2,128,1536]{2,1,0:T(8,128)(2,1)S(1)}, u32[]{:S(2)}) copy-start(bf16[2,128,1536]{2,1,0:T(8,128)(2,1)S(1)} %fusion.23) | copy-start | bytes 2359300
  561.0 46.4 %collective-permute-start.38 = (bf16[1,128,1536]{2,1,0:T(8,128)(2,1)}, bf16[1,128,1536]{2,1,0:T(8,128)(2,1)}, u32[]{:S(2)}, u32[]{:S(2)}) collective-permute-start(bf16[1,128,1536]{2,1,0:T(8,128)(2,1)} %slice.444), channel_id=1, source_target_pairs={{0,16},{2,18},{4,20},{6,22},{8,24},{10,26},{12,28},{14,30},{16,0},... | collective-permute-start | bytes 1179656 | tf_op jit(solution)/shard_map/ppermute | solution.py:453
  584.5 50.8 %collective-permute-start.24 = (bf16[512,1536]{1,0:T(8,128)(2,1)}, bf16[512,1536]{1,0:T(8,128)(2,1)}, u32[]{:S(2)}, u32[]{:S(2)}) collective-permute-start(bf16[512,1536]{1,0:T(8,128)(2,1)} %after.19), channel_id=1, source_target_pairs={{0,4},{2,6},{4,0},{6,2},{8,12},{10,14},{12,8},{14,10},{16,20},{18,... | collective-permute-start | bytes 4718600 | tf_op jit(solution)/shard_map/ppermute | solution.py:453
  591.4 15.1 %collective-permute-start.39 = (bf16[2,128,1280]{2,1,0:T(8,128)(2,1)S(1)}, bf16[2,128,1280]{2,1,0:T(8,128)(2,1)S(1)}, u32[]{:S(2)}, u32[]{:S(2)}) collective-permute-start(bf16[2,128,1280]{2,1,0:T(8,128)(2,1)S(1)} %bitcast.112), channel_id=1, source_target_pairs={{0,8},{2,10},{4,12},{6,14},{8,0},{10,2},{12,4},{14,6},{16,24},{18,... | collective-permute-start | bytes 1966088 | tf_op jit(solution)/shard_map/ppermute | solution.py:453
  599.3 29.2 %collective-permute-start.20 = (bf16[320,2048]{1,0:T(8,128)(2,1)S(1)}, bf16[320,2048]{1,0:T(8,128)(2,1)S(1)}, u32[]{:S(2)}, u32[]{:S(2)}) collective-permute-start(bf16[320,2048]{1,0:T(8,128)(2,1)S(1)} %fusion.10.mine_ref), channel_id=1, source_target_pairs={{0,1},{1,0},{2,3},{3,2},{4,5},{5,4},{6,7},{7,6},{8,9},{9,8},{10,11... | collective-permute-start | bytes 3932168 | tf_op jit(solution)/shard_map/ppermute | solution.py:456
  606.7 15.2 %collective-permute-start.40 = (bf16[1,128,1280]{2,1,0:T(8,128)(2,1)S(1)}, bf16[1,128,1280]{2,1,0:T(8,128)(2,1)S(1)}, u32[]{:S(2)}, u32[]{:S(2)}) collective-permute-start(bf16[1,128,1280]{2,1,0:T(8,128)(2,1)S(1)} %slice.448), channel_id=1, source_target_pairs={{0,16},{2,18},{4,20},{6,22},{8,24},{10,26},{12,28},{14,30},{16,0},... | collective-permute-start | bytes 983048 | tf_op jit(solution)/shard_map/ppermute | solution.py:453
  608.6 27.4 %collective-permute-start.23 = (bf16[320,1536]{1,0:T(8,128)(2,1)S(1)}, bf16[320,1536]{1,0:T(8,128)(2,1)S(1)}, u32[]{:S(2)}, u32[]{:S(2)}) collective-permute-start(bf16[320,1536]{1,0:T(8,128)(2,1)S(1)} %pad_maximum_fusion.8.refs_2_), channel_id=1, source_target_pairs={{0,2},{2,0},{4,6},{6,4},{8,10},{10,8},{12,14},{14,12},{16,18},{18,... | collective-permute-start | bytes 2949128 | tf_op jit(solution)/shard_map/ppermute | solution.py:453
  641.0 34.0 %collective-permute-start.25 = (bf16[512,1536]{1,0:T(8,128)(2,1)S(1)}, bf16[512,1536]{1,0:T(8,128)(2,1)S(1)}, u32[]{:S(2)}, u32[]{:S(2)}) collective-permute-start(bf16[512,1536]{1,0:T(8,128)(2,1)S(1)} %side_product.22), channel_id=1, source_target_pairs={{0,4},{2,6},{4,0},{6,2},{8,12},{10,14},{12,8},{14,10},{16,20},{18,... | collective-permute-start | bytes 4718600 | tf_op jit(solution)/shard_map/ppermute | solution.py:453
  651.7 29.9 %collective-permute-start.41 = (bf16[2,128,1536]{2,1,0:T(8,128)(2,1)}, bf16[2,128,1536]{2,1,0:T(8,128)(2,1)}, u32[]{:S(2)}, u32[]{:S(2)}) collective-permute-start(bf16[2,128,1536]{2,1,0:T(8,128)(2,1)} %bitcast.37), channel_id=1, source_target_pairs={{0,8},{2,10},{4,12},{6,14},{8,0},{10,2},{12,4},{14,6},{16,24},{18,... | collective-permute-start | bytes 2359304 | tf_op jit(solution)/shard_map/ppermute | solution.py:453
  676.7 4.2 collective-permute-start.21
  676.8 31.4 %collective-permute-start.29 = (bf16[512,1280]{1,0:T(8,128)(2,1)}, bf16[512,1280]{1,0:T(8,128)(2,1)S(1)}, u32[]{:S(2)}, u32[]{:S(2)}) collective-permute-start(bf16[512,1280]{1,0:T(8,128)(2,1)} %after.21), channel_id=1, source_target_pairs={{0,4},{2,6},{4,0},{6,2},{8,12},{10,14},{12,8},{14,10},{16,20},{18,... | collective-permute-start | bytes 3932168 | tf_op jit(solution)/shard_map/ppermute | solution.py:453
  683.0 31.5 %collective-permute-start.42 = (bf16[1,128,1536]{2,1,0:T(8,128)(2,1)S(1)}, bf16[1,128,1536]{2,1,0:T(8,128)(2,1)S(1)}, u32[]{:S(2)}, u32[]{:S(2)}) collective-permute-start(bf16[1,128,1536]{2,1,0:T(8,128)(2,1)S(1)} %slice.452), channel_id=1, source_target_pairs={{0,16},{2,18},{4,20},{6,22},{8,24},{10,26},{12,28},{14,30},{16,0},... | collective-permute-start | bytes 1179656 | tf_op jit(solution)/shard_map/ppermute | solution.py:453
  689.5 18.6 %copy-start.5 = (bf16[320,2816]{1,0:T(8,128)(2,1)S(1)}, bf16[320,2816]{1,0:T(8,128)(2,1)}, u32[]{:S(2)}) copy-start(bf16[320,2816]{1,0:T(8,128)(2,1)} %get-tuple-element.53.refs_2_) | copy-start | bytes 5406724
  689.7 28.5 %collective-permute-start.35 = (bf16[2,128,1536]{2,1,0:T(8,128)(2,1)S(1)}, bf16[2,128,1536]{2,1,0:T(8,128)(2,1)}, u32[]{:S(2)}, u32[]{:S(2)}) collective-permute-start(bf16[2,128,1536]{2,1,0:T(8,128)(2,1)S(1)} %bitcast.111), channel_id=1, source_target_pairs={{0,8},{2,10},{4,12},{6,14},{8,0},{10,2},{12,4},{14,6},{16,24},{18,... | collective-permute-start | bytes 2359304 | tf_op jit(solution)/shard_map/ppermute | solution.py:453
  713.5 26.2 %collective-permute-start.43 = (bf16[2,128,1280]{2,1,0:T(8,128)(2,1)}, bf16[2,128,1280]{2,1,0:T(8,128)(2,1)}, u32[]{:S(2)}, u32[]{:S(2)}) collective-permute-start(bf16[2,128,1280]{2,1,0:T(8,128)(2,1)} %bitcast.40), channel_id=1, source_target_pairs={{0,8},{2,10},{4,12},{6,14},{8,0},{10,2},{12,4},{14,6},{16,24},{18,... | collective-permute-start | bytes 1966088 | tf_op jit(solution)/shard_map/ppermute | solution.py:453
  714.6 48.1 %collective-permute-start.26 = (f32[4,2,128]{2,1,0:T(2,128)}, f32[4,2,128]{2,1,0:T(2,128)S(1)}, u32[]{:S(2)}, u32[]{:S(2)}) collective-permute-start(f32[4,2,128]{2,1,0:T(2,128)} %after.20), channel_id=1, source_target_pairs={{0,4},{2,6},{4,0},{6,2},{8,12},{10,14},{12,8},{14,10},{16,20},{18,... | collective-permute-start | bytes 12296 | tf_op jit(solution)/shard_map/ppermute | solution.py:453
  720.8 20.3 %collective-permute-start.36 = (bf16[1,128,1536]{2,1,0:T(8,128)(2,1)S(1)}, bf16[1,128,1536]{2,1,0:T(8,128)(2,1)S(1)}, u32[]{:S(2)}, u32[]{:S(2)}) collective-permute-start(bf16[1,128,1536]{2,1,0:T(8,128)(2,1)S(1)} %slice.436), channel_id=1, source_target_pairs={{0,16},{2,18},{4,20},{6,22},{8,24},{10,26},{12,28},{14,30},{16,0},... | collective-permute-start | bytes 1179656 | tf_op jit(solution)/shard_map/ppermute | solution.py:453
  720.8 36.5 %collective-permute-start.30 = (bf16[512,1024]{1,0:T(8,128)(2,1)}, bf16[512,1024]{1,0:T(8,128)(2,1)S(1)}, u32[]{:S(2)}, u32[]{:S(2)}) collective-permute-start(bf16[512,1024]{1,0:T(8,128)(2,1)} %after.22), channel_id=1, source_target_pairs={{0,4},{2,6},{4,0},{6,2},{8,12},{10,14},{12,8},{14,10},{16,20},{18,... | collective-permute-start | bytes 3145736 | tf_op jit(solution)/shard_map/ppermute | solution.py:453
  741.0 16.2 %collective-permute-start.44 = (bf16[1,128,1280]{2,1,0:T(8,128)(2,1)S(1)}, bf16[1,128,1280]{2,1,0:T(8,128)(2,1)S(1)}, u32[]{:S(2)}, u32[]{:S(2)}) collective-permute-start(bf16[1,128,1280]{2,1,0:T(8,128)(2,1)S(1)} %slice.456), channel_id=1, source_target_pairs={{0,16},{2,18},{4,20},{6,22},{8,24},{10,26},{12,28},{14,30},{16,0},... | collective-permute-start | bytes 983048 | tf_op jit(solution)/shard_map/ppermute | solution.py:453
  741.2 16.1 %copy-start.30 = (bf16[320,1024]{1,0:T(8,128)(2,1)S(1)}, bf16[320,1024]{1,0:T(8,128)(2,1)}, u32[]{:S(2)}) copy-start(bf16[320,1024]{1,0:T(8,128)(2,1)} %copy-done.28) | copy-start | bytes 1966084
  741.2 16.1 %copy-start.32 = (bf16[320,1024]{1,0:T(8,128)(2,1)S(1)}, bf16[320,1024]{1,0:T(8,128)(2,1)}, u32[]{:S(2)}) copy-start(bf16[320,1024]{1,0:T(8,128)(2,1)} %copy-done.31) | copy-start | bytes 1966084
  741.2 16.1 %copy-start.34 = (bf16[320,1024]{1,0:T(8,128)(2,1)S(1)}, bf16[320,1024]{1,0:T(8,128)(2,1)}, u32[]{:S(2)}) copy-start(bf16[320,1024]{1,0:T(8,128)(2,1)} %copy-done.33) | copy-start | bytes 1966084
  760.8 13.9 %collective-permute-start.32 = (bf16[2,128,1024]{2,1,0:T(8,128)(2,1)S(1)}, bf16[2,128,1024]{2,1,0:T(8,128)(2,1)S(1)}, u32[]{:S(2)}, u32[]{:S(2)}) collective-permute-start(bf16[2,128,1024]{2,1,0:T(8,128)(2,1)S(1)} %bitcast.113), channel_id=1, source_target_pairs={{0,8},{2,10},{4,12},{6,14},{8,0},{10,2},{12,4},{14,6},{16,24},{18,... | collective-permute-start | bytes 1572872 | tf_op jit(solution)/shard_map/ppermute | solution.py:453
  764.0 12.3 %collective-permute-start.31 = (f32[2,2,128]{2,1,0:T(2,128)S(1)}, f32[2,2,128]{2,1,0:T(2,128)S(1)}, u32[]{:S(2)}, u32[]{:S(2)}) collective-permute-start(f32[2,2,128]{2,1,0:T(2,128)S(1)} %slice.424), channel_id=1, source_target_pairs={{0,8},{2,10},{4,12},{6,14},{8,0},{10,2},{12,4},{14,6},{16,24},{18,... | collective-permute-start | bytes 6152 | tf_op jit(solution)/shard_map/ppermute | solution.py:453
  775.0 14.0 %collective-permute-start.34 = (bf16[1,128,1024]{2,1,0:T(8,128)(2,1)S(1)}, bf16[1,128,1024]{2,1,0:T(8,128)(2,1)S(1)}, u32[]{:S(2)}, u32[]{:S(2)}) collective-permute-start(bf16[1,128,1024]{2,1,0:T(8,128)(2,1)S(1)} %slice.431), channel_id=1, source_target_pairs={{0,16},{2,18},{4,20},{6,22},{8,24},{10,26},{12,28},{14,30},{16,0},... | collective-permute-start | bytes 786440 | tf_op jit(solution)/shard_map/ppermute | solution.py:453
  777.5 13.1 %collective-permute-start.33 = (f32[1,2,128]{2,1,0:T(2,128)S(1)}, f32[1,2,128]{2,1,0:T(2,128)S(1)}, u32[]{:S(2)}, u32[]{:S(2)}) collective-permute-start(f32[1,2,128]{2,1,0:T(2,128)S(1)} %slice.429), channel_id=1, source_target_pairs={{0,16},{2,18},{4,20},{6,22},{8,24},{10,26},{12,28},{14,30},{16,0},... | collective-permute-start | bytes 3080 | tf_op jit(solution)/shard_map/ppermute | solution.py:453
  (65 other events, 276.1 us)
Sparse Core Ops, SparseCore 0:
  11.6 96.7 all-gather.2
  110.6 202.9 all-gather.4

commit v3 on v1

--- a/solution.py
+++ b/solution.py
@@ -1,4 +1,5 @@
 import functools
+import math
 
 import jax
 import jax.numpy as jnp
@@ -10,7 +11,22 @@
 HD = 128
 EPSILON = 1e-05
 NEGATIVE = -1e30
-VMEM_LIMIT = 48 * 1024 * 1024
+MIB = 1024 * 1024
+
+
+def hint(microseconds):
+    return pl.CostEstimate(
+        flops=int(microseconds * 5e8), bytes_accessed=int(microseconds * 1.8e6), transcendentals=0
+    )
+
+
+FAR_FIRST = ("o",)
+ORDER = (
+    "fA", "fB", "PdA", "PdB", "F", "SdA", "H", "PgA", "SdB", "N", "SdA", "M", "A", "SgA", "SdB",
+    "K", "PgB", "Sk", "V", "SdA", "SdA", "Sk", "SgA", "PuA", "SgB", "Sk", "SdB", "Sk", "R",
+    "Po", "SgB", "Pq", "T", "SuA", "PuB", "So", "SgA", "Sq", "I", "SuA", "So", "SgB", "Sq",
+    "SuA", "SuB", "So", "Sn", "Sq", "Sn", "SuB", "Sn", "SuB", "Sn",
+)
 
 bf16 = jnp.bfloat16
 f32 = jnp.float32
@@ -24,12 +40,42 @@
     return lax.dot_general(a, b, (((ca,), (cb,)), ((), ())), preferred_element_type=f32)
 
 
-def params(**kwargs):
-    return pltpu.CompilerParams(vmem_limit_bytes=VMEM_LIMIT, **kwargs)
+def params(room=16 * MIB):
+    return pltpu.CompilerParams(vmem_limit_bytes=min(room, 56 * MIB))
 
 
 def turn(v, cosine, sine):
     return v * cosine + pltpu.roll(v, HD // 2, 1) * sine
+
+
+def call(
+    kernel, token, args, in_specs, outs, out_specs, name, takes, grid=(), scratch=(), others=(), aliases=None,
+    room=16 * MIB,
+):
+    waits = [*([] if token is None else [token]), *others]
+    unread = pl.BlockSpec(memory_space=pl.ANY)
+    count = len(args)
+
+    def body(*refs):
+        rest = refs[count + len(waits) :]
+        kernel(*refs[:count], *rest[: len(outs)], *rest[len(outs) + 1 :])
+
+    return pl.pallas_call(
+        body,
+        grid=grid,
+        in_specs=[*in_specs, *[unread] * len(waits)],
+        out_specs=[*out_specs, unread],
+        out_shape=[*outs, jax.ShapeDtypeStruct((8, 128), f32)],
+        scratch_shapes=list(scratch),
+        input_output_aliases=aliases or {},
+        compiler_params=params(room),
+        cost_estimate=hint(takes),
+        name=name,
+    )(*args, *waits)
+
+
+def like(*shape, dtype=bf16):
+    return jax.ShapeDtypeStruct(shape, dtype)
 
 
 def rope_kernel(q_cols, k_cols, raw_ref, cos_ref, sin_ref, q_ref, kv_ref):
@@ -42,25 +88,23 @@
     kv_ref[:, k_cols:] = raw_ref[:, q_cols + k_cols :].astype(bf16)
 
 
-def rope(raw, cosine, sine, rows, q_cols, k_cols):
-    total = raw.shape[0]
-    width = raw.shape[1]
+def rope(raw, cosine, sine, rows, q_cols, k_cols, token=None):
+    total, width = raw.shape
     table = pl.BlockSpec((rows, HD), lambda i: (0, 0))
-    return pl.pallas_call(
+    return call(
         functools.partial(rope_kernel, q_cols, k_cols),
-        grid=(total // rows,),
-        in_specs=[pl.BlockSpec((rows, width), lambda i: (i, 0)), table, table],
-        out_specs=[
+        token,
+        (raw, cosine, sine),
+        [pl.BlockSpec((rows, width), lambda i: (i, 0)), table, table],
+        [like(total, q_cols), like(total, 2 * k_cols)],
+        [
             pl.BlockSpec((rows, q_cols), lambda i: (i, 0)),
             pl.BlockSpec((rows, 2 * k_cols), lambda i: (i, 0)),
         ],
-        out_shape=[
-            jax.ShapeDtypeStruct((total, q_cols), bf16),
-            jax.ShapeDtypeStruct((total, 2 * k_cols), bf16),
-        ],
-        compiler_params=params(),
-        name="rope",
-    )(raw, cosine, sine)
+        "rope",
+        2,
+        grid=(total // rows,),
+    )
 
 
 def heads_to_rows(block, kv, group):
@@ -93,6 +137,10 @@
         log_ref[kv] = top + jnp.log(total)
 
 
+def score_room(kpos, qpos):
+    return 4 * MIB + 14 * 4 * kpos.size * qpos.size
+
+
 def attend(q, near, far, qpos, kpos, rows, local_kv, group):
     total, width = q.shape
     seqs = total // rows
@@ -116,7 +164,8 @@
             jax.ShapeDtypeStruct((total, width), bf16),
             jax.ShapeDtypeStruct((seqs * local_kv, group * rows, 1), f32),
         ],
-        compiler_params=params(),
+        compiler_params=params(score_room(kpos, qpos)),
+        cost_estimate=hint(9),
         name="attend",
     )(q, near, far, qpos, kpos)
 
@@ -153,17 +202,19 @@
             dfar_ref[:, 0, :, c : c + HD] = d[half:].reshape(-1, rows, HD)
 
 
-def attend_back(q, near, far, qpos, kpos, log, grad, cosine, sine, rows, local_kv, group):
+def attend_back(
+    q, near, far, qpos, kpos, log, grad, cosine, sine, rows, local_kv, group, token, others
+):
     total, width = q.shape
-    seqs = total // rows
     blocks, _, _, kv_width = near.shape
     kv_spec = pl.BlockSpec((blocks, 1, rows, kv_width), lambda i: (0, i, 0, 0))
     row_spec = pl.BlockSpec((rows, width), lambda i: (i, 0))
     table = pl.BlockSpec((rows, HD), lambda i: (0, 0))
-    return pl.pallas_call(
+    return call(
         functools.partial(attend_back_kernel, local_kv, group),
-        grid=(seqs,),
-        in_specs=[
+        token,
+        (q, near, far, qpos, kpos, log, grad, cosine, sine),
+        [
             row_spec,
             kv_spec,
             kv_spec,
@@ -174,15 +225,14 @@
             table,
             table,
         ],
-        out_specs=[row_spec, kv_spec, kv_spec],
-        out_shape=[
-            jax.ShapeDtypeStruct((total, width), bf16),
-            jax.ShapeDtypeStruct(near.shape, bf16),
-            jax.ShapeDtypeStruct(far.shape, bf16),
-        ],
-        compiler_params=params(),
-        name="attend_back",
-    )(q, near, far, qpos, kpos, log, grad, cosine, sine)
+        [like(total, width), like(*near.shape), like(*far.shape)],
+        [row_spec, kv_spec, kv_spec],
+        "attend_back",
+        13,
+        grid=(total // rows,),
+        others=others,
+        room=score_room(kpos, qpos),
+    )
 
 
 def arrange_kernel(block, order_ref, a_ref, keep_ref, send_ref):
@@ -210,8 +260,224 @@
         out_specs=[pl.BlockSpec(memory_space=pltpu.VMEM)] * 2,
         out_shape=[out, out],
         compiler_params=params(),
+        cost_estimate=hint(1),
         name="arrange",
     )(order, a)
+
+
+def forward_kernel(hidden_ref, gate_w_ref, up_w_ref, *refs):
+    gate_ref, up_ref, product_ref = refs[-3:]
+    hidden = hidden_ref[...]
+    gate = dot(hidden, gate_w_ref[...], 1, 0)
+    up = dot(hidden, up_w_ref[...], 1, 0)
+    gate_ref[...] = gate
+    up_ref[...] = up
+    product_ref[...] = (gate * jax.nn.sigmoid(gate) * up).astype(bf16)
+
+
+def feed_forward(hidden, weights, units, columns, before, token):
+    rows, width = hidden.shape
+    start, count = columns
+    tile = math.gcd(math.gcd(start, count), math.gcd(units, 256))
+    tiles, first = units // tile, start // tile
+    column = pl.BlockSpec((rows, tile), lambda i: (0, first + i))
+    return call(
+        forward_kernel,
+        token,
+        (hidden, weights, weights, *before),
+        [
+            pl.BlockSpec((rows, width), lambda i: (0, 0)),
+            pl.BlockSpec((width, tile), lambda i: (0, first + i)),
+            pl.BlockSpec((width, tile), lambda i: (0, tiles + first + i)),
+            *[pl.BlockSpec(memory_space=pl.ANY)] * len(before),
+        ],
+        [like(rows, units, dtype=f32), like(rows, units, dtype=f32), like(rows, count)],
+        [column, column, pl.BlockSpec((rows, tile), lambda i: (0, i))],
+        "feed_forward",
+        17 * count / units,
+        grid=(count // tile,),
+        aliases={3: 0, 4: 1} if before else None,
+    )
+
+
+def backward_kernel(
+    down_grad_ref, gate_ref, up_ref, gate_w_ref, up_w_ref, down_w_ref, grads_ref, partial_ref, sum_ref
+):
+    product_grad = dot(down_grad_ref[...], down_w_ref[...], 1, 0)
+    gate, up = gate_ref[...], up_ref[...]
+    sigmoid = jax.nn.sigmoid(gate)
+    gate_grad = (product_grad * up * (sigmoid * (1.0 + gate * (1.0 - sigmoid)))).astype(bf16)
+    up_grad = (product_grad * gate * sigmoid).astype(bf16)
+    grads_ref[0] = gate_grad
+    grads_ref[1] = up_grad
+    term = dot(gate_grad, gate_w_ref[...], 1, 1) + dot(up_grad, up_w_ref[...], 1, 1)
+
+    @pl.when(pl.program_id(0) == 0)
+    def _():
+        sum_ref[...] = term
+
+    @pl.when(pl.program_id(0) != 0)
+    def _():
+        sum_ref[...] += term
+
+    @pl.when(pl.program_id(0) == pl.num_programs(0) - 1)
+    def _():
+        partial_ref[...] = sum_ref[...].astype(bf16)
+
+
+def feed_forward_back(down_grad, gate, up, weights, units, token):
+    rows, width = down_grad.shape
+    tile = math.gcd(units, 256)
+    tiles = units // tile
+    whole = pl.BlockSpec((rows, width), lambda i: (0, 0))
+    column = pl.BlockSpec((rows, tile), lambda i: (0, i))
+    return call(
+        backward_kernel,
+        token,
+        (down_grad, gate, up, weights, weights, weights),
+        [
+            whole,
+            column,
+            column,
+            pl.BlockSpec((width, tile), lambda i: (0, i)),
+            pl.BlockSpec((width, tile), lambda i: (0, tiles + i)),
+            pl.BlockSpec((width, tile), lambda i: (0, 2 * tiles + i)),
+        ],
+        [like(2, rows, units), like(rows, width)],
+        [pl.BlockSpec((2, rows, tile), lambda i: (0, 0, i)), whole],
+        "feed_forward_back",
+        28,
+        grid=(tiles,),
+        scratch=[pltpu.VMEM((rows, width), f32)],
+    )
+
+
+def turned_kernel(a_ref, w_ref, out_ref):
+    out_ref[...] = dot(a_ref[...], w_ref[...], 1, 1).astype(bf16)
+
+
+def times_turned(a, weights, at, token):
+    rows, depth = a.shape
+    height = weights.shape[0]
+    tile = math.gcd(height, 256)
+    return call(
+        turned_kernel,
+        token,
+        (a, weights),
+        [
+            pl.BlockSpec((rows, depth), lambda i: (0, 0)),
+            pl.BlockSpec((tile, depth), lambda i: (i, at)),
+        ],
+        [like(rows, height)],
+        [pl.BlockSpec((rows, tile), lambda i: (0, i))],
+        "times_turned",
+        9,
+        grid=(height // tile,),
+        room=48 * MIB,
+    )
+
+
+def product_kernel(blocks, a_ref, a2_ref, b_ref, b2_ref, *out_refs):
+    for out_ref, chosen in zip(out_refs, blocks, strict=True):
+        sides = []
+        for ref in (a_ref, a2_ref):
+            parts = [ref[:, start:end] for start, end in chosen]
+            sides.append(parts[0] if len(parts) == 1 else jnp.concatenate(parts, axis=1))
+        out = dot(sides[0], b_ref[...], 0, 0) + dot(sides[1], b2_ref[...], 0, 0)
+        out_ref[...] = out.astype(bf16)
+
+
+def side_products(side, b, b2, which, columns, blocks, token):
+    a, a2 = side
+    rows, width = a.shape
+    start, count = columns
+    tile = 768 if math.gcd(start, count) % 768 == 0 else math.gcd(start, count)
+    first = start // tile
+    whole = pl.BlockSpec((rows, width), lambda i: (0, 0))
+    b_spec = pl.BlockSpec((None, rows, tile), lambda i: (which, 0, first + i))
+    return call(
+        functools.partial(product_kernel, blocks),
+        token,
+        (a, a2, b, b2),
+        [whole, whole, b_spec, b_spec],
+        [like(width // 2, count)] * 2,
+        [pl.BlockSpec((width // 2, tile), lambda i: (0, i))] * 2,
+        "side_products",
+        6,
+        grid=(count // tile,),
+    )
+
+
+def fold_kernel(kept_ref, received_ref, *out_refs):
+    height = out_refs[0].shape[0]
+    for i, out_ref in enumerate(out_refs):
+        part = slice(i * height, (i + 1) * height)
+        out = kept_ref[part].astype(f32) + received_ref[part].astype(f32)
+        out_ref[...] = out.astype(out_ref.dtype)
+
+
+def fold(kept, received, last, token):
+    rows, width = kept.shape
+    whole = pl.BlockSpec(memory_space=pltpu.VMEM)
+    outs = [like(rows, width, dtype=f32)] if last else [like(rows // 2, width, dtype=kept.dtype)] * 2
+    return call(
+        fold_kernel, token, (kept, received), [whole] * 2, outs, [whole] * len(outs), "fold", 1.5,
+        room=max(16 * MIB, 4 * MIB + 4 * kept.size * kept.dtype.itemsize),
+    )
+
+
+def hold_kernel(*refs):
+    pass
+
+
+def hold(v, token):
+    anywhere = pl.BlockSpec(memory_space=pl.ANY)
+    out = like(*v.shape, dtype=v.dtype)
+    return call(
+        hold_kernel, token, (v,), [anywhere], [out], [anywhere], "hold", 0.1, aliases={0: 0}
+    )
+
+
+def norm_back_kernel(
+    mine_ref, theirs_ref, v_ref, gain_ref, base_ref, grad_ref, low_ref, gain_grad_ref
+):
+    hidden_grad = mine_ref[...].astype(f32) + theirs_ref[...].astype(f32)
+    v = v_ref[...].astype(f32)
+    scale = rms_scale(v)
+    normed = v * scale
+    gain_grad = jnp.sum(hidden_grad * normed, axis=0, keepdims=True)
+
+    @pl.when(pl.program_id(0) == 0)
+    def _():
+        gain_grad_ref[...] = gain_grad
+
+    @pl.when(pl.program_id(0) != 0)
+    def _():
+        gain_grad_ref[...] += gain_grad
+
+    g = hidden_grad * gain_ref[...]
+    out = base_ref[...].astype(f32) + scale * (
+        g - normed * jnp.mean(g * normed, axis=-1, keepdims=True)
+    )
+    grad_ref[...] = out
+    low_ref[...] = out.astype(bf16)
+
+
+def norm_back(mine, theirs, v, gain, base, rows, token):
+    total, width = mine.shape
+    spec = pl.BlockSpec((rows, width), lambda i: (i, 0))
+    row = pl.BlockSpec((1, width), lambda i: (0, 0))
+    return call(
+        norm_back_kernel,
+        token,
+        (mine, theirs, v, gain, base),
+        [spec, spec, spec, row, spec],
+        [like(total, width, dtype=f32), like(total, width), like(1, width, dtype=f32)],
+        [spec, spec, row],
+        "norm_back",
+        6.5,
+        grid=(total // rows,),
+    )
 
 
 def local(
@@ -251,7 +517,11 @@
         mine = lax.optimization_barrier(partial_rows.astype(bf16))
         return mine.astype(f32) + tensor_flip(mine).astype(f32)
 
-    near_places = [far * 4 + pair * 2 for pair in range(2) for far in range(groups)]
+    far_bits = [1 << b for b in range(groups.bit_length() - 1)]
+    fars = [0]
+    for bit in reversed(far_bits):
+        fars = fars + [far + bit for far in fars]
+    near_places = [far * 4 + pair * 2 for pair in range(2) for far in fars]
     places = near_places + [place + 1 for place in near_places]
     owners = jnp.bitwise_xor(me, jnp.asarray(places, jnp.int32))
 
@@ -272,13 +542,13 @@
         "dp", axis=0, tiled=True,
     )
     second = lax.all_gather(
-        jnp.concatenate([gate_weight, up_weight], axis=1), "dp", axis=0, tiled=True
-    )
-    down_turned = lax.all_gather(down_weight.T, "dp", axis=0, tiled=True)
+        jnp.concatenate([gate_weight, up_weight, down_weight.T], axis=1), "dp", axis=0, tiled=True
+    )
+    down_turned = second[:, 2 * hidden_units :]
     qkv_cols = q_cols + 2 * k_cols
     qkv_full = first[:, :qkv_cols]
     out_turned = first[:, qkv_cols : qkv_cols + q_cols]
-    gain_attn = first[:, qkv_cols + q_cols].astype(f32)[None, :]
+    gain_attn_row = first[:, qkv_cols + q_cols].astype(f32)[None, :]
     gain_mlp = first[:, qkv_cols + q_cols + 1].astype(f32)[None, :]
 
     dead_slot = jnp.argmin(active.reshape(-1))
@@ -299,17 +569,17 @@
             axis=0,
         )
 
-    token_rows = pick(tokens).astype(f32)
+    token_low = lax.optimization_barrier(pick(tokens))
+    token_rows = token_low.astype(f32)
     down_grad = lax.optimization_barrier(pick(cotangent))
-    upstream = down_grad.astype(f32)
-
-    attn_scale = rms_scale(token_rows)
-    hidden = (token_rows * attn_scale * gain_attn).astype(bf16)
+
+    hidden = (token_rows * rms_scale(token_rows) * gain_attn_row).astype(bf16)
     qkv_raw = dot(hidden, qkv_full, 1, 0)
-    queries, kv_own = rope(qkv_raw, cosine, sine, rows, q_cols, k_cols)
+    queries, kv_own, _ = rope(qkv_raw, cosine, sine, rows, q_cols, k_cols)
     kv_own = kv_own.reshape(1, live_seqs, rows, 2 * k_cols)
-    kv_far = jnp.concatenate([kv_own] + [flip(kv_own, 4 * k) for k in range(1, groups)], axis=0)
-    kv_near = jnp.concatenate([kv_far, flip(kv_far, 2)], axis=0)
+    kv_near = kv_own
+    for bits in [4 * bit for bit in reversed(far_bits)] + [2]:
+        kv_near = jnp.concatenate([kv_near, flip(kv_near, bits)], axis=0)
     kv_other = flip(kv_near, 1)
     mixed_out, log_total = attend(
         queries, kv_near, kv_other, qpos, kpos, rows, local_kv, group
@@ -317,100 +587,174 @@
     branch = tensor_total(dot(mixed_out, out_turned, 1, 1))
     middle = token_rows + branch
 
-    mlp_scale = rms_scale(middle)
-    normed_mlp = middle * mlp_scale
-    hidden_mlp = (normed_mlp * gain_mlp).astype(bf16)
-    gate_up = dot(hidden_mlp, second, 1, 0)
-    gate_values, up_values = gate_up[:, :hidden_units], gate_up[:, hidden_units:]
-    sigmoid_gate = jax.nn.sigmoid(gate_values)
-    silu_gate = gate_values * sigmoid_gate
-    product = (silu_gate * up_values).astype(bf16)
-
+    hidden_mlp = (middle * rms_scale(middle) * gain_mlp).astype(bf16)
     def side(a):
         keep, send = arrange(a, owners)
-        return jnp.concatenate([keep, flip(send, 1)], axis=0)
-
-    def both_cores(b):
-        return jnp.concatenate([b, flip(b, 1)], axis=0)
-
-    def summed(a_side, b):
-        half = groups * block
-        sent = dot(a_side[:, half:], b, 0, 0).astype(bf16)
-        kept = dot(a_side[:, :half], b, 0, 0)
-        pair = (kept + flip(sent, 2).astype(f32)).reshape(groups, block, b.shape[1])
-        out = pair[0]
-        for k in range(1, groups):
-            out = out + flip(pair[k].astype(bf16), 4 * k).astype(f32)
-        return out
-
-    grad_down = summed(side(down_grad), both_cores(product)).T
-    down_values = tensor_total(dot(product, down_turned, 1, 1))
+        return keep, flip(send, 1)
+
+    token = [None]
+
+    def run(kernel, *args, **kwargs):
+        *outs, token[0] = kernel(*args, **kwargs, token=token[0])
+        return outs if len(outs) > 1 else outs[0]
+
+    class Total:
+        def __init__(self, kept, received, bits):
+            self.kept, self.received, self.bits, self.out = kept, received, list(bits), None
+
+        def step(self):
+            if self.out is not None:
+                return
+            if not self.bits:
+                self.out = run(fold, self.kept, self.received, True)
+                return
+            self.kept, sent = run(fold, self.kept, self.received, False)
+            self.received = flip(sent, self.bits.pop(0))
+
+        def end(self):
+            while self.out is None:
+                self.step()
+            return self.out
+
+    far_flips = [4 * bit for bit in far_bits]
+    far_first = FAR_FIRST if block % 128 == 0 else ()
+
+    def weight_total(name, *args):
+        if name in far_first:
+            places = [pair * groups + far for far in range(groups) for pair in range(2)]
+            spans = [(place * block, (place + 1) * block) for place in places]
+            blocks, bits = [spans[:groups], spans[groups:]], [*far_flips, 2]
+        else:
+            half = groups * block
+            blocks, bits = [[(0, half)], [(half, 2 * half)]], [2, *far_flips]
+        kept, sent = run(side_products, *args, blocks)
+        return Total(kept, flip(sent, bits[0]), bits[1:])
+
+    split_at = -(-hidden_units // 512) * 256
+    columns = ((0, split_at), (split_at, hidden_units - split_at))
+    down_side, mlp_side, attn_side = side(down_grad), side(hidden_mlp), side(hidden)
+    mixed2 = flip(mixed_out, 1)
+    arrived = [down_side[1], mlp_side[1], attn_side[1], mixed2]
+    (token[0],) = call(hold_kernel, None, (), [], [], [], "hold", 0.1, others=arrived)
+
+    totals, made = {}, {}
+    kv_cols = 2 * k_cols
+    chunks = {"A": columns[0], "B": columns[1]}
+
+    def send_products(name):
+        if name[0] == "d":
+            product, product2 = made["product" + name[1]]
+            args = (down_side, product[None], product2[None], 0, (0, product.shape[1]))
+        elif name[0] in "gu":
+            which = "gu".index(name[0])
+            args = (mlp_side, made["grads"], made["grads2"], which, chunks[name[1]])
+        elif name == "q":
+            args = (attn_side, made["qkv_grad"][None], made["qkv_grad2"][None], 0, (0, qkv_cols))
+        else:
+            args = (made["out_side"], mixed_out[None], mixed2[None], 0, (0, q_cols))
+        totals[name] = weight_total(name, *args)
+
+    def feed(name):
+        before = made.get("gate_up", ())
+        *made["gate_up"], product = run(
+            feed_forward, hidden_mlp, second, hidden_units, chunks[name], before
+        )
+        made["product" + name] = product, flip(product, 1)
+
+    def feed_back():
+        made["grads"], made["partial"] = run(
+            feed_forward_back, down_grad, *made["gate_up"], second, hidden_units
+        )
+
+    def exchange():
+        grads, partial = run(hold, made["grads"]), run(hold, made["partial"])
+        made.update(grads=grads, grads2=flip(grads, 1), partial=partial, theirs=tensor_flip(partial))
+
+    def middle_back():
+        made["middle_grad"], made["branch_grad"], made["gain_mlp"] = run(
+            norm_back, made["partial"], made["theirs"], middle, gain_mlp, down_grad, rows
+        )
+
+    def mixed_back():
+        made["out_side"] = side(made["branch_grad"])
+        made["mixed_grad"] = dot(made["branch_grad"], out_turned, 1, 0).astype(bf16)
+
+    def attention_back():
+        mixed_grad = made["mixed_grad"]
+        made["query_grad"], made["near"], made["other"] = run(
+            attend_back, queries, kv_near, kv_other, qpos, kpos, log_total, mixed_grad,
+            cosine, sine, rows, local_kv, group, others=[made["out_side"][1]],
+        )
+
+    def keys_back():
+        other = run(hold, made["other"])
+        totals["k"] = Total(
+            made["near"].reshape(-1, kv_cols), flip(other.reshape(-1, kv_cols), 1), [2, *far_flips]
+        )
+
+    def turn_back():
+        dkv = totals["k"].end()
+        key_grad, _ = run(
+            rope, jnp.concatenate([dkv[:, :k_cols], dkv], axis=1), cosine, -sine, rows, k_cols, k_cols
+        )
+        qkv_grad = jnp.concatenate(
+            [made["query_grad"], key_grad, dkv[:, k_cols:].astype(bf16)], axis=1
+        )
+        made.update(qkv_grad=qkv_grad, qkv_grad2=flip(qkv_grad, 1))
+
+    def attention_partial():
+        made["attn"] = run(times_turned, made["qkv_grad"], first, 0)
+        made["attn_theirs"] = tensor_flip(made["attn"])
+
+    def input_back():
+        made["input_grad"], _, gain_attn = run(
+            norm_back, made["attn"], made["attn_theirs"], token_low, gain_attn_row,
+            made["middle_grad"], rows,
+        )
+        gains = jnp.concatenate([gain_attn, made["gain_mlp"]]).reshape(2, n_dp, block)
+        gains = jnp.take(gains, owners, axis=1).transpose(1, 0, 2).reshape(n_dp, 2 * block)
+        totals["n"] = Total(gains[: 2 * groups], flip(gains[2 * groups :], 1), [2, *far_flips])
+
+    def down_value():
+        product = jnp.concatenate([made["product" + name][0] for name in "AB"], axis=1)
+        made["down"] = run(times_turned, product, second, 2)
+        made["down_theirs"] = tensor_flip(made["down"])
+
+    actions = {
+        "F": feed_back, "H": exchange, "N": middle_back, "M": mixed_back, "A": attention_back, "K": keys_back,
+        "R": turn_back, "T": attention_partial, "I": input_back, "V": down_value,
+    }
+    for entry in ORDER:
+        if entry in actions:
+            actions[entry]()
+        elif entry[0] == "f":
+            feed(entry[1])
+        elif entry[0] == "P":
+            send_products(entry[1:])
+        else:
+            totals[entry[1:]].step()
+    finished = {name: v.end() for name, v in totals.items()}
+    down_partial, down_theirs = made["down"], made["down_theirs"]
+    input_grad, gains, grad_out, grad_qkv = (
+        made["input_grad"], finished["n"], finished["o"], finished["q"],
+    )
+    grad_down, grad_gate, grad_up = [[finished[m + c] for c in "AB"] for m in "dgu"]
+    down_values = down_partial.astype(f32) + down_theirs.astype(f32)
     result = unpick((middle + down_values).astype(bf16), tokens)
-
-    product_grad = dot(down_grad, down_turned, 1, 0)
-    gate_grad = (
-        product_grad * up_values * (sigmoid_gate * (1.0 + gate_values * (1.0 - sigmoid_gate)))
-    ).astype(bf16)
-    up_grad = (product_grad * silu_gate).astype(bf16)
-    gate_up_grad = jnp.concatenate([gate_grad, up_grad], axis=1)
-    mlp_side = side(hidden_mlp)
-    grad_gate = summed(mlp_side, both_cores(gate_grad))
-    grad_up = summed(mlp_side, both_cores(up_grad))
-    hidden_mlp_grad = tensor_total(dot(gate_up_grad, second, 1, 1))
-    gain_mlp_rows = jnp.sum(hidden_mlp_grad * normed_mlp, axis=0)
-    normed_grad = hidden_mlp_grad * gain_mlp
-    middle_grad = upstream + mlp_scale * (
-        normed_grad - normed_mlp * jnp.mean(normed_grad * normed_mlp, axis=-1, keepdims=True)
-    )
-
-    branch_grad = middle_grad.astype(bf16)
-    grad_out = summed(side(branch_grad), both_cores(mixed_out)).T
-    mixed_grad = dot(branch_grad, out_turned, 1, 0).astype(bf16)
-    query_grad, dkv_near, dkv_other = attend_back(
-        queries, kv_near, kv_other, qpos, kpos, log_total, mixed_grad, cosine, sine,
-        rows, local_kv, group,
-    )
-    dkv_near = dkv_near.astype(f32) + flip(dkv_other, 1).astype(f32)
-    dkv_far = dkv_near[:groups] + flip(dkv_near[groups:].astype(bf16), 2).astype(f32)
-    dkv = dkv_far[0]
-    for k in range(1, groups):
-        dkv = dkv + flip(dkv_far[k].astype(bf16), 4 * k).astype(f32)
-    dkv = dkv.reshape(total, 2 * k_cols)
-    key_grad, _ = rope(
-        jnp.concatenate([dkv[:, :k_cols], dkv], axis=1), cosine, -sine, rows, k_cols, k_cols
-    )
-    qkv_grad = jnp.concatenate([query_grad, key_grad, dkv[:, k_cols:].astype(bf16)], axis=1)
-    grad_qkv = summed(side(hidden), both_cores(qkv_grad))
-    hidden_grad = tensor_total(dot(qkv_grad, qkv_full, 1, 1))
-    normed_attn = token_rows * attn_scale
-    gain_attn_rows = jnp.sum(hidden_grad * normed_attn, axis=0)
-    normed_attn_grad = hidden_grad * gain_attn
-    input_grad = middle_grad + attn_scale * (
-        normed_attn_grad
-        - normed_attn * jnp.mean(normed_attn_grad * normed_attn, axis=-1, keepdims=True)
-    )
     input_grad = unpick(input_grad, cotangent.astype(f32))
-
-    gain_rows = jnp.stack([gain_attn_rows, gain_mlp_rows]).reshape(2, n_dp, block)
-    gain_rows = jnp.take(gain_rows, owners, axis=1)
-    gain_rows = gain_rows[:, : 2 * groups] + flip(gain_rows[:, 2 * groups :], 1)
-    gain_rows = gain_rows[:, :groups] + flip(gain_rows[:, groups:], 2)
-    gain_own = gain_rows[:, 0]
-    for k in range(1, groups):
-        gain_own = gain_own + flip(gain_rows[:, k], 4 * k)
 
     return (
         result,
         input_grad,
-        gain_own[0],
+        gains[0, :block],
         grad_qkv[:, :q_cols],
         grad_qkv[:, q_cols : q_cols + k_cols],
         grad_qkv[:, q_cols + k_cols :],
-        grad_out,
-        gain_own[1],
-        grad_gate,
-        grad_up,
-        grad_down,
+        grad_out.T,
+        gains[0, block:],
+        jnp.concatenate(grad_gate, axis=1),
+        jnp.concatenate(grad_up, axis=1),
+        jnp.concatenate(grad_down, axis=1).T,
     )
 
 

time: 939 us -> 682 us (0.73)
  waiting for transfers between devices: 622 us -> 372 us
  Pallas kernels: 29.4 us -> 155 us
  matrix products: 120 us -> 13.8 us
  starting transfers between devices: 67.7 us -> 36.5 us
  local copies, waits for them, and re-layouts: 21.5 us -> 46 us
  other arithmetic: 50.3 us -> 28.3 us
    ppermute x44 -> x45, waiting for transfers between devices: 382 us -> 243 us  [flip(): return lax.ppermute(v, 'dp', [(i, i ^ bits) for i in range(n_dp)])]
    pallas_call x3 -> x54, Pallas kernels: 16.4 us -> 143 us  [call(): pl.pallas_call(body, grid=grid, in_specs=[*in_specs, *[unread] * len(wait...]
    dot_general x18 -> x3, matrix products: 120 us -> 13.8 us  [dot(): lax.dot_general(a, b, (((ca,), (cb,)), ((), ())), preferred_element_type=...]
    all_gather x2 -> x1, waiting for transfers between devices: 75 us -> 22.2 us  [local(): lax.all_gather(jnp.concatenate([gate_weight, up_weight, down_weight.T], a...]
    ppermute x4, waiting for transfers between devices: 75.4 us -> 25.4 us  [tensor_flip(): return lax.ppermute(v, 'tensor', [(0, 1), (1, 0)])]
    ppermute x44 -> x45, starting transfers between devices: 62.5 us -> 30.5 us  [flip(): return lax.ppermute(v, 'dp', [(i, i ^ bits) for i in range(n_dp)])]
    unnamed x111 -> x202, local copies, waits for them, and re-layouts: 14 us -> 41.1 us
    add x10 -> x0, other arithmetic: 14.7 us -> none  [the longest x3 4.93 us: summed(): out = out + flip(pair[k].astype(bf16), 4 * k).astype(f32)]
  transfers between devices with their start and end apart: 51 -> 51, of which waited for: 25 -> 26; matrix products, arithmetic and copies ran while one was open for 16% -> 7% of each run, Pallas kernels for 3% -> 22%
where the time goes in v3:
time: 682 us; the launch traced here: 671 us
  waiting for transfers between devices  372 us (55%)
  Pallas kernels  155 us (23%)
  local copies, waits for them, and re-layouts  46 us (7%)
  starting transfers between devices  36.5 us (5%)
  other arithmetic  28.3 us (4%)
  between operations  19 us (3%)
  matrix products  13.8 us (2%)
    ppermute x45, waiting for transfers between devices, flip(): return lax.ppermute(v, 'dp', [(i, i ^ bits) for i in range(n_dp)])  243 us
    pallas_call x54, Pallas kernels, call(): pl.pallas_call(body, grid=grid, in_specs=[*in_specs, *[unread] * len(wait...  143 us
    all_gather x1, waiting for transfers between devices, local(): lax.all_gather(jnp.concatenate([query_weight, key_weight, value_weight, o...  81.9 us
    unnamed x202, local copies, waits for them, and re-layouts  41.1 us
    ppermute x45, starting transfers between devices, flip(): return lax.ppermute(v, 'dp', [(i, i ^ bits) for i in range(n_dp)])  30.5 us
    ppermute x4, waiting for transfers between devices, tensor_flip(): return lax.ppermute(v, 'tensor', [(0, 1), (1, 0)])  25.4 us
    all_gather x1, waiting for transfers between devices, local(): lax.all_gather(jnp.concatenate([gate_weight, up_weight, down_weight.T], a...  22.2 us
    dot_general x3, matrix products, dot(): lax.dot_general(a, b, (((ca,), (cb,)), ((), ())), preferred_element_type=...  13.8 us
  transfers between devices with their start and end apart: 51, of which 26 were waited for; matrix products, arithmetic and copies ran while one was open for 7% of the time, Pallas kernels for 22%

profile of v3, /device:TPU:0, one launch (start us, length us, event | category | flops | bytes accessed | tf_op | source)
XLA Modules:
  0.0 671.2 jit_solution(13898584324859210156)
XLA Ops:
  13.2 2.6 pad_maximum_fusion.2
  21.7 2.4 slice_select_fusion.1
  24.9 81.9 %all-gather.3.cloned.1.call-done.refs_1_ = bf16[2048,2688]{1,0:T(8,128)(2,1)} async-done(((bf16[128,2688]{1,0:T(8,128)(2,1)}), bf16[2048,2688]{1,0:T(8,128)(2,1)}) %all-gather.3.cloned.1.call-update) | async-done | bytes 11010064 | tf_op jit(solution)/shard_map/all_gather | solution.py:540
  106.8 1.8 convert_reduce_fusion
  109.6 5.4 fusion.refs_0_
  117.5 23.5 %collective-permute-done = bf16[1,5,64,512]{3,2,1,0:T(8,128)(2,1)S(1)} collective-permute-done((bf16[1,5,64,512]{3,2,1,0:T(8,128)(2,1)S(1)}, bf16[1,5,64,512]{3,2,1,0:T(8,128)(2,1)S(1)}, u32[]{:S(2)}, u32[]{:S(2)}) %collective-permute-start) | collective-permute-done | bytes 327712 | tf_op jit(solution)/shard_map/ppermute | solution.py:511
  141.1 31.2 %collective-permute-done.1 = bf16[2,5,64,512]{3,2,1,0:T(8,128)(2,1)S(1)} collective-permute-done((bf16[2,5,64,512]{3,2,1,0:T(8,128)(2,1)S(1)}, bf16[2,5,64,512]{3,2,1,0:T(8,128)(2,1)S(1)}, u32[]{:S(2)}, u32[]{:S(2)}) %collective-permute-start.1) | collective-permute-done | bytes 655392 | tf_op jit(solution)/shard_map/ppermute | solution.py:511
  173.1 58.4 %collective-permute-done.2 = bf16[4,5,64,512]{3,2,1,0:T(8,128)(2,1)S(1)} collective-permute-done((bf16[4,5,64,512]{3,2,1,0:T(8,128)(2,1)S(1)}, bf16[4,5,64,512]{3,2,1,0:T(8,128)(2,1)S(1)}, u32[]{:S(2)}, u32[]{:S(2)}) %collective-permute-start.2) | collective-permute-done | bytes 1310752 | tf_op jit(solution)/shard_map/ppermute | solution.py:511
  233.4 4.9 collective-permute-done.3.far_ref.refs_2_
  238.3 8.6 %attend.1 = (bf16[320,1024]{1,0:T(8,128)(2,1)S(1)}, f32[10,256,1]{2,1,0:T(8,128)S(1)}) custom-call(bf16[320,1024]{1,0:T(8,128)(2,1)S(1)} %get-tuple-element.168.q_ref.refs_0_, bf16[8,5,64,512]{3,2,1,0:T(8,128)(2,1)} %pad_maximum_fusion.1.near_ref.refs_1_, bf16[8,5,64,512]{3,2,1,0:T(8,128)(2,1)} %collective-permute-done.3.far_ref.refs_2_, ...), custom_call_target="tpu_custom_call" | custom-call | flops 4499999744 | bytes 16200000 | tf_op jit(solution)/shard_map/attend/pallas_call | solution.py:149
  247.0 4.5 fusion.6
  257.1 25.4 %collective-permute-done.4 = bf16[320,2048]{1,0:T(8,128)(2,1)S(1)} collective-permute-done((bf16[320,2048]{1,0:T(8,128)(2,1)S(1)}, bf16[320,2048]{1,0:T(8,128)(2,1)S(1)}, u32[]{:S(2)}, u32[]{:S(2)}) %collective-permute-start.4) | collective-permute-done | bytes 1310752 | tf_op jit(solution)/shard_map/ppermute | solution.py:514
  286.4 2.1 collective-permute-done.6.refs_1_
  291.1 22.2 %all-gather.5.cloned.1.call-done.refs_1_.refs_2_.refs_3_.refs_4_.refs_5_ = bf16[2048,8448]{1,0:T(8,128)(2,1)} async-done(((bf16[128,8448]{1,0:T(8,128)(2,1)}), bf16[2048,8448]{1,0:T(8,128)(2,1)}) %all-gather.5.cloned.1.call-update) | async-done | bytes 34603024 | tf_op jit(solution)/shard_map/all_gather | solution.py:544
  314.6 8.6 %feed_forward.2 = (f32[320,2816]{1,0:T(8,128)S(1)}, f32[320,2816]{1,0:T(8,128)S(1)}, bf16[320,1536]{1,0:T(8,128)(2,1)S(1)}, f32[8,128]{1,0:T(8,128)S(1)}) custom-call(bf16[320,2048]{1,0:T(8,128)(2,1)S(1)} %copy-done.4, bf16[2048,8448]{1,0:T(8,128)(2,1)} %all-gather.5.cloned.1.call-done.refs_1_.refs_2_.refs_3_.refs_4_.refs_5_, ...), custom_call_target="tpu_custom_call" | custom-call | flops 4636363776 | bytes 16690909 | tf_op jit(solution)/shard_map/feed_forward/pallas_call | solution.py:63
  323.6 7.6 %feed_forward.3 = (f32[320,2816]{1,0:T(8,128)S(1)}, f32[320,2816]{1,0:T(8,128)S(1)}, bf16[320,1280]{1,0:T(8,128)(2,1)S(1)}, f32[8,128]{1,0:T(8,128)S(1)}) custom-call(bf16[320,2048]{1,0:T(8,128)(2,1)S(1)} %copy-done.4, ...), custom_call_target="tpu_custom_call", output_to_operand_aliasing={{0}: (3, {}), {1}: (4, {})} | custom-call | flops 3863636480 | bytes 13909090 | tf_op jit(solution)/shard_map/feed_forward/pallas_call | solution.py:63
  331.5 4.2 side_products.8
  335.9 2.9 side_products.9
  338.8 27.0 %feed_forward_back.1 = (bf16[2,320,2816]{2,1,0:T(8,128)(2,1)S(1)}, bf16[320,2048]{1,0:T(8,128)(2,1)S(1)}, f32[8,128]{1,0:T(8,128)S(1)}) custom-call(bf16[320,2048]{1,0:T(8,128)(2,1)S(1)} %bitcast.55, f32[320,2816]{1,0:T(8,128)S(1)} %get-tuple-element.180.refs_1_, f32[320,2816]{1,0:T(8,128)S(1)} %get-tuple-element.181.refs_2_, ...), custom_call_target="tpu_custom_call" | custom-call | flops 14000000000 | bytes 50400000 | tf_op jit(solution)/shard_map/feed_forward_back/pallas_call | solution.py:63
  365.8 6.5 collective-permute-done.11.refs_1_
  374.6 4.5 collective-permute-done.14.refs_3_
  379.1 4.1 side_products.10
  383.6 20.9 %collective-permute-done.13.refs_1_ = bf16[512,1280]{1,0:T(8,128)(2,1)S(1)} collective-permute-done((bf16[512,1280]{1,0:T(8,128)(2,1)S(1)}, bf16[512,1280]{1,0:T(8,128)(2,1)S(1)}, u32[]{:S(2)}, u32[]{:S(2)}) %collective-permute-start.13) | collective-permute-done | bytes 1310752 | tf_op jit(solution)/shard_map/ppermute | solution.py:511
  404.8 2.4 norm_back.2
  410.0 3.9 fusion.12.refs_6_
  413.9 12.6 %attend_back.1 = (bf16[320,1024]{1,0:T(8,128)(2,1)S(1)}, bf16[8,5,64,512]{3,2,1,0:T(8,128)(2,1)S(1)}, bf16[8,5,64,512]{3,2,1,0:T(8,128)(2,1)S(1)}, f32[8,128]{1,0:T(8,128)S(1)}) custom-call(bf16[320,1024]{1,0:T(8,128)(2,1)S(1)} %copy-done.71, bf16[8,5,64,512]{3,2,1,0:T(8,128)(2,1)} %pad_maximum_fusion.1.near_ref.refs_1_, ...), custom_call_target="tpu_custom_call" | custom-call | flops 6499999744 | bytes 23400000 | tf_op jit(solution)/shard_map/attend_back/pallas_call | solution.py:63
  426.5 11.2 %collective-permute-done.18.refs_1_ = bf16[512,1536]{1,0:T(8,128)(2,1)S(1)} collective-permute-done((bf16[512,1536]{1,0:T(8,128)(2,1)S(1)}, bf16[512,1536]{1,0:T(8,128)(2,1)S(1)}, u32[]{:S(2)}, u32[]{:S(2)}) %collective-permute-start.18) | collective-permute-done | bytes 1572896 | tf_op jit(solution)/shard_map/ppermute | solution.py:511
  440.7 4.8 side_products.11
  446.8 1.7 collective-permute-start.24
  448.8 3.1 collective-permute-start.25
  451.9 9.2 %times_turned.2 = (bf16[320,2048]{1,0:T(8,128)(2,1)S(1)}, f32[8,128]{1,0:T(8,128)S(1)}) custom-call(bf16[320,2816]{1,0:T(8,128)(2,1)S(1)} %pad_maximum_fusion.3.refs_0_, bf16[2048,8448]{1,0:T(8,128)(2,1)} %all-gather.5.cloned.1.call-done.refs_1_.refs_2_.refs_3_.refs_4_.refs_5_, f32[8,128]{1,0:T(8,128)S(1)} %get-tuple-element.219.refs_2_), custom_call_target="tpu_custom_call" | custom-call | flops 4499999744 | bytes 16200000 | tf_op jit(solution)/shard_map/times_turned/pallas_call | solution.py:63
  461.1 7.4 %collective-permute-done.22.refs_1_ = bf16[128,1536]{1,0:T(8,128)(2,1)S(1)} collective-permute-done((bf16[128,1536]{1,0:T(8,128)(2,1)S(1)}, bf16[128,1536]{1,0:T(8,128)(2,1)S(1)}, u32[]{:S(2)}, u32[]{:S(2)}) %collective-permute-start.22) | collective-permute-done | bytes 393248 | tf_op jit(solution)/shard_map/ppermute | solution.py:511
  469.5 8.8 %collective-permute-done.21.refs_1_ = bf16[1280,512]{1,0:T(8,128)(2,1)S(1)} collective-permute-done((bf16[1280,512]{1,0:T(8,128)(2,1)S(1)}, bf16[1280,512]{1,0:T(8,128)(2,1)S(1)}, u32[]{:S(2)}, u32[]{:S(2)}) %collective-permute-start.21) | collective-permute-done | bytes 1310752 | tf_op jit(solution)/shard_map/ppermute | solution.py:511
  480.1 2.0 convert_element_type.98
  483.5 3.1 collective-permute-start.27
  489.2 2.1 fold.40
  491.3 2.2 copy-done.8
  493.5 2.0 copy-done.33
  495.5 4.9 side_products.12
  500.4 4.9 collective-permute-done.24.refs_1_
  508.4 3.1 collective-permute-start.29
  512.8 12.2 %collective-permute-done.26.refs_1_ = bf16[320,512]{1,0:T(8,128)(2,1)S(1)} collective-permute-done((bf16[320,512]{1,0:T(8,128)(2,1)S(1)}, bf16[320,512]{1,0:T(8,128)(2,1)S(1)}, u32[]{:S(2)}, u32[]{:S(2)}) %collective-permute-start.26) | collective-permute-done | bytes 327712 | tf_op jit(solution)/shard_map/ppermute | solution.py:511
  525.2 2.4 rope.3
  531.7 3.3 side_products.13
  535.1 7.0 %collective-permute-done.29.refs_1_ = bf16[256,1280]{1,0:T(8,128)(2,1)S(1)} collective-permute-done((bf16[256,1280]{1,0:T(8,128)(2,1)S(1)}, bf16[256,1280]{1,0:T(8,128)(2,1)S(1)}, u32[]{:S(2)}, u32[]{:S(2)}) %collective-permute-start.29) | collective-permute-done | bytes 655392 | tf_op jit(solution)/shard_map/ppermute | solution.py:511
  542.9 4.8 side_products.14
  548.0 8.1 %times_turned.3 = (bf16[320,2048]{1,0:T(8,128)(2,1)}, f32[8,128]{1,0:T(8,128)S(1)}) custom-call(bf16[320,1536]{1,0:T(8,128)(2,1)S(1)} %get-tuple-element.365.refs_0_, bf16[2048,2688]{1,0:T(8,128)(2,1)} %all-gather.3.cloned.1.call-done.refs_1_, f32[8,128]{1,0:T(8,128)S(1)} %get-tuple-element.254.refs_2_), custom_call_target="tpu_custom_call" | custom-call | flops 4499999744 | bytes 16200000 | tf_op jit(solution)/shard_map/times_turned/pallas_call | solution.py:63
  562.1 2.0 copy-done.34
  564.1 4.8 side_products.15
  570.0 2.3 fold.47
  573.1 2.2 collective-permute-start.36
  576.5 2.9 copy.55
  583.2 1.7 collective-permute-start.39
  587.1 2.0 collective-permute-start.41
  589.1 5.6 norm_back.3
  594.7 2.1 fold.50
  597.9 9.2 %collective-permute-done.36.refs_1_ = bf16[256,1024]{1,0:T(8,128)(2,1)} collective-permute-done((bf16[256,1024]{1,0:T(8,128)(2,1)}, bf16[256,1024]{1,0:T(8,128)(2,1)}, u32[]{:S(2)}, u32[]{:S(2)}) %collective-permute-start.36) | collective-permute-done | bytes 524320 | tf_op jit(solution)/shard_map/ppermute | solution.py:511
  609.2 2.1 slice_select_fusion
  616.3 5.4 collective-permute-done.41.refs_1_
  623.1 12.4 %collective-permute-done.40.refs_1_ = bf16[128,1536]{1,0:T(8,128)(2,1)S(1)} collective-permute-done((bf16[128,1536]{1,0:T(8,128)(2,1)}, bf16[128,1536]{1,0:T(8,128)(2,1)S(1)}, u32[]{:S(2)}, u32[]{:S(2)}) %collective-permute-start.40) | collective-permute-done | bytes 393248 | tf_op jit(solution)/shard_map/ppermute | solution.py:511
  643.3 7.3 %collective-permute-done.46.refs_1_ = bf16[256,1280]{1,0:T(8,128)(2,1)S(1)} collective-permute-done((bf16[256,1280]{1,0:T(8,128)(2,1)S(1)}, bf16[256,1280]{1,0:T(8,128)(2,1)S(1)}, u32[]{:S(2)}, u32[]{:S(2)}) %collective-permute-start.46) | collective-permute-done | bytes 655392 | tf_op jit(solution)/shard_map/ppermute | solution.py:511
  650.9 1.9 pad_maximum_fusion
  653.8 2.4 collective-permute-start.45
  657.7 2.6 collective-permute-start.47
  (358 shorter events, 94.7 us)
Async XLA Ops:
  7.2 99.6 %all-gather.3.cloned.1.call-start = ((), (), s32[]{:S(2)}) async-start(), calls=%async_computation | async-start | bytes 11698176 | tf_op jit(solution)/shard_map/all_gather | solution.py:540
  12.9 300.4 %all-gather.5.cloned.1.call-start = ((), (), s32[]{:S(2)}) async-start(), calls=%async_computation.1 | async-start | bytes 36765696 | tf_op jit(solution)/shard_map/all_gather | solution.py:544
  24.1 84.9 %copy-start = (bf16[5,64,2048]{2,1,0:T(8,128)(2,1)}, bf16[5,64,2048]{2,1,0:T(8,128)(2,1)S(1)}, u32[]{:S(2)}) copy-start(bf16[5,64,2048]{2,1,0:T(8,128)(2,1)S(1)} %get-tuple-element.376) | copy-start | bytes 3932164
  24.1 228.9 %copy-start.5 = (bf16[5,64,2048]{2,1,0:T(8,128)(2,1)}, bf16[5,64,2048]{2,1,0:T(8,128)(2,1)S(1)}, u32[]{:S(2)}) copy-start(bf16[5,64,2048]{2,1,0:T(8,128)(2,1)S(1)} %get-tuple-element.375) | copy-start | bytes 3932164
  115.9 122.4 %copy-start.70 = (bf16[320,1024]{1,0:T(8,128)(2,1)}, bf16[320,1024]{1,0:T(8,128)(2,1)S(1)}, u32[]{:S(2)}) copy-start(bf16[320,1024]{1,0:T(8,128)(2,1)S(1)} %get-tuple-element.168.q_ref.refs_0_) | copy-start | bytes 1966084
  115.9 25.1 %collective-permute-start = (bf16[1,5,64,512]{3,2,1,0:T(8,128)(2,1)S(1)}, bf16[1,5,64,512]{3,2,1,0:T(8,128)(2,1)S(1)}, u32[]{:S(2)}, u32[]{:S(2)}) collective-permute-start(bf16[1,5,64,512]{3,2,1,0:T(8,128)(2,1)S(1)} %bitcast.59), channel_id=1, source_target_pairs={{0,16},{2,18},{4,20},{6,22},{8,24},{10,26},{12,28},{14,30},{16,0},... | collective-permute-start | bytes 983048 | tf_op jit(solution)/shard_map/ppermute | solution.py:511
  141.1 31.3 %collective-permute-start.1 = (bf16[2,5,64,512]{3,2,1,0:T(8,128)(2,1)S(1)}, bf16[2,5,64,512]{3,2,1,0:T(8,128)(2,1)S(1)}, u32[]{:S(2)}, u32[]{:S(2)}) collective-permute-start(bf16[2,5,64,512]{3,2,1,0:T(8,128)(2,1)S(1)} %pad_maximum_fusion.10), channel_id=1, source_target_pairs={{0,8},{2,10},{4,12},{6,14},{8,0},{10,2},{12,4},{14,6},{16,24},{18,... | collective-permute-start | bytes 1966088 | tf_op jit(solution)/shard_map/ppermute | solution.py:511
  172.4 60.8 %copy-start.92 = (s32[16]{0:T(128)S(1)}, s32[16]{0:T(128)}, u32[]{:S(2)}) copy-start(s32[16]{0:T(128)} %constant.56.clone) | copy-start | bytes 196
  172.5 59.0 %collective-permute-start.2 = (bf16[4,5,64,512]{3,2,1,0:T(8,128)(2,1)S(1)}, bf16[4,5,64,512]{3,2,1,0:T(8,128)(2,1)S(1)}, u32[]{:S(2)}, u32[]{:S(2)}) collective-permute-start(bf16[4,5,64,512]{3,2,1,0:T(8,128)(2,1)S(1)} %pad_maximum_fusion.7), channel_id=1, source_target_pairs={{0,4},{2,6},{4,0},{6,2},{8,12},{10,14},{12,8},{14,10},{16,20},{18,... | collective-permute-start | bytes 3932168 | tf_op jit(solution)/shard_map/ppermute | solution.py:511
  233.1 5.3 collective-permute-start.3
  251.5 31.0 %collective-permute-start.4 = (bf16[320,2048]{1,0:T(8,128)(2,1)S(1)}, bf16[320,2048]{1,0:T(8,128)(2,1)S(1)}, u32[]{:S(2)}, u32[]{:S(2)}) collective-permute-start(bf16[320,2048]{1,0:T(8,128)(2,1)S(1)} %fusion.6), channel_id=1, source_target_pairs={{0,1},{1,0},{2,3},{3,2},{4,5},{5,4},{6,7},{7,6},{8,9},{9,8},{10,11... | collective-permute-start | bytes 3932168 | tf_op jit(solution)/shard_map/ppermute | solution.py:514
  253.1 29.4 %copy-start.1 = (bf16[5,64,2048]{2,1,0:T(8,128)(2,1)S(1)}, bf16[5,64,2048]{2,1,0:T(8,128)(2,1)}, u32[]{:S(2)}) copy-start(bf16[5,64,2048]{2,1,0:T(8,128)(2,1)} %copy-done) | copy-start | bytes 3932164
  254.9 31.6 %collective-permute-start.5 = (bf16[320,1024]{1,0:T(8,128)(2,1)S(1)}, bf16[320,1024]{1,0:T(8,128)(2,1)S(1)}, u32[]{:S(2)}, u32[]{:S(2)}) collective-permute-start(bf16[320,1024]{1,0:T(8,128)(2,1)S(1)} %get-tuple-element.171), channel_id=1, source_target_pairs={{0,2},{2,0},{4,6},{6,4},{8,10},{10,8},{12,14},{14,12},{16,18},{18,... | collective-permute-start | bytes 1966088 | tf_op jit(solution)/shard_map/ppermute | solution.py:511
  256.6 29.8 %collective-permute-start.7 = (bf16[320,1024]{1,0:T(8,128)(2,1)S(1)}, bf16[320,1024]{1,0:T(8,128)(2,1)S(1)}, u32[]{:S(2)}, u32[]{:S(2)}) collective-permute-start(bf16[320,1024]{1,0:T(8,128)(2,1)S(1)} %get-tuple-element.173), channel_id=1, source_target_pairs={{0,2},{2,0},{4,6},{6,4},{8,10},{10,8},{12,14},{14,12},{16,18},{18,... | collective-permute-start | bytes 1966088 | tf_op jit(solution)/shard_map/ppermute | solution.py:511
  257.1 29.3 %collective-permute-start.8 = (bf16[320,1024]{1,0:T(8,128)(2,1)S(1)}, bf16[320,1024]{1,0:T(8,128)(2,1)S(1)}, u32[]{:S(2)}, u32[]{:S(2)}) collective-permute-start(bf16[320,1024]{1,0:T(8,128)(2,1)S(1)} %get-tuple-element.170), channel_id=1, source_target_pairs={{0,2},{2,0},{4,6},{6,4},{8,10},{10,8},{12,14},{14,12},{16,18},{18,... | collective-permute-start | bytes 1966088 | tf_op jit(solution)/shard_map/ppermute | solution.py:511
  286.4 2.1 collective-permute-start.6
  288.5 202.8 %copy-start.18 = (bf16[320,1024]{1,0:T(8,128)(2,1)}, bf16[320,1024]{1,0:T(8,128)(2,1)S(1)}, u32[]{:S(2)}) copy-start(bf16[320,1024]{1,0:T(8,128)(2,1)S(1)} %collective-permute-done.6.refs_1_) | copy-start | bytes 1966084
  323.2 8.2 %collective-permute-start.10 = (bf16[320,1536]{1,0:T(8,128)(2,1)S(1)}, bf16[320,1536]{1,0:T(8,128)(2,1)S(1)}, u32[]{:S(2)}, u32[]{:S(2)}) collective-permute-start(bf16[320,1536]{1,0:T(8,128)(2,1)S(1)} %get-tuple-element.174), channel_id=1, source_target_pairs={{0,2},{2,0},{4,6},{6,4},{8,10},{10,8},{12,14},{14,12},{16,18},{18,... | collective-permute-start | bytes 2949128 | tf_op jit(solution)/shard_map/ppermute | solution.py:511
  331.1 4.8 collective-permute-start.9
  335.7 36.6 %collective-permute-start.11 = (bf16[512,1536]{1,0:T(8,128)(2,1)S(1)}, bf16[512,1536]{1,0:T(8,128)(2,1)S(1)}, u32[]{:S(2)}, u32[]{:S(2)}) collective-permute-start(bf16[512,1536]{1,0:T(8,128)(2,1)S(1)} %get-tuple-element.189), channel_id=1, source_target_pairs={{0,4},{2,6},{4,0},{6,2},{8,12},{10,14},{12,8},{14,10},{16,20},{18,... | collective-permute-start | bytes 4718600 | tf_op jit(solution)/shard_map/ppermute | solution.py:511
  372.7 68.0 %copy-start.7 = (bf16[2,320,2816]{2,1,0:T(8,128)(2,1)}, bf16[2,320,2816]{2,1,0:T(8,128)(2,1)S(1)}, u32[]{:S(2)}) copy-start(bf16[2,320,2816]{2,1,0:T(8,128)(2,1)S(1)} %get-tuple-element.197.refs_2_) | copy-start | bytes 10813444
  372.7 6.4 collective-permute-start.14
  372.8 31.6 %collective-permute-start.13 = (bf16[512,1280]{1,0:T(8,128)(2,1)S(1)}, bf16[512,1280]{1,0:T(8,128)(2,1)S(1)}, u32[]{:S(2)}, u32[]{:S(2)}) collective-permute-start(bf16[512,1280]{1,0:T(8,128)(2,1)S(1)} %get-tuple-element.195), channel_id=1, source_target_pairs={{0,4},{2,6},{4,0},{6,2},{8,12},{10,14},{12,8},{14,10},{16,20},{18,... | collective-permute-start | bytes 3932168 | tf_op jit(solution)/shard_map/ppermute | solution.py:511
  373.2 31.6 %collective-permute-start.12 = (bf16[320,2048]{1,0:T(8,128)(2,1)S(1)}, bf16[320,2048]{1,0:T(8,128)(2,1)S(1)}, u32[]{:S(2)}, u32[]{:S(2)}) collective-permute-start(bf16[320,2048]{1,0:T(8,128)(2,1)S(1)} %get-tuple-element.193.refs_0_), channel_id=1, source_target_pairs={{0,1},{1,0},{2,3},{3,2},{4,5},{5,4},{6,7},{7,6},{8,9},{9,8},{10,11... | collective-permute-start | bytes 3932168 | tf_op jit(solution)/shard_map/ppermute | solution.py:514
  374.6 35.1 %collective-permute-start.15 = (bf16[256,1536]{1,0:T(8,128)(2,1)S(1)}, bf16[256,1536]{1,0:T(8,128)(2,1)S(1)}, u32[]{:S(2)}, u32[]{:S(2)}) collective-permute-start(bf16[256,1536]{1,0:T(8,128)(2,1)S(1)} %get-tuple-element.203), channel_id=1, source_target_pairs={{0,8},{2,10},{4,12},{6,14},{8,0},{10,2},{12,4},{14,6},{16,24},{18,... | collective-permute-start | bytes 2359304 | tf_op jit(solution)/shard_map/ppermute | solution.py:511
  379.1 61.6 %copy-start.32 = (bf16[2,320,2816]{2,1,0:T(8,128)(2,1)}, bf16[2,320,2816]{2,1,0:T(8,128)(2,1)S(1)}, u32[]{:S(2)}) copy-start(bf16[2,320,2816]{2,1,0:T(8,128)(2,1)S(1)} %collective-permute-done.14.refs_3_) | copy-start | bytes 10813444
  383.2 54.5 %collective-permute-start.18 = (bf16[512,1536]{1,0:T(8,128)(2,1)S(1)}, bf16[512,1536]{1,0:T(8,128)(2,1)S(1)}, u32[]{:S(2)}, u32[]{:S(2)}) collective-permute-start(bf16[512,1536]{1,0:T(8,128)(2,1)S(1)} %get-tuple-element.212), channel_id=1, source_target_pairs={{0,4},{2,6},{4,0},{6,2},{8,12},{10,14},{12,8},{14,10},{16,20},{18,... | collective-permute-start | bytes 4718600 | tf_op jit(solution)/shard_map/ppermute | solution.py:511
  409.6 4.3 collective-permute-start.16
  409.7 30.1 %collective-permute-start.17 = (bf16[256,1280]{1,0:T(8,128)(2,1)S(1)}, bf16[256,1280]{1,0:T(8,128)(2,1)S(1)}, u32[]{:S(2)}, u32[]{:S(2)}) collective-permute-start(bf16[256,1280]{1,0:T(8,128)(2,1)S(1)} %get-tuple-element.210), channel_id=1, source_target_pairs={{0,8},{2,10},{4,12},{6,14},{8,0},{10,2},{12,4},{14,6},{16,24},{18,... | collective-permute-start | bytes 1966088 | tf_op jit(solution)/shard_map/ppermute | solution.py:511
  413.9 12.6 %copy-start.43 = (bf16[320,1024]{1,0:T(8,128)(2,1)}, bf16[320,1024]{1,0:T(8,128)(2,1)S(1)}, u32[]{:S(2)}) copy-start(bf16[320,1024]{1,0:T(8,128)(2,1)S(1)} %collective-permute-done.16.refs_10_.refs_1_) | copy-start | bytes 1966084
  440.0 5.5 collective-permute-start.19
  446.6 31.7 %collective-permute-start.21 = (bf16[1280,512]{1,0:T(8,128)(2,1)S(1)}, bf16[1280,512]{1,0:T(8,128)(2,1)S(1)}, u32[]{:S(2)}, u32[]{:S(2)}) collective-permute-start(bf16[1280,512]{1,0:T(8,128)(2,1)S(1)} %get-tuple-element.223), channel_id=1, source_target_pairs={{0,4},{2,6},{4,0},{6,2},{8,12},{10,14},{12,8},{14,10},{16,20},{18,... | collective-permute-start | bytes 3932168 | tf_op jit(solution)/shard_map/ppermute | solution.py:511
  446.8 58.5 %collective-permute-start.24 = (bf16[512,1280]{1,0:T(8,128)(2,1)}, bf16[512,1280]{1,0:T(8,128)(2,1)}, u32[]{:S(2)}, u32[]{:S(2)}) collective-permute-start(bf16[512,1280]{1,0:T(8,128)(2,1)} %get-tuple-element.231), channel_id=1, source_target_pairs={{0,4},{2,6},{4,0},{6,2},{8,12},{10,14},{12,8},{14,10},{16,20},{18,... | collective-permute-start | bytes 3932168 | tf_op jit(solution)/shard_map/ppermute | solution.py:511
  448.7 19.7 %collective-permute-start.22 = (bf16[128,1536]{1,0:T(8,128)(2,1)S(1)}, bf16[128,1536]{1,0:T(8,128)(2,1)S(1)}, u32[]{:S(2)}, u32[]{:S(2)}) collective-permute-start(bf16[128,1536]{1,0:T(8,128)(2,1)S(1)} %get-tuple-element.225), channel_id=1, source_target_pairs={{0,16},{2,18},{4,20},{6,22},{8,24},{10,26},{12,28},{14,30},{16,0},... | collective-permute-start | bytes 1179656 | tf_op jit(solution)/shard_map/ppermute | solution.py:511
  448.8 39.3 %collective-permute-start.25 = (bf16[256,1536]{1,0:T(8,128)(2,1)}, bf16[256,1536]{1,0:T(8,128)(2,1)}, u32[]{:S(2)}, u32[]{:S(2)}) collective-permute-start(bf16[256,1536]{1,0:T(8,128)(2,1)} %get-tuple-element.233), channel_id=1, source_target_pairs={{0,8},{2,10},{4,12},{6,14},{8,0},{10,2},{12,4},{14,6},{16,24},{18,... | collective-permute-start | bytes 2359304 | tf_op jit(solution)/shard_map/ppermute | solution.py:511
  461.0 18.2 %copy-start.12 = (bf16[320,2048]{1,0:T(8,128)(2,1)}, bf16[320,2048]{1,0:T(8,128)(2,1)S(1)}, u32[]{:S(2)}) copy-start(bf16[320,2048]{1,0:T(8,128)(2,1)S(1)} %get-tuple-element.220) | copy-start | bytes 3932164
  480.1 26.8 %collective-permute-start.23 = (bf16[640,512]{1,0:T(8,128)(2,1)}, bf16[640,512]{1,0:T(8,128)(2,1)}, u32[]{:S(2)}, u32[]{:S(2)}) collective-permute-start(bf16[640,512]{1,0:T(8,128)(2,1)} %get-tuple-element.229), channel_id=1, source_target_pairs={{0,8},{2,10},{4,12},{6,14},{8,0},{10,2},{12,4},{14,6},{16,24},{18,... | collective-permute-start | bytes 1966088 | tf_op jit(solution)/shard_map/ppermute | solution.py:511
  483.5 28.3 %collective-permute-start.27 = (bf16[128,1280]{1,0:T(8,128)(2,1)}, bf16[128,1280]{1,0:T(8,128)(2,1)S(1)}, u32[]{:S(2)}, u32[]{:S(2)}) collective-permute-start(bf16[128,1280]{1,0:T(8,128)(2,1)} %copy-done.45), channel_id=1, source_target_pairs={{0,16},{2,18},{4,20},{6,22},{8,24},{10,26},{12,28},{14,30},{16,0},... | collective-permute-start | bytes 983048 | tf_op jit(solution)/shard_map/ppermute | solution.py:511
  486.6 41.3 %collective-permute-start.20 = (bf16[320,2048]{1,0:T(8,128)(2,1)}, bf16[320,2048]{1,0:T(8,128)(2,1)S(1)}, u32[]{:S(2)}, u32[]{:S(2)}) collective-permute-start(bf16[320,2048]{1,0:T(8,128)(2,1)} %copy-done.12), channel_id=1, source_target_pairs={{0,1},{1,0},{2,3},{3,2},{4,5},{5,4},{6,7},{7,6},{8,9},{9,8},{10,11... | collective-permute-start | bytes 3932168 | tf_op jit(solution)/shard_map/ppermute | solution.py:514
  508.3 16.7 %collective-permute-start.26 = (bf16[320,512]{1,0:T(8,128)(2,1)S(1)}, bf16[320,512]{1,0:T(8,128)(2,1)S(1)}, u32[]{:S(2)}, u32[]{:S(2)}) collective-permute-start(bf16[320,512]{1,0:T(8,128)(2,1)S(1)} %get-tuple-element.239), channel_id=1, source_target_pairs={{0,16},{2,18},{4,20},{6,22},{8,24},{10,26},{12,28},{14,30},{16,0},... | collective-permute-start | bytes 983048 | tf_op jit(solution)/shard_map/ppermute | solution.py:511
  508.4 33.7 %collective-permute-start.29 = (bf16[256,1280]{1,0:T(8,128)(2,1)S(1)}, bf16[256,1280]{1,0:T(8,128)(2,1)S(1)}, u32[]{:S(2)}, u32[]{:S(2)}) collective-permute-start(bf16[256,1280]{1,0:T(8,128)(2,1)S(1)} %get-tuple-element.249), channel_id=1, source_target_pairs={{0,8},{2,10},{4,12},{6,14},{8,0},{10,2},{12,4},{14,6},{16,24},{18,... | collective-permute-start | bytes 1966088 | tf_op jit(solution)/shard_map/ppermute | solution.py:511
  511.5 48.4 %collective-permute-start.34 = (bf16[512,1536]{1,0:T(8,128)(2,1)}, bf16[512,1536]{1,0:T(8,128)(2,1)S(1)}, u32[]{:S(2)}, u32[]{:S(2)}) collective-permute-start(bf16[512,1536]{1,0:T(8,128)(2,1)} %get-tuple-element.264), channel_id=1, source_target_pairs={{0,4},{2,6},{4,0},{6,2},{8,12},{10,14},{12,8},{14,10},{16,20},{18,... | collective-permute-start | bytes 4718600 | tf_op jit(solution)/shard_map/ppermute | solution.py:511
  511.8 67.6 %collective-permute-start.32 = (bf16[128,1536]{1,0:T(8,128)(2,1)}, bf16[128,1536]{1,0:T(8,128)(2,1)}, u32[]{:S(2)}, u32[]{:S(2)}) collective-permute-start(bf16[128,1536]{1,0:T(8,128)(2,1)} %get-tuple-element.260), channel_id=1, source_target_pairs={{0,16},{2,18},{4,20},{6,22},{8,24},{10,26},{12,28},{14,30},{16,0},... | collective-permute-start | bytes 1179656 | tf_op jit(solution)/shard_map/ppermute | solution.py:511
  527.8 15.1 %collective-permute-start.28 = (bf16[320,1536]{1,0:T(8,128)(2,1)S(1)}, bf16[320,1536]{1,0:T(8,128)(2,1)S(1)}, u32[]{:S(2)}, u32[]{:S(2)}) collective-permute-start(bf16[320,1536]{1,0:T(8,128)(2,1)S(1)} %get-tuple-element.365.refs_0_), channel_id=1, source_target_pairs={{0,2},{2,0},{4,6},{6,4},{8,10},{10,8},{12,14},{14,12},{16,18},{18,... | collective-permute-start | bytes 2949128 | tf_op jit(solution)/shard_map/ppermute | solution.py:511
  535.1 12.7 %copy-start.52 = (bf16[512,1024]{1,0:T(8,128)(2,1)}, bf16[512,1024]{1,0:T(8,128)(2,1)S(1)}, u32[]{:S(2)}) copy-start(bf16[512,1024]{1,0:T(8,128)(2,1)S(1)} %get-tuple-element.261.refs_0_) | copy-start | bytes 3145732
  535.1 34.9 %collective-permute-start.33 = (bf16[512,1024]{1,0:T(8,128)(2,1)}, bf16[512,1024]{1,0:T(8,128)(2,1)}, u32[]{:S(2)}, u32[]{:S(2)}) collective-permute-start(bf16[512,1024]{1,0:T(8,128)(2,1)} %get-tuple-element.262), channel_id=1, source_target_pairs={{0,8},{2,10},{4,12},{6,14},{8,0},{10,2},{12,4},{14,6},{16,24},{18,... | collective-permute-start | bytes 3145736 | tf_op jit(solution)/shard_map/ppermute | solution.py:511
  547.7 35.5 %collective-permute-start.31 = (bf16[512,1536]{1,0:T(8,128)(2,1)}, bf16[512,1536]{1,0:T(8,128)(2,1)S(1)}, u32[]{:S(2)}, u32[]{:S(2)}) collective-permute-start(bf16[512,1536]{1,0:T(8,128)(2,1)} %get-tuple-element.258), channel_id=1, source_target_pairs={{0,4},{2,6},{4,0},{6,2},{8,12},{10,14},{12,8},{14,10},{16,20},{18,... | collective-permute-start | bytes 4718600 | tf_op jit(solution)/shard_map/ppermute | solution.py:511
  556.2 30.9 %collective-permute-start.30 = (bf16[320,2048]{1,0:T(8,128)(2,1)}, bf16[320,2048]{1,0:T(8,128)(2,1)}, u32[]{:S(2)}, u32[]{:S(2)}) collective-permute-start(bf16[320,2048]{1,0:T(8,128)(2,1)} %get-tuple-element.255.refs_0_), channel_id=1, source_target_pairs={{0,1},{1,0},{2,3},{3,2},{4,5},{5,4},{6,7},{7,6},{8,9},{9,8},{10,11... | collective-permute-start | bytes 3932168 | tf_op jit(solution)/shard_map/ppermute | solution.py:514
  562.0 32.7 %collective-permute-start.37 = (bf16[256,1536]{1,0:T(8,128)(2,1)}, bf16[256,1536]{1,0:T(8,128)(2,1)}, u32[]{:S(2)}, u32[]{:S(2)}) collective-permute-start(bf16[256,1536]{1,0:T(8,128)(2,1)} %get-tuple-element.277), channel_id=1, source_target_pairs={{0,8},{2,10},{4,12},{6,14},{8,0},{10,2},{12,4},{14,6},{16,24},{18,... | collective-permute-start | bytes 2359304 | tf_op jit(solution)/shard_map/ppermute | solution.py:511
  573.1 34.0 %collective-permute-start.36 = (bf16[256,1024]{1,0:T(8,128)(2,1)}, bf16[256,1024]{1,0:T(8,128)(2,1)}, u32[]{:S(2)}, u32[]{:S(2)}) collective-permute-start(bf16[256,1024]{1,0:T(8,128)(2,1)} %get-tuple-element.275), channel_id=1, source_target_pairs={{0,16},{2,18},{4,20},{6,22},{8,24},{10,26},{12,28},{14,30},{16,0},... | collective-permute-start | bytes 1572872 | tf_op jit(solution)/shard_map/ppermute | solution.py:511
  579.4 33.7 %collective-permute-start.42 = (bf16[128,1280]{1,0:T(8,128)(2,1)}, bf16[128,1280]{1,0:T(8,128)(2,1)}, u32[]{:S(2)}, u32[]{:S(2)}) collective-permute-start(bf16[128,1280]{1,0:T(8,128)(2,1)} %get-tuple-element.289), channel_id=1, source_target_pairs={{0,16},{2,18},{4,20},{6,22},{8,24},{10,26},{12,28},{14,30},{16,0},... | collective-permute-start | bytes 983048 | tf_op jit(solution)/shard_map/ppermute | solution.py:511
  583.2 52.4 %collective-permute-start.39 = (bf16[512,1280]{1,0:T(8,128)(2,1)}, bf16[512,1280]{1,0:T(8,128)(2,1)}, u32[]{:S(2)}, u32[]{:S(2)}) collective-permute-start(bf16[512,1280]{1,0:T(8,128)(2,1)} %get-tuple-element.283), channel_id=1, source_target_pairs={{0,4},{2,6},{4,0},{6,2},{8,12},{10,14},{12,8},{14,10},{16,20},{18,... | collective-permute-start | bytes 3932168 | tf_op jit(solution)/shard_map/ppermute | solution.py:511
  587.1 34.6 %collective-permute-start.41 = (bf16[256,1536]{1,0:T(8,128)(2,1)}, bf16[256,1536]{1,0:T(8,128)(2,1)}, u32[]{:S(2)}, u32[]{:S(2)}) collective-permute-start(bf16[256,1536]{1,0:T(8,128)(2,1)} %get-tuple-element.287), channel_id=1, source_target_pairs={{0,8},{2,10},{4,12},{6,14},{8,0},{10,2},{12,4},{14,6},{16,24},{18,... | collective-permute-start | bytes 2359304 | tf_op jit(solution)/shard_map/ppermute | solution.py:511
  594.7 14.5 %copy-start.82 = (f32[6,64,2048]{2,1,0:T(8,128)S(1)}, f32[6,64,2048]{2,1,0:T(8,128)}, u32[]{:S(2)}) copy-start(f32[6,64,2048]{2,1,0:T(8,128)} %convert_element_type.98) | copy-start | bytes 9437188
  597.6 37.9 %collective-permute-start.40 = (bf16[128,1536]{1,0:T(8,128)(2,1)}, bf16[128,1536]{1,0:T(8,128)(2,1)S(1)}, u32[]{:S(2)}, u32[]{:S(2)}) collective-permute-start(bf16[128,1536]{1,0:T(8,128)(2,1)} %get-tuple-element.285), channel_id=1, source_target_pairs={{0,16},{2,18},{4,20},{6,22},{8,24},{10,26},{12,28},{14,30},{16,0},... | collective-permute-start | bytes 1179656 | tf_op jit(solution)/shard_map/ppermute | solution.py:511
  609.0 29.6 %collective-permute-start.38 = (bf16[128,1024]{1,0:T(8,128)(2,1)S(1)}, bf16[128,1024]{1,0:T(8,128)(2,1)}, u32[]{:S(2)}, u32[]{:S(2)}) collective-permute-start(bf16[128,1024]{1,0:T(8,128)(2,1)S(1)} %get-tuple-element.281), channel_id=1, source_target_pairs={{0,4},{2,6},{4,0},{6,2},{8,12},{10,14},{12,8},{14,10},{16,20},{18,... | collective-permute-start | bytes 786440 | tf_op jit(solution)/shard_map/ppermute | solution.py:511
  613.1 26.5 %collective-permute-start.35 = (f32[8,256]{1,0:T(8,128)S(1)}, f32[8,256]{1,0:T(8,128)S(1)}, u32[]{:S(2)}, u32[]{:S(2)}) collective-permute-start(f32[8,256]{1,0:T(8,128)S(1)} %bitcast.79), channel_id=1, source_target_pairs={{0,2},{2,0},{4,6},{6,4},{8,10},{10,8},{12,14},{14,12},{16,18},{18,... | collective-permute-start | bytes 24584 | tf_op jit(solution)/shard_map/ppermute | solution.py:511
  616.3 19.2 %copy-start.69 = (bf16[128,1536]{1,0:T(8,128)(2,1)S(1)}, bf16[128,1536]{1,0:T(8,128)(2,1)}, u32[]{:S(2)}) copy-start(bf16[128,1536]{1,0:T(8,128)(2,1)} %copy-done.68) | copy-start | bytes 1179652
  623.0 19.1 %collective-permute-start.44 = (bf16[128,1536]{1,0:T(8,128)(2,1)S(1)}, bf16[128,1536]{1,0:T(8,128)(2,1)S(1)}, u32[]{:S(2)}, u32[]{:S(2)}) collective-permute-start(bf16[128,1536]{1,0:T(8,128)(2,1)S(1)} %get-tuple-element.299), channel_id=1, source_target_pairs={{0,16},{2,18},{4,20},{6,22},{8,24},{10,26},{12,28},{14,30},{16,0},... | collective-permute-start | bytes 1179656 | tf_op jit(solution)/shard_map/ppermute | solution.py:511
  637.3 13.4 %collective-permute-start.46 = (bf16[256,1280]{1,0:T(8,128)(2,1)S(1)}, bf16[256,1280]{1,0:T(8,128)(2,1)S(1)}, u32[]{:S(2)}, u32[]{:S(2)}) collective-permute-start(bf16[256,1280]{1,0:T(8,128)(2,1)S(1)} %get-tuple-element.305), channel_id=1, source_target_pairs={{0,8},{2,10},{4,12},{6,14},{8,0},{10,2},{12,4},{14,6},{16,24},{18,... | collective-permute-start | bytes 1966088 | tf_op jit(solution)/shard_map/ppermute | solution.py:511
  639.6 3.7 collective-permute-start.43
  650.8 10.5 %collective-permute-start.48 = (bf16[128,1280]{1,0:T(8,128)(2,1)S(1)}, bf16[128,1280]{1,0:T(8,128)(2,1)S(1)}, u32[]{:S(2)}, u32[]{:S(2)}) collective-permute-start(bf16[128,1280]{1,0:T(8,128)(2,1)S(1)} %get-tuple-element.311), channel_id=1, source_target_pairs={{0,16},{2,18},{4,20},{6,22},{8,24},{10,26},{12,28},{14,30},{16,0},... | collective-permute-start | bytes 983048 | tf_op jit(solution)/shard_map/ppermute | solution.py:511
  653.8 3.9 collective-permute-start.45
  657.7 4.5 collective-permute-start.47
  (82 other events, 304.7 us)
Sparse Core Ops, SparseCore 0:
  13.0 93.7 all-gather.2
  108.4 204.8 all-gather.4

commit v4 on v3

--- a/solution.py
+++ b/solution.py
@@ -22,10 +22,10 @@
 
 FAR_FIRST = ("o",)
 ORDER = (
-    "fA", "fB", "PdA", "PdB", "F", "SdA", "H", "PgA", "SdB", "N", "SdA", "M", "A", "SgA", "SdB",
-    "K", "PgB", "Sk", "V", "SdA", "SdA", "Sk", "SgA", "PuA", "SgB", "Sk", "SdB", "Sk", "R",
-    "Po", "SgB", "Pq", "T", "SuA", "PuB", "So", "SgA", "Sq", "I", "SuA", "So", "SgB", "Sq",
-    "SuA", "SuB", "So", "Sn", "Sq", "Sn", "SuB", "Sn", "SuB", "Sn",
+    "fA", "fB", "PdA", "PdB", "F", "SdA", "H", "PgA", "SdA", "SdB", "N", "M", "PgB", "A", "SdB",
+    "SgA", "K", "Sk", "Sk", "V", "SdA", "PuA", "SgA", "SdA", "Sk", "SgB", "SdB", "Sk", "Po",
+    "R", "SgB", "Pq", "T", "SuA", "PuB", "So", "SgA", "Sq", "I", "So", "SuA", "SuB", "Sq",
+    "SgB", "SuA", "Sn", "SuB", "So", "Sq", "Sn", "Sn", "SuB", "Sn",
 )
 
 bf16 = jnp.bfloat16
@@ -40,7 +40,7 @@
     return lax.dot_general(a, b, (((ca,), (cb,)), ((), ())), preferred_element_type=f32)
 
 
-def params(room=16 * MIB):
+def params(room=20 * MIB):
     return pltpu.CompilerParams(vmem_limit_bytes=min(room, 56 * MIB))
 
 
@@ -50,7 +50,7 @@
 
 def call(
     kernel, token, args, in_specs, outs, out_specs, name, takes, grid=(), scratch=(), others=(), aliases=None,
-    room=16 * MIB,
+    room=20 * MIB,
 ):
     waits = [*([] if token is None else [token]), *others]
     unread = pl.BlockSpec(memory_space=pl.ANY)
@@ -422,7 +422,7 @@
     outs = [like(rows, width, dtype=f32)] if last else [like(rows // 2, width, dtype=kept.dtype)] * 2
     return call(
         fold_kernel, token, (kept, received), [whole] * 2, outs, [whole] * len(outs), "fold", 1.5,
-        room=max(16 * MIB, 4 * MIB + 4 * kept.size * kept.dtype.itemsize),
+        room=max(20 * MIB, 4 * MIB + 4 * kept.size * kept.dtype.itemsize),
     )
 
 

time: 682 us -> 688 us (level)
    unnamed x202 -> x210, local copies, waits for them, and re-layouts: 41.1 us -> 36.1 us
  transfers between devices with their start and end apart: 51 -> 51, of which waited for: 26 -> 25; matrix products, arithmetic and copies ran while one was open for 7% -> 8% of each run, Pallas kernels for 22% -> 22%
where the time goes in v4:
time: 688 us; the launch traced here: 677 us
  waiting for transfers between devices  376 us (55%)
  Pallas kernels  159 us (23%)
  local copies, waits for them, and re-layouts  41 us (6%)
  starting transfers between devices  37.4 us (5%)
  other arithmetic  31.9 us (5%)
  between operations  19 us (3%)
  matrix products  13.4 us (2%)
    ppermute x45, waiting for transfers between devices, flip(): return lax.ppermute(v, 'dp', [(i, i ^ bits) for i in range(n_dp)])  245 us
    pallas_call x54, Pallas kernels, call(): pl.pallas_call(body, grid=grid, in_specs=[*in_specs, *[unread] * len(wait...  147 us
    all_gather x1, waiting for transfers between devices, local(): lax.all_gather(jnp.concatenate([query_weight, key_weight, value_weight, o...  81.9 us
    unnamed x210, local copies, waits for them, and re-layouts  36.1 us
    ppermute x45, starting transfers between devices, flip(): return lax.ppermute(v, 'dp', [(i, i ^ bits) for i in range(n_dp)])  32.3 us
    ppermute x4, waiting for transfers between devices, tensor_flip(): return lax.ppermute(v, 'tensor', [(0, 1), (1, 0)])  26.8 us
    all_gather x1, waiting for transfers between devices, local(): lax.all_gather(jnp.concatenate([gate_weight, up_weight, down_weight.T], a...  21.7 us
  transfers between devices with their start and end apart: 51, of which 25 were waited for; matrix products, arithmetic and copies ran while one was open for 8% of the time, Pallas kernels for 22%

profile of v4, /device:TPU:0, one launch (start us, length us, event | category | flops | bytes accessed | tf_op | source)
XLA Modules:
  0.0 677.3 jit_solution(1933975836962199009)
XLA Ops:
  13.2 2.6 pad_maximum_fusion.2
  21.6 2.4 slice_select_fusion.1
  24.9 81.9 %all-gather.3.cloned.1.call-done.refs_1_ = bf16[2048,2688]{1,0:T(8,128)(2,1)} async-done(((bf16[128,2688]{1,0:T(8,128)(2,1)}), bf16[2048,2688]{1,0:T(8,128)(2,1)}) %all-gather.3.cloned.1.call-update) | async-done | bytes 11010064 | tf_op jit(solution)/shard_map/all_gather | solution.py:540
  106.8 1.8 convert_reduce_fusion
  109.6 5.4 fusion.refs_0_
  117.5 23.5 %collective-permute-done = bf16[1,5,64,512]{3,2,1,0:T(8,128)(2,1)S(1)} collective-permute-done((bf16[1,5,64,512]{3,2,1,0:T(8,128)(2,1)S(1)}, bf16[1,5,64,512]{3,2,1,0:T(8,128)(2,1)S(1)}, u32[]{:S(2)}, u32[]{:S(2)}) %collective-permute-start) | collective-permute-done | bytes 327712 | tf_op jit(solution)/shard_map/ppermute | solution.py:511
  141.1 31.2 %collective-permute-done.1 = bf16[2,5,64,512]{3,2,1,0:T(8,128)(2,1)S(1)} collective-permute-done((bf16[2,5,64,512]{3,2,1,0:T(8,128)(2,1)S(1)}, bf16[2,5,64,512]{3,2,1,0:T(8,128)(2,1)S(1)}, u32[]{:S(2)}, u32[]{:S(2)}) %collective-permute-start.1) | collective-permute-done | bytes 655392 | tf_op jit(solution)/shard_map/ppermute | solution.py:511
  173.1 58.4 %collective-permute-done.2 = bf16[4,5,64,512]{3,2,1,0:T(8,128)(2,1)S(1)} collective-permute-done((bf16[4,5,64,512]{3,2,1,0:T(8,128)(2,1)S(1)}, bf16[4,5,64,512]{3,2,1,0:T(8,128)(2,1)S(1)}, u32[]{:S(2)}, u32[]{:S(2)}) %collective-permute-start.2) | collective-permute-done | bytes 1310752 | tf_op jit(solution)/shard_map/ppermute | solution.py:511
  233.4 4.9 collective-permute-done.3.far_ref.refs_2_
  238.3 8.6 %attend.1 = (bf16[320,1024]{1,0:T(8,128)(2,1)S(1)}, f32[10,256,1]{2,1,0:T(8,128)S(1)}) custom-call(bf16[320,1024]{1,0:T(8,128)(2,1)S(1)} %get-tuple-element.168.q_ref.refs_0_, bf16[8,5,64,512]{3,2,1,0:T(8,128)(2,1)} %pad_maximum_fusion.1.near_ref.refs_1_, bf16[8,5,64,512]{3,2,1,0:T(8,128)(2,1)} %collective-permute-done.3.far_ref.refs_2_, ...), custom_call_target="tpu_custom_call" | custom-call | flops 4499999744 | bytes 16200000 | tf_op jit(solution)/shard_map/attend/pallas_call | solution.py:149
  248.1 4.2 fusion.6
  257.9 25.1 %collective-permute-done.4 = bf16[320,2048]{1,0:T(8,128)(2,1)S(1)} collective-permute-done((bf16[320,2048]{1,0:T(8,128)(2,1)S(1)}, bf16[320,2048]{1,0:T(8,128)(2,1)S(1)}, u32[]{:S(2)}, u32[]{:S(2)}) %collective-permute-start.4) | collective-permute-done | bytes 1310752 | tf_op jit(solution)/shard_map/ppermute | solution.py:514
  287.0 2.1 collective-permute-done.6.refs_1_
  291.6 21.7 %all-gather.5.cloned.1.call-done.refs_1_.refs_2_.refs_3_.refs_4_.refs_5_ = bf16[2048,8448]{1,0:T(8,128)(2,1)} async-done(((bf16[128,8448]{1,0:T(8,128)(2,1)}), bf16[2048,8448]{1,0:T(8,128)(2,1)}) %all-gather.5.cloned.1.call-update) | async-done | bytes 34603024 | tf_op jit(solution)/shard_map/all_gather | solution.py:544
  314.6 8.6 %feed_forward.2 = (f32[320,2816]{1,0:T(8,128)S(1)}, f32[320,2816]{1,0:T(8,128)S(1)}, bf16[320,1536]{1,0:T(8,128)(2,1)S(1)}, f32[8,128]{1,0:T(8,128)S(1)}) custom-call(bf16[320,2048]{1,0:T(8,128)(2,1)S(1)} %copy-done.4, bf16[2048,8448]{1,0:T(8,128)(2,1)} %all-gather.5.cloned.1.call-done.refs_1_.refs_2_.refs_3_.refs_4_.refs_5_, ...), custom_call_target="tpu_custom_call" | custom-call | flops 4636363776 | bytes 16690909 | tf_op jit(solution)/shard_map/feed_forward/pallas_call | solution.py:63
  323.6 7.6 %feed_forward.3 = (f32[320,2816]{1,0:T(8,128)S(1)}, f32[320,2816]{1,0:T(8,128)S(1)}, bf16[320,1280]{1,0:T(8,128)(2,1)S(1)}, f32[8,128]{1,0:T(8,128)S(1)}) custom-call(bf16[320,2048]{1,0:T(8,128)(2,1)S(1)} %copy-done.4, ...), custom_call_target="tpu_custom_call", output_to_operand_aliasing={{0}: (3, {}), {1}: (4, {})} | custom-call | flops 3863636480 | bytes 13909090 | tf_op jit(solution)/shard_map/feed_forward/pallas_call | solution.py:63
  331.5 4.2 side_products.8
  335.9 2.9 side_products.9
  338.8 27.0 %feed_forward_back.1 = (bf16[2,320,2816]{2,1,0:T(8,128)(2,1)S(1)}, bf16[320,2048]{1,0:T(8,128)(2,1)S(1)}, f32[8,128]{1,0:T(8,128)S(1)}) custom-call(bf16[320,2048]{1,0:T(8,128)(2,1)S(1)} %bitcast.55, f32[320,2816]{1,0:T(8,128)S(1)} %get-tuple-element.180.refs_1_, f32[320,2816]{1,0:T(8,128)S(1)} %get-tuple-element.181.refs_2_, ...), custom_call_target="tpu_custom_call" | custom-call | flops 14000000000 | bytes 50400000 | tf_op jit(solution)/shard_map/feed_forward_back/pallas_call | solution.py:63
  365.8 6.5 collective-permute-done.11.refs_1_
  374.6 4.5 collective-permute-done.15.refs_3_
  379.1 4.1 side_products.10
  383.6 10.3 %collective-permute-done.14.refs_1_ = bf16[256,1536]{1,0:T(8,128)(2,1)S(1)} collective-permute-done((bf16[256,1536]{1,0:T(8,128)(2,1)S(1)}, bf16[256,1536]{1,0:T(8,128)(2,1)S(1)}, u32[]{:S(2)}, u32[]{:S(2)}) %collective-permute-start.14) | collective-permute-done | bytes 786464 | tf_op jit(solution)/shard_map/ppermute | solution.py:511
  394.8 9.6 %collective-permute-done.13.refs_1_ = bf16[512,1280]{1,0:T(8,128)(2,1)S(1)} collective-permute-done((bf16[512,1280]{1,0:T(8,128)(2,1)S(1)}, bf16[512,1280]{1,0:T(8,128)(2,1)S(1)}, u32[]{:S(2)}, u32[]{:S(2)}) %collective-permute-start.13) | collective-permute-done | bytes 1310752 | tf_op jit(solution)/shard_map/ppermute | solution.py:511
  404.7 2.4 norm_back.2
  410.4 3.7 fusion.12.refs_6_
  414.2 4.8 side_products.11
  420.1 12.7 %attend_back.1 = (bf16[320,1024]{1,0:T(8,128)(2,1)S(1)}, bf16[8,5,64,512]{3,2,1,0:T(8,128)(2,1)S(1)}, bf16[8,5,64,512]{3,2,1,0:T(8,128)(2,1)S(1)}, f32[8,128]{1,0:T(8,128)S(1)}) custom-call(bf16[320,1024]{1,0:T(8,128)(2,1)S(1)} %copy-done.72, bf16[8,5,64,512]{3,2,1,0:T(8,128)(2,1)} %pad_maximum_fusion.1.near_ref.refs_1_, ...), custom_call_target="tpu_custom_call" | custom-call | flops 6499999744 | bytes 23400000 | tf_op jit(solution)/shard_map/attend_back/pallas_call | solution.py:63
  434.5 3.2 collective-permute-done.17.refs_1_
  439.7 4.9 collective-permute-done.19.refs_1_
  447.6 2.8 collective-permute-start.26
  450.7 26.2 %collective-permute-done.20.refs_1_ = bf16[1280,512]{1,0:T(8,128)(2,1)S(1)} collective-permute-done((bf16[1280,512]{1,0:T(8,128)(2,1)S(1)}, bf16[1280,512]{1,0:T(8,128)(2,1)S(1)}, u32[]{:S(2)}, u32[]{:S(2)}) %collective-permute-start.20) | collective-permute-done | bytes 1310752 | tf_op jit(solution)/shard_map/ppermute | solution.py:511
  478.0 9.4 %times_turned.2 = (bf16[320,2048]{1,0:T(8,128)(2,1)S(1)}, f32[8,128]{1,0:T(8,128)S(1)}) custom-call(bf16[320,2816]{1,0:T(8,128)(2,1)S(1)} %pad_maximum_fusion.3.refs_0_, bf16[2048,8448]{1,0:T(8,128)(2,1)} %all-gather.5.cloned.1.call-done.refs_1_.refs_2_.refs_3_.refs_4_.refs_5_, f32[8,128]{1,0:T(8,128)S(1)} %get-tuple-element.222.refs_2_), custom_call_target="tpu_custom_call" | custom-call | flops 4499999744 | bytes 16200000 | tf_op jit(solution)/shard_map/times_turned/pallas_call | solution.py:63
  489.2 2.0 copy-done.30
  491.2 4.1 side_products.12
  495.4 2.0 fold.40
  499.0 2.0 fold.41
  501.7 2.9 collective-permute-start.25
  504.6 2.0 convert_element_type.98
  511.2 2.3 fold.42
  513.5 1.9 collective-permute-start.29
  516.4 11.4 %collective-permute-done.25.refs_1_ = bf16[320,512]{1,0:T(8,128)(2,1)} collective-permute-done((bf16[320,512]{1,0:T(8,128)(2,1)}, bf16[320,512]{1,0:T(8,128)(2,1)}, u32[]{:S(2)}, u32[]{:S(2)}) %collective-permute-start.25) | collective-permute-done | bytes 327712 | tf_op jit(solution)/shard_map/ppermute | solution.py:511
  530.6 2.4 side_products.13
  533.0 2.2 rope.3
  537.8 3.0 copy.55
  542.5 1.9 fold.45
  545.2 2.1 add_convert_fusion
  547.3 6.2 side_products.14
  555.1 8.8 %times_turned.3 = (bf16[320,2048]{1,0:T(8,128)(2,1)}, f32[8,128]{1,0:T(8,128)S(1)}) custom-call(bf16[320,1536]{1,0:T(8,128)(2,1)} %get-tuple-element.365.refs_0_, bf16[2048,2688]{1,0:T(8,128)(2,1)} %all-gather.3.cloned.1.call-done.refs_1_, f32[8,128]{1,0:T(8,128)S(1)} %get-tuple-element.254.refs_2_), custom_call_target="tpu_custom_call" | custom-call | flops 4499999744 | bytes 16200000 | tf_op jit(solution)/shard_map/times_turned/pallas_call | solution.py:63
  566.0 2.3 fold.46
  568.3 2.1 collective-permute-start.36
  570.4 4.2 side_products.15
  578.5 1.8 collective-permute-start.39
  581.6 7.3 %collective-permute-done.31.refs_1_ = bf16[512,1536]{1,0:T(8,128)(2,1)S(1)} collective-permute-done((bf16[512,1536]{1,0:T(8,128)(2,1)}, bf16[512,1536]{1,0:T(8,128)(2,1)S(1)}, u32[]{:S(2)}, u32[]{:S(2)}) %collective-permute-start.31) | collective-permute-done | bytes 1572896 | tf_op jit(solution)/shard_map/ppermute | solution.py:511
  593.7 5.2 norm_back.3
  599.0 11.3 %collective-permute-done.37.refs_1_ = bf16[256,1024]{1,0:T(8,128)(2,1)S(1)} collective-permute-done((bf16[256,1024]{1,0:T(8,128)(2,1)S(1)}, bf16[256,1024]{1,0:T(8,128)(2,1)S(1)}, u32[]{:S(2)}, u32[]{:S(2)}) %collective-permute-start.37) | collective-permute-done | bytes 524320 | tf_op jit(solution)/shard_map/ppermute | solution.py:511
  613.3 2.1 slice_select_fusion
  615.4 2.2 collective-permute-done.41.refs_1_
  620.7 4.0 pad_maximum_fusion
  624.7 7.8 %collective-permute-done.40.refs_1_ = bf16[256,1536]{1,0:T(8,128)(2,1)} collective-permute-done((bf16[256,1536]{1,0:T(8,128)(2,1)}, bf16[256,1536]{1,0:T(8,128)(2,1)}, u32[]{:S(2)}, u32[]{:S(2)}) %collective-permute-start.40) | collective-permute-done | bytes 786464 | tf_op jit(solution)/shard_map/ppermute | solution.py:511
  632.9 2.0 fold.53
  638.4 13.4 %collective-permute-done.45.refs_1_ = bf16[256,1280]{1,0:T(8,128)(2,1)} collective-permute-done((bf16[256,1280]{1,0:T(8,128)(2,1)}, bf16[256,1280]{1,0:T(8,128)(2,1)}, u32[]{:S(2)}, u32[]{:S(2)}) %collective-permute-start.45) | collective-permute-done | bytes 655392 | tf_op jit(solution)/shard_map/ppermute | solution.py:511
  657.8 2.5 collective-permute-start.46
  663.7 4.5 collective-permute-done.48.refs_1_
  (366 shorter events, 98.7 us)
Async XLA Ops:
  7.2 99.6 %all-gather.3.cloned.1.call-start = ((), (), s32[]{:S(2)}) async-start(), calls=%async_computation | async-start | bytes 11698176 | tf_op jit(solution)/shard_map/all_gather | solution.py:540
  12.9 300.4 %all-gather.5.cloned.1.call-start = ((), (), s32[]{:S(2)}) async-start(), calls=%async_computation.1 | async-start | bytes 36765696 | tf_op jit(solution)/shard_map/all_gather | solution.py:544
  24.1 84.9 %copy-start = (bf16[5,64,2048]{2,1,0:T(8,128)(2,1)}, bf16[5,64,2048]{2,1,0:T(8,128)(2,1)S(1)}, u32[]{:S(2)}) copy-start(bf16[5,64,2048]{2,1,0:T(8,128)(2,1)S(1)} %get-tuple-element.376) | copy-start | bytes 3932164
  24.1 229.7 %copy-start.5 = (bf16[5,64,2048]{2,1,0:T(8,128)(2,1)}, bf16[5,64,2048]{2,1,0:T(8,128)(2,1)S(1)}, u32[]{:S(2)}) copy-start(bf16[5,64,2048]{2,1,0:T(8,128)(2,1)S(1)} %get-tuple-element.375) | copy-start | bytes 3932164
  115.9 122.4 %copy-start.71 = (bf16[320,1024]{1,0:T(8,128)(2,1)}, bf16[320,1024]{1,0:T(8,128)(2,1)S(1)}, u32[]{:S(2)}) copy-start(bf16[320,1024]{1,0:T(8,128)(2,1)S(1)} %get-tuple-element.168.q_ref.refs_0_) | copy-start | bytes 1966084
  115.9 25.1 %collective-permute-start = (bf16[1,5,64,512]{3,2,1,0:T(8,128)(2,1)S(1)}, bf16[1,5,64,512]{3,2,1,0:T(8,128)(2,1)S(1)}, u32[]{:S(2)}, u32[]{:S(2)}) collective-permute-start(bf16[1,5,64,512]{3,2,1,0:T(8,128)(2,1)S(1)} %bitcast.59), channel_id=1, source_target_pairs={{0,16},{2,18},{4,20},{6,22},{8,24},{10,26},{12,28},{14,30},{16,0},... | collective-permute-start | bytes 983048 | tf_op jit(solution)/shard_map/ppermute | solution.py:511
  141.1 31.3 %collective-permute-start.1 = (bf16[2,5,64,512]{3,2,1,0:T(8,128)(2,1)S(1)}, bf16[2,5,64,512]{3,2,1,0:T(8,128)(2,1)S(1)}, u32[]{:S(2)}, u32[]{:S(2)}) collective-permute-start(bf16[2,5,64,512]{3,2,1,0:T(8,128)(2,1)S(1)} %pad_maximum_fusion.10), channel_id=1, source_target_pairs={{0,8},{2,10},{4,12},{6,14},{8,0},{10,2},{12,4},{14,6},{16,24},{18,... | collective-permute-start | bytes 1966088 | tf_op jit(solution)/shard_map/ppermute | solution.py:511
  172.5 60.8 %copy-start.96 = (s32[16]{0:T(128)S(1)}, s32[16]{0:T(128)}, u32[]{:S(2)}) copy-start(s32[16]{0:T(128)} %constant.56.clone) | copy-start | bytes 196
  172.5 59.0 %collective-permute-start.2 = (bf16[4,5,64,512]{3,2,1,0:T(8,128)(2,1)S(1)}, bf16[4,5,64,512]{3,2,1,0:T(8,128)(2,1)S(1)}, u32[]{:S(2)}, u32[]{:S(2)}) collective-permute-start(bf16[4,5,64,512]{3,2,1,0:T(8,128)(2,1)S(1)} %pad_maximum_fusion.7), channel_id=1, source_target_pairs={{0,4},{2,6},{4,0},{6,2},{8,12},{10,14},{12,8},{14,10},{16,20},{18,... | collective-permute-start | bytes 3932168 | tf_op jit(solution)/shard_map/ppermute | solution.py:511
  233.1 5.3 collective-permute-start.3
  252.3 30.7 %collective-permute-start.4 = (bf16[320,2048]{1,0:T(8,128)(2,1)S(1)}, bf16[320,2048]{1,0:T(8,128)(2,1)S(1)}, u32[]{:S(2)}, u32[]{:S(2)}) collective-permute-start(bf16[320,2048]{1,0:T(8,128)(2,1)S(1)} %fusion.6), channel_id=1, source_target_pairs={{0,1},{1,0},{2,3},{3,2},{4,5},{5,4},{6,7},{7,6},{8,9},{9,8},{10,11... | collective-permute-start | bytes 3932168 | tf_op jit(solution)/shard_map/ppermute | solution.py:514
  253.8 29.2 %copy-start.1 = (bf16[5,64,2048]{2,1,0:T(8,128)(2,1)S(1)}, bf16[5,64,2048]{2,1,0:T(8,128)(2,1)}, u32[]{:S(2)}) copy-start(bf16[5,64,2048]{2,1,0:T(8,128)(2,1)} %copy-done) | copy-start | bytes 3932164
  255.6 31.4 %collective-permute-start.5 = (bf16[320,1024]{1,0:T(8,128)(2,1)S(1)}, bf16[320,1024]{1,0:T(8,128)(2,1)S(1)}, u32[]{:S(2)}, u32[]{:S(2)}) collective-permute-start(bf16[320,1024]{1,0:T(8,128)(2,1)S(1)} %get-tuple-element.171), channel_id=1, source_target_pairs={{0,2},{2,0},{4,6},{6,4},{8,10},{10,8},{12,14},{14,12},{16,18},{18,... | collective-permute-start | bytes 1966088 | tf_op jit(solution)/shard_map/ppermute | solution.py:511
  257.4 29.6 %collective-permute-start.7 = (bf16[320,1024]{1,0:T(8,128)(2,1)S(1)}, bf16[320,1024]{1,0:T(8,128)(2,1)S(1)}, u32[]{:S(2)}, u32[]{:S(2)}) collective-permute-start(bf16[320,1024]{1,0:T(8,128)(2,1)S(1)} %get-tuple-element.173), channel_id=1, source_target_pairs={{0,2},{2,0},{4,6},{6,4},{8,10},{10,8},{12,14},{14,12},{16,18},{18,... | collective-permute-start | bytes 1966088 | tf_op jit(solution)/shard_map/ppermute | solution.py:511
  257.9 29.1 %collective-permute-start.8 = (bf16[320,1024]{1,0:T(8,128)(2,1)S(1)}, bf16[320,1024]{1,0:T(8,128)(2,1)S(1)}, u32[]{:S(2)}, u32[]{:S(2)}) collective-permute-start(bf16[320,1024]{1,0:T(8,128)(2,1)S(1)} %get-tuple-element.170), channel_id=1, source_target_pairs={{0,2},{2,0},{4,6},{6,4},{8,10},{10,8},{12,14},{14,12},{16,18},{18,... | collective-permute-start | bytes 1966088 | tf_op jit(solution)/shard_map/ppermute | solution.py:511
  287.0 2.1 collective-permute-start.6
  289.1 125.1 %copy-start.16 = (bf16[320,1024]{1,0:T(8,128)(2,1)}, bf16[320,1024]{1,0:T(8,128)(2,1)S(1)}, u32[]{:S(2)}) copy-start(bf16[320,1024]{1,0:T(8,128)(2,1)S(1)} %collective-permute-done.6.refs_1_) | copy-start | bytes 1966084
  323.2 8.2 %collective-permute-start.10 = (bf16[320,1536]{1,0:T(8,128)(2,1)S(1)}, bf16[320,1536]{1,0:T(8,128)(2,1)S(1)}, u32[]{:S(2)}, u32[]{:S(2)}) collective-permute-start(bf16[320,1536]{1,0:T(8,128)(2,1)S(1)} %get-tuple-element.174), channel_id=1, source_target_pairs={{0,2},{2,0},{4,6},{6,4},{8,10},{10,8},{12,14},{14,12},{16,18},{18,... | collective-permute-start | bytes 2949128 | tf_op jit(solution)/shard_map/ppermute | solution.py:511
  331.1 4.7 collective-permute-start.9
  335.7 36.6 %collective-permute-start.11 = (bf16[512,1536]{1,0:T(8,128)(2,1)S(1)}, bf16[512,1536]{1,0:T(8,128)(2,1)S(1)}, u32[]{:S(2)}, u32[]{:S(2)}) collective-permute-start(bf16[512,1536]{1,0:T(8,128)(2,1)S(1)} %get-tuple-element.189), channel_id=1, source_target_pairs={{0,4},{2,6},{4,0},{6,2},{8,12},{10,14},{12,8},{14,10},{16,20},{18,... | collective-permute-start | bytes 4718600 | tf_op jit(solution)/shard_map/ppermute | solution.py:511
  372.7 115.8 %copy-start.7 = (bf16[2,320,2816]{2,1,0:T(8,128)(2,1)}, bf16[2,320,2816]{2,1,0:T(8,128)(2,1)S(1)}, u32[]{:S(2)}) copy-start(bf16[2,320,2816]{2,1,0:T(8,128)(2,1)S(1)} %get-tuple-element.199.refs_2_) | copy-start | bytes 10813444
  372.7 6.4 collective-permute-start.15
  372.8 31.6 %collective-permute-start.13 = (bf16[512,1280]{1,0:T(8,128)(2,1)S(1)}, bf16[512,1280]{1,0:T(8,128)(2,1)S(1)}, u32[]{:S(2)}, u32[]{:S(2)}) collective-permute-start(bf16[512,1280]{1,0:T(8,128)(2,1)S(1)} %get-tuple-element.195), channel_id=1, source_target_pairs={{0,4},{2,6},{4,0},{6,2},{8,12},{10,14},{12,8},{14,10},{16,20},{18,... | collective-permute-start | bytes 3932168 | tf_op jit(solution)/shard_map/ppermute | solution.py:511
  373.1 31.6 %collective-permute-start.12 = (bf16[320,2048]{1,0:T(8,128)(2,1)S(1)}, bf16[320,2048]{1,0:T(8,128)(2,1)S(1)}, u32[]{:S(2)}, u32[]{:S(2)}) collective-permute-start(bf16[320,2048]{1,0:T(8,128)(2,1)S(1)} %get-tuple-element.193.refs_0_), channel_id=1, source_target_pairs={{0,1},{1,0},{2,3},{3,2},{4,5},{5,4},{6,7},{7,6},{8,9},{9,8},{10,11... | collective-permute-start | bytes 3932168 | tf_op jit(solution)/shard_map/ppermute | solution.py:514
  374.6 19.3 %collective-permute-start.14 = (bf16[256,1536]{1,0:T(8,128)(2,1)S(1)}, bf16[256,1536]{1,0:T(8,128)(2,1)S(1)}, u32[]{:S(2)}, u32[]{:S(2)}) collective-permute-start(bf16[256,1536]{1,0:T(8,128)(2,1)S(1)} %get-tuple-element.197), channel_id=1, source_target_pairs={{0,8},{2,10},{4,12},{6,14},{8,0},{10,2},{12,4},{14,6},{16,24},{18,... | collective-permute-start | bytes 2359304 | tf_op jit(solution)/shard_map/ppermute | solution.py:511
  379.1 35.1 %copy-start.29 = (bf16[2,320,2816]{2,1,0:T(8,128)(2,1)}, bf16[2,320,2816]{2,1,0:T(8,128)(2,1)S(1)}, u32[]{:S(2)}) copy-start(bf16[2,320,2816]{2,1,0:T(8,128)(2,1)S(1)} %collective-permute-done.15.refs_3_) | copy-start | bytes 10813444
  383.2 54.4 %collective-permute-start.17 = (bf16[512,1536]{1,0:T(8,128)(2,1)S(1)}, bf16[512,1536]{1,0:T(8,128)(2,1)S(1)}, u32[]{:S(2)}, u32[]{:S(2)}) collective-permute-start(bf16[512,1536]{1,0:T(8,128)(2,1)S(1)} %get-tuple-element.211), channel_id=1, source_target_pairs={{0,4},{2,6},{4,0},{6,2},{8,12},{10,14},{12,8},{14,10},{16,20},{18,... | collective-permute-start | bytes 4718600 | tf_op jit(solution)/shard_map/ppermute | solution.py:511
  410.4 9.7 %collective-permute-start.16 = (bf16[320,1024]{1,0:T(8,128)(2,1)S(1)}, bf16[320,1024]{1,0:T(8,128)(2,1)S(1)}, u32[]{:S(2)}, u32[]{:S(2)}) collective-permute-start(bf16[320,1024]{1,0:T(8,128)(2,1)S(1)} %get-tuple-element.207), channel_id=1, source_target_pairs={{0,2},{2,0},{4,6},{6,4},{8,10},{10,8},{12,14},{14,12},{16,18},{18,... | collective-permute-start | bytes 1966088 | tf_op jit(solution)/shard_map/ppermute | solution.py:511
  410.4 22.4 %collective-permute-start.18 = (bf16[256,1280]{1,0:T(8,128)(2,1)S(1)}, bf16[256,1280]{1,0:T(8,128)(2,1)S(1)}, u32[]{:S(2)}, u32[]{:S(2)}) collective-permute-start(bf16[256,1280]{1,0:T(8,128)(2,1)S(1)} %get-tuple-element.213), channel_id=1, source_target_pairs={{0,8},{2,10},{4,12},{6,14},{8,0},{10,2},{12,4},{14,6},{16,24},{18,... | collective-permute-start | bytes 1966088 | tf_op jit(solution)/shard_map/ppermute | solution.py:511
  439.7 4.9 collective-permute-start.19
  445.2 31.7 %collective-permute-start.20 = (bf16[1280,512]{1,0:T(8,128)(2,1)S(1)}, bf16[1280,512]{1,0:T(8,128)(2,1)S(1)}, u32[]{:S(2)}, u32[]{:S(2)}) collective-permute-start(bf16[1280,512]{1,0:T(8,128)(2,1)S(1)} %get-tuple-element.220), channel_id=1, source_target_pairs={{0,4},{2,6},{4,0},{6,2},{8,12},{10,14},{12,8},{14,10},{16,20},{18,... | collective-permute-start | bytes 3932168 | tf_op jit(solution)/shard_map/ppermute | solution.py:511
  445.7 41.8 %collective-permute-start.24 = (bf16[128,1536]{1,0:T(8,128)(2,1)}, bf16[128,1536]{1,0:T(8,128)(2,1)S(1)}, u32[]{:S(2)}, u32[]{:S(2)}) collective-permute-start(bf16[128,1536]{1,0:T(8,128)(2,1)} %get-tuple-element.230), channel_id=1, source_target_pairs={{0,16},{2,18},{4,20},{6,22},{8,24},{10,26},{12,28},{14,30},{16,0},... | collective-permute-start | bytes 1179656 | tf_op jit(solution)/shard_map/ppermute | solution.py:511
  446.3 62.1 %collective-permute-start.27 = (bf16[512,1280]{1,0:T(8,128)(2,1)}, bf16[512,1280]{1,0:T(8,128)(2,1)}, u32[]{:S(2)}, u32[]{:S(2)}) collective-permute-start(bf16[512,1280]{1,0:T(8,128)(2,1)} %get-tuple-element.240), channel_id=1, source_target_pairs={{0,4},{2,6},{4,0},{6,2},{8,12},{10,14},{12,8},{14,10},{16,20},{18,... | collective-permute-start | bytes 3932168 | tf_op jit(solution)/shard_map/ppermute | solution.py:511
  447.6 65.9 %collective-permute-start.26 = (bf16[128,1280]{1,0:T(8,128)(2,1)}, bf16[128,1280]{1,0:T(8,128)(2,1)}, u32[]{:S(2)}, u32[]{:S(2)}) collective-permute-start(bf16[128,1280]{1,0:T(8,128)(2,1)} %get-tuple-element.238), channel_id=1, source_target_pairs={{0,16},{2,18},{4,20},{6,22},{8,24},{10,26},{12,28},{14,30},{16,0},... | collective-permute-start | bytes 983048 | tf_op jit(solution)/shard_map/ppermute | solution.py:511
  450.4 45.0 %collective-permute-start.23 = (bf16[256,1536]{1,0:T(8,128)(2,1)}, bf16[256,1536]{1,0:T(8,128)(2,1)}, u32[]{:S(2)}, u32[]{:S(2)}) collective-permute-start(bf16[256,1536]{1,0:T(8,128)(2,1)} %get-tuple-element.228), channel_id=1, source_target_pairs={{0,8},{2,10},{4,12},{6,14},{8,0},{10,2},{12,4},{14,6},{16,24},{18,... | collective-permute-start | bytes 2359304 | tf_op jit(solution)/shard_map/ppermute | solution.py:511
  478.0 21.0 %collective-permute-start.22 = (bf16[640,512]{1,0:T(8,128)(2,1)}, bf16[640,512]{1,0:T(8,128)(2,1)}, u32[]{:S(2)}, u32[]{:S(2)}) collective-permute-start(bf16[640,512]{1,0:T(8,128)(2,1)} %get-tuple-element.226), channel_id=1, source_target_pairs={{0,8},{2,10},{4,12},{6,14},{8,0},{10,2},{12,4},{14,6},{16,24},{18,... | collective-permute-start | bytes 1966088 | tf_op jit(solution)/shard_map/ppermute | solution.py:511
  501.7 26.1 %collective-permute-start.25 = (bf16[320,512]{1,0:T(8,128)(2,1)}, bf16[320,512]{1,0:T(8,128)(2,1)}, u32[]{:S(2)}, u32[]{:S(2)}) collective-permute-start(bf16[320,512]{1,0:T(8,128)(2,1)} %get-tuple-element.236), channel_id=1, source_target_pairs={{0,16},{2,18},{4,20},{6,22},{8,24},{10,26},{12,28},{14,30},{16,0},... | collective-permute-start | bytes 983048 | tf_op jit(solution)/shard_map/ppermute | solution.py:511
  508.0 57.9 %collective-permute-start.34 = (bf16[512,1536]{1,0:T(8,128)(2,1)}, bf16[512,1536]{1,0:T(8,128)(2,1)}, u32[]{:S(2)}, u32[]{:S(2)}) collective-permute-start(bf16[512,1536]{1,0:T(8,128)(2,1)} %copy-done.32), channel_id=1, source_target_pairs={{0,4},{2,6},{4,0},{6,2},{8,12},{10,14},{12,8},{14,10},{16,20},{18,... | collective-permute-start | bytes 4718600 | tf_op jit(solution)/shard_map/ppermute | solution.py:511
  508.3 70.2 %collective-permute-start.32 = (bf16[128,1536]{1,0:T(8,128)(2,1)}, bf16[128,1536]{1,0:T(8,128)(2,1)}, u32[]{:S(2)}, u32[]{:S(2)}) collective-permute-start(bf16[128,1536]{1,0:T(8,128)(2,1)} %copy-done.40), channel_id=1, source_target_pairs={{0,16},{2,18},{4,20},{6,22},{8,24},{10,26},{12,28},{14,30},{16,0},... | collective-permute-start | bytes 1179656 | tf_op jit(solution)/shard_map/ppermute | solution.py:511
  508.4 36.8 %collective-permute-start.21 = (bf16[320,2048]{1,0:T(8,128)(2,1)}, bf16[320,2048]{1,0:T(8,128)(2,1)}, u32[]{:S(2)}, u32[]{:S(2)}) collective-permute-start(bf16[320,2048]{1,0:T(8,128)(2,1)} %copy-done.13), channel_id=1, source_target_pairs={{0,1},{1,0},{2,3},{3,2},{4,5},{5,4},{6,7},{7,6},{8,9},{9,8},{10,11... | collective-permute-start | bytes 3932168 | tf_op jit(solution)/shard_map/ppermute | solution.py:514
  513.5 14.3 %copy-start.80 = (bf16[320,512]{1,0:T(8,128)(2,1)S(1)}, bf16[320,512]{1,0:T(8,128)(2,1)}, u32[]{:S(2)}) copy-start(bf16[320,512]{1,0:T(8,128)(2,1)} %copy-done.79) | copy-start | bytes 983044
  513.5 29.0 %collective-permute-start.29 = (bf16[256,1280]{1,0:T(8,128)(2,1)}, bf16[256,1280]{1,0:T(8,128)(2,1)}, u32[]{:S(2)}, u32[]{:S(2)}) collective-permute-start(bf16[256,1280]{1,0:T(8,128)(2,1)} %get-tuple-element.251), channel_id=1, source_target_pairs={{0,8},{2,10},{4,12},{6,14},{8,0},{10,2},{12,4},{14,6},{16,24},{18,... | collective-permute-start | bytes 1966088 | tf_op jit(solution)/shard_map/ppermute | solution.py:511
  536.6 10.6 %collective-permute-start.28 = (bf16[320,1536]{1,0:T(8,128)(2,1)}, bf16[320,1536]{1,0:T(8,128)(2,1)}, u32[]{:S(2)}, u32[]{:S(2)}) collective-permute-start(bf16[320,1536]{1,0:T(8,128)(2,1)} %get-tuple-element.365.refs_0_), channel_id=1, source_target_pairs={{0,2},{2,0},{4,6},{6,4},{8,10},{10,8},{12,14},{14,12},{16,18},{18,... | collective-permute-start | bytes 2949128 | tf_op jit(solution)/shard_map/ppermute | solution.py:511
  542.5 32.1 %collective-permute-start.33 = (bf16[512,1024]{1,0:T(8,128)(2,1)}, bf16[512,1024]{1,0:T(8,128)(2,1)}, u32[]{:S(2)}, u32[]{:S(2)}) collective-permute-start(bf16[512,1024]{1,0:T(8,128)(2,1)} %copy-done.33), channel_id=1, source_target_pairs={{0,8},{2,10},{4,12},{6,14},{8,0},{10,2},{12,4},{14,6},{16,24},{18,... | collective-permute-start | bytes 3145736 | tf_op jit(solution)/shard_map/ppermute | solution.py:511
  547.3 17.2 %copy-start.88 = (bf16[320,2048]{1,0:T(8,128)(2,1)}, bf16[320,2048]{1,0:T(8,128)(2,1)S(1)}, u32[]{:S(2)}) copy-start(bf16[320,2048]{1,0:T(8,128)(2,1)S(1)} %add_convert_fusion) | copy-start | bytes 3932164
  553.5 35.4 %collective-permute-start.31 = (bf16[512,1536]{1,0:T(8,128)(2,1)}, bf16[512,1536]{1,0:T(8,128)(2,1)S(1)}, u32[]{:S(2)}, u32[]{:S(2)}) collective-permute-start(bf16[512,1536]{1,0:T(8,128)(2,1)} %get-tuple-element.258), channel_id=1, source_target_pairs={{0,4},{2,6},{4,0},{6,2},{8,12},{10,14},{12,8},{14,10},{16,20},{18,... | collective-permute-start | bytes 4718600 | tf_op jit(solution)/shard_map/ppermute | solution.py:511
  555.1 15.2 %copy-start.31 = (bf16[2,320,2816]{2,1,0:T(8,128)(2,1)S(1)}, bf16[2,320,2816]{2,1,0:T(8,128)(2,1)}, u32[]{:S(2)}) copy-start(bf16[2,320,2816]{2,1,0:T(8,128)(2,1)} %copy-done.29) | copy-start | bytes 10813444
  563.9 28.2 %collective-permute-start.30 = (bf16[320,2048]{1,0:T(8,128)(2,1)}, bf16[320,2048]{1,0:T(8,128)(2,1)S(1)}, u32[]{:S(2)}, u32[]{:S(2)}) collective-permute-start(bf16[320,2048]{1,0:T(8,128)(2,1)} %get-tuple-element.255.refs_0_), channel_id=1, source_target_pairs={{0,1},{1,0},{2,3},{3,2},{4,5},{5,4},{6,7},{7,6},{8,9},{9,8},{10,11... | collective-permute-start | bytes 3932168 | tf_op jit(solution)/shard_map/ppermute | solution.py:514
  568.3 42.9 %collective-permute-start.36 = (bf16[256,1536]{1,0:T(8,128)(2,1)S(1)}, bf16[256,1536]{1,0:T(8,128)(2,1)S(1)}, u32[]{:S(2)}, u32[]{:S(2)}) collective-permute-start(bf16[256,1536]{1,0:T(8,128)(2,1)S(1)} %get-tuple-element.275), channel_id=1, source_target_pairs={{0,8},{2,10},{4,12},{6,14},{8,0},{10,2},{12,4},{14,6},{16,24},{18,... | collective-permute-start | bytes 2359304 | tf_op jit(solution)/shard_map/ppermute | solution.py:511
  576.1 34.2 %collective-permute-start.37 = (bf16[256,1024]{1,0:T(8,128)(2,1)S(1)}, bf16[256,1024]{1,0:T(8,128)(2,1)S(1)}, u32[]{:S(2)}, u32[]{:S(2)}) collective-permute-start(bf16[256,1024]{1,0:T(8,128)(2,1)S(1)} %get-tuple-element.277), channel_id=1, source_target_pairs={{0,16},{2,18},{4,20},{6,22},{8,24},{10,26},{12,28},{14,30},{16,0},... | collective-permute-start | bytes 1572872 | tf_op jit(solution)/shard_map/ppermute | solution.py:511
  578.5 56.3 %collective-permute-start.39 = (bf16[128,1280]{1,0:T(8,128)(2,1)}, bf16[128,1280]{1,0:T(8,128)(2,1)}, u32[]{:S(2)}, u32[]{:S(2)}) collective-permute-start(bf16[128,1280]{1,0:T(8,128)(2,1)} %get-tuple-element.283), channel_id=1, source_target_pairs={{0,16},{2,18},{4,20},{6,22},{8,24},{10,26},{12,28},{14,30},{16,0},... | collective-permute-start | bytes 983048 | tf_op jit(solution)/shard_map/ppermute | solution.py:511
  588.9 28.7 %collective-permute-start.41 = (bf16[512,1280]{1,0:T(8,128)(2,1)S(1)}, bf16[512,1280]{1,0:T(8,128)(2,1)S(1)}, u32[]{:S(2)}, u32[]{:S(2)}) collective-permute-start(bf16[512,1280]{1,0:T(8,128)(2,1)S(1)} %get-tuple-element.287), channel_id=1, source_target_pairs={{0,4},{2,6},{4,0},{6,2},{8,12},{10,14},{12,8},{14,10},{16,20},{18,... | collective-permute-start | bytes 3932168 | tf_op jit(solution)/shard_map/ppermute | solution.py:511
  592.1 40.4 %collective-permute-start.40 = (bf16[256,1536]{1,0:T(8,128)(2,1)}, bf16[256,1536]{1,0:T(8,128)(2,1)}, u32[]{:S(2)}, u32[]{:S(2)}) collective-permute-start(bf16[256,1536]{1,0:T(8,128)(2,1)} %get-tuple-element.285), channel_id=1, source_target_pairs={{0,8},{2,10},{4,12},{6,14},{8,0},{10,2},{12,4},{14,6},{16,24},{18,... | collective-permute-start | bytes 2359304 | tf_op jit(solution)/shard_map/ppermute | solution.py:511
  612.1 24.5 %collective-permute-start.38 = (bf16[128,1536]{1,0:T(8,128)(2,1)S(1)}, bf16[128,1536]{1,0:T(8,128)(2,1)S(1)}, u32[]{:S(2)}, u32[]{:S(2)}) collective-permute-start(bf16[128,1536]{1,0:T(8,128)(2,1)S(1)} %get-tuple-element.281), channel_id=1, source_target_pairs={{0,16},{2,18},{4,20},{6,22},{8,24},{10,26},{12,28},{14,30},{16,0},... | collective-permute-start | bytes 1179656 | tf_op jit(solution)/shard_map/ppermute | solution.py:511
  618.7 33.2 %collective-permute-start.45 = (bf16[256,1280]{1,0:T(8,128)(2,1)}, bf16[256,1280]{1,0:T(8,128)(2,1)}, u32[]{:S(2)}, u32[]{:S(2)}) collective-permute-start(bf16[256,1280]{1,0:T(8,128)(2,1)} %get-tuple-element.300), channel_id=1, source_target_pairs={{0,8},{2,10},{4,12},{6,14},{8,0},{10,2},{12,4},{14,6},{16,24},{18,... | collective-permute-start | bytes 1966088 | tf_op jit(solution)/shard_map/ppermute | solution.py:511
  620.6 16.0 %collective-permute-start.35 = (f32[8,256]{1,0:T(8,128)S(1)}, f32[8,256]{1,0:T(8,128)S(1)}, u32[]{:S(2)}, u32[]{:S(2)}) collective-permute-start(f32[8,256]{1,0:T(8,128)S(1)} %bitcast.78), channel_id=1, source_target_pairs={{0,2},{2,0},{4,6},{6,4},{8,10},{10,8},{12,14},{14,12},{16,18},{18,... | collective-permute-start | bytes 24584 | tf_op jit(solution)/shard_map/ppermute | solution.py:511
  632.5 21.9 %collective-permute-start.44 = (bf16[128,1024]{1,0:T(8,128)(2,1)S(1)}, bf16[128,1024]{1,0:T(8,128)(2,1)S(1)}, u32[]{:S(2)}, u32[]{:S(2)}) collective-permute-start(bf16[128,1024]{1,0:T(8,128)(2,1)S(1)} %copy-done.42), channel_id=1, source_target_pairs={{0,4},{2,6},{4,0},{6,2},{8,12},{10,14},{12,8},{14,10},{16,20},{18,... | collective-permute-start | bytes 786440 | tf_op jit(solution)/shard_map/ppermute | solution.py:511
  634.9 21.8 %collective-permute-start.43 = (bf16[128,1536]{1,0:T(8,128)(2,1)}, bf16[128,1536]{1,0:T(8,128)(2,1)}, u32[]{:S(2)}, u32[]{:S(2)}) collective-permute-start(bf16[128,1536]{1,0:T(8,128)(2,1)} %get-tuple-element.296), channel_id=1, source_target_pairs={{0,16},{2,18},{4,20},{6,22},{8,24},{10,26},{12,28},{14,30},{16,0},... | collective-permute-start | bytes 1179656 | tf_op jit(solution)/shard_map/ppermute | solution.py:511
  636.6 15.2 %copy-start.46 = (bf16[256,1280]{1,0:T(8,128)(2,1)S(1)}, bf16[256,1280]{1,0:T(8,128)(2,1)}, u32[]{:S(2)}) copy-start(bf16[256,1280]{1,0:T(8,128)(2,1)} %copy-done.45) | copy-start | bytes 1966084
  636.7 17.7 %copy-start.82 = (bf16[128,1024]{1,0:T(8,128)(2,1)S(1)}, bf16[128,1024]{1,0:T(8,128)(2,1)}, u32[]{:S(2)}) copy-start(bf16[128,1024]{1,0:T(8,128)(2,1)} %copy-done.81) | copy-start | bytes 786436
  636.7 21.0 %collective-permute-start.42 = (f32[4,256]{1,0:T(4,128)S(1)}, f32[4,256]{1,0:T(4,128)S(1)}, u32[]{:S(2)}, u32[]{:S(2)}) collective-permute-start(f32[4,256]{1,0:T(4,128)S(1)} %get-tuple-element.294), channel_id=1, source_target_pairs={{0,4},{2,6},{4,0},{6,2},{8,12},{10,14},{12,8},{14,10},{16,20},{18,... | collective-permute-start | bytes 12296 | tf_op jit(solution)/shard_map/ppermute | solution.py:511
  653.8 14.5 %collective-permute-start.48 = (bf16[128,1280]{1,0:T(8,128)(2,1)S(1)}, bf16[128,1280]{1,0:T(8,128)(2,1)S(1)}, u32[]{:S(2)}, u32[]{:S(2)}) collective-permute-start(bf16[128,1280]{1,0:T(8,128)(2,1)S(1)} %get-tuple-element.311), channel_id=1, source_target_pairs={{0,16},{2,18},{4,20},{6,22},{8,24},{10,26},{12,28},{14,30},{16,0},... | collective-permute-start | bytes 983048 | tf_op jit(solution)/shard_map/ppermute | solution.py:511
  657.8 4.3 collective-permute-start.46
  662.1 7.4 %collective-permute-start.47 = (f32[1,256]{1,0:T(1,128)S(1)}, f32[1,256]{1,0:T(1,128)S(1)}, u32[]{:S(2)}, u32[]{:S(2)}) collective-permute-start(f32[1,256]{1,0:T(1,128)S(1)} %get-tuple-element.309), channel_id=1, source_target_pairs={{0,16},{2,18},{4,20},{6,22},{8,24},{10,26},{12,28},{14,30},{16,0},... | collective-permute-start | bytes 3080 | tf_op jit(solution)/shard_map/ppermute | solution.py:511
  (86 other events, 332.7 us)
Sparse Core Ops, SparseCore 0:
  13.0 93.7 all-gather.2
  108.4 204.8 all-gather.4

commit v5 on v3

--- a/solution.py
+++ b/solution.py
@@ -40,7 +40,7 @@
     return lax.dot_general(a, b, (((ca,), (cb,)), ((), ())), preferred_element_type=f32)
 
 
-def params(room=16 * MIB):
+def params(room=20 * MIB):
     return pltpu.CompilerParams(vmem_limit_bytes=min(room, 56 * MIB))
 
 
@@ -50,7 +50,7 @@
 
 def call(
     kernel, token, args, in_specs, outs, out_specs, name, takes, grid=(), scratch=(), others=(), aliases=None,
-    room=16 * MIB,
+    room=20 * MIB,
 ):
     waits = [*([] if token is None else [token]), *others]
     unread = pl.BlockSpec(memory_space=pl.ANY)
@@ -422,7 +422,7 @@
     outs = [like(rows, width, dtype=f32)] if last else [like(rows // 2, width, dtype=kept.dtype)] * 2
     return call(
         fold_kernel, token, (kept, received), [whole] * 2, outs, [whole] * len(outs), "fold", 1.5,
-        room=max(16 * MIB, 4 * MIB + 4 * kept.size * kept.dtype.itemsize),
+        room=max(20 * MIB, 4 * MIB + 4 * kept.size * kept.dtype.itemsize),
     )
 
 

time: 682 us -> 684 us (level)
  transfers between devices with their start and end apart: 51 -> 51, of which waited for: 26 -> 28; matrix products, arithmetic and copies ran while one was open for 7% -> 7% of each run, Pallas kernels for 22% -> 22%
where the time goes in v5:
time: 684 us; the launch traced here: 673 us
  waiting for transfers between devices  377 us (55%)
  Pallas kernels  155 us (23%)
  local copies, waits for them, and re-layouts  43.2 us (6%)
  starting transfers between devices  36.8 us (5%)
  other arithmetic  28.4 us (4%)
  between operations  19 us (3%)
  matrix products  13.8 us (2%)
    ppermute x45, waiting for transfers between devices, flip(): return lax.ppermute(v, 'dp', [(i, i ^ bits) for i in range(n_dp)])  247 us
    pallas_call x54, Pallas kernels, call(): pl.pallas_call(body, grid=grid, in_specs=[*in_specs, *[unread] * len(wait...  143 us
    all_gather x1, waiting for transfers between devices, local(): lax.all_gather(jnp.concatenate([query_weight, key_weight, value_weight, o...  81.9 us
    unnamed x202, local copies, waits for them, and re-layouts  38.4 us
    ppermute x45, starting transfers between devices, flip(): return lax.ppermute(v, 'dp', [(i, i ^ bits) for i in range(n_dp)])  30.8 us
    ppermute x4, waiting for transfers between devices, tensor_flip(): return lax.ppermute(v, 'tensor', [(0, 1), (1, 0)])  26.2 us
    all_gather x1, waiting for transfers between devices, local(): lax.all_gather(jnp.concatenate([gate_weight, up_weight, down_weight.T], a...  22.1 us
    dot_general x3, matrix products, dot(): lax.dot_general(a, b, (((ca,), (cb,)), ((), ())), preferred_element_type=...  13.8 us
  transfers between devices with their start and end apart: 51, of which 28 were waited for; matrix products, arithmetic and copies ran while one was open for 7% of the time, Pallas kernels for 22%

profile of v5, /device:TPU:0, one launch (start us, length us, event | category | flops | bytes accessed | tf_op | source)
XLA Modules:
  0.0 673.2 jit_solution(17757280256415726552)
XLA Ops:
  13.2 2.6 pad_maximum_fusion.2
  21.7 2.4 slice_select_fusion.1
  24.9 81.9 %all-gather.3.cloned.1.call-done.refs_1_ = bf16[2048,2688]{1,0:T(8,128)(2,1)} async-done(((bf16[128,2688]{1,0:T(8,128)(2,1)}), bf16[2048,2688]{1,0:T(8,128)(2,1)}) %all-gather.3.cloned.1.call-update) | async-done | bytes 11010064 | tf_op jit(solution)/shard_map/all_gather | solution.py:540
  106.8 1.8 convert_reduce_fusion
  109.6 5.4 fusion.refs_0_
  117.5 23.5 %collective-permute-done = bf16[1,5,64,512]{3,2,1,0:T(8,128)(2,1)S(1)} collective-permute-done((bf16[1,5,64,512]{3,2,1,0:T(8,128)(2,1)S(1)}, bf16[1,5,64,512]{3,2,1,0:T(8,128)(2,1)S(1)}, u32[]{:S(2)}, u32[]{:S(2)}) %collective-permute-start) | collective-permute-done | bytes 327712 | tf_op jit(solution)/shard_map/ppermute | solution.py:511
  141.1 31.2 %collective-permute-done.1 = bf16[2,5,64,512]{3,2,1,0:T(8,128)(2,1)S(1)} collective-permute-done((bf16[2,5,64,512]{3,2,1,0:T(8,128)(2,1)S(1)}, bf16[2,5,64,512]{3,2,1,0:T(8,128)(2,1)S(1)}, u32[]{:S(2)}, u32[]{:S(2)}) %collective-permute-start.1) | collective-permute-done | bytes 655392 | tf_op jit(solution)/shard_map/ppermute | solution.py:511
  173.1 58.4 %collective-permute-done.2 = bf16[4,5,64,512]{3,2,1,0:T(8,128)(2,1)S(1)} collective-permute-done((bf16[4,5,64,512]{3,2,1,0:T(8,128)(2,1)S(1)}, bf16[4,5,64,512]{3,2,1,0:T(8,128)(2,1)S(1)}, u32[]{:S(2)}, u32[]{:S(2)}) %collective-permute-start.2) | collective-permute-done | bytes 1310752 | tf_op jit(solution)/shard_map/ppermute | solution.py:511
  233.4 4.9 collective-permute-done.3.far_ref.refs_2_
  238.3 8.6 %attend.1 = (bf16[320,1024]{1,0:T(8,128)(2,1)S(1)}, f32[10,256,1]{2,1,0:T(8,128)S(1)}) custom-call(bf16[320,1024]{1,0:T(8,128)(2,1)S(1)} %get-tuple-element.168.q_ref.refs_0_, bf16[8,5,64,512]{3,2,1,0:T(8,128)(2,1)} %pad_maximum_fusion.1.near_ref.refs_1_, bf16[8,5,64,512]{3,2,1,0:T(8,128)(2,1)} %collective-permute-done.3.far_ref.refs_2_, ...), custom_call_target="tpu_custom_call" | custom-call | flops 4499999744 | bytes 16200000 | tf_op jit(solution)/shard_map/attend/pallas_call | solution.py:149
  247.0 4.5 fusion.6
  256.3 26.2 %collective-permute-done.4 = bf16[320,2048]{1,0:T(8,128)(2,1)S(1)} collective-permute-done((bf16[320,2048]{1,0:T(8,128)(2,1)S(1)}, bf16[320,2048]{1,0:T(8,128)(2,1)S(1)}, u32[]{:S(2)}, u32[]{:S(2)}) %collective-permute-start.4) | collective-permute-done | bytes 1310752 | tf_op jit(solution)/shard_map/ppermute | solution.py:514
  286.5 2.1 collective-permute-done.6.refs_1_
  291.2 22.1 %all-gather.5.cloned.1.call-done.refs_1_.refs_2_.refs_3_.refs_4_.refs_5_ = bf16[2048,8448]{1,0:T(8,128)(2,1)} async-done(((bf16[128,8448]{1,0:T(8,128)(2,1)}), bf16[2048,8448]{1,0:T(8,128)(2,1)}) %all-gather.5.cloned.1.call-update) | async-done | bytes 34603024 | tf_op jit(solution)/shard_map/all_gather | solution.py:544
  314.6 8.6 %feed_forward.2 = (f32[320,2816]{1,0:T(8,128)S(1)}, f32[320,2816]{1,0:T(8,128)S(1)}, bf16[320,1536]{1,0:T(8,128)(2,1)S(1)}, f32[8,128]{1,0:T(8,128)S(1)}) custom-call(bf16[320,2048]{1,0:T(8,128)(2,1)S(1)} %copy-done.4, bf16[2048,8448]{1,0:T(8,128)(2,1)} %all-gather.5.cloned.1.call-done.refs_1_.refs_2_.refs_3_.refs_4_.refs_5_, ...), custom_call_target="tpu_custom_call" | custom-call | flops 4636363776 | bytes 16690909 | tf_op jit(solution)/shard_map/feed_forward/pallas_call | solution.py:63
  323.6 7.6 %feed_forward.3 = (f32[320,2816]{1,0:T(8,128)S(1)}, f32[320,2816]{1,0:T(8,128)S(1)}, bf16[320,1280]{1,0:T(8,128)(2,1)S(1)}, f32[8,128]{1,0:T(8,128)S(1)}) custom-call(bf16[320,2048]{1,0:T(8,128)(2,1)S(1)} %copy-done.4, ...), custom_call_target="tpu_custom_call", output_to_operand_aliasing={{0}: (3, {}), {1}: (4, {})} | custom-call | flops 3863636480 | bytes 13909090 | tf_op jit(solution)/shard_map/feed_forward/pallas_call | solution.py:63
  331.5 4.2 side_products.8
  335.9 2.9 side_products.9
  338.8 27.0 %feed_forward_back.1 = (bf16[2,320,2816]{2,1,0:T(8,128)(2,1)S(1)}, bf16[320,2048]{1,0:T(8,128)(2,1)S(1)}, f32[8,128]{1,0:T(8,128)S(1)}) custom-call(bf16[320,2048]{1,0:T(8,128)(2,1)S(1)} %bitcast.55, f32[320,2816]{1,0:T(8,128)S(1)} %get-tuple-element.180.refs_1_, f32[320,2816]{1,0:T(8,128)S(1)} %get-tuple-element.181.refs_2_, ...), custom_call_target="tpu_custom_call" | custom-call | flops 14000000000 | bytes 50400000 | tf_op jit(solution)/shard_map/feed_forward_back/pallas_call | solution.py:63
  365.9 6.4 collective-permute-done.11.refs_1_
  374.6 4.5 collective-permute-done.14.refs_3_
  379.1 4.1 side_products.10
  383.6 20.9 %collective-permute-done.13.refs_1_ = bf16[512,1280]{1,0:T(8,128)(2,1)S(1)} collective-permute-done((bf16[512,1280]{1,0:T(8,128)(2,1)S(1)}, bf16[512,1280]{1,0:T(8,128)(2,1)S(1)}, u32[]{:S(2)}, u32[]{:S(2)}) %collective-permute-start.13) | collective-permute-done | bytes 1310752 | tf_op jit(solution)/shard_map/ppermute | solution.py:511
  404.8 2.4 norm_back.2
  408.7 3.9 fusion.12.refs_6_
  412.6 12.6 %attend_back.1 = (bf16[320,1024]{1,0:T(8,128)(2,1)S(1)}, bf16[8,5,64,512]{3,2,1,0:T(8,128)(2,1)S(1)}, bf16[8,5,64,512]{3,2,1,0:T(8,128)(2,1)S(1)}, f32[8,128]{1,0:T(8,128)S(1)}) custom-call(bf16[320,1024]{1,0:T(8,128)(2,1)S(1)} %copy-done.71, bf16[8,5,64,512]{3,2,1,0:T(8,128)(2,1)} %pad_maximum_fusion.1.near_ref.refs_1_, ...), custom_call_target="tpu_custom_call" | custom-call | flops 6499999744 | bytes 23400000 | tf_op jit(solution)/shard_map/attend_back/pallas_call | solution.py:63
  425.2 12.5 %collective-permute-done.18.refs_1_ = bf16[512,1536]{1,0:T(8,128)(2,1)S(1)} collective-permute-done((bf16[512,1536]{1,0:T(8,128)(2,1)S(1)}, bf16[512,1536]{1,0:T(8,128)(2,1)S(1)}, u32[]{:S(2)}, u32[]{:S(2)}) %collective-permute-start.18) | collective-permute-done | bytes 1572896 | tf_op jit(solution)/shard_map/ppermute | solution.py:511
  440.1 4.8 side_products.11
  448.2 3.1 collective-permute-start.25
  451.3 9.2 %times_turned.2 = (bf16[320,2048]{1,0:T(8,128)(2,1)S(1)}, f32[8,128]{1,0:T(8,128)S(1)}) custom-call(bf16[320,2816]{1,0:T(8,128)(2,1)S(1)} %pad_maximum_fusion.3.refs_0_, bf16[2048,8448]{1,0:T(8,128)(2,1)} %all-gather.5.cloned.1.call-done.refs_1_.refs_2_.refs_3_.refs_4_.refs_5_, f32[8,128]{1,0:T(8,128)S(1)} %get-tuple-element.219.refs_2_), custom_call_target="tpu_custom_call" | custom-call | flops 4499999744 | bytes 16200000 | tf_op jit(solution)/shard_map/times_turned/pallas_call | solution.py:63
  460.5 8.0 %collective-permute-done.22.refs_1_ = bf16[128,1536]{1,0:T(8,128)(2,1)S(1)} collective-permute-done((bf16[128,1536]{1,0:T(8,128)(2,1)S(1)}, bf16[128,1536]{1,0:T(8,128)(2,1)S(1)}, u32[]{:S(2)}, u32[]{:S(2)}) %collective-permute-start.22) | collective-permute-done | bytes 393248 | tf_op jit(solution)/shard_map/ppermute | solution.py:511
  469.4 8.1 %collective-permute-done.21.refs_1_ = bf16[1280,512]{1,0:T(8,128)(2,1)S(1)} collective-permute-done((bf16[1280,512]{1,0:T(8,128)(2,1)S(1)}, bf16[1280,512]{1,0:T(8,128)(2,1)S(1)}, u32[]{:S(2)}, u32[]{:S(2)}) %collective-permute-start.21) | collective-permute-done | bytes 1310752 | tf_op jit(solution)/shard_map/ppermute | solution.py:511
  479.5 2.0 convert_element_type.98
  482.8 3.1 collective-permute-start.27
  488.6 2.1 fold.40
  490.6 2.2 copy-done.8
  492.8 2.0 copy-done.33
  494.8 4.9 side_products.12
  499.8 5.5 collective-permute-done.24.refs_1_
  508.4 3.1 collective-permute-start.29
  512.7 12.9 %collective-permute-done.26.refs_1_ = bf16[320,512]{1,0:T(8,128)(2,1)S(1)} collective-permute-done((bf16[320,512]{1,0:T(8,128)(2,1)S(1)}, bf16[320,512]{1,0:T(8,128)(2,1)S(1)}, u32[]{:S(2)}, u32[]{:S(2)}) %collective-permute-start.26) | collective-permute-done | bytes 327712 | tf_op jit(solution)/shard_map/ppermute | solution.py:511
  525.8 2.4 rope.3
  532.3 3.3 side_products.13
  535.7 6.8 %collective-permute-done.29.refs_1_ = bf16[256,1280]{1,0:T(8,128)(2,1)S(1)} collective-permute-done((bf16[256,1280]{1,0:T(8,128)(2,1)S(1)}, bf16[256,1280]{1,0:T(8,128)(2,1)S(1)}, u32[]{:S(2)}, u32[]{:S(2)}) %collective-permute-start.29) | collective-permute-done | bytes 655392 | tf_op jit(solution)/shard_map/ppermute | solution.py:511
  543.3 4.8 side_products.14
  548.4 8.1 %times_turned.3 = (bf16[320,2048]{1,0:T(8,128)(2,1)}, f32[8,128]{1,0:T(8,128)S(1)}) custom-call(bf16[320,1536]{1,0:T(8,128)(2,1)S(1)} %get-tuple-element.365.refs_0_, bf16[2048,2688]{1,0:T(8,128)(2,1)} %all-gather.3.cloned.1.call-done.refs_1_, f32[8,128]{1,0:T(8,128)S(1)} %get-tuple-element.254.refs_2_), custom_call_target="tpu_custom_call" | custom-call | flops 4499999744 | bytes 16200000 | tf_op jit(solution)/shard_map/times_turned/pallas_call | solution.py:63
  562.5 2.0 copy-done.34
  564.5 4.8 side_products.15
  570.4 2.3 fold.47
  573.4 2.1 collective-permute-start.36
  576.7 2.9 copy.55
  587.5 2.0 collective-permute-start.41
  589.5 5.6 norm_back.3
  595.1 2.1 fold.50
  598.1 9.7 %collective-permute-done.36.refs_1_ = bf16[256,1024]{1,0:T(8,128)(2,1)} collective-permute-done((bf16[256,1024]{1,0:T(8,128)(2,1)}, bf16[256,1024]{1,0:T(8,128)(2,1)}, u32[]{:S(2)}, u32[]{:S(2)}) %collective-permute-start.36) | collective-permute-done | bytes 524320 | tf_op jit(solution)/shard_map/ppermute | solution.py:511
  610.0 2.1 slice_select_fusion
  612.8 1.9 collective-permute-done.42.refs_1_
  617.9 3.8 collective-permute-done.41.refs_1_
  623.1 14.4 %collective-permute-done.40.refs_1_ = bf16[128,1536]{1,0:T(8,128)(2,1)S(1)} collective-permute-done((bf16[128,1536]{1,0:T(8,128)(2,1)}, bf16[128,1536]{1,0:T(8,128)(2,1)S(1)}, u32[]{:S(2)}, u32[]{:S(2)}) %collective-permute-start.40) | collective-permute-done | bytes 393248 | tf_op jit(solution)/shard_map/ppermute | solution.py:511
  641.6 1.8 collective-permute-start.43
  645.3 7.7 %collective-permute-done.46.refs_1_ = bf16[256,1280]{1,0:T(8,128)(2,1)S(1)} collective-permute-done((bf16[256,1280]{1,0:T(8,128)(2,1)S(1)}, bf16[256,1280]{1,0:T(8,128)(2,1)S(1)}, u32[]{:S(2)}, u32[]{:S(2)}) %collective-permute-start.46) | collective-permute-done | bytes 655392 | tf_op jit(solution)/shard_map/ppermute | solution.py:511
  653.2 2.0 pad_maximum_fusion
  656.2 2.0 collective-permute-start.45
  659.7 2.9 collective-permute-start.47
  (358 shorter events, 92.3 us)
Async XLA Ops:
  7.2 99.6 %all-gather.3.cloned.1.call-start = ((), (), s32[]{:S(2)}) async-start(), calls=%async_computation | async-start | bytes 11698176 | tf_op jit(solution)/shard_map/all_gather | solution.py:540
  12.9 300.4 %all-gather.5.cloned.1.call-start = ((), (), s32[]{:S(2)}) async-start(), calls=%async_computation.1 | async-start | bytes 36765696 | tf_op jit(solution)/shard_map/all_gather | solution.py:544
  24.1 84.9 %copy-start = (bf16[5,64,2048]{2,1,0:T(8,128)(2,1)}, bf16[5,64,2048]{2,1,0:T(8,128)(2,1)S(1)}, u32[]{:S(2)}) copy-start(bf16[5,64,2048]{2,1,0:T(8,128)(2,1)S(1)} %get-tuple-element.376) | copy-start | bytes 3932164
  24.1 228.9 %copy-start.5 = (bf16[5,64,2048]{2,1,0:T(8,128)(2,1)}, bf16[5,64,2048]{2,1,0:T(8,128)(2,1)S(1)}, u32[]{:S(2)}) copy-start(bf16[5,64,2048]{2,1,0:T(8,128)(2,1)S(1)} %get-tuple-element.375) | copy-start | bytes 3932164
  115.9 122.4 %copy-start.70 = (bf16[320,1024]{1,0:T(8,128)(2,1)}, bf16[320,1024]{1,0:T(8,128)(2,1)S(1)}, u32[]{:S(2)}) copy-start(bf16[320,1024]{1,0:T(8,128)(2,1)S(1)} %get-tuple-element.168.q_ref.refs_0_) | copy-start | bytes 1966084
  115.9 25.1 %collective-permute-start = (bf16[1,5,64,512]{3,2,1,0:T(8,128)(2,1)S(1)}, bf16[1,5,64,512]{3,2,1,0:T(8,128)(2,1)S(1)}, u32[]{:S(2)}, u32[]{:S(2)}) collective-permute-start(bf16[1,5,64,512]{3,2,1,0:T(8,128)(2,1)S(1)} %bitcast.59), channel_id=1, source_target_pairs={{0,16},{2,18},{4,20},{6,22},{8,24},{10,26},{12,28},{14,30},{16,0},... | collective-permute-start | bytes 983048 | tf_op jit(solution)/shard_map/ppermute | solution.py:511
  141.1 31.3 %collective-permute-start.1 = (bf16[2,5,64,512]{3,2,1,0:T(8,128)(2,1)S(1)}, bf16[2,5,64,512]{3,2,1,0:T(8,128)(2,1)S(1)}, u32[]{:S(2)}, u32[]{:S(2)}) collective-permute-start(bf16[2,5,64,512]{3,2,1,0:T(8,128)(2,1)S(1)} %pad_maximum_fusion.10), channel_id=1, source_target_pairs={{0,8},{2,10},{4,12},{6,14},{8,0},{10,2},{12,4},{14,6},{16,24},{18,... | collective-permute-start | bytes 1966088 | tf_op jit(solution)/shard_map/ppermute | solution.py:511
  172.4 60.8 %copy-start.92 = (s32[16]{0:T(128)S(1)}, s32[16]{0:T(128)}, u32[]{:S(2)}) copy-start(s32[16]{0:T(128)} %constant.56.clone) | copy-start | bytes 196
  172.5 59.0 %collective-permute-start.2 = (bf16[4,5,64,512]{3,2,1,0:T(8,128)(2,1)S(1)}, bf16[4,5,64,512]{3,2,1,0:T(8,128)(2,1)S(1)}, u32[]{:S(2)}, u32[]{:S(2)}) collective-permute-start(bf16[4,5,64,512]{3,2,1,0:T(8,128)(2,1)S(1)} %pad_maximum_fusion.7), channel_id=1, source_target_pairs={{0,4},{2,6},{4,0},{6,2},{8,12},{10,14},{12,8},{14,10},{16,20},{18,... | collective-permute-start | bytes 3932168 | tf_op jit(solution)/shard_map/ppermute | solution.py:511
  233.1 5.3 collective-permute-start.3
  251.5 31.0 %collective-permute-start.4 = (bf16[320,2048]{1,0:T(8,128)(2,1)S(1)}, bf16[320,2048]{1,0:T(8,128)(2,1)S(1)}, u32[]{:S(2)}, u32[]{:S(2)}) collective-permute-start(bf16[320,2048]{1,0:T(8,128)(2,1)S(1)} %fusion.6), channel_id=1, source_target_pairs={{0,1},{1,0},{2,3},{3,2},{4,5},{5,4},{6,7},{7,6},{8,9},{9,8},{10,11... | collective-permute-start | bytes 3932168 | tf_op jit(solution)/shard_map/ppermute | solution.py:514
  253.1 29.5 %copy-start.1 = (bf16[5,64,2048]{2,1,0:T(8,128)(2,1)S(1)}, bf16[5,64,2048]{2,1,0:T(8,128)(2,1)}, u32[]{:S(2)}) copy-start(bf16[5,64,2048]{2,1,0:T(8,128)(2,1)} %copy-done) | copy-start | bytes 3932164
  254.0 32.5 %collective-permute-start.5 = (bf16[320,1024]{1,0:T(8,128)(2,1)S(1)}, bf16[320,1024]{1,0:T(8,128)(2,1)S(1)}, u32[]{:S(2)}, u32[]{:S(2)}) collective-permute-start(bf16[320,1024]{1,0:T(8,128)(2,1)S(1)} %get-tuple-element.171), channel_id=1, source_target_pairs={{0,2},{2,0},{4,6},{6,4},{8,10},{10,8},{12,14},{14,12},{16,18},{18,... | collective-permute-start | bytes 1966088 | tf_op jit(solution)/shard_map/ppermute | solution.py:511
  255.8 30.6 %collective-permute-start.7 = (bf16[320,1024]{1,0:T(8,128)(2,1)S(1)}, bf16[320,1024]{1,0:T(8,128)(2,1)S(1)}, u32[]{:S(2)}, u32[]{:S(2)}) collective-permute-start(bf16[320,1024]{1,0:T(8,128)(2,1)S(1)} %get-tuple-element.173), channel_id=1, source_target_pairs={{0,2},{2,0},{4,6},{6,4},{8,10},{10,8},{12,14},{14,12},{16,18},{18,... | collective-permute-start | bytes 1966088 | tf_op jit(solution)/shard_map/ppermute | solution.py:511
  256.3 30.1 %collective-permute-start.8 = (bf16[320,1024]{1,0:T(8,128)(2,1)S(1)}, bf16[320,1024]{1,0:T(8,128)(2,1)S(1)}, u32[]{:S(2)}, u32[]{:S(2)}) collective-permute-start(bf16[320,1024]{1,0:T(8,128)(2,1)S(1)} %get-tuple-element.170), channel_id=1, source_target_pairs={{0,2},{2,0},{4,6},{6,4},{8,10},{10,8},{12,14},{14,12},{16,18},{18,... | collective-permute-start | bytes 1966088 | tf_op jit(solution)/shard_map/ppermute | solution.py:511
  286.4 2.1 collective-permute-start.6
  288.5 202.1 %copy-start.18 = (bf16[320,1024]{1,0:T(8,128)(2,1)}, bf16[320,1024]{1,0:T(8,128)(2,1)S(1)}, u32[]{:S(2)}) copy-start(bf16[320,1024]{1,0:T(8,128)(2,1)S(1)} %collective-permute-done.6.refs_1_) | copy-start | bytes 1966084
  323.2 8.2 %collective-permute-start.10 = (bf16[320,1536]{1,0:T(8,128)(2,1)S(1)}, bf16[320,1536]{1,0:T(8,128)(2,1)S(1)}, u32[]{:S(2)}, u32[]{:S(2)}) collective-permute-start(bf16[320,1536]{1,0:T(8,128)(2,1)S(1)} %get-tuple-element.174), channel_id=1, source_target_pairs={{0,2},{2,0},{4,6},{6,4},{8,10},{10,8},{12,14},{14,12},{16,18},{18,... | collective-permute-start | bytes 2949128 | tf_op jit(solution)/shard_map/ppermute | solution.py:511
  331.1 4.8 collective-permute-start.9
  335.7 36.6 %collective-permute-start.11 = (bf16[512,1536]{1,0:T(8,128)(2,1)S(1)}, bf16[512,1536]{1,0:T(8,128)(2,1)S(1)}, u32[]{:S(2)}, u32[]{:S(2)}) collective-permute-start(bf16[512,1536]{1,0:T(8,128)(2,1)S(1)} %get-tuple-element.189), channel_id=1, source_target_pairs={{0,4},{2,6},{4,0},{6,2},{8,12},{10,14},{12,8},{14,10},{16,20},{18,... | collective-permute-start | bytes 4718600 | tf_op jit(solution)/shard_map/ppermute | solution.py:511
  372.7 67.4 %copy-start.7 = (bf16[2,320,2816]{2,1,0:T(8,128)(2,1)}, bf16[2,320,2816]{2,1,0:T(8,128)(2,1)S(1)}, u32[]{:S(2)}) copy-start(bf16[2,320,2816]{2,1,0:T(8,128)(2,1)S(1)} %get-tuple-element.197.refs_2_) | copy-start | bytes 10813444
  372.7 6.4 collective-permute-start.14
  372.8 31.6 %collective-permute-start.13 = (bf16[512,1280]{1,0:T(8,128)(2,1)S(1)}, bf16[512,1280]{1,0:T(8,128)(2,1)S(1)}, u32[]{:S(2)}, u32[]{:S(2)}) collective-permute-start(bf16[512,1280]{1,0:T(8,128)(2,1)S(1)} %get-tuple-element.195), channel_id=1, source_target_pairs={{0,4},{2,6},{4,0},{6,2},{8,12},{10,14},{12,8},{14,10},{16,20},{18,... | collective-permute-start | bytes 3932168 | tf_op jit(solution)/shard_map/ppermute | solution.py:511
  373.2 31.6 %collective-permute-start.12 = (bf16[320,2048]{1,0:T(8,128)(2,1)S(1)}, bf16[320,2048]{1,0:T(8,128)(2,1)S(1)}, u32[]{:S(2)}, u32[]{:S(2)}) collective-permute-start(bf16[320,2048]{1,0:T(8,128)(2,1)S(1)} %get-tuple-element.193.refs_0_), channel_id=1, source_target_pairs={{0,1},{1,0},{2,3},{3,2},{4,5},{5,4},{6,7},{7,6},{8,9},{9,8},{10,11... | collective-permute-start | bytes 3932168 | tf_op jit(solution)/shard_map/ppermute | solution.py:514
  374.6 33.7 %collective-permute-start.15 = (bf16[256,1536]{1,0:T(8,128)(2,1)S(1)}, bf16[256,1536]{1,0:T(8,128)(2,1)S(1)}, u32[]{:S(2)}, u32[]{:S(2)}) collective-permute-start(bf16[256,1536]{1,0:T(8,128)(2,1)S(1)} %get-tuple-element.203), channel_id=1, source_target_pairs={{0,8},{2,10},{4,12},{6,14},{8,0},{10,2},{12,4},{14,6},{16,24},{18,... | collective-permute-start | bytes 2359304 | tf_op jit(solution)/shard_map/ppermute | solution.py:511
  379.1 61.0 %copy-start.32 = (bf16[2,320,2816]{2,1,0:T(8,128)(2,1)}, bf16[2,320,2816]{2,1,0:T(8,128)(2,1)S(1)}, u32[]{:S(2)}) copy-start(bf16[2,320,2816]{2,1,0:T(8,128)(2,1)S(1)} %collective-permute-done.14.refs_3_) | copy-start | bytes 10813444
  383.2 54.5 %collective-permute-start.18 = (bf16[512,1536]{1,0:T(8,128)(2,1)S(1)}, bf16[512,1536]{1,0:T(8,128)(2,1)S(1)}, u32[]{:S(2)}, u32[]{:S(2)}) collective-permute-start(bf16[512,1536]{1,0:T(8,128)(2,1)S(1)} %get-tuple-element.212), channel_id=1, source_target_pairs={{0,4},{2,6},{4,0},{6,2},{8,12},{10,14},{12,8},{14,10},{16,20},{18,... | collective-permute-start | bytes 4718600 | tf_op jit(solution)/shard_map/ppermute | solution.py:511
  408.1 4.4 collective-permute-start.16
  408.2 31.6 %collective-permute-start.17 = (bf16[256,1280]{1,0:T(8,128)(2,1)S(1)}, bf16[256,1280]{1,0:T(8,128)(2,1)S(1)}, u32[]{:S(2)}, u32[]{:S(2)}) collective-permute-start(bf16[256,1280]{1,0:T(8,128)(2,1)S(1)} %get-tuple-element.210), channel_id=1, source_target_pairs={{0,8},{2,10},{4,12},{6,14},{8,0},{10,2},{12,4},{14,6},{16,24},{18,... | collective-permute-start | bytes 1966088 | tf_op jit(solution)/shard_map/ppermute | solution.py:511
  425.2 13.7 %copy-start.26 = (bf16[320,1024]{1,0:T(8,128)(2,1)}, bf16[320,1024]{1,0:T(8,128)(2,1)S(1)}, u32[]{:S(2)}) copy-start(bf16[320,1024]{1,0:T(8,128)(2,1)S(1)} %get-tuple-element.221) | copy-start | bytes 1966084
  440.0 5.0 collective-permute-start.19
  446.0 31.6 %collective-permute-start.21 = (bf16[1280,512]{1,0:T(8,128)(2,1)S(1)}, bf16[1280,512]{1,0:T(8,128)(2,1)S(1)}, u32[]{:S(2)}, u32[]{:S(2)}) collective-permute-start(bf16[1280,512]{1,0:T(8,128)(2,1)S(1)} %get-tuple-element.223), channel_id=1, source_target_pairs={{0,4},{2,6},{4,0},{6,2},{8,12},{10,14},{12,8},{14,10},{16,20},{18,... | collective-permute-start | bytes 3932168 | tf_op jit(solution)/shard_map/ppermute | solution.py:511
  446.3 59.1 %collective-permute-start.24 = (bf16[512,1280]{1,0:T(8,128)(2,1)}, bf16[512,1280]{1,0:T(8,128)(2,1)}, u32[]{:S(2)}, u32[]{:S(2)}) collective-permute-start(bf16[512,1280]{1,0:T(8,128)(2,1)} %get-tuple-element.231), channel_id=1, source_target_pairs={{0,4},{2,6},{4,0},{6,2},{8,12},{10,14},{12,8},{14,10},{16,20},{18,... | collective-permute-start | bytes 3932168 | tf_op jit(solution)/shard_map/ppermute | solution.py:511
  448.1 20.3 %collective-permute-start.22 = (bf16[128,1536]{1,0:T(8,128)(2,1)S(1)}, bf16[128,1536]{1,0:T(8,128)(2,1)S(1)}, u32[]{:S(2)}, u32[]{:S(2)}) collective-permute-start(bf16[128,1536]{1,0:T(8,128)(2,1)S(1)} %get-tuple-element.225), channel_id=1, source_target_pairs={{0,16},{2,18},{4,20},{6,22},{8,24},{10,26},{12,28},{14,30},{16,0},... | collective-permute-start | bytes 1179656 | tf_op jit(solution)/shard_map/ppermute | solution.py:511
  448.2 39.2 %collective-permute-start.25 = (bf16[256,1536]{1,0:T(8,128)(2,1)}, bf16[256,1536]{1,0:T(8,128)(2,1)}, u32[]{:S(2)}, u32[]{:S(2)}) collective-permute-start(bf16[256,1536]{1,0:T(8,128)(2,1)} %get-tuple-element.233), channel_id=1, source_target_pairs={{0,8},{2,10},{4,12},{6,14},{8,0},{10,2},{12,4},{14,6},{16,24},{18,... | collective-permute-start | bytes 2359304 | tf_op jit(solution)/shard_map/ppermute | solution.py:511
  460.5 18.2 %copy-start.12 = (bf16[320,2048]{1,0:T(8,128)(2,1)}, bf16[320,2048]{1,0:T(8,128)(2,1)S(1)}, u32[]{:S(2)}) copy-start(bf16[320,2048]{1,0:T(8,128)(2,1)S(1)} %get-tuple-element.220) | copy-start | bytes 3932164
  479.5 27.5 %collective-permute-start.23 = (bf16[640,512]{1,0:T(8,128)(2,1)}, bf16[640,512]{1,0:T(8,128)(2,1)}, u32[]{:S(2)}, u32[]{:S(2)}) collective-permute-start(bf16[640,512]{1,0:T(8,128)(2,1)} %get-tuple-element.229), channel_id=1, source_target_pairs={{0,8},{2,10},{4,12},{6,14},{8,0},{10,2},{12,4},{14,6},{16,24},{18,... | collective-permute-start | bytes 1966088 | tf_op jit(solution)/shard_map/ppermute | solution.py:511
  482.8 29.0 %collective-permute-start.27 = (bf16[128,1280]{1,0:T(8,128)(2,1)}, bf16[128,1280]{1,0:T(8,128)(2,1)S(1)}, u32[]{:S(2)}, u32[]{:S(2)}) collective-permute-start(bf16[128,1280]{1,0:T(8,128)(2,1)} %copy-done.45), channel_id=1, source_target_pairs={{0,16},{2,18},{4,20},{6,22},{8,24},{10,26},{12,28},{14,30},{16,0},... | collective-permute-start | bytes 983048 | tf_op jit(solution)/shard_map/ppermute | solution.py:511
  486.0 42.5 %collective-permute-start.20 = (bf16[320,2048]{1,0:T(8,128)(2,1)}, bf16[320,2048]{1,0:T(8,128)(2,1)S(1)}, u32[]{:S(2)}, u32[]{:S(2)}) collective-permute-start(bf16[320,2048]{1,0:T(8,128)(2,1)} %copy-done.12), channel_id=1, source_target_pairs={{0,1},{1,0},{2,3},{3,2},{4,5},{5,4},{6,7},{7,6},{8,9},{9,8},{10,11... | collective-permute-start | bytes 3932168 | tf_op jit(solution)/shard_map/ppermute | solution.py:514
  508.3 17.4 %collective-permute-start.26 = (bf16[320,512]{1,0:T(8,128)(2,1)S(1)}, bf16[320,512]{1,0:T(8,128)(2,1)S(1)}, u32[]{:S(2)}, u32[]{:S(2)}) collective-permute-start(bf16[320,512]{1,0:T(8,128)(2,1)S(1)} %get-tuple-element.239), channel_id=1, source_target_pairs={{0,16},{2,18},{4,20},{6,22},{8,24},{10,26},{12,28},{14,30},{16,0},... | collective-permute-start | bytes 983048 | tf_op jit(solution)/shard_map/ppermute | solution.py:511
  508.4 34.1 %collective-permute-start.29 = (bf16[256,1280]{1,0:T(8,128)(2,1)S(1)}, bf16[256,1280]{1,0:T(8,128)(2,1)S(1)}, u32[]{:S(2)}, u32[]{:S(2)}) collective-permute-start(bf16[256,1280]{1,0:T(8,128)(2,1)S(1)} %get-tuple-element.249), channel_id=1, source_target_pairs={{0,8},{2,10},{4,12},{6,14},{8,0},{10,2},{12,4},{14,6},{16,24},{18,... | collective-permute-start | bytes 1966088 | tf_op jit(solution)/shard_map/ppermute | solution.py:511
  511.5 48.8 %collective-permute-start.34 = (bf16[512,1536]{1,0:T(8,128)(2,1)}, bf16[512,1536]{1,0:T(8,128)(2,1)S(1)}, u32[]{:S(2)}, u32[]{:S(2)}) collective-permute-start(bf16[512,1536]{1,0:T(8,128)(2,1)} %get-tuple-element.264), channel_id=1, source_target_pairs={{0,4},{2,6},{4,0},{6,2},{8,12},{10,14},{12,8},{14,10},{16,20},{18,... | collective-permute-start | bytes 4718600 | tf_op jit(solution)/shard_map/ppermute | solution.py:511
  511.8 67.8 %collective-permute-start.32 = (bf16[128,1536]{1,0:T(8,128)(2,1)}, bf16[128,1536]{1,0:T(8,128)(2,1)}, u32[]{:S(2)}, u32[]{:S(2)}) collective-permute-start(bf16[128,1536]{1,0:T(8,128)(2,1)} %get-tuple-element.260), channel_id=1, source_target_pairs={{0,16},{2,18},{4,20},{6,22},{8,24},{10,26},{12,28},{14,30},{16,0},... | collective-permute-start | bytes 1179656 | tf_op jit(solution)/shard_map/ppermute | solution.py:511
  528.4 14.9 %collective-permute-start.28 = (bf16[320,1536]{1,0:T(8,128)(2,1)S(1)}, bf16[320,1536]{1,0:T(8,128)(2,1)S(1)}, u32[]{:S(2)}, u32[]{:S(2)}) collective-permute-start(bf16[320,1536]{1,0:T(8,128)(2,1)S(1)} %get-tuple-element.365.refs_0_), channel_id=1, source_target_pairs={{0,2},{2,0},{4,6},{6,4},{8,10},{10,8},{12,14},{14,12},{16,18},{18,... | collective-permute-start | bytes 2949128 | tf_op jit(solution)/shard_map/ppermute | solution.py:511
  535.7 34.7 %collective-permute-start.33 = (bf16[512,1024]{1,0:T(8,128)(2,1)}, bf16[512,1024]{1,0:T(8,128)(2,1)}, u32[]{:S(2)}, u32[]{:S(2)}) collective-permute-start(bf16[512,1024]{1,0:T(8,128)(2,1)} %get-tuple-element.262), channel_id=1, source_target_pairs={{0,8},{2,10},{4,12},{6,14},{8,0},{10,2},{12,4},{14,6},{16,24},{18,... | collective-permute-start | bytes 3145736 | tf_op jit(solution)/shard_map/ppermute | solution.py:511
  548.1 35.5 %collective-permute-start.31 = (bf16[512,1536]{1,0:T(8,128)(2,1)}, bf16[512,1536]{1,0:T(8,128)(2,1)S(1)}, u32[]{:S(2)}, u32[]{:S(2)}) collective-permute-start(bf16[512,1536]{1,0:T(8,128)(2,1)} %get-tuple-element.258), channel_id=1, source_target_pairs={{0,4},{2,6},{4,0},{6,2},{8,12},{10,14},{12,8},{14,10},{16,20},{18,... | collective-permute-start | bytes 4718600 | tf_op jit(solution)/shard_map/ppermute | solution.py:511
  556.6 30.9 %collective-permute-start.30 = (bf16[320,2048]{1,0:T(8,128)(2,1)}, bf16[320,2048]{1,0:T(8,128)(2,1)}, u32[]{:S(2)}, u32[]{:S(2)}) collective-permute-start(bf16[320,2048]{1,0:T(8,128)(2,1)} %get-tuple-element.255.refs_0_), channel_id=1, source_target_pairs={{0,1},{1,0},{2,3},{3,2},{4,5},{5,4},{6,7},{7,6},{8,9},{9,8},{10,11... | collective-permute-start | bytes 3932168 | tf_op jit(solution)/shard_map/ppermute | solution.py:514
  562.4 32.7 %collective-permute-start.37 = (bf16[256,1536]{1,0:T(8,128)(2,1)}, bf16[256,1536]{1,0:T(8,128)(2,1)}, u32[]{:S(2)}, u32[]{:S(2)}) collective-permute-start(bf16[256,1536]{1,0:T(8,128)(2,1)} %get-tuple-element.277), channel_id=1, source_target_pairs={{0,8},{2,10},{4,12},{6,14},{8,0},{10,2},{12,4},{14,6},{16,24},{18,... | collective-permute-start | bytes 2359304 | tf_op jit(solution)/shard_map/ppermute | solution.py:511
  573.4 34.3 %collective-permute-start.36 = (bf16[256,1024]{1,0:T(8,128)(2,1)}, bf16[256,1024]{1,0:T(8,128)(2,1)}, u32[]{:S(2)}, u32[]{:S(2)}) collective-permute-start(bf16[256,1024]{1,0:T(8,128)(2,1)} %get-tuple-element.275), channel_id=1, source_target_pairs={{0,16},{2,18},{4,20},{6,22},{8,24},{10,26},{12,28},{14,30},{16,0},... | collective-permute-start | bytes 1572872 | tf_op jit(solution)/shard_map/ppermute | solution.py:511
  579.6 35.0 %collective-permute-start.42 = (bf16[128,1280]{1,0:T(8,128)(2,1)}, bf16[128,1280]{1,0:T(8,128)(2,1)}, u32[]{:S(2)}, u32[]{:S(2)}) collective-permute-start(bf16[128,1280]{1,0:T(8,128)(2,1)} %get-tuple-element.289), channel_id=1, source_target_pairs={{0,16},{2,18},{4,20},{6,22},{8,24},{10,26},{12,28},{14,30},{16,0},... | collective-permute-start | bytes 983048 | tf_op jit(solution)/shard_map/ppermute | solution.py:511
  583.6 53.9 %collective-permute-start.39 = (bf16[512,1280]{1,0:T(8,128)(2,1)}, bf16[512,1280]{1,0:T(8,128)(2,1)}, u32[]{:S(2)}, u32[]{:S(2)}) collective-permute-start(bf16[512,1280]{1,0:T(8,128)(2,1)} %get-tuple-element.283), channel_id=1, source_target_pairs={{0,4},{2,6},{4,0},{6,2},{8,12},{10,14},{12,8},{14,10},{16,20},{18,... | collective-permute-start | bytes 3932168 | tf_op jit(solution)/shard_map/ppermute | solution.py:511
  587.5 34.2 %collective-permute-start.41 = (bf16[256,1536]{1,0:T(8,128)(2,1)}, bf16[256,1536]{1,0:T(8,128)(2,1)}, u32[]{:S(2)}, u32[]{:S(2)}) collective-permute-start(bf16[256,1536]{1,0:T(8,128)(2,1)} %get-tuple-element.287), channel_id=1, source_target_pairs={{0,8},{2,10},{4,12},{6,14},{8,0},{10,2},{12,4},{14,6},{16,24},{18,... | collective-permute-start | bytes 2359304 | tf_op jit(solution)/shard_map/ppermute | solution.py:511
  595.1 14.9 %copy-start.82 = (f32[6,64,2048]{2,1,0:T(8,128)S(1)}, f32[6,64,2048]{2,1,0:T(8,128)}, u32[]{:S(2)}) copy-start(f32[6,64,2048]{2,1,0:T(8,128)} %convert_element_type.98) | copy-start | bytes 9437188
  598.0 39.5 %collective-permute-start.40 = (bf16[128,1536]{1,0:T(8,128)(2,1)}, bf16[128,1536]{1,0:T(8,128)(2,1)S(1)}, u32[]{:S(2)}, u32[]{:S(2)}) collective-permute-start(bf16[128,1536]{1,0:T(8,128)(2,1)} %get-tuple-element.285), channel_id=1, source_target_pairs={{0,16},{2,18},{4,20},{6,22},{8,24},{10,26},{12,28},{14,30},{16,0},... | collective-permute-start | bytes 1179656 | tf_op jit(solution)/shard_map/ppermute | solution.py:511
  609.7 30.9 %collective-permute-start.38 = (bf16[128,1024]{1,0:T(8,128)(2,1)S(1)}, bf16[128,1024]{1,0:T(8,128)(2,1)}, u32[]{:S(2)}, u32[]{:S(2)}) collective-permute-start(bf16[128,1024]{1,0:T(8,128)(2,1)S(1)} %get-tuple-element.281), channel_id=1, source_target_pairs={{0,4},{2,6},{4,0},{6,2},{8,12},{10,14},{12,8},{14,10},{16,20},{18,... | collective-permute-start | bytes 786440 | tf_op jit(solution)/shard_map/ppermute | solution.py:511
  614.7 26.9 %collective-permute-start.35 = (f32[8,256]{1,0:T(8,128)S(1)}, f32[8,256]{1,0:T(8,128)S(1)}, u32[]{:S(2)}, u32[]{:S(2)}) collective-permute-start(f32[8,256]{1,0:T(8,128)S(1)} %bitcast.79), channel_id=1, source_target_pairs={{0,2},{2,0},{4,6},{6,4},{8,10},{10,8},{12,14},{14,12},{16,18},{18,... | collective-permute-start | bytes 24584 | tf_op jit(solution)/shard_map/ppermute | solution.py:511
  617.9 19.6 %copy-start.69 = (bf16[128,1536]{1,0:T(8,128)(2,1)S(1)}, bf16[128,1536]{1,0:T(8,128)(2,1)}, u32[]{:S(2)}) copy-start(bf16[128,1536]{1,0:T(8,128)(2,1)} %copy-done.68) | copy-start | bytes 1179652
  623.0 14.6 %copy-start.47 = (bf16[512,1280]{1,0:T(8,128)(2,1)S(1)}, bf16[512,1280]{1,0:T(8,128)(2,1)}, u32[]{:S(2)}) copy-start(bf16[512,1280]{1,0:T(8,128)(2,1)} %copy-done.46) | copy-start | bytes 3932164
  623.0 20.4 %collective-permute-start.44 = (bf16[128,1536]{1,0:T(8,128)(2,1)S(1)}, bf16[128,1536]{1,0:T(8,128)(2,1)S(1)}, u32[]{:S(2)}, u32[]{:S(2)}) collective-permute-start(bf16[128,1536]{1,0:T(8,128)(2,1)S(1)} %get-tuple-element.299), channel_id=1, source_target_pairs={{0,16},{2,18},{4,20},{6,22},{8,24},{10,26},{12,28},{14,30},{16,0},... | collective-permute-start | bytes 1179656 | tf_op jit(solution)/shard_map/ppermute | solution.py:511
  639.3 13.7 %collective-permute-start.46 = (bf16[256,1280]{1,0:T(8,128)(2,1)S(1)}, bf16[256,1280]{1,0:T(8,128)(2,1)S(1)}, u32[]{:S(2)}, u32[]{:S(2)}) collective-permute-start(bf16[256,1280]{1,0:T(8,128)(2,1)S(1)} %get-tuple-element.305), channel_id=1, source_target_pairs={{0,8},{2,10},{4,12},{6,14},{8,0},{10,2},{12,4},{14,6},{16,24},{18,... | collective-permute-start | bytes 1966088 | tf_op jit(solution)/shard_map/ppermute | solution.py:511
  641.6 3.7 collective-permute-start.43
  653.1 10.5 %collective-permute-start.48 = (bf16[128,1280]{1,0:T(8,128)(2,1)S(1)}, bf16[128,1280]{1,0:T(8,128)(2,1)S(1)}, u32[]{:S(2)}, u32[]{:S(2)}) collective-permute-start(bf16[128,1280]{1,0:T(8,128)(2,1)S(1)} %get-tuple-element.311), channel_id=1, source_target_pairs={{0,16},{2,18},{4,20},{6,22},{8,24},{10,26},{12,28},{14,30},{16,0},... | collective-permute-start | bytes 983048 | tf_op jit(solution)/shard_map/ppermute | solution.py:511
  656.2 3.6 collective-permute-start.45
  659.7 4.5 collective-permute-start.47
  (82 other events, 307.4 us)
Sparse Core Ops, SparseCore 0:
  13.0 93.7 all-gather.2
  108.4 204.8 all-gather.4

commit v6 on v3

--- a/solution.py
+++ b/solution.py
@@ -16,7 +16,7 @@
 
 def hint(microseconds):
     return pl.CostEstimate(
-        flops=int(microseconds * 5e8), bytes_accessed=int(microseconds * 1.8e6), transcendentals=0
+        flops=int(microseconds * 3.5e8), bytes_accessed=int(microseconds * 1.26e6), transcendentals=0
     )
 
 

time: 682 us -> 693 us (1.016)
  waiting for transfers between devices: 372 us -> 381 us
    ppermute x45, waiting for transfers between devices: 243 us -> 252 us  [flip(): return lax.ppermute(v, 'dp', [(i, i ^ bits) for i in range(n_dp)])]
    unnamed x202 -> x176, local copies, waits for them, and re-layouts: 41.1 us -> 40.1 us
  transfers between devices with their start and end apart: 51 -> 51, of which waited for: 26 -> 25; matrix products, arithmetic and copies ran while one was open for 7% -> 7% of each run, Pallas kernels for 22% -> 21%
where the time goes in v6:
time: 693 us; the launch traced here: 683 us
  waiting for transfers between devices  381 us (55%)
  Pallas kernels  155 us (22%)
  local copies, waits for them, and re-layouts  45 us (6%)
  starting transfers between devices  42.3 us (6%)
  other arithmetic  27.6 us (4%)
  between operations  19 us (3%)
  matrix products  13.5 us (2%)
    ppermute x45, waiting for transfers between devices, flip(): return lax.ppermute(v, 'dp', [(i, i ^ bits) for i in range(n_dp)])  252 us
    pallas_call x54, Pallas kernels, call(): pl.pallas_call(body, grid=grid, in_specs=[*in_specs, *[unread] * len(wait...  143 us
    all_gather x1, waiting for transfers between devices, local(): lax.all_gather(jnp.concatenate([query_weight, key_weight, value_weight, o...  82 us
    unnamed x176, local copies, waits for them, and re-layouts  40.1 us
    ppermute x45, starting transfers between devices, flip(): return lax.ppermute(v, 'dp', [(i, i ^ bits) for i in range(n_dp)])  36.3 us
    ppermute x4, waiting for transfers between devices, tensor_flip(): return lax.ppermute(v, 'tensor', [(0, 1), (1, 0)])  25.1 us
    all_gather x1, waiting for transfers between devices, local(): lax.all_gather(jnp.concatenate([gate_weight, up_weight, down_weight.T], a...  21.5 us
  transfers between devices with their start and end apart: 51, of which 25 were waited for; matrix products, arithmetic and copies ran while one was open for 7% of the time, Pallas kernels for 21%

profile of v6, /device:TPU:0, one launch (start us, length us, event | category | flops | bytes accessed | tf_op | source)
XLA Modules:
  0.0 683.1 jit_solution(9309268887550984722)
XLA Ops:
  13.2 2.6 pad_maximum_fusion.2
  21.6 2.4 slice_select_fusion.1
  24.8 82.0 %all-gather.3.cloned.1.call-done.refs_1_ = bf16[2048,2688]{1,0:T(8,128)(2,1)} async-done(((bf16[128,2688]{1,0:T(8,128)(2,1)}), bf16[2048,2688]{1,0:T(8,128)(2,1)}) %all-gather.3.cloned.1.call-update) | async-done | bytes 11010064 | tf_op jit(solution)/shard_map/all_gather | solution.py:540
  106.8 1.9 convert_reduce_fusion
  109.7 5.4 fusion.refs_0_
  117.6 23.5 %collective-permute-done = bf16[1,5,64,512]{3,2,1,0:T(8,128)(2,1)S(1)} collective-permute-done((bf16[1,5,64,512]{3,2,1,0:T(8,128)(2,1)S(1)}, bf16[1,5,64,512]{3,2,1,0:T(8,128)(2,1)S(1)}, u32[]{:S(2)}, u32[]{:S(2)}) %collective-permute-start) | collective-permute-done | bytes 327712 | tf_op jit(solution)/shard_map/ppermute | solution.py:511
  141.2 31.2 %collective-permute-done.1 = bf16[2,5,64,512]{3,2,1,0:T(8,128)(2,1)S(1)} collective-permute-done((bf16[2,5,64,512]{3,2,1,0:T(8,128)(2,1)S(1)}, bf16[2,5,64,512]{3,2,1,0:T(8,128)(2,1)S(1)}, u32[]{:S(2)}, u32[]{:S(2)}) %collective-permute-start.1) | collective-permute-done | bytes 655392 | tf_op jit(solution)/shard_map/ppermute | solution.py:511
  173.2 58.4 %collective-permute-done.2 = bf16[4,5,64,512]{3,2,1,0:T(8,128)(2,1)S(1)} collective-permute-done((bf16[4,5,64,512]{3,2,1,0:T(8,128)(2,1)S(1)}, bf16[4,5,64,512]{3,2,1,0:T(8,128)(2,1)S(1)}, u32[]{:S(2)}, u32[]{:S(2)}) %collective-permute-start.2) | collective-permute-done | bytes 1310752 | tf_op jit(solution)/shard_map/ppermute | solution.py:511
  233.5 4.9 collective-permute-done.3.far_ref.refs_2_
  238.5 8.6 %attend.1 = (bf16[320,1024]{1,0:T(8,128)(2,1)S(1)}, f32[10,256,1]{2,1,0:T(8,128)S(1)}) custom-call(bf16[320,1024]{1,0:T(8,128)(2,1)S(1)} %get-tuple-element.168.q_ref.refs_0_, bf16[8,5,64,512]{3,2,1,0:T(8,128)(2,1)} %pad_maximum_fusion.1.near_ref.refs_1_, bf16[8,5,64,512]{3,2,1,0:T(8,128)(2,1)} %collective-permute-done.3.far_ref.refs_2_, ...), custom_call_target="tpu_custom_call" | custom-call | flops 3150000128 | bytes 11340000 | tf_op jit(solution)/shard_map/attend/pallas_call | solution.py:149
  248.2 4.3 fusion.6
  258.0 25.1 %collective-permute-done.4 = bf16[320,2048]{1,0:T(8,128)(2,1)S(1)} collective-permute-done((bf16[320,2048]{1,0:T(8,128)(2,1)S(1)}, bf16[320,2048]{1,0:T(8,128)(2,1)S(1)}, u32[]{:S(2)}, u32[]{:S(2)}) %collective-permute-start.4) | collective-permute-done | bytes 1310752 | tf_op jit(solution)/shard_map/ppermute | solution.py:514
  287.1 2.1 collective-permute-done.6.refs_1_
  291.7 21.5 %all-gather.5.cloned.1.call-done.refs_1_.refs_2_.refs_3_.refs_4_.refs_5_ = bf16[2048,8448]{1,0:T(8,128)(2,1)} async-done(((bf16[128,8448]{1,0:T(8,128)(2,1)}), bf16[2048,8448]{1,0:T(8,128)(2,1)}) %all-gather.5.cloned.1.call-update) | async-done | bytes 34603024 | tf_op jit(solution)/shard_map/all_gather | solution.py:544
  314.6 8.6 %feed_forward.2 = (f32[320,2816]{1,0:T(8,128)S(1)}, f32[320,2816]{1,0:T(8,128)S(1)}, bf16[320,1536]{1,0:T(8,128)(2,1)S(1)}, f32[8,128]{1,0:T(8,128)S(1)}) custom-call(bf16[320,2048]{1,0:T(8,128)(2,1)S(1)} %copy-done.10, bf16[2048,8448]{1,0:T(8,128)(2,1)} %all-gather.5.cloned.1.call-done.refs_1_.refs_2_.refs_3_.refs_4_.refs_5_, ...), custom_call_target="tpu_custom_call" | custom-call | flops 3245454592 | bytes 11683636 | tf_op jit(solution)/shard_map/feed_forward/pallas_call | solution.py:63
  323.5 7.6 %feed_forward.3 = (f32[320,2816]{1,0:T(8,128)S(1)}, f32[320,2816]{1,0:T(8,128)S(1)}, bf16[320,1280]{1,0:T(8,128)(2,1)S(1)}, f32[8,128]{1,0:T(8,128)S(1)}) custom-call(bf16[320,2048]{1,0:T(8,128)(2,1)S(1)} %copy-done.10, ...), custom_call_target="tpu_custom_call", output_to_operand_aliasing={{0}: (3, {}), {1}: (4, {})} | custom-call | flops 2704545536 | bytes 9736363 | tf_op jit(solution)/shard_map/feed_forward/pallas_call | solution.py:63
  331.4 4.2 side_products.8
  335.8 2.9 side_products.9
  338.7 27.0 %feed_forward_back.1 = (bf16[2,320,2816]{2,1,0:T(8,128)(2,1)S(1)}, bf16[320,2048]{1,0:T(8,128)(2,1)S(1)}, f32[8,128]{1,0:T(8,128)S(1)}) custom-call(bf16[320,2048]{1,0:T(8,128)(2,1)S(1)} %bitcast.55, f32[320,2816]{1,0:T(8,128)S(1)} %get-tuple-element.180.refs_1_, f32[320,2816]{1,0:T(8,128)S(1)} %get-tuple-element.181.refs_2_, ...), custom_call_target="tpu_custom_call" | custom-call | flops 9799999488 | bytes 35280000 | tf_op jit(solution)/shard_map/feed_forward_back/pallas_call | solution.py:63
  365.8 6.5 collective-permute-done.11.refs_1_
  374.6 4.5 collective-permute-done.14.refs_3_
  379.0 4.1 side_products.10
  383.5 20.9 %collective-permute-done.13.refs_1_ = bf16[512,1280]{1,0:T(8,128)(2,1)S(1)} collective-permute-done((bf16[512,1280]{1,0:T(8,128)(2,1)S(1)}, bf16[512,1280]{1,0:T(8,128)(2,1)S(1)}, u32[]{:S(2)}, u32[]{:S(2)}) %collective-permute-start.13) | collective-permute-done | bytes 1310752 | tf_op jit(solution)/shard_map/ppermute | solution.py:511
  404.7 2.4 norm_back.2
  409.7 3.8 fusion.12.refs_6_
  414.6 12.6 %attend_back.1 = (bf16[320,1024]{1,0:T(8,128)(2,1)S(1)}, bf16[8,5,64,512]{3,2,1,0:T(8,128)(2,1)S(1)}, bf16[8,5,64,512]{3,2,1,0:T(8,128)(2,1)S(1)}, f32[8,128]{1,0:T(8,128)S(1)}) custom-call(bf16[320,1024]{1,0:T(8,128)(2,1)S(1)} %copy-done.60, bf16[8,5,64,512]{3,2,1,0:T(8,128)(2,1)} %pad_maximum_fusion.1.near_ref.refs_1_, ...), custom_call_target="tpu_custom_call" | custom-call | flops 4550000128 | bytes 16380000 | tf_op jit(solution)/shard_map/attend_back/pallas_call | solution.py:63
  427.3 10.3 %collective-permute-done.18.refs_1_ = bf16[512,1536]{1,0:T(8,128)(2,1)S(1)} collective-permute-done((bf16[512,1536]{1,0:T(8,128)(2,1)S(1)}, bf16[512,1536]{1,0:T(8,128)(2,1)S(1)}, u32[]{:S(2)}, u32[]{:S(2)}) %collective-permute-start.18) | collective-permute-done | bytes 1572896 | tf_op jit(solution)/shard_map/ppermute | solution.py:511
  440.6 4.8 side_products.11
  446.8 3.2 collective-permute-start.25
  451.9 10.0 %times_turned.2 = (bf16[320,2048]{1,0:T(8,128)(2,1)}, f32[8,128]{1,0:T(8,128)S(1)}) custom-call(bf16[320,2816]{1,0:T(8,128)(2,1)S(1)} %pad_maximum_fusion.3.refs_0_, bf16[2048,8448]{1,0:T(8,128)(2,1)} %all-gather.5.cloned.1.call-done.refs_1_.refs_2_.refs_3_.refs_4_.refs_5_, f32[8,128]{1,0:T(8,128)S(1)} %get-tuple-element.219.refs_2_), custom_call_target="tpu_custom_call" | custom-call | flops 3150000128 | bytes 11340000 | tf_op jit(solution)/shard_map/times_turned/pallas_call | solution.py:63
  461.9 5.6 collective-permute-done.22.refs_1_
  468.4 9.7 %collective-permute-done.21.refs_1_ = bf16[1280,512]{1,0:T(8,128)(2,1)S(1)} collective-permute-done((bf16[1280,512]{1,0:T(8,128)(2,1)S(1)}, bf16[1280,512]{1,0:T(8,128)(2,1)S(1)}, u32[]{:S(2)}, u32[]{:S(2)}) %collective-permute-start.21) | collective-permute-done | bytes 1310752 | tf_op jit(solution)/shard_map/ppermute | solution.py:511
  481.5 2.0 convert_element_type.98
  484.8 3.3 collective-permute-start.27
  489.3 2.0 fold.40
  492.0 2.0 copy-done.1
  494.0 2.0 copy-done.4
  496.0 5.0 side_products.12
  501.0 4.9 collective-permute-done.24.refs_1_
  508.9 3.3 collective-permute-start.29
  512.6 13.8 %collective-permute-done.26.refs_1_ = bf16[320,512]{1,0:T(8,128)(2,1)S(1)} collective-permute-done((bf16[320,512]{1,0:T(8,128)(2,1)S(1)}, bf16[320,512]{1,0:T(8,128)(2,1)S(1)}, u32[]{:S(2)}, u32[]{:S(2)}) %collective-permute-start.26) | collective-permute-done | bytes 327712 | tf_op jit(solution)/shard_map/ppermute | solution.py:511
  526.6 2.4 rope.3
  529.2 2.4 add_convert_fusion
  533.3 3.4 side_products.13
  536.7 4.7 collective-permute-done.29.refs_1_
  541.7 4.9 side_products.14
  548.0 8.0 %times_turned.3 = (bf16[320,2048]{1,0:T(8,128)(2,1)}, f32[8,128]{1,0:T(8,128)S(1)}) custom-call(bf16[320,1536]{1,0:T(8,128)(2,1)S(1)} %get-tuple-element.365.refs_0_, bf16[2048,2688]{1,0:T(8,128)(2,1)} %all-gather.3.cloned.1.call-done.refs_1_, f32[8,128]{1,0:T(8,128)S(1)} %get-tuple-element.254.refs_2_), custom_call_target="tpu_custom_call" | custom-call | flops 3150000128 | bytes 11340000 | tf_op jit(solution)/shard_map/times_turned/pallas_call | solution.py:63
  560.1 3.0 copy.55
  565.3 2.0 copy-done.2
  567.3 2.0 copy-done.5
  569.3 4.8 side_products.15
  574.1 3.3 collective-permute-start.37
  582.9 2.5 collective-permute-done.31.refs_1_
  585.4 2.6 fold.49
  588.0 3.5 collective-permute-start.41
  591.4 5.7 norm_back.3
  597.1 1.9 slice_select_fusion
  599.9 7.2 %collective-permute-done.37.refs_1_ = bf16[256,1536]{1,0:T(8,128)(2,1)S(1)} collective-permute-done((bf16[256,1536]{1,0:T(8,128)(2,1)S(1)}, bf16[256,1536]{1,0:T(8,128)(2,1)S(1)}, u32[]{:S(2)}, u32[]{:S(2)}) %collective-permute-start.37) | collective-permute-done | bytes 786464 | tf_op jit(solution)/shard_map/ppermute | solution.py:511
  614.0 17.4 %collective-permute-done.41.refs_1_ = bf16[256,1536]{1,0:T(8,128)(2,1)} collective-permute-done((bf16[256,1536]{1,0:T(8,128)(2,1)}, bf16[256,1536]{1,0:T(8,128)(2,1)}, u32[]{:S(2)}, u32[]{:S(2)}) %collective-permute-start.41) | collective-permute-done | bytes 786464 | tf_op jit(solution)/shard_map/ppermute | solution.py:511
  634.3 2.2 collective-permute-start.44
  640.4 15.5 %collective-permute-done.44.refs_1_ = bf16[128,1536]{1,0:T(8,128)(2,1)S(1)} collective-permute-done((bf16[128,1536]{1,0:T(8,128)(2,1)S(1)}, bf16[128,1536]{1,0:T(8,128)(2,1)S(1)}, u32[]{:S(2)}, u32[]{:S(2)}) %collective-permute-start.44) | collective-permute-done | bytes 393248 | tf_op jit(solution)/shard_map/ppermute | solution.py:511
  656.1 2.1 collective-permute-done.46.refs_1_
  666.2 2.2 collective-permute-start.47
  668.3 5.7 collective-permute-done.48.refs_1_
  (332 shorter events, 93.9 us)
Async XLA Ops:
  7.2 99.6 %all-gather.3.cloned.1.call-start = ((), (), s32[]{:S(2)}) async-start(), calls=%async_computation | async-start | bytes 11698176 | tf_op jit(solution)/shard_map/all_gather | solution.py:540
  12.9 300.4 %all-gather.5.cloned.1.call-start = ((), (), s32[]{:S(2)}) async-start(), calls=%async_computation.1 | async-start | bytes 36765696 | tf_op jit(solution)/shard_map/all_gather | solution.py:544
  24.0 85.0 %copy-start.6 = (bf16[5,64,2048]{2,1,0:T(8,128)(2,1)}, bf16[5,64,2048]{2,1,0:T(8,128)(2,1)S(1)}, u32[]{:S(2)}) copy-start(bf16[5,64,2048]{2,1,0:T(8,128)(2,1)S(1)} %get-tuple-element.376) | copy-start | bytes 3932164
  24.0 229.9 %copy-start.11 = (bf16[5,64,2048]{2,1,0:T(8,128)(2,1)}, bf16[5,64,2048]{2,1,0:T(8,128)(2,1)S(1)}, u32[]{:S(2)}) copy-start(bf16[5,64,2048]{2,1,0:T(8,128)(2,1)S(1)} %get-tuple-element.375) | copy-start | bytes 3932164
  116.0 122.5 %copy-start.59 = (bf16[320,1024]{1,0:T(8,128)(2,1)}, bf16[320,1024]{1,0:T(8,128)(2,1)S(1)}, u32[]{:S(2)}) copy-start(bf16[320,1024]{1,0:T(8,128)(2,1)S(1)} %get-tuple-element.168.q_ref.refs_0_) | copy-start | bytes 1966084
  116.0 25.1 %collective-permute-start = (bf16[1,5,64,512]{3,2,1,0:T(8,128)(2,1)S(1)}, bf16[1,5,64,512]{3,2,1,0:T(8,128)(2,1)S(1)}, u32[]{:S(2)}, u32[]{:S(2)}) collective-permute-start(bf16[1,5,64,512]{3,2,1,0:T(8,128)(2,1)S(1)} %bitcast.59), channel_id=1, source_target_pairs={{0,16},{2,18},{4,20},{6,22},{8,24},{10,26},{12,28},{14,30},{16,0},... | collective-permute-start | bytes 983048 | tf_op jit(solution)/shard_map/ppermute | solution.py:511
  141.2 31.3 %collective-permute-start.1 = (bf16[2,5,64,512]{3,2,1,0:T(8,128)(2,1)S(1)}, bf16[2,5,64,512]{3,2,1,0:T(8,128)(2,1)S(1)}, u32[]{:S(2)}, u32[]{:S(2)}) collective-permute-start(bf16[2,5,64,512]{3,2,1,0:T(8,128)(2,1)S(1)} %pad_maximum_fusion.10), channel_id=1, source_target_pairs={{0,8},{2,10},{4,12},{6,14},{8,0},{10,2},{12,4},{14,6},{16,24},{18,... | collective-permute-start | bytes 1966088 | tf_op jit(solution)/shard_map/ppermute | solution.py:511
  172.5 60.8 %copy-start.79 = (s32[16]{0:T(128)S(1)}, s32[16]{0:T(128)}, u32[]{:S(2)}) copy-start(s32[16]{0:T(128)} %constant.56.clone) | copy-start | bytes 196
  172.6 59.0 %collective-permute-start.2 = (bf16[4,5,64,512]{3,2,1,0:T(8,128)(2,1)S(1)}, bf16[4,5,64,512]{3,2,1,0:T(8,128)(2,1)S(1)}, u32[]{:S(2)}, u32[]{:S(2)}) collective-permute-start(bf16[4,5,64,512]{3,2,1,0:T(8,128)(2,1)S(1)} %pad_maximum_fusion.7), channel_id=1, source_target_pairs={{0,4},{2,6},{4,0},{6,2},{8,12},{10,14},{12,8},{14,10},{16,20},{18,... | collective-permute-start | bytes 3932168 | tf_op jit(solution)/shard_map/ppermute | solution.py:511
  233.2 5.3 collective-permute-start.3
  248.2 9.9 %copy-start.43 = (bf16[320,1024]{1,0:T(8,128)(2,1)}, bf16[320,1024]{1,0:T(8,128)(2,1)S(1)}, u32[]{:S(2)}) copy-start(bf16[320,1024]{1,0:T(8,128)(2,1)S(1)} %get-tuple-element.170) | copy-start | bytes 1966084
  252.4 30.7 %copy-start.7 = (bf16[5,64,2048]{2,1,0:T(8,128)(2,1)S(1)}, bf16[5,64,2048]{2,1,0:T(8,128)(2,1)}, u32[]{:S(2)}) copy-start(bf16[5,64,2048]{2,1,0:T(8,128)(2,1)} %copy-done.6) | copy-start | bytes 3932164
  252.4 30.7 %collective-permute-start.4 = (bf16[320,2048]{1,0:T(8,128)(2,1)S(1)}, bf16[320,2048]{1,0:T(8,128)(2,1)S(1)}, u32[]{:S(2)}, u32[]{:S(2)}) collective-permute-start(bf16[320,2048]{1,0:T(8,128)(2,1)S(1)} %fusion.6), channel_id=1, source_target_pairs={{0,1},{1,0},{2,3},{3,2},{4,5},{5,4},{6,7},{7,6},{8,9},{9,8},{10,11... | collective-permute-start | bytes 3932168 | tf_op jit(solution)/shard_map/ppermute | solution.py:514
  255.8 31.3 %collective-permute-start.5 = (bf16[320,1024]{1,0:T(8,128)(2,1)S(1)}, bf16[320,1024]{1,0:T(8,128)(2,1)S(1)}, u32[]{:S(2)}, u32[]{:S(2)}) collective-permute-start(bf16[320,1024]{1,0:T(8,128)(2,1)S(1)} %get-tuple-element.171), channel_id=1, source_target_pairs={{0,2},{2,0},{4,6},{6,4},{8,10},{10,8},{12,14},{14,12},{16,18},{18,... | collective-permute-start | bytes 1966088 | tf_op jit(solution)/shard_map/ppermute | solution.py:511
  257.5 29.6 %collective-permute-start.7 = (bf16[320,1024]{1,0:T(8,128)(2,1)S(1)}, bf16[320,1024]{1,0:T(8,128)(2,1)S(1)}, u32[]{:S(2)}, u32[]{:S(2)}) collective-permute-start(bf16[320,1024]{1,0:T(8,128)(2,1)S(1)} %get-tuple-element.173), channel_id=1, source_target_pairs={{0,2},{2,0},{4,6},{6,4},{8,10},{10,8},{12,14},{14,12},{16,18},{18,... | collective-permute-start | bytes 1966088 | tf_op jit(solution)/shard_map/ppermute | solution.py:511
  258.0 29.1 %collective-permute-start.8 = (bf16[320,1024]{1,0:T(8,128)(2,1)S(1)}, bf16[320,1024]{1,0:T(8,128)(2,1)S(1)}, u32[]{:S(2)}, u32[]{:S(2)}) collective-permute-start(bf16[320,1024]{1,0:T(8,128)(2,1)S(1)} %get-tuple-element.170), channel_id=1, source_target_pairs={{0,2},{2,0},{4,6},{6,4},{8,10},{10,8},{12,14},{14,12},{16,18},{18,... | collective-permute-start | bytes 1966088 | tf_op jit(solution)/shard_map/ppermute | solution.py:511
  287.1 2.1 collective-permute-start.6
  323.2 8.2 %collective-permute-start.10 = (bf16[320,1536]{1,0:T(8,128)(2,1)S(1)}, bf16[320,1536]{1,0:T(8,128)(2,1)S(1)}, u32[]{:S(2)}, u32[]{:S(2)}) collective-permute-start(bf16[320,1536]{1,0:T(8,128)(2,1)S(1)} %get-tuple-element.174), channel_id=1, source_target_pairs={{0,2},{2,0},{4,6},{6,4},{8,10},{10,8},{12,14},{14,12},{16,18},{18,... | collective-permute-start | bytes 2949128 | tf_op jit(solution)/shard_map/ppermute | solution.py:511
  331.1 4.7 collective-permute-start.9
  335.6 36.6 %collective-permute-start.11 = (bf16[512,1536]{1,0:T(8,128)(2,1)S(1)}, bf16[512,1536]{1,0:T(8,128)(2,1)S(1)}, u32[]{:S(2)}, u32[]{:S(2)}) collective-permute-start(bf16[512,1536]{1,0:T(8,128)(2,1)S(1)} %get-tuple-element.189), channel_id=1, source_target_pairs={{0,4},{2,6},{4,0},{6,2},{8,12},{10,14},{12,8},{14,10},{16,20},{18,... | collective-permute-start | bytes 4718600 | tf_op jit(solution)/shard_map/ppermute | solution.py:511
  372.6 68.0 %copy-start = (bf16[2,320,2816]{2,1,0:T(8,128)(2,1)}, bf16[2,320,2816]{2,1,0:T(8,128)(2,1)S(1)}, u32[]{:S(2)}) copy-start(bf16[2,320,2816]{2,1,0:T(8,128)(2,1)S(1)} %get-tuple-element.197.refs_2_) | copy-start | bytes 10813444
  372.7 6.4 collective-permute-start.14
  372.7 31.6 %collective-permute-start.13 = (bf16[512,1280]{1,0:T(8,128)(2,1)S(1)}, bf16[512,1280]{1,0:T(8,128)(2,1)S(1)}, u32[]{:S(2)}, u32[]{:S(2)}) collective-permute-start(bf16[512,1280]{1,0:T(8,128)(2,1)S(1)} %get-tuple-element.195), channel_id=1, source_target_pairs={{0,4},{2,6},{4,0},{6,2},{8,12},{10,14},{12,8},{14,10},{16,20},{18,... | collective-permute-start | bytes 3932168 | tf_op jit(solution)/shard_map/ppermute | solution.py:511
  373.1 31.6 %collective-permute-start.12 = (bf16[320,2048]{1,0:T(8,128)(2,1)S(1)}, bf16[320,2048]{1,0:T(8,128)(2,1)S(1)}, u32[]{:S(2)}, u32[]{:S(2)}) collective-permute-start(bf16[320,2048]{1,0:T(8,128)(2,1)S(1)} %get-tuple-element.193.refs_0_), channel_id=1, source_target_pairs={{0,1},{1,0},{2,3},{3,2},{4,5},{5,4},{6,7},{7,6},{8,9},{9,8},{10,11... | collective-permute-start | bytes 3932168 | tf_op jit(solution)/shard_map/ppermute | solution.py:514
  379.0 61.6 %copy-start.3 = (bf16[2,320,2816]{2,1,0:T(8,128)(2,1)}, bf16[2,320,2816]{2,1,0:T(8,128)(2,1)S(1)}, u32[]{:S(2)}) copy-start(bf16[2,320,2816]{2,1,0:T(8,128)(2,1)S(1)} %collective-permute-done.14.refs_3_) | copy-start | bytes 10813444
  383.2 54.5 %collective-permute-start.18 = (bf16[512,1536]{1,0:T(8,128)(2,1)S(1)}, bf16[512,1536]{1,0:T(8,128)(2,1)S(1)}, u32[]{:S(2)}, u32[]{:S(2)}) collective-permute-start(bf16[512,1536]{1,0:T(8,128)(2,1)S(1)} %get-tuple-element.212), channel_id=1, source_target_pairs={{0,4},{2,6},{4,0},{6,2},{8,12},{10,14},{12,8},{14,10},{16,20},{18,... | collective-permute-start | bytes 4718600 | tf_op jit(solution)/shard_map/ppermute | solution.py:511
  383.5 30.1 %collective-permute-start.15 = (bf16[256,1536]{1,0:T(8,128)(2,1)S(1)}, bf16[256,1536]{1,0:T(8,128)(2,1)S(1)}, u32[]{:S(2)}, u32[]{:S(2)}) collective-permute-start(bf16[256,1536]{1,0:T(8,128)(2,1)S(1)} %get-tuple-element.203), channel_id=1, source_target_pairs={{0,8},{2,10},{4,12},{6,14},{8,0},{10,2},{12,4},{14,6},{16,24},{18,... | collective-permute-start | bytes 2359304 | tf_op jit(solution)/shard_map/ppermute | solution.py:511
  409.5 4.2 collective-permute-start.16
  409.6 30.1 %collective-permute-start.17 = (bf16[256,1280]{1,0:T(8,128)(2,1)S(1)}, bf16[256,1280]{1,0:T(8,128)(2,1)S(1)}, u32[]{:S(2)}, u32[]{:S(2)}) collective-permute-start(bf16[256,1280]{1,0:T(8,128)(2,1)S(1)} %get-tuple-element.210), channel_id=1, source_target_pairs={{0,8},{2,10},{4,12},{6,14},{8,0},{10,2},{12,4},{14,6},{16,24},{18,... | collective-permute-start | bytes 1966088 | tf_op jit(solution)/shard_map/ppermute | solution.py:511
  413.8 13.5 %copy-start.47 = (bf16[320,1024]{1,0:T(8,128)(2,1)}, bf16[320,1024]{1,0:T(8,128)(2,1)S(1)}, u32[]{:S(2)}) copy-start(bf16[320,1024]{1,0:T(8,128)(2,1)S(1)} %collective-permute-done.16.refs_10_.refs_1_) | copy-start | bytes 1966084
  427.3 11.6 %copy-start.35 = (bf16[320,1024]{1,0:T(8,128)(2,1)}, bf16[320,1024]{1,0:T(8,128)(2,1)S(1)}, u32[]{:S(2)}) copy-start(bf16[320,1024]{1,0:T(8,128)(2,1)S(1)} %get-tuple-element.221) | copy-start | bytes 1966084
  440.6 4.9 collective-permute-start.19
  446.5 31.6 %collective-permute-start.21 = (bf16[1280,512]{1,0:T(8,128)(2,1)S(1)}, bf16[1280,512]{1,0:T(8,128)(2,1)S(1)}, u32[]{:S(2)}, u32[]{:S(2)}) collective-permute-start(bf16[1280,512]{1,0:T(8,128)(2,1)S(1)} %get-tuple-element.223), channel_id=1, source_target_pairs={{0,4},{2,6},{4,0},{6,2},{8,12},{10,14},{12,8},{14,10},{16,20},{18,... | collective-permute-start | bytes 3932168 | tf_op jit(solution)/shard_map/ppermute | solution.py:511
  446.8 20.7 %collective-permute-start.22 = (bf16[128,1536]{1,0:T(8,128)(2,1)S(1)}, bf16[128,1536]{1,0:T(8,128)(2,1)S(1)}, u32[]{:S(2)}, u32[]{:S(2)}) collective-permute-start(bf16[128,1536]{1,0:T(8,128)(2,1)S(1)} %get-tuple-element.225), channel_id=1, source_target_pairs={{0,16},{2,18},{4,20},{6,22},{8,24},{10,26},{12,28},{14,30},{16,0},... | collective-permute-start | bytes 1179656 | tf_op jit(solution)/shard_map/ppermute | solution.py:511
  446.8 41.3 %collective-permute-start.25 = (bf16[256,1536]{1,0:T(8,128)(2,1)}, bf16[256,1536]{1,0:T(8,128)(2,1)}, u32[]{:S(2)}, u32[]{:S(2)}) collective-permute-start(bf16[256,1536]{1,0:T(8,128)(2,1)} %get-tuple-element.233), channel_id=1, source_target_pairs={{0,8},{2,10},{4,12},{6,14},{8,0},{10,2},{12,4},{14,6},{16,24},{18,... | collective-permute-start | bytes 2359304 | tf_op jit(solution)/shard_map/ppermute | solution.py:511
  450.0 55.9 %collective-permute-start.24 = (bf16[512,1280]{1,0:T(8,128)(2,1)}, bf16[512,1280]{1,0:T(8,128)(2,1)}, u32[]{:S(2)}, u32[]{:S(2)}) collective-permute-start(bf16[512,1280]{1,0:T(8,128)(2,1)} %get-tuple-element.231), channel_id=1, source_target_pairs={{0,4},{2,6},{4,0},{6,2},{8,12},{10,14},{12,8},{14,10},{16,20},{18,... | collective-permute-start | bytes 3932168 | tf_op jit(solution)/shard_map/ppermute | solution.py:511
  468.4 13.1 %copy-start.73 = (bf16[6,64,2048]{2,1,0:T(8,128)(2,1)S(1)}, bf16[6,64,2048]{2,1,0:T(8,128)(2,1)}, u32[]{:S(2)}) copy-start(bf16[6,64,2048]{2,1,0:T(8,128)(2,1)} %param.15) | copy-start | bytes 4718596
  480.0 27.5 %collective-permute-start.23 = (bf16[640,512]{1,0:T(8,128)(2,1)}, bf16[640,512]{1,0:T(8,128)(2,1)}, u32[]{:S(2)}, u32[]{:S(2)}) collective-permute-start(bf16[640,512]{1,0:T(8,128)(2,1)} %get-tuple-element.229), channel_id=1, source_target_pairs={{0,8},{2,10},{4,12},{6,14},{8,0},{10,2},{12,4},{14,6},{16,24},{18,... | collective-permute-start | bytes 1966088 | tf_op jit(solution)/shard_map/ppermute | solution.py:511
  480.0 49.2 %collective-permute-start.20 = (bf16[320,2048]{1,0:T(8,128)(2,1)}, bf16[320,2048]{1,0:T(8,128)(2,1)}, u32[]{:S(2)}, u32[]{:S(2)}) collective-permute-start(bf16[320,2048]{1,0:T(8,128)(2,1)} %get-tuple-element.220), channel_id=1, source_target_pairs={{0,1},{1,0},{2,3},{3,2},{4,5},{5,4},{6,7},{7,6},{8,9},{9,8},{10,11... | collective-permute-start | bytes 3932168 | tf_op jit(solution)/shard_map/ppermute | solution.py:514
  484.8 27.7 %collective-permute-start.27 = (bf16[128,1280]{1,0:T(8,128)(2,1)}, bf16[128,1280]{1,0:T(8,128)(2,1)S(1)}, u32[]{:S(2)}, u32[]{:S(2)}) collective-permute-start(bf16[128,1280]{1,0:T(8,128)(2,1)} %copy-done.54), channel_id=1, source_target_pairs={{0,16},{2,18},{4,20},{6,22},{8,24},{10,26},{12,28},{14,30},{16,0},... | collective-permute-start | bytes 983048 | tf_op jit(solution)/shard_map/ppermute | solution.py:511
  508.8 17.5 %collective-permute-start.26 = (bf16[320,512]{1,0:T(8,128)(2,1)S(1)}, bf16[320,512]{1,0:T(8,128)(2,1)S(1)}, u32[]{:S(2)}, u32[]{:S(2)}) collective-permute-start(bf16[320,512]{1,0:T(8,128)(2,1)S(1)} %get-tuple-element.239), channel_id=1, source_target_pairs={{0,16},{2,18},{4,20},{6,22},{8,24},{10,26},{12,28},{14,30},{16,0},... | collective-permute-start | bytes 983048 | tf_op jit(solution)/shard_map/ppermute | solution.py:511
  508.9 32.5 %collective-permute-start.29 = (bf16[256,1280]{1,0:T(8,128)(2,1)S(1)}, bf16[256,1280]{1,0:T(8,128)(2,1)S(1)}, u32[]{:S(2)}, u32[]{:S(2)}) collective-permute-start(bf16[256,1280]{1,0:T(8,128)(2,1)S(1)} %get-tuple-element.249), channel_id=1, source_target_pairs={{0,8},{2,10},{4,12},{6,14},{8,0},{10,2},{12,4},{14,6},{16,24},{18,... | collective-permute-start | bytes 1966088 | tf_op jit(solution)/shard_map/ppermute | solution.py:511
  512.2 50.9 %collective-permute-start.34 = (bf16[512,1536]{1,0:T(8,128)(2,1)}, bf16[512,1536]{1,0:T(8,128)(2,1)}, u32[]{:S(2)}, u32[]{:S(2)}) collective-permute-start(bf16[512,1536]{1,0:T(8,128)(2,1)} %get-tuple-element.264), channel_id=1, source_target_pairs={{0,4},{2,6},{4,0},{6,2},{8,12},{10,14},{12,8},{14,10},{16,20},{18,... | collective-permute-start | bytes 4718600 | tf_op jit(solution)/shard_map/ppermute | solution.py:511
  512.5 66.5 %collective-permute-start.32 = (bf16[128,1536]{1,0:T(8,128)(2,1)}, bf16[128,1536]{1,0:T(8,128)(2,1)}, u32[]{:S(2)}, u32[]{:S(2)}) collective-permute-start(bf16[128,1536]{1,0:T(8,128)(2,1)} %get-tuple-element.260), channel_id=1, source_target_pairs={{0,16},{2,18},{4,20},{6,22},{8,24},{10,26},{12,28},{14,30},{16,0},... | collective-permute-start | bytes 1179656 | tf_op jit(solution)/shard_map/ppermute | solution.py:511
  529.2 12.5 %collective-permute-start.28 = (bf16[320,1536]{1,0:T(8,128)(2,1)S(1)}, bf16[320,1536]{1,0:T(8,128)(2,1)S(1)}, u32[]{:S(2)}, u32[]{:S(2)}) collective-permute-start(bf16[320,1536]{1,0:T(8,128)(2,1)S(1)} %get-tuple-element.365.refs_0_), channel_id=1, source_target_pairs={{0,2},{2,0},{4,6},{6,4},{8,10},{10,8},{12,14},{14,12},{16,18},{18,... | collective-permute-start | bytes 2949128 | tf_op jit(solution)/shard_map/ppermute | solution.py:511
  536.7 37.4 %collective-permute-start.33 = (bf16[512,1024]{1,0:T(8,128)(2,1)}, bf16[512,1024]{1,0:T(8,128)(2,1)}, u32[]{:S(2)}, u32[]{:S(2)}) collective-permute-start(bf16[512,1024]{1,0:T(8,128)(2,1)} %get-tuple-element.262), channel_id=1, source_target_pairs={{0,8},{2,10},{4,12},{6,14},{8,0},{10,2},{12,4},{14,6},{16,24},{18,... | collective-permute-start | bytes 3145736 | tf_op jit(solution)/shard_map/ppermute | solution.py:511
  547.7 37.6 %collective-permute-start.31 = (bf16[512,1536]{1,0:T(8,128)(2,1)}, bf16[512,1536]{1,0:T(8,128)(2,1)}, u32[]{:S(2)}, u32[]{:S(2)}) collective-permute-start(bf16[512,1536]{1,0:T(8,128)(2,1)} %get-tuple-element.258), channel_id=1, source_target_pairs={{0,4},{2,6},{4,0},{6,2},{8,12},{10,14},{12,8},{14,10},{16,20},{18,... | collective-permute-start | bytes 4718600 | tf_op jit(solution)/shard_map/ppermute | solution.py:511
  556.0 31.9 %collective-permute-start.30 = (bf16[320,2048]{1,0:T(8,128)(2,1)}, bf16[320,2048]{1,0:T(8,128)(2,1)}, u32[]{:S(2)}, u32[]{:S(2)}) collective-permute-start(bf16[320,2048]{1,0:T(8,128)(2,1)} %get-tuple-element.255.refs_0_), channel_id=1, source_target_pairs={{0,1},{1,0},{2,3},{3,2},{4,5},{5,4},{6,7},{7,6},{8,9},{9,8},{10,11... | collective-permute-start | bytes 3932168 | tf_op jit(solution)/shard_map/ppermute | solution.py:514
  563.1 48.7 %collective-permute-start.42 = (bf16[128,1280]{1,0:T(8,128)(2,1)}, bf16[128,1280]{1,0:T(8,128)(2,1)}, u32[]{:S(2)}, u32[]{:S(2)}) collective-permute-start(bf16[128,1280]{1,0:T(8,128)(2,1)} %copy-done.53), channel_id=1, source_target_pairs={{0,16},{2,18},{4,20},{6,22},{8,24},{10,26},{12,28},{14,30},{16,0},... | collective-permute-start | bytes 983048 | tf_op jit(solution)/shard_map/ppermute | solution.py:511
  574.1 33.0 %collective-permute-start.37 = (bf16[256,1536]{1,0:T(8,128)(2,1)S(1)}, bf16[256,1536]{1,0:T(8,128)(2,1)S(1)}, u32[]{:S(2)}, u32[]{:S(2)}) collective-permute-start(bf16[256,1536]{1,0:T(8,128)(2,1)S(1)} %get-tuple-element.277), channel_id=1, source_target_pairs={{0,8},{2,10},{4,12},{6,14},{8,0},{10,2},{12,4},{14,6},{16,24},{18,... | collective-permute-start | bytes 2359304 | tf_op jit(solution)/shard_map/ppermute | solution.py:511
  579.0 54.8 %collective-permute-start.39 = (bf16[512,1280]{1,0:T(8,128)(2,1)}, bf16[512,1280]{1,0:T(8,128)(2,1)S(1)}, u32[]{:S(2)}, u32[]{:S(2)}) collective-permute-start(bf16[512,1280]{1,0:T(8,128)(2,1)} %get-tuple-element.283), channel_id=1, source_target_pairs={{0,4},{2,6},{4,0},{6,2},{8,12},{10,14},{12,8},{14,10},{16,20},{18,... | collective-permute-start | bytes 3932168 | tf_op jit(solution)/shard_map/ppermute | solution.py:511
  580.8 10.7 %copy-start.66 = (f32[320,2048]{1,0:T(8,128)S(1)}, f32[320,2048]{1,0:T(8,128)}, u32[]{:S(2)}) copy-start(f32[320,2048]{1,0:T(8,128)} %copy-done.65) | copy-start | bytes 7864324
  585.4 22.6 %collective-permute-start.36 = (bf16[256,1024]{1,0:T(8,128)(2,1)S(1)}, bf16[256,1024]{1,0:T(8,128)(2,1)S(1)}, u32[]{:S(2)}, u32[]{:S(2)}) collective-permute-start(bf16[256,1024]{1,0:T(8,128)(2,1)S(1)} %get-tuple-element.275), channel_id=1, source_target_pairs={{0,16},{2,18},{4,20},{6,22},{8,24},{10,26},{12,28},{14,30},{16,0},... | collective-permute-start | bytes 1572872 | tf_op jit(solution)/shard_map/ppermute | solution.py:511
  588.0 43.3 %collective-permute-start.41 = (bf16[256,1536]{1,0:T(8,128)(2,1)}, bf16[256,1536]{1,0:T(8,128)(2,1)}, u32[]{:S(2)}, u32[]{:S(2)}) collective-permute-start(bf16[256,1536]{1,0:T(8,128)(2,1)} %get-tuple-element.287), channel_id=1, source_target_pairs={{0,8},{2,10},{4,12},{6,14},{8,0},{10,2},{12,4},{14,6},{16,24},{18,... | collective-permute-start | bytes 2359304 | tf_op jit(solution)/shard_map/ppermute | solution.py:511
  607.9 24.7 %collective-permute-start.40 = (bf16[128,1536]{1,0:T(8,128)(2,1)}, bf16[128,1536]{1,0:T(8,128)(2,1)}, u32[]{:S(2)}, u32[]{:S(2)}) collective-permute-start(bf16[128,1536]{1,0:T(8,128)(2,1)} %get-tuple-element.285), channel_id=1, source_target_pairs={{0,16},{2,18},{4,20},{6,22},{8,24},{10,26},{12,28},{14,30},{16,0},... | collective-permute-start | bytes 1179656 | tf_op jit(solution)/shard_map/ppermute | solution.py:511
  609.5 28.2 %collective-permute-start.38 = (bf16[128,1024]{1,0:T(8,128)(2,1)}, bf16[128,1024]{1,0:T(8,128)(2,1)}, u32[]{:S(2)}, u32[]{:S(2)}) collective-permute-start(bf16[128,1024]{1,0:T(8,128)(2,1)} %get-tuple-element.281), channel_id=1, source_target_pairs={{0,4},{2,6},{4,0},{6,2},{8,12},{10,14},{12,8},{14,10},{16,20},{18,... | collective-permute-start | bytes 786440 | tf_op jit(solution)/shard_map/ppermute | solution.py:511
  612.8 19.9 %copy-start.58 = (bf16[128,1536]{1,0:T(8,128)(2,1)S(1)}, bf16[128,1536]{1,0:T(8,128)(2,1)}, u32[]{:S(2)}) copy-start(bf16[128,1536]{1,0:T(8,128)(2,1)} %copy-done.57) | copy-start | bytes 1179652
  634.1 24.1 %collective-permute-start.46 = (bf16[256,1280]{1,0:T(8,128)(2,1)S(1)}, bf16[256,1280]{1,0:T(8,128)(2,1)S(1)}, u32[]{:S(2)}, u32[]{:S(2)}) collective-permute-start(bf16[256,1280]{1,0:T(8,128)(2,1)S(1)} %get-tuple-element.305), channel_id=1, source_target_pairs={{0,8},{2,10},{4,12},{6,14},{8,0},{10,2},{12,4},{14,6},{16,24},{18,... | collective-permute-start | bytes 1966088 | tf_op jit(solution)/shard_map/ppermute | solution.py:511
  634.2 4.5 collective-permute-start.35
  634.3 21.7 %collective-permute-start.44 = (bf16[128,1536]{1,0:T(8,128)(2,1)S(1)}, bf16[128,1536]{1,0:T(8,128)(2,1)S(1)}, u32[]{:S(2)}, u32[]{:S(2)}) collective-permute-start(bf16[128,1536]{1,0:T(8,128)(2,1)S(1)} %get-tuple-element.299), channel_id=1, source_target_pairs={{0,16},{2,18},{4,20},{6,22},{8,24},{10,26},{12,28},{14,30},{16,0},... | collective-permute-start | bytes 1179656 | tf_op jit(solution)/shard_map/ppermute | solution.py:511
  638.7 17.4 %collective-permute-start.43 = (f32[4,256]{1,0:T(4,128)S(1)}, f32[4,256]{1,0:T(4,128)S(1)}, u32[]{:S(2)}, u32[]{:S(2)}) collective-permute-start(f32[4,256]{1,0:T(4,128)S(1)} %get-tuple-element.297), channel_id=1, source_target_pairs={{0,4},{2,6},{4,0},{6,2},{8,12},{10,14},{12,8},{14,10},{16,20},{18,... | collective-permute-start | bytes 12296 | tf_op jit(solution)/shard_map/ppermute | solution.py:511
  658.3 15.7 %collective-permute-start.48 = (bf16[128,1280]{1,0:T(8,128)(2,1)S(1)}, bf16[128,1280]{1,0:T(8,128)(2,1)S(1)}, u32[]{:S(2)}, u32[]{:S(2)}) collective-permute-start(bf16[128,1280]{1,0:T(8,128)(2,1)S(1)} %get-tuple-element.311), channel_id=1, source_target_pairs={{0,16},{2,18},{4,20},{6,22},{8,24},{10,26},{12,28},{14,30},{16,0},... | collective-permute-start | bytes 983048 | tf_op jit(solution)/shard_map/ppermute | solution.py:511
  662.6 3.6 collective-permute-start.45
  666.2 7.9 %collective-permute-start.47 = (f32[1,256]{1,0:T(1,128)S(1)}, f32[1,256]{1,0:T(1,128)S(1)}, u32[]{:S(2)}, u32[]{:S(2)}) collective-permute-start(f32[1,256]{1,0:T(1,128)S(1)} %get-tuple-element.309), channel_id=1, source_target_pairs={{0,16},{2,18},{4,20},{6,22},{8,24},{10,26},{12,28},{14,30},{16,0},... | collective-permute-start | bytes 3080 | tf_op jit(solution)/shard_map/ppermute | solution.py:511
  (69 other events, 217.6 us)
Sparse Core Ops, SparseCore 0:
  13.0 93.7 all-gather.2
  108.4 204.7 all-gather.4
